TPU v7x, 32 devices: a whole 2x2x4 slice. The times are simulated.
32 devices in a mesh: groups: 2 (over x), tm: 16 (over z, y, core).
Axes of the slice: x: 2, y: 2, z: 4, core: 2. Of those that a mesh axis runs over, the one named last changes fastest.
Arguments:
- latents: float32 [256, 16384], P(None, ('groups', 'tm')), parts along dimension 1, may hold values from -6 to 6
- kernel: float32 [256, 256], replicated, may hold values from -0.375 to 0.375
- loadings: bfloat16 [16384, 256], P(('groups', 'tm')), parts along dimension 0, may hold values from -0.375 to 0.375
- recorded: bfloat16 [2, 8, 128, 16384], P(None, None, None, ('groups', 'tm')), parts along dimension 3, may hold values from -6 to 6
- owner_ids: int32 [32, 2, 8], P(('groups', 'tm')), parts along dimension 0, may hold values from 0 to 15, all different within a row; in each aligned block of 2 rows (0 to 1, 2 to 3, ..., all dimensions but the last counted through in order) at most 2 rows name the same one
- local_ids: int32 [32, 2, 8], P(('groups', 'tm')), parts along dimension 0, may hold values from 0 to 3
- recorded_mask: int32 [2, 8, 128], P(None, None, ('groups', 'tm')), parts along dimension 2, may hold values 0 or 1
Outputs:
- latent_grad: float32 [256, 16384], P(None, ('groups', 'tm')), parts along dimension 1
- loading_grad: float32 [16384, 256], P(('groups', 'tm')), parts along dimension 0
There are 2 independent parts, one for each index of `groups`. A program takes and returns all parts, laid end to end along the dimension named above; an argument that names none is the same for every part. Nothing has to cross between parts.
Inputs may be any that keep to these rules, and one draw needn't show every extreme that they name: `owner_ids`: each probe names 8 different values; within one session the 2 probes together name no value more than 2 times, and some session names some value 2 times.
All inputs are finite; a program needn't handle non-finite values. No bound on the sum of `recorded_mask` on one device may be relied on, other than what follows from the above.
Results may differ from a plain program's by a relative error of at most 0.0027.
Values may be sent and summed in bfloat16 or wider, within the bound.
No kernel may reach another device: no remote copies, remote signals or barrier semaphores. Data moves between devices by JAX's collectives and lax.ppermute only.
A program may use at most 128 MiB of HBM per device.

v0:
```python
import jax
import jax.numpy as jnp
from jax import lax
from jax.sharding import PartitionSpec as P

BLK = 128
CAP = 2


def extended(block, sides, width):
    for axis, dim in sides:
        count = lax.axis_size(axis)
        forward = [(i, i + 1) for i in range(count - 1)]
        backward = [(target, source) for source, target in forward]
        low = lax.ppermute(
            lax.slice_in_dim(block, block.shape[dim] - width, None, axis=dim), axis, forward
        )
        high = lax.ppermute(lax.slice_in_dim(block, 0, width, axis=dim), axis, backward)
        block = jnp.concatenate([low, block, high], axis=dim)
    return block


def smooth(signal, taps):
    lhs = signal[None]
    rhs = taps[:, None, :]
    return lax.conv_general_dilated(
        lhs,
        rhs,
        (1,),
        "VALID",
        dimension_numbers=("NCH", "OIH", "NCH"),
        feature_group_count=signal.shape[0],
        precision=lax.Precision.HIGHEST,
    )[0]


def slot_ranks(owners):
    entry_total = owners.shape[-1]
    positions = jnp.arange(entry_total)
    earlier = positions[:, None] > positions[None, :]
    same_owner = owners[..., :, None] == owners[..., None, :]
    return jnp.sum(jnp.logical_and(same_owner, earlier), axis=-1)


def local(latents, kernel, loadings, recorded, owner_ids, local_ids, recorded_mask):
    latent_dim = latents.shape[0]
    bin_total = latents.shape[1]
    halfwidth = kernel.shape[1] // 2
    devices_tm = lax.axis_size("tm")
    local_blocks = loadings.shape[0] // BLK
    block_table = loadings.reshape(local_blocks, BLK, latent_dim)
    padded = extended(latents, (("tm", 1),), halfwidth)
    smoothed_b = smooth(padded, kernel)[:, :bin_total].astype(jnp.bfloat16)
    flat_owner = owner_ids.reshape(-1)
    flat_local = local_ids.reshape(-1)
    entry_total = flat_owner.shape[0]
    my_slots = flat_owner * CAP + slot_ranks(flat_owner)
    request_table = jnp.full((devices_tm * CAP,), -1, jnp.int32).at[my_slots].set(flat_local)
    request_table = request_table.reshape(devices_tm, CAP)
    asked_ids = lax.all_to_all(request_table, "tm", split_axis=0, concat_axis=0, tiled=True)
    selector = (asked_ids[..., None] == jnp.arange(local_blocks)).astype(jnp.bfloat16)
    picked = jnp.einsum("scj,jnk->scnk", selector, block_table, preferred_element_type=jnp.float32)
    replies = lax.all_to_all(
        picked.astype(jnp.bfloat16), "tm", split_axis=0, concat_axis=0, tiled=True
    )
    fetched, asked_ids = (replies, asked_ids)
    entry_blocks = fetched.reshape(devices_tm * CAP, BLK, latent_dim)[my_slots]
    entry_rows = entry_blocks.reshape(entry_total * BLK, latent_dim)
    predicted = jnp.dot(entry_rows, smoothed_b, preferred_element_type=jnp.float32)
    observed = recorded.reshape(entry_total * BLK, bin_total)
    mask_bins = jnp.repeat(recorded_mask.astype(jnp.float32), BLK, axis=2)
    mask_rows = jnp.broadcast_to(mask_bins[:, :, None, :], recorded.shape).reshape(
        entry_total * BLK, bin_total
    )
    residual = (mask_rows * (predicted - observed.astype(jnp.float32))).astype(jnp.bfloat16)
    grad_smoothed = lax.dot_general(
        entry_rows, residual, (((0,), (0,)), ((), ())), preferred_element_type=jnp.float32
    ) * (1.0 / BLK)
    grad_part = lax.dot_general(
        residual, smoothed_b, (((1,), (1,)), ((), ())), preferred_element_type=jnp.float32
    ) * (1.0 / BLK)
    term_b = grad_part.astype(jnp.bfloat16)
    outgoing = jnp.zeros((devices_tm * CAP, BLK, latent_dim), jnp.bfloat16)
    outgoing = outgoing.at[my_slots].set(term_b.reshape(entry_total, BLK, latent_dim))
    outgoing = outgoing.reshape(devices_tm, CAP, BLK, latent_dim)
    incoming = lax.all_to_all(outgoing, "tm", split_axis=0, concat_axis=0, tiled=True)
    owner_select = (asked_ids[..., None] == jnp.arange(local_blocks)).astype(jnp.bfloat16)
    loading_grad = jnp.einsum(
        "scj,scnk->jnk", owner_select, incoming, preferred_element_type=jnp.float32
    )
    loading_grad = loading_grad.reshape(local_blocks * BLK, latent_dim)
    reversed_taps = kernel[:, ::-1]
    grad_padded = extended(grad_smoothed, (("tm", 1),), halfwidth)
    latent_grad = smooth(grad_padded, reversed_taps)[:, 1 : bin_total + 1]
    return (latent_grad, loading_grad)


def solution(mesh):
    return jax.shard_map(
        local,
        mesh=mesh,
        in_specs=(
            P(None, ("groups", "tm")),
            P(),
            P(("groups", "tm"), None),
            P(None, None, None, ("groups", "tm")),
            P(("groups", "tm"), None, None),
            P(("groups", "tm"), None, None),
            P(None, None, ("groups", "tm")),
        ),
        out_specs=(P(None, ("groups", "tm")), P(("groups", "tm"), None)),
        check_vma=False,
    )
```

profile of v0, /device:TPU:13, one launch (start us, length us, event | category | flops | bytes accessed | tf_op | source)
XLA Modules:
  0.0 175.4 jit_solution(13084118451204904543)
XLA Ops:
  0.6 0.8 eq.16
  1.4 0.7 broadcast_multiply_fusion
  2.1 0.8 reshape.90
  2.8 0.2 convert_reduce_fusion
  3.0 0.1 mul.29
  3.1 0.6 scatter_custom_fusion
  3.7 0.1 all_to_all.12
  3.8 10.2 %all_to_all.19 = s32[16,1,2]{2,1,0:T(1,128)S(1)} all-to-all(s32[16,1,2]{2,1,0:T(1,128)S(1)} %bitcast.68), channel_id=1, replica_groups=mesh['groups'=2,'tm'=16] {'tm'}, dimensions={0} | all-to-all | bytes 256 | tf_op jit(solution)/shard_map/all_to_all | solution.py:60
  14.0 0.1 copy.45
  14.0 1.7 convolution_convert_fusion
  15.8 2.0 %copy.47 = bf16[16,2,128,256]{3,2,1,0:T(8,128)(2,1)} copy(bf16[16,2,128,256]{3,0,2,1:T(8,128)(2,1)S(1)} %convolution_convert_fusion) | data formatting | bytes 4194304 | tf_op jit(solution)/shard_map/convert_element_type | solution.py:64
  17.8 0.0 copy-start.4
  17.8 0.0 copy-start.5
  17.8 0.0 copy-start.2
  17.9 6.4 %all-to-all-start.1 = ((bf16[16,2,128,256]{3,2,1,0:T(8,128)(2,1)}), bf16[16,2,128,256]{3,2,1,0:T(8,128)(2,1)S(1)}, u32[]{:S(2)}, u32[]{:S(2)}) async-start(bf16[16,2,128,256]{3,2,1,0:T(8,128)(2,1)} %copy.47), calls=%async_computation.1 | async-start | bytes 4194304 | tf_op jit(solution)/shard_map/all_to_all | solution.py:63
  24.2 0.0 copy-done.4
  24.2 0.2 copy.48
  24.4 0.7 fusion.23
  25.1 3.3 %collective-permute-start = (f32[256,128]{0,1:T(8,128)}, f32[256,128]{0,1:T(8,128)S(1)}, u32[]{:S(2)}, u32[]{:S(2)}) collective-permute-start(f32[256,128]{0,1:T(8,128)} %get-tuple-element.12), channel_id=1, source_target_pairs={{0,1},{1,2},{2,3},{3,4},{4,5},{5,6},{6,7},{7,8},{8,9},{9,10},{10,1... | collective-permute-start | bytes 393224 | tf_op jit(solution)/shard_map/ppermute | solution.py:15
  28.5 1.9 %collective-permute-start.1 = (f32[256,128]{0,1:T(8,128)}, f32[256,128]{0,1:T(8,128)S(1)}, u32[]{:S(2)}, u32[]{:S(2)}) collective-permute-start(f32[256,128]{0,1:T(8,128)} %get-tuple-element.13), channel_id=1, source_target_pairs={{1,0},{2,1},{3,2},{4,3},{5,4},{6,5},{7,6},{8,7},{9,8},{10,9},{11,1... | collective-permute-start | bytes 393224 | tf_op jit(solution)/shard_map/ppermute | solution.py:18
  30.4 0.0 copy-done.5
  30.4 0.1 broadcast_bitcast_fusion
  30.5 0.0 copy-done.2
  30.5 0.2 copy.51
  30.7 40.7 %collective-permute-done = f32[256,128]{0,1:T(8,128)S(1)} collective-permute-done((f32[256,128]{0,1:T(8,128)}, f32[256,128]{0,1:T(8,128)S(1)}, u32[]{:S(2)}, u32[]{:S(2)}) %collective-permute-start) | collective-permute-done | bytes 131104 | tf_op jit(solution)/shard_map/ppermute | solution.py:15
  71.4 1.6 collective-permute-done.1
  73.0 0.1 pad_maximum_fusion
  73.1 0.5 broadcast_in_dim.41
  73.6 21.1 %convolution_convert_fusion.1 = bf16[1,256,513]{1,0,2:T(2,128)(2,1)S(1)} fusion(f32[1,256,768]{1,0,2:T(1,128)S(1)} %broadcast_in_dim.41, f32[256,1,256]{0,1,2:T(1,128)S(1)} %copy.51), kind=kOutput, calls=%fused_computation.11 | convolution fusion | flops 403570944 | bytes 1311232 | tf_op jit(solution)/shard_map/conv_general_dilated | solution.py:26
  94.8 0.0 all-to-all-done.1
  94.8 0.6 gather_fusion
  95.4 2.3 %fusion.1 = bf16[2048,512]{1,0:T(8,128)(2,1)S(1)} fusion(bf16[2048,512]{1,0:T(8,128)(2,1)} %bitcast.60, bf16[2048,256]{1,0:T(8,128)(2,1)S(1)} %bitcast.57, f32[2,8,512]{2,1,0:T(8,128)S(1)} %broadcast_bitcast_fusion, bf16[256,513]{0,1:T(8,128)(2,1)S(1)} %bitcast.61), kind=kOutput, calls=%fused_computation.5 | convolution fusion | flops 541065216 | bytes 5537792 | tf_op jit(solution)/shard_map/dot_general | solution.py:69
  97.8 0.0 copy-start
  97.8 1.7 fusion.2
  99.5 0.0 copy-done
  99.5 0.2 broadcast_in_dim.45
  99.7 2.3 %scatter_fusion = bf16[32,128,256]{2,1,0:T(8,128)(2,1)S(1)} fusion(bf16[32,128,256]{2,1,0:T(8,128)(2,1)S(1)} %broadcast_in_dim.45, s32[16]{0:T(128)S(1)} %fusion.19, bf16[16,128,256]{2,1,0:T(8,128)(2,1)} %bitcast.63), kind=kCustom, calls=%fused_computation.2 | custom fusion | bytes 3145792 | tf_op jit(solution)/shard_map/scatter | solution.py:84
  102.0 3.5 %copy.54 = bf16[16,2,128,256]{3,1,2,0:T(2,128)(2,1)} copy(bf16[16,2,128,256]{3,2,1,0:T(8,128)(2,1)S(1)} %bitcast.55) | data formatting | bytes 4194304 | tf_op jit(solution)/shard_map/reshape | solution.py:85
  105.5 4.5 %all-to-all-start.2 = ((bf16[16,2,128,256]{3,1,2,0:T(2,128)(2,1)}), bf16[16,2,128,256]{3,1,2,0:T(2,128)(2,1)S(1)}, u32[]{:S(2)}, u32[]{:S(2)}) async-start(bf16[16,2,128,256]{3,1,2,0:T(2,128)(2,1)} %copy.54), calls=%async_computation.2 | async-start | bytes 4194304 | tf_op jit(solution)/shard_map/all_to_all | solution.py:86
  110.0 0.0 copy-start.3
  110.0 2.4 %convolution_multiply_fusion.1 = f32[256,512]{1,0:T(8,128)S(1)} fusion(bf16[2048,256]{1,0:T(8,128)(2,1)S(1)} %bitcast.58, bf16[2048,512]{1,0:T(8,128)(2,1)} %copy-done), kind=kOutput, calls=%fused_computation.12 | convolution fusion | flops 537001984 | bytes 3670016 | tf_op jit(solution)/shard_map/dot_general | solution.py:76
  112.4 0.0 copy-start.1
  112.4 0.8 copy-done.1
  113.2 3.3 %collective-permute-start.2 = (f32[256,128]{1,0:T(8,128)S(1)}, f32[256,128]{1,0:T(8,128)S(1)}, u32[]{:S(2)}, u32[]{:S(2)}) collective-permute-start(f32[256,128]{1,0:T(8,128)S(1)} %get-tuple-element.10), channel_id=1, source_target_pairs={{0,1},{1,2},{2,3},{3,4},{4,5},{5,6},{6,7},{7,8},{8,9},{9,10},{10,1... | collective-permute-start | bytes 393224 | tf_op jit(solution)/shard_map/ppermute | solution.py:15
  116.5 2.1 %collective-permute-start.3 = (f32[256,128]{1,0:T(8,128)S(1)}, f32[256,128]{1,0:T(8,128)}, u32[]{:S(2)}, u32[]{:S(2)}) collective-permute-start(f32[256,128]{1,0:T(8,128)S(1)} %get-tuple-element.11), channel_id=1, source_target_pairs={{1,0},{2,1},{3,2},{4,3},{5,4},{6,5},{7,6},{8,7},{9,8},{10,9},{11,1... | collective-permute-start | bytes 393224 | tf_op jit(solution)/shard_map/ppermute | solution.py:18
  118.6 0.0 copy-done.3
  118.6 0.4 rev.3
  119.0 0.2 copy.53
  119.2 37.9 %collective-permute-done.2 = f32[256,128]{1,0:T(8,128)S(1)} collective-permute-done((f32[256,128]{1,0:T(8,128)S(1)}, f32[256,128]{1,0:T(8,128)S(1)}, u32[]{:S(2)}, u32[]{:S(2)}) %collective-permute-start.2) | collective-permute-done | bytes 131104 | tf_op jit(solution)/shard_map/ppermute | solution.py:15
  157.1 1.8 %collective-permute-done.3 = f32[256,128]{1,0:T(8,128)} collective-permute-done((f32[256,128]{1,0:T(8,128)S(1)}, f32[256,128]{1,0:T(8,128)}, u32[]{:S(2)}, u32[]{:S(2)}) %collective-permute-start.3) | collective-permute-done | bytes 131104 | tf_op jit(solution)/shard_map/ppermute | solution.py:18
  158.9 1.2 maximum_bitcast_fusion
  160.0 1.7 copy.52
  161.8 10.3 %fusion.24 = f32[1,256,513]{1,0,2:T(1,128)S(1)} fusion(f32[1,256,768]{1,0,2:T(1,128)} %copy.52, f32[256,1,256]{0,1,2:T(1,128)S(1)} %copy.53), kind=kOutput, calls=%fused_computation.40 | convolution fusion | flops 403439616 | bytes 1573888 | tf_op jit(solution)/shard_map/conv_general_dilated | solution.py:26
  172.2 1.0 copy.57
  173.2 0.0 all-to-all-done.2
  173.2 1.3 fusion.5
  174.5 0.9 copy.56
  (7 shorter events, 0.2 us)
Async XLA Ops:
  17.8 6.4 %copy-start.4 = (f32[256,512]{1,0:T(8,128)S(1)}, f32[256,512]{1,0:T(8,128)}, u32[]{:S(2)}) copy-start(f32[256,512]{1,0:T(8,128)} %param.7) | copy-start | bytes 1572868
  17.8 12.6 %copy-start.5 = (s32[2,8,4]{1,2,0:T(4,128)S(1)}, s32[2,8,4]{1,2,0:T(4,128)}, u32[]{:S(2)}) copy-start(s32[2,8,4]{1,2,0:T(4,128)} %param.13) | copy-start | bytes 772
  17.8 12.7 %copy-start.2 = (f32[256,256]{1,0:T(8,128)S(1)}, f32[256,256]{1,0:T(8,128)}, u32[]{:S(2)}) copy-start(f32[256,256]{1,0:T(8,128)} %param.8) | copy-start | bytes 786436
  17.9 76.9 %all-to-all-start.1 = ((bf16[16,2,128,256]{3,2,1,0:T(8,128)(2,1)}), bf16[16,2,128,256]{3,2,1,0:T(8,128)(2,1)S(1)}, u32[]{:S(2)}, u32[]{:S(2)}) async-start(bf16[16,2,128,256]{3,2,1,0:T(8,128)(2,1)} %copy.47), calls=%async_computation.1 | async-start | bytes 4194304 | tf_op jit(solution)/shard_map/all_to_all | solution.py:63
  25.1 46.3 %collective-permute-start = (f32[256,128]{0,1:T(8,128)}, f32[256,128]{0,1:T(8,128)S(1)}, u32[]{:S(2)}, u32[]{:S(2)}) collective-permute-start(f32[256,128]{0,1:T(8,128)} %get-tuple-element.12), channel_id=1, source_target_pairs={{0,1},{1,2},{2,3},{3,4},{4,5},{5,6},{6,7},{7,8},{8,9},{9,10},{10,1... | collective-permute-start | bytes 393224 | tf_op jit(solution)/shard_map/ppermute | solution.py:15
  28.5 44.5 %collective-permute-start.1 = (f32[256,128]{0,1:T(8,128)}, f32[256,128]{0,1:T(8,128)S(1)}, u32[]{:S(2)}, u32[]{:S(2)}) collective-permute-start(f32[256,128]{0,1:T(8,128)} %get-tuple-element.13), channel_id=1, source_target_pairs={{1,0},{2,1},{3,2},{4,3},{5,4},{6,5},{7,6},{8,7},{9,8},{10,9},{11,1... | collective-permute-start | bytes 393224 | tf_op jit(solution)/shard_map/ppermute | solution.py:18
  97.8 1.7 copy-start
  105.5 67.7 %all-to-all-start.2 = ((bf16[16,2,128,256]{3,1,2,0:T(2,128)(2,1)}), bf16[16,2,128,256]{3,1,2,0:T(2,128)(2,1)S(1)}, u32[]{:S(2)}, u32[]{:S(2)}) async-start(bf16[16,2,128,256]{3,1,2,0:T(2,128)(2,1)} %copy.54), calls=%async_computation.2 | async-start | bytes 4194304 | tf_op jit(solution)/shard_map/all_to_all | solution.py:86
  110.0 8.6 %copy-start.3 = (f32[256,256]{1,0:T(8,128)S(1)}, f32[256,256]{1,0:T(8,128)}, u32[]{:S(2)}) copy-start(f32[256,256]{1,0:T(8,128)} %param.8) | copy-start | bytes 786436
  112.4 0.8 copy-start.1
  113.2 43.9 %collective-permute-start.2 = (f32[256,128]{1,0:T(8,128)S(1)}, f32[256,128]{1,0:T(8,128)S(1)}, u32[]{:S(2)}, u32[]{:S(2)}) collective-permute-start(f32[256,128]{1,0:T(8,128)S(1)} %get-tuple-element.10), channel_id=1, source_target_pairs={{0,1},{1,2},{2,3},{3,4},{4,5},{5,6},{6,7},{7,8},{8,9},{9,10},{10,1... | collective-permute-start | bytes 393224 | tf_op jit(solution)/shard_map/ppermute | solution.py:15
  116.5 42.3 %collective-permute-start.3 = (f32[256,128]{1,0:T(8,128)S(1)}, f32[256,128]{1,0:T(8,128)}, u32[]{:S(2)}, u32[]{:S(2)}) collective-permute-start(f32[256,128]{1,0:T(8,128)S(1)} %get-tuple-element.11), channel_id=1, source_target_pairs={{1,0},{2,1},{3,2},{4,3},{5,4},{6,5},{7,6},{8,7},{9,8},{10,9},{11,1... | collective-permute-start | bytes 393224 | tf_op jit(solution)/shard_map/ppermute | solution.py:18
where the time goes:
time: 176 us; the launch traced here: 175 us
  waiting for transfers between devices  82 us (47%)
  matrix products  40.9 us (23%)
  starting transfers between devices  21.6 us (12%)
  local copies, waits for them, and re-layouts  17.8 us (10%)
  blocking collectives  10.2 us (6%)
  other arithmetic  2.1 us (1%)
    ppermute x2, waiting for transfers between devices, extended(): lax.ppermute(lax.slice_in_dim(block, block.shape[dim] - width, None, axis...  78.6 us
    conv_general_dilated x2, matrix products, smooth(): lax.conv_general_dilated(lhs, rhs, (1,), 'VALID', dimension_numbers=('NCH...  31.5 us
    all_to_all x1, blocking collectives, local(): lax.all_to_all(request_table, 'tm', split_axis=0, concat_axis=0, tiled=True)  10.2 us
    ppermute x2, starting transfers between devices, extended(): lax.ppermute(lax.slice_in_dim(block, block.shape[dim] - width, None, axis...  6.68 us
    all_to_all x1, starting transfers between devices, local(): lax.all_to_all(picked.astype(jnp.bfloat16), 'tm', split_axis=0, concat_ax...  6.37 us
    all_to_all x1, starting transfers between devices, local(): lax.all_to_all(outgoing, 'tm', split_axis=0, concat_axis=0, tiled=True)  4.49 us
    ppermute x2, starting transfers between devices, extended(): lax.ppermute(lax.slice_in_dim(block, 0, width, axis=dim), axis, backward)  4.02 us
  transfers between devices with their start and end apart: 6, of which 4 were waited for; matrix products, arithmetic and copies ran while one was open for 23% of the time, Pallas kernels for 0%

commit v1 on v0

v1 whole, which is shorter than its diff:
```python
import functools

import jax
import jax.numpy as jnp
import numpy as np
from jax import lax
from jax.experimental import pallas as pl
from jax.experimental.pallas import tpu as pltpu
from jax.sharding import PartitionSpec as P

BLK = 128
ROW = 4
F32 = jnp.float32
BF16 = jnp.bfloat16
VMEM = pl.BlockSpec(memory_space=pltpu.VMEM)
ANY = pl.BlockSpec(memory_space=pl.ANY)


def split_const(a):
    high = a.astype(jnp.bfloat16)
    low = (a - high.astype(np.float64)).astype(jnp.bfloat16)
    return high, low


@functools.lru_cache(maxsize=None)
def dft_tables(length, outputs, first):
    half = length // 2
    t = np.arange(length)[:, None]
    f = np.arange(half)[None, :]
    angle = 2 * np.pi * ((t * f) % length) / length
    cos, sin = np.cos(angle), np.sin(angle)
    sin[:, 0] = 1 - 2 * (np.arange(length) % 2)
    forward = np.concatenate([cos, sin], axis=1)
    weight = np.full((half,), 2.0 / length)
    weight[0] = 1.0 / length
    inverse = (forward * np.concatenate([weight, weight])[None, :]).T
    inverse = inverse[:, first : first + outputs]
    return split_const(forward) + split_const(inverse)


def dot3(a, b_high, b_low):
    high = a.astype(BF16)
    low = (a - high.astype(F32)).astype(BF16)
    out = jnp.dot(high, b_high, preferred_element_type=F32)
    out += jnp.dot(low, b_high, preferred_element_type=F32)
    out += jnp.dot(high, b_low, preferred_element_type=F32)
    return out


def product(signal, taps, sign):
    half = signal.shape[1] // 2
    xr, xi = signal[:, :half], signal[:, half:]
    kr, ki = taps[:, :half], taps[:, half:]
    first = lax.broadcasted_iota(jnp.int32, kr.shape, 1) == 0
    kr_i = jnp.where(first, ki, kr)
    ki_x = jnp.where(first, 0.0, ki) * sign
    return jnp.concatenate([xr * kr + xi * ki_x, xi * kr_i - xr * ki_x], axis=1)


def smooth_kernel(low, mid, high, taps, fh, fl, wh, wl, out, spectrum):
    width = low.shape[1]
    bins = mid.shape[1]
    k_spec = dot3(taps[...], fh[: taps.shape[1]], fl[: taps.shape[1]])
    spectrum[...] = k_spec
    x_spec = dot3(mid[...], fh[width : width + bins], fl[width : width + bins])
    x_spec += dot3(low[...], fh[:width], fl[:width])
    x_spec += dot3(high[...], fh[width + bins :], fl[width + bins :])
    out[...] = dot3(product(x_spec, k_spec, 1.0), wh[...], wl[...]).astype(out.dtype)


def unsmooth_kernel(low, mid, high, k_spec, fh, fl, wh, wl, out):
    width = low.shape[1]
    bins = mid.shape[1]
    x_spec = dot3(mid[...], fh[width : width + bins], fl[width : width + bins])
    x_spec += dot3(low[...], fh[:width], fl[:width])
    x_spec += dot3(high[...], fh[width + bins :], fl[width + bins :])
    out[...] = dot3(product(x_spec, k_spec[...], -1.0), wh[...], wl[...])


def session_kernel(
    same, place, mask, mine, theirs, smoothed, recorded, grad, keep, send, rows, resid, sem
):
    entries = rows.shape[0]
    bins = smoothed.shape[1]

    def fetch(e, _):
        source = pl.ds(pl.multiple_of(place[0, e] * BLK, BLK), BLK)

        @pl.when(same[e] == 1)
        def _():
            pltpu.make_async_copy(mine.at[source], rows.at[e], sem.at[e]).start()

        @pl.when(same[e] == 0)
        def _():
            pltpu.make_async_copy(theirs.at[source], rows.at[e], sem.at[e]).start()

        return 0

    lax.fori_loop(0, entries, fetch, 0)
    keep[...] = jnp.zeros_like(keep)
    send[...] = jnp.zeros_like(send)
    grad[...] = jnp.zeros_like(grad)

    def pair(step, _):
        for half in range(2):
            e = step * 2 + half
            pltpu.make_async_copy(mine.at[pl.ds(0, BLK)], rows.at[e], sem.at[e]).wait()
        block = rows[pl.ds(step * 2, 2)].reshape(2 * BLK, rows.shape[2])
        predicted = jnp.dot(block, smoothed[...], preferred_element_type=F32)
        for half in range(2):
            e = step * 2 + half
            for t in range(bins // BLK):
                cut = slice(t * BLK, (t + 1) * BLK)
                weight = mask[e * (bins // BLK) + t].astype(F32)
                part = predicted[half * BLK : (half + 1) * BLK, cut]
                seen = recorded[e, :, cut].astype(F32)
                resid[half * BLK : (half + 1) * BLK, cut] = (weight * (part - seen)).astype(BF16)
        grad[...] += lax.dot_general(
            block, resid[...], (((0,), (0,)), ((), ())), preferred_element_type=F32
        ) * (1.0 / BLK)
        term = lax.dot_general(
            resid[...], smoothed[...], (((1,), (1,)), ((), ())), preferred_element_type=F32
        ) * (1.0 / BLK)
        for half in range(2):
            e = step * 2 + half
            mine_term = term[half * BLK : (half + 1) * BLK].astype(BF16)
            target = pl.ds(pl.multiple_of(place[1, e] * BLK, BLK), BLK)

            @pl.when(same[e] == 1)
            def _():
                keep[target] = (keep[target].astype(F32) + mine_term.astype(F32)).astype(BF16)

            @pl.when(same[e] == 0)
            def _():
                send[target] = (send[target].astype(F32) + mine_term.astype(F32)).astype(BF16)

        return 0

    lax.fori_loop(0, entries // 2, pair, 0)


def local(latents, kernel, loadings, recorded, owner_ids, local_ids, recorded_mask):
    latent_dim, bins = latents.shape
    taps = kernel.shape[1]
    halfwidth = taps // 2
    count = lax.axis_size("tm")
    chain = count // ROW
    local_blocks = loadings.shape[0] // BLK
    chunk = loadings.shape[0]
    me = lax.axis_index("tm")
    my_z, my_y, my_c = me // ROW, (me // 2) % 2, me % 2

    def permute(x, pairs):
        return lax.ppermute(x, "tm", pairs)

    def along(x, zs, step):
        return permute(x, [(z * ROW + w, (z + step) * ROW + w) for z in zs for w in range(ROW)])

    def flip(x, bit):
        return permute(x, [(i, i ^ bit) for i in range(count)])

    order = [sorted(range(chain), key=lambda d: (abs(d - z), -d)) for z in range(chain)]
    near = np.zeros((chain, chain), np.int32)
    for z in range(chain):
        for rank, d in enumerate(order[z]):
            near[z, d] = rank

    def choose(options):
        distinct = []
        for o in options:
            if not any(o is d for d in distinct):
                distinct.append(o)
        value = distinct[0]
        for d in distinct[1:]:
            hit = jnp.asarray([o is d for o in options])[my_z]
            value = jnp.where(hit, d, value)
        return value

    up_one = [(i, i + 1) for i in range(count - 1)]
    down_one = [(i + 1, i) for i in range(count - 1)]

    low = permute(latents[:, bins - halfwidth :], up_one)
    high = permute(latents[:, :halfwidth], down_one)

    from_low, from_high = [loadings], [loadings]
    across = [flip(loadings, 2)]
    for r in range(1, chain):
        from_low.append(along(from_low[-1], range(r - 1, chain - 1), 1))
        from_high.append(along(from_high[-1], range(1, chain - r + 1), -1))
    arrived = [loadings]
    for k in range(1, chain):
        options = []
        for z in range(chain):
            d = order[z][k]
            options.append(from_low[z - d] if d < z else from_high[d - z])
        arrived.append(choose(options))
        across.append(flip(arrived[-1], 2))
    mine = jnp.concatenate(arrived + across)
    theirs = flip(mine, 1)

    length = bins + 2 * halfwidth
    fh, fl, wh, wl = dft_tables(length, bins, 0)
    mxu = latent_dim * length * (length + bins) * 6
    smoothed, spectrum = pl.pallas_call(
        smooth_kernel,
        out_shape=(
            jax.ShapeDtypeStruct((latent_dim, bins), BF16),
            jax.ShapeDtypeStruct((latent_dim, length), F32),
        ),
        in_specs=[VMEM] * 8,
        out_specs=(VMEM, VMEM),
        compiler_params=pltpu.CompilerParams(vmem_limit_bytes=40 * 2**20),
        cost_estimate=pl.CostEstimate(flops=mxu, bytes_accessed=6 * 2**20, transcendentals=0),
        name="smooth",
    )(low, latents, high, kernel, fh, fl, wh, wl)

    owner = owner_ids.reshape(-1)
    slot = local_ids.reshape(-1)
    entries = owner.shape[0]
    owner_z, owner_y, owner_c = owner // ROW, (owner // 2) % 2, owner % 2
    same = (owner_c == my_c).astype(jnp.int32)
    rank = jnp.asarray(near)[my_z][owner_z]
    crossed = (owner_y != my_y).astype(jnp.int32)
    place = jnp.stack(
        [
            (crossed * chain + rank) * local_blocks + slot,
            (crossed * chain + chain - 1 - rank) * local_blocks + slot,
        ]
    )
    table = count // 2 * chunk
    grad, keep, send = pl.pallas_call(
        session_kernel,
        out_shape=(
            jax.ShapeDtypeStruct((latent_dim, bins), F32),
            jax.ShapeDtypeStruct((table, latent_dim), BF16),
            jax.ShapeDtypeStruct((table, latent_dim), BF16),
        ),
        in_specs=[pl.BlockSpec(memory_space=pltpu.SMEM)] * 3 + [ANY, ANY, VMEM, VMEM],
        out_specs=(VMEM, VMEM, VMEM),
        scratch_shapes=[
            pltpu.VMEM((entries, BLK, latent_dim), BF16),
            pltpu.VMEM((2 * BLK, bins), BF16),
            pltpu.SemaphoreType.DMA((entries,)),
        ],
        compiler_params=pltpu.CompilerParams(vmem_limit_bytes=56 * 2**20),
        cost_estimate=pl.CostEstimate(
            flops=6 * entries * BLK * latent_dim * bins, bytes_accessed=8 * 2**20, transcendentals=0
        ),
        name="session",
    )(
        same,
        place,
        recorded_mask.reshape(-1),
        mine,
        theirs,
        smoothed,
        recorded.reshape(entries, BLK, bins),
    )

    grad_low = permute(grad[:, bins - halfwidth :], up_one)
    grad_high = permute(grad[:, :halfwidth], down_one)
    got = flip(send, 1)

    keep = keep.reshape(2, chain, chunk, latent_dim)
    got = got.reshape(2, chain, chunk, latent_dim)
    sums = []
    for k in range(chain):
        out = (keep[1, k].astype(F32) + got[1, k].astype(F32)).astype(BF16)
        back = flip(out, 2)
        sums.append(keep[0, k].astype(F32) + got[0, k].astype(F32) + back.astype(F32))
    rise = fall = None
    for r in range(1, chain):
        far = chain - r
        up_from, down_from = range(0, r), range(far, chain)
        pick_up = choose([sums[chain - 1 - near[z, z + far]] if z in up_from else sums[0] for z in range(chain)])
        pick_down = choose(
            [sums[chain - 1 - near[z, z - far]] if z in down_from else sums[0] for z in range(chain)]
        )
        if rise is not None:
            pick_up += rise.astype(F32)
            pick_down += fall.astype(F32)
        rise = along(pick_up.astype(BF16), up_from, 1)
        fall = along(pick_down.astype(BF16), down_from, -1)
    loading_grad = sums[-1]
    if rise is not None:
        loading_grad = loading_grad + rise.astype(F32) + fall.astype(F32)

    fh, fl, wh, wl = dft_tables(length, bins, 2 * halfwidth)
    latent_grad = pl.pallas_call(
        unsmooth_kernel,
        out_shape=jax.ShapeDtypeStruct((latent_dim, bins), F32),
        in_specs=[VMEM] * 8,
        out_specs=VMEM,
        compiler_params=pltpu.CompilerParams(vmem_limit_bytes=40 * 2**20),
        cost_estimate=pl.CostEstimate(flops=mxu, bytes_accessed=6 * 2**20, transcendentals=0),
        name="unsmooth",
    )(grad_low, grad, grad_high, spectrum, fh, fl, wh, wl)
    return latent_grad, loading_grad


def solution(mesh):
    return jax.shard_map(
        local,
        mesh=mesh,
        in_specs=(
            P(None, ("groups", "tm")),
            P(),
            P(("groups", "tm"), None),
            P(None, None, None, ("groups", "tm")),
            P(("groups", "tm"), None, None),
            P(("groups", "tm"), None, None),
            P(None, None, ("groups", "tm")),
        ),
        out_specs=(P(None, ("groups", "tm")), P(("groups", "tm"), None)),
        check_vma=False,
    )
```

time: 176 us -> 135 us (0.77)
  the two profiles are of different devices: /device:TPU:13 before, /device:TPU:0 now
where the time goes in v1:
time: 135 us; the launch traced here: 134 us
  starting transfers between devices  48.8 us (36%)
  waiting for transfers between devices  30.9 us (23%)
  local copies, waits for them, and re-layouts  18.9 us (14%)
  Pallas kernels  17.9 us (13%)
  other arithmetic  16.6 us (12%)
    ppermute x26, starting transfers between devices, permute(): return lax.ppermute(x, 'tm', pairs)  48.8 us
    ppermute x26, waiting for transfers between devices, permute(): return lax.ppermute(x, 'tm', pairs)  30.9 us
    pallas_call x1, Pallas kernels, local(): pl.pallas_call(session_kernel, out_shape=(jax.ShapeDtypeStruct((latent_di...  10.2 us
    unnamed x37, local copies, waits for them, and re-layouts  7.97 us
    unnamed x3, other arithmetic  6.51 us
    dynamic_slice x5, local copies, waits for them, and re-layouts, choose(): hit = jnp.asarray([o is d for o in options])[my_z]  5.67 us
    pallas_call x1, Pallas kernels, local(): pl.pallas_call(unsmooth_kernel, out_shape=jax.ShapeDtypeStruct((latent_di...  4.1 us
    pallas_call x1, Pallas kernels, local(): pl.pallas_call(smooth_kernel, out_shape=(jax.ShapeDtypeStruct((latent_dim...  3.59 us
  transfers between devices with their start and end apart: 26, of which 9 were waited for; matrix products, arithmetic and copies ran while one was open for 22% of the time, Pallas kernels for 6%

profile of v1, /device:TPU:0, one launch (start us, length us, event | category | flops | bytes accessed | tf_op | source)
XLA Modules:
  0.0 134.1 jit_solution(10702232607221266850)
XLA Ops:
  0.6 1.3 collective-permute-start.1
  1.9 5.6 %collective-permute-start = (bf16[512,256]{1,0:T(8,128)(2,1)}, bf16[512,256]{1,0:T(8,128)(2,1)S(1)}, u32[]{:S(2)}, u32[]{:S(2)}) collective-permute-start(bf16[512,256]{1,0:T(8,128)(2,1)} %param.29), channel_id=1, source_target_pairs={{0,4},{1,5},{2,6},{3,7},{4,8},{5,9},{6,10},{7,11},{8,12},{9,13},{1... | collective-permute-start | bytes 786440 | tf_op jit(solution)/shard_map/ppermute | solution.py:154
  7.5 4.6 %collective-permute-done.1 = bf16[512,256]{1,0:T(8,128)(2,1)S(1)} collective-permute-done((bf16[512,256]{1,0:T(8,128)(2,1)}, bf16[512,256]{1,0:T(8,128)(2,1)S(1)}, u32[]{:S(2)}, u32[]{:S(2)}) %collective-permute-start.1) | collective-permute-done | bytes 262176 | tf_op jit(solution)/shard_map/ppermute | solution.py:154
  12.1 1.3 collective-permute-start.3
  13.4 0.7 collective-permute-start.2
  14.1 1.7 %collective-permute-start.6 = (bf16[512,256]{1,0:T(8,128)(2,1)}, bf16[512,256]{1,0:T(8,128)(2,1)}, u32[]{:S(2)}, u32[]{:S(2)}) collective-permute-start(bf16[512,256]{1,0:T(8,128)(2,1)} %param.29), channel_id=1, source_target_pairs={{0,2},{1,3},{2,0},{3,1},{4,6},{5,7},{6,4},{7,5},{8,10},{9,11},{10,... | collective-permute-start | bytes 786440 | tf_op jit(solution)/shard_map/ppermute | solution.py:154
  15.8 1.3 dynamic_slice.41
  17.1 1.2 dynamic_slice.42
  18.3 1.3 dynamic_slice.39
  19.6 1.3 dynamic_slice.37
  20.9 1.7 %constant_dynamic-update-slice_fusion.7 = bf16[4096,256]{1,0:T(8,128)(2,1)} fusion(bf16[512,256]{1,0:T(8,128)(2,1)} %param.29), kind=kLoop, calls=%fused_computation.29 | loop fusion | bytes 524288
  22.6 1.3 collective-permute-start.5
  23.9 0.7 collective-permute-start.4
  24.6 1.5 %constant_dynamic-update-slice_fusion.6 = (bf16[4096,256]{1,0:T(8,128)(2,1)}, bf16[512,256]{1,0:T(8,128)(2,1)S(1)}) fusion(bf16[4096,256]{1,0:T(8,128)(2,1)} %constant_dynamic-update-slice_fusion.7, bf16[512,256]{1,0:T(8,128)(2,1)S(1)} %collective-permute-done, bf16[512,256]{1,0:T(8,128)(2,1)S(1)} %collective-permute-done.1, pred[]{:T(512)} %bitcast.3), kind=kLoop, calls=%fused_computation.28 | loop fusion | flops 131072 | bytes 1049088
  26.4 2.1 %constant_dynamic-update-slice_fusion.5 = (bf16[4096,256]{1,0:T(8,128)(2,1)}, bf16[512,256]{1,0:T(8,128)(2,1)S(1)}) fusion(bf16[4096,256]{1,0:T(8,128)(2,1)} %get-tuple-element.16, bf16[512,256]{1,0:T(8,128)(2,1)S(1)} %collective-permute-done.2, bf16[512,256]{1,0:T(8,128)(2,1)S(1)} %collective-permute-done, bf16[512,256]{1,0:T(8,128)(2,1)S(1)} %collective-permute-done.3, ...), kind=kLoop, calls=%fused_computation.27 | loop fusion | flops 262144 | bytes 1311744
  28.5 1.7 %collective-permute-start.8 = (bf16[512,256]{1,0:T(8,128)(2,1)S(1)}, bf16[512,256]{1,0:T(8,128)(2,1)S(1)}, u32[]{:S(2)}, u32[]{:S(2)}) collective-permute-start(bf16[512,256]{1,0:T(8,128)(2,1)S(1)} %get-tuple-element.15), channel_id=1, source_target_pairs={{0,2},{1,3},{2,0},{3,1},{4,6},{5,7},{6,4},{7,5},{8,10},{9,11},{10,... | collective-permute-start | bytes 786440 | tf_op jit(solution)/shard_map/ppermute | solution.py:154
  30.1 3.7 %collective-permute-done.5 = bf16[512,256]{1,0:T(8,128)(2,1)S(1)} collective-permute-done((bf16[512,256]{1,0:T(8,128)(2,1)S(1)}, bf16[512,256]{1,0:T(8,128)(2,1)S(1)}, u32[]{:S(2)}, u32[]{:S(2)}) %collective-permute-start.5) | collective-permute-done | bytes 262176 | tf_op jit(solution)/shard_map/ppermute | solution.py:154
  34.0 3.0 %constant_dynamic-update-slice_fusion.4 = (bf16[4096,256]{1,0:T(8,128)(2,1)}, bf16[512,256]{1,0:T(8,128)(2,1)S(1)}) fusion(bf16[4096,256]{1,0:T(8,128)(2,1)} %get-tuple-element.14, bf16[512,256]{1,0:T(8,128)(2,1)S(1)} %collective-permute-done.4, bf16[512,256]{1,0:T(8,128)(2,1)} %copy-done.11, bf16[512,256]{1,0:T(8,128)(2,1)S(1)} %collective-permute-done.3, ...), kind=kLoop, calls=%fused_computation.26 | loop fusion | flops 393216 | bytes 1574400
  37.4 1.7 %constant_dynamic-update-slice_fusion.3 = bf16[4096,256]{1,0:T(8,128)(2,1)} fusion(bf16[4096,256]{1,0:T(8,128)(2,1)} %get-tuple-element.12, bf16[512,256]{1,0:T(8,128)(2,1)} %collective-permute-done.6), kind=kLoop, calls=%fused_computation.25 | loop fusion | bytes 524288
  39.1 0.7 constant_dynamic-update-slice_fusion.2
  40.0 0.7 constant_dynamic-update-slice_fusion.1
  40.7 3.4 %collective-permute-done.9 = bf16[512,256]{1,0:T(8,128)(2,1)S(1)} collective-permute-done((bf16[512,256]{1,0:T(8,128)(2,1)S(1)}, bf16[512,256]{1,0:T(8,128)(2,1)S(1)}, u32[]{:S(2)}, u32[]{:S(2)}) %collective-permute-start.9) | collective-permute-done | bytes 262176 | tf_op jit(solution)/shard_map/ppermute | solution.py:154
  44.1 0.7 constant_dynamic-update-slice_fusion.mine
  44.9 0.7 fusion.15
  45.6 1.3 collective-permute-start.12
  46.9 3.0 %collective-permute-start.11 = (f32[256,128]{1,0:T(8,128)S(1)}, f32[256,128]{1,0:T(8,128)S(1)}, u32[]{:S(2)}, u32[]{:S(2)}) collective-permute-start(f32[256,128]{1,0:T(8,128)S(1)} %get-tuple-element.31), channel_id=1, source_target_pairs={{0,1},{1,2},{2,3},{3,4},{4,5},{5,6},{6,7},{7,8},{8,9},{9,10},{10,1... | collective-permute-start | bytes 393224 | tf_op jit(solution)/shard_map/ppermute | solution.py:154
  50.0 0.6 reshape.298
  50.6 0.6 reshape.299
  51.2 0.6 reshape.301
  51.8 0.7 dynamic-slice_bitcast_fusion
  52.6 0.7 gather_fusion
  53.2 0.7 fusion.10
  53.9 1.2 fusion.12
  55.0 1.2 compare_convert_fusion.same
  56.4 0.6 reshape.302.mask
  57.0 1.2 pad_add_fusion.place
  58.2 1.1 copy-done.8
  59.3 1.1 copy-done.9
  60.4 3.6 %smooth.1 = (bf16[256,512]{1,0:T(8,128)(2,1)S(1)}, f32[256,768]{1,0:T(8,128)S(1)}) custom-call(f32[256,128]{1,0:T(8,128)S(1)} %collective-permute-done.11.low, f32[256,512]{1,0:T(8,128)S(1)} %copy-done.6, f32[256,128]{1,0:T(8,128)S(1)} %collective-permute-done.12.high, f32[256,256]{1,0:T(8,128)S(1)} %copy-done.7, bf16[768,768]{1,0:T(8,128)(2,1)S(1)} %copy-done.2, ...), custom_call_target="tpu_custom_call" | custom-call | flops 1509949440 | bytes 6291456 | tf_op jit(solution)/shard_map/smooth/pallas_call | solution.py:204
  64.1 0.7 copy-done.5
  64.8 10.2 %session.1 = (f32[256,512]{1,0:T(8,128)}, bf16[4096,256]{1,0:T(8,128)(2,1)}, bf16[4096,256]{1,0:T(8,128)(2,1)}) custom-call(s32[16]{0:T(128)} %compare_convert_fusion.same, s32[2,16]{1,0:T(2,128)} %pad_add_fusion.place, s32[64]{0:T(128)} %reshape.302.mask, bf16[4096,256]{1,0:T(8,128)(2,1)} %constant_dynamic-update-slice_fusion.mine, ...), custom_call_target="tpu_custom_call" | custom-call | flops 1610612736 | bytes 8388608 | tf_op jit(solution)/shard_map/session/pallas_call | solution.py:231
  74.9 1.8 %collective-permute-start.15 = (bf16[4096,256]{1,0:T(8,128)(2,1)}, bf16[4096,256]{1,0:T(8,128)(2,1)S(1)}, u32[]{:S(2)}, u32[]{:S(2)}) collective-permute-start(bf16[4096,256]{1,0:T(8,128)(2,1)} %get-tuple-element.11), channel_id=1, source_target_pairs={{0,1},{1,0},{2,3},{3,2},{4,5},{5,4},{6,7},{7,6},{8,9},{9,8},{10,11... | collective-permute-start | bytes 6291464 | tf_op jit(solution)/shard_map/ppermute | solution.py:154
  76.7 4.0 %collective-permute-done.15 = bf16[4096,256]{1,0:T(8,128)(2,1)S(1)} collective-permute-done((bf16[4096,256]{1,0:T(8,128)(2,1)}, bf16[4096,256]{1,0:T(8,128)(2,1)S(1)}, u32[]{:S(2)}, u32[]{:S(2)}) %collective-permute-start.15) | collective-permute-done | bytes 2097184 | tf_op jit(solution)/shard_map/ppermute | solution.py:154
  80.7 1.4 %fusion.2 = (bf16[512,256]{1,0:T(8,128)(2,1)S(1)}, bf16[512,256]{1,0:T(8,128)(2,1)S(1)}, bf16[512,256]{1,0:T(8,128)(2,1)S(1)}, bf16[512,256]{1,0:T(8,128)(2,1)S(1)}) fusion(bf16[2,4,512,256]{3,2,1,0:T(8,128)(2,1)S(1)} %bitcast.68, bf16[2,4,512,256]{3,2,1,0:T(8,128)(2,1)} %bitcast.63), kind=kLoop, calls=%fused_computation.15 | loop fusion | flops 2097152 | bytes 3145728 | tf_op jit(solution)/shard_map/convert_element_type | solution.py:268
  82.2 4.3 %collective-permute-start.17 = (bf16[512,256]{1,0:T(8,128)(2,1)S(1)}, bf16[512,256]{1,0:T(8,128)(2,1)S(1)}, u32[]{:S(2)}, u32[]{:S(2)}) collective-permute-start(bf16[512,256]{1,0:T(8,128)(2,1)S(1)} %get-tuple-element.27), channel_id=1, source_target_pairs={{0,2},{1,3},{2,0},{3,1},{4,6},{5,7},{6,4},{7,5},{8,10},{9,11},{10,... | collective-permute-start | bytes 786440 | tf_op jit(solution)/shard_map/ppermute | solution.py:154
  86.6 7.1 %collective-permute-done.17 = bf16[512,256]{1,0:T(8,128)(2,1)S(1)} collective-permute-done((bf16[512,256]{1,0:T(8,128)(2,1)S(1)}, bf16[512,256]{1,0:T(8,128)(2,1)S(1)}, u32[]{:S(2)}, u32[]{:S(2)}) %collective-permute-start.17) | collective-permute-done | bytes 262176 | tf_op jit(solution)/shard_map/ppermute | solution.py:154
  93.8 0.7 collective-permute-start.23
  94.5 4.6 %collective-permute-start.20 = (bf16[512,256]{1,0:T(8,128)(2,1)S(1)}, bf16[512,256]{1,0:T(8,128)(2,1)S(1)}, u32[]{:S(2)}, u32[]{:S(2)}) collective-permute-start(bf16[512,256]{1,0:T(8,128)(2,1)S(1)} %fusion.13), channel_id=1, source_target_pairs={{0,4},{1,5},{2,6},{3,7},{16,20},{17,21},{18,22},{19,23}} | collective-permute-start | bytes 786440 | tf_op jit(solution)/shard_map/ppermute | solution.py:154
  99.0 0.6 dynamic_slice.44
  99.6 1.4 %collective-permute-start.18 = (bf16[512,256]{1,0:T(8,128)(2,1)S(1)}, bf16[512,256]{1,0:T(8,128)(2,1)S(1)}, u32[]{:S(2)}, u32[]{:S(2)}) collective-permute-start(bf16[512,256]{1,0:T(8,128)(2,1)S(1)} %get-tuple-element.26), channel_id=1, source_target_pairs={{0,2},{1,3},{2,0},{3,1},{4,6},{5,7},{6,4},{7,5},{8,10},{9,11},{10,... | collective-permute-start | bytes 786440 | tf_op jit(solution)/shard_map/ppermute | solution.py:154
  101.1 2.6 %collective-permute-done.20 = bf16[512,256]{1,0:T(8,128)(2,1)S(1)} collective-permute-done((bf16[512,256]{1,0:T(8,128)(2,1)S(1)}, bf16[512,256]{1,0:T(8,128)(2,1)S(1)}, u32[]{:S(2)}, u32[]{:S(2)}) %collective-permute-start.20) | collective-permute-done | bytes 262176 | tf_op jit(solution)/shard_map/ppermute | solution.py:154
  103.7 1.6 %add_convert_fusion.3 = (bf16[512,256]{1,0:T(8,128)(2,1)S(1)}, bf16[512,256]{1,0:T(8,128)(2,1)S(1)}) fusion(bf16[512,256]{1,0:T(8,128)(2,1)S(1)} %collective-permute-done.20, pred[]{:T(512)} %bitcast.16, bf16[512,256]{1,0:T(8,128)(2,1)S(1)} %collective-permute-done.19, bf16[2,4,512,256]{3,2,1,0:T(8,128)(2,1)S(1)} %bitcast.70, ...), kind=kLoop, calls=%fused_computation.10 | loop fusion | flops 2359296 | bytes 2621442 | tf_op jit(solution)/shard_map/convert_element_type | solution.py:282
  105.4 4.5 %collective-permute-start.21 = (bf16[512,256]{1,0:T(8,128)(2,1)S(1)}, bf16[512,256]{1,0:T(8,128)(2,1)S(1)}, u32[]{:S(2)}, u32[]{:S(2)}) collective-permute-start(bf16[512,256]{1,0:T(8,128)(2,1)S(1)} %get-tuple-element.22), channel_id=1, source_target_pairs={{0,4},{1,5},{2,6},{3,7},{4,8},{5,9},{6,10},{7,11},{16,20},{17,21},... | collective-permute-start | bytes 786440 | tf_op jit(solution)/shard_map/ppermute | solution.py:154
  109.9 0.7 collective-permute-start.24
  110.7 1.3 collective-permute-start.14
  112.0 3.0 %collective-permute-start.13 = (f32[256,128]{1,0:T(8,128)S(1)}, f32[256,128]{1,0:T(8,128)S(1)}, u32[]{:S(2)}, u32[]{:S(2)}) collective-permute-start(f32[256,128]{1,0:T(8,128)S(1)} %get-tuple-element.29), channel_id=1, source_target_pairs={{0,1},{1,2},{2,3},{3,4},{4,5},{5,6},{6,7},{7,8},{8,9},{9,10},{10,1... | collective-permute-start | bytes 393224 | tf_op jit(solution)/shard_map/ppermute | solution.py:154
  115.0 1.5 %collective-permute-start.16 = (bf16[512,256]{1,0:T(8,128)(2,1)S(1)}, bf16[512,256]{1,0:T(8,128)(2,1)S(1)}, u32[]{:S(2)}, u32[]{:S(2)}) collective-permute-start(bf16[512,256]{1,0:T(8,128)(2,1)S(1)} %get-tuple-element.24), channel_id=1, source_target_pairs={{0,2},{1,3},{2,0},{3,1},{4,6},{5,7},{6,4},{7,5},{8,10},{9,11},{10,... | collective-permute-start | bytes 786440 | tf_op jit(solution)/shard_map/ppermute | solution.py:154
  116.5 1.7 %add_convert_fusion.2 = (bf16[512,256]{1,0:T(8,128)(2,1)S(1)}, bf16[512,256]{1,0:T(8,128)(2,1)S(1)}) fusion(bf16[512,256]{1,0:T(8,128)(2,1)S(1)} %collective-permute-done.21, bf16[512,256]{1,0:T(8,128)(2,1)S(1)} %collective-permute-done.18, pred[]{:T(512)} %bitcast.3, bf16[2,4,512,256]{3,2,1,0:T(8,128)(2,1)S(1)} %bitcast.71, ...), kind=kLoop, calls=%fused_computation.9 | loop fusion | flops 3145728 | bytes 3407874 | tf_op jit(solution)/shard_map/convert_element_type | solution.py:282
  118.2 4.1 %collective-permute-start.22 = (bf16[512,256]{1,0:T(8,128)(2,1)S(1)}, bf16[512,256]{1,0:T(8,128)(2,1)S(1)}, u32[]{:S(2)}, u32[]{:S(2)}) collective-permute-start(bf16[512,256]{1,0:T(8,128)(2,1)S(1)} %get-tuple-element.20), channel_id=1, source_target_pairs={{0,4},{1,5},{2,6},{3,7},{4,8},{5,9},{6,10},{7,11},{8,12},{9,13},{1... | collective-permute-start | bytes 786440 | tf_op jit(solution)/shard_map/ppermute | solution.py:154
  122.4 1.3 collective-permute-start.25
  123.7 4.1 %unsmooth.1 = f32[256,512]{1,0:T(8,128)} custom-call(f32[256,128]{1,0:T(8,128)S(1)} %collective-permute-done.13.low, f32[256,512]{1,0:T(8,128)S(1)} %copy-done, f32[256,128]{1,0:T(8,128)S(1)} %collective-permute-done.14.high, f32[256,768]{1,0:T(8,128)S(1)} %get-tuple-element.9.k_spec, bf16[768,768]{1,0:T(8,128)(2,1)S(1)} %copy-done.2, ...), custom_call_target="tpu_custom_call" | custom-call | flops 1509949440 | bytes 6291456 | tf_op jit(solution)/shard_map/unsmooth/pallas_call | solution.py:289
  127.8 1.2 collective-permute-done.22
  129.0 4.1 %collective-permute-done.25 = bf16[512,256]{1,0:T(8,128)(2,1)S(1)} collective-permute-done((bf16[512,256]{1,0:T(8,128)(2,1)S(1)}, bf16[512,256]{1,0:T(8,128)(2,1)S(1)}, u32[]{:S(2)}, u32[]{:S(2)}) %collective-permute-start.25) | collective-permute-done | bytes 262176 | tf_op jit(solution)/shard_map/ppermute | solution.py:154
  133.1 0.9 fusion.1
  (57 shorter events, 1.5 us)
Async XLA Ops:
  0.6 11.4 %collective-permute-start.1 = (bf16[512,256]{1,0:T(8,128)(2,1)}, bf16[512,256]{1,0:T(8,128)(2,1)S(1)}, u32[]{:S(2)}, u32[]{:S(2)}) collective-permute-start(bf16[512,256]{1,0:T(8,128)(2,1)} %param.29), channel_id=1, source_target_pairs={{4,0},{5,1},{6,2},{7,3},{8,4},{9,5},{10,6},{11,7},{12,8},{13,9},{1... | collective-permute-start | bytes 786440 | tf_op jit(solution)/shard_map/ppermute | solution.py:154
  1.9 11.4 %collective-permute-start = (bf16[512,256]{1,0:T(8,128)(2,1)}, bf16[512,256]{1,0:T(8,128)(2,1)S(1)}, u32[]{:S(2)}, u32[]{:S(2)}) collective-permute-start(bf16[512,256]{1,0:T(8,128)(2,1)} %param.29), channel_id=1, source_target_pairs={{0,4},{1,5},{2,6},{3,7},{4,8},{5,9},{6,10},{7,11},{8,12},{9,13},{1... | collective-permute-start | bytes 786440 | tf_op jit(solution)/shard_map/ppermute | solution.py:154
  12.1 10.5 %collective-permute-start.3 = (bf16[512,256]{1,0:T(8,128)(2,1)S(1)}, bf16[512,256]{1,0:T(8,128)(2,1)S(1)}, u32[]{:S(2)}, u32[]{:S(2)}) collective-permute-start(bf16[512,256]{1,0:T(8,128)(2,1)S(1)} %collective-permute-done.1), channel_id=1, source_target_pairs={{4,0},{5,1},{6,2},{7,3},{8,4},{9,5},{10,6},{11,7},{20,16},{21,17},... | collective-permute-start | bytes 786440 | tf_op jit(solution)/shard_map/ppermute | solution.py:154
  13.4 10.5 %collective-permute-start.2 = (bf16[512,256]{1,0:T(8,128)(2,1)S(1)}, bf16[512,256]{1,0:T(8,128)(2,1)S(1)}, u32[]{:S(2)}, u32[]{:S(2)}) collective-permute-start(bf16[512,256]{1,0:T(8,128)(2,1)S(1)} %collective-permute-done), channel_id=1, source_target_pairs={{4,8},{5,9},{6,10},{7,11},{8,12},{9,13},{10,14},{11,15},{20,24},{2... | collective-permute-start | bytes 786440 | tf_op jit(solution)/shard_map/ppermute | solution.py:154
  14.1 23.4 %collective-permute-start.6 = (bf16[512,256]{1,0:T(8,128)(2,1)}, bf16[512,256]{1,0:T(8,128)(2,1)}, u32[]{:S(2)}, u32[]{:S(2)}) collective-permute-start(bf16[512,256]{1,0:T(8,128)(2,1)} %param.29), channel_id=1, source_target_pairs={{0,2},{1,3},{2,0},{3,1},{4,6},{5,7},{6,4},{7,5},{8,10},{9,11},{10,... | collective-permute-start | bytes 786440 | tf_op jit(solution)/shard_map/ppermute | solution.py:154
  22.6 11.3 %collective-permute-start.5 = (bf16[512,256]{1,0:T(8,128)(2,1)S(1)}, bf16[512,256]{1,0:T(8,128)(2,1)S(1)}, u32[]{:S(2)}, u32[]{:S(2)}) collective-permute-start(bf16[512,256]{1,0:T(8,128)(2,1)S(1)} %collective-permute-done.3), channel_id=1, source_target_pairs={{4,0},{5,1},{6,2},{7,3},{20,16},{21,17},{22,18},{23,19}} | collective-permute-start | bytes 786440 | tf_op jit(solution)/shard_map/ppermute | solution.py:154
  23.9 10.0 %copy-start.11 = (bf16[512,256]{1,0:T(8,128)(2,1)}, bf16[512,256]{1,0:T(8,128)(2,1)S(1)}, u32[]{:S(2)}) copy-start(bf16[512,256]{1,0:T(8,128)(2,1)S(1)} %collective-permute-done.2) | copy-start | bytes 786436
  23.9 10.0 %collective-permute-start.4 = (bf16[512,256]{1,0:T(8,128)(2,1)S(1)}, bf16[512,256]{1,0:T(8,128)(2,1)S(1)}, u32[]{:S(2)}, u32[]{:S(2)}) collective-permute-start(bf16[512,256]{1,0:T(8,128)(2,1)S(1)} %collective-permute-done.2), channel_id=1, source_target_pairs={{8,12},{9,13},{10,14},{11,15},{24,28},{25,29},{26,30},{27,31}} | collective-permute-start | bytes 786440 | tf_op jit(solution)/shard_map/ppermute | solution.py:154
  26.0 13.1 %collective-permute-start.7 = (bf16[512,256]{1,0:T(8,128)(2,1)S(1)}, bf16[512,256]{1,0:T(8,128)(2,1)S(1)}, u32[]{:S(2)}, u32[]{:S(2)}) collective-permute-start(bf16[512,256]{1,0:T(8,128)(2,1)S(1)} %get-tuple-element.17), channel_id=1, source_target_pairs={{0,2},{1,3},{2,0},{3,1},{4,6},{5,7},{6,4},{7,5},{8,10},{9,11},{10,... | collective-permute-start | bytes 786440 | tf_op jit(solution)/shard_map/ppermute | solution.py:154
  28.5 16.4 %copy-start.6 = (f32[256,512]{1,0:T(8,128)S(1)}, f32[256,512]{1,0:T(8,128)}, u32[]{:S(2)}) copy-start(f32[256,512]{1,0:T(8,128)} %mid.1) | copy-start | bytes 1572868
  28.5 11.5 %collective-permute-start.8 = (bf16[512,256]{1,0:T(8,128)(2,1)S(1)}, bf16[512,256]{1,0:T(8,128)(2,1)S(1)}, u32[]{:S(2)}, u32[]{:S(2)}) collective-permute-start(bf16[512,256]{1,0:T(8,128)(2,1)S(1)} %get-tuple-element.15), channel_id=1, source_target_pairs={{0,2},{1,3},{2,0},{3,1},{4,6},{5,7},{6,4},{7,5},{8,10},{9,11},{10,... | collective-permute-start | bytes 786440 | tf_op jit(solution)/shard_map/ppermute | solution.py:154
  33.9 16.0 %copy-start.13 = (s32[1,2,8]{2,1,0:T(2,128)S(1)}, s32[1,2,8]{2,1,0:T(2,128)}, u32[]{:S(2)}) copy-start(s32[1,2,8]{2,1,0:T(2,128)} %param.31) | copy-start | bytes 196
  33.9 17.3 %copy-start.14 = (s32[1,2,8]{2,1,0:T(2,128)S(1)}, s32[1,2,8]{2,1,0:T(2,128)}, u32[]{:S(2)}) copy-start(s32[1,2,8]{2,1,0:T(2,128)} %param.32) | copy-start | bytes 196
  33.9 22.4 %copy-start.12 = (s32[2,8,4]{1,2,0:T(4,128)S(1)}, s32[2,8,4]{1,2,0:T(4,128)}, u32[]{:S(2)}) copy-start(s32[2,8,4]{1,2,0:T(4,128)} %param.33) | copy-start | bytes 772
  33.9 24.2 %copy-start.1 = (bf16[768,768]{1,0:T(8,128)(2,1)S(1)}, bf16[768,768]{1,0:T(8,128)(2,1)}, u32[]{:S(2)}) copy-start(bf16[768,768]{1,0:T(8,128)(2,1)} %constant.108.clone.fl) | copy-start | bytes 3538948
  33.9 24.2 %copy-start.2 = (bf16[768,768]{1,0:T(8,128)(2,1)S(1)}, bf16[768,768]{1,0:T(8,128)(2,1)}, u32[]{:S(2)}) copy-start(bf16[768,768]{1,0:T(8,128)(2,1)} %constant.107.clone.fh) | copy-start | bytes 3538948
  34.0 24.2 %copy-start.7 = (f32[256,256]{1,0:T(8,128)S(1)}, f32[256,256]{1,0:T(8,128)}, u32[]{:S(2)}) copy-start(f32[256,256]{1,0:T(8,128)} %taps.1) | copy-start | bytes 786436
  36.9 7.2 %collective-permute-start.9 = (bf16[512,256]{1,0:T(8,128)(2,1)S(1)}, bf16[512,256]{1,0:T(8,128)(2,1)S(1)}, u32[]{:S(2)}, u32[]{:S(2)}) collective-permute-start(bf16[512,256]{1,0:T(8,128)(2,1)S(1)} %get-tuple-element.13), channel_id=1, source_target_pairs={{0,2},{1,3},{2,0},{3,1},{4,6},{5,7},{6,4},{7,5},{8,10},{9,11},{10,... | collective-permute-start | bytes 786440 | tf_op jit(solution)/shard_map/ppermute | solution.py:154
  44.9 19.9 %collective-permute-start.10 = (bf16[4096,256]{1,0:T(8,128)(2,1)}, bf16[4096,256]{1,0:T(8,128)(2,1)}, u32[]{:S(2)}, u32[]{:S(2)}) collective-permute-start(bf16[4096,256]{1,0:T(8,128)(2,1)} %constant_dynamic-update-slice_fusion.mine), channel_id=1, source_target_pairs={{0,1},{1,0},{2,3},{3,2},{4,5},{5,4},{6,7},{7,6},{8,9},{9,8},{10,11... | collective-permute-start | bytes 6291464 | tf_op jit(solution)/shard_map/ppermute | solution.py:154
  45.6 12.6 %collective-permute-start.12 = (f32[256,128]{1,0:T(8,128)}, f32[256,128]{1,0:T(8,128)S(1)}, u32[]{:S(2)}, u32[]{:S(2)}) collective-permute-start(f32[256,128]{1,0:T(8,128)} %get-tuple-element.30), channel_id=1, source_target_pairs={{1,0},{2,1},{3,2},{4,3},{5,4},{6,5},{7,6},{8,7},{9,8},{10,9},{11,1... | collective-permute-start | bytes 393224 | tf_op jit(solution)/shard_map/ppermute | solution.py:154
  46.9 11.3 %collective-permute-start.11 = (f32[256,128]{1,0:T(8,128)S(1)}, f32[256,128]{1,0:T(8,128)S(1)}, u32[]{:S(2)}, u32[]{:S(2)}) collective-permute-start(f32[256,128]{1,0:T(8,128)S(1)} %get-tuple-element.31), channel_id=1, source_target_pairs={{0,1},{1,2},{2,3},{3,4},{4,5},{5,6},{6,7},{7,8},{8,9},{9,10},{10,1... | collective-permute-start | bytes 393224 | tf_op jit(solution)/shard_map/ppermute | solution.py:154
  58.2 1.1 copy-start.8
  59.3 1.1 copy-start.9
  64.0 0.7 copy-start.5
  74.9 18.7 %copy-start.10 = (bf16[4096,256]{1,0:T(8,128)(2,1)S(1)}, bf16[4096,256]{1,0:T(8,128)(2,1)}, u32[]{:S(2)}) copy-start(bf16[4096,256]{1,0:T(8,128)(2,1)} %get-tuple-element.10) | copy-start | bytes 6291460
  74.9 5.8 %collective-permute-start.15 = (bf16[4096,256]{1,0:T(8,128)(2,1)}, bf16[4096,256]{1,0:T(8,128)(2,1)S(1)}, u32[]{:S(2)}, u32[]{:S(2)}) collective-permute-start(bf16[4096,256]{1,0:T(8,128)(2,1)} %get-tuple-element.11), channel_id=1, source_target_pairs={{0,1},{1,0},{2,3},{3,2},{4,5},{5,4},{6,7},{7,6},{8,9},{9,8},{10,11... | collective-permute-start | bytes 6291464 | tf_op jit(solution)/shard_map/ppermute | solution.py:154
  80.7 18.3 %copy-start.15 = (pred[4]{0:T(512)(128)(4,1)S(1)}, pred[4]{0:T(512)(128)(4,1)}, u32[]{:S(2)}) copy-start(pred[4]{0:T(512)(128)(4,1)} %constant.112.clone) | copy-start | bytes 16
  82.2 28.4 %copy-start = (f32[256,512]{1,0:T(8,128)S(1)}, f32[256,512]{1,0:T(8,128)}, u32[]{:S(2)}) copy-start(f32[256,512]{1,0:T(8,128)} %get-tuple-element.8.mid) | copy-start | bytes 1572868
  82.2 11.5 %collective-permute-start.17 = (bf16[512,256]{1,0:T(8,128)(2,1)S(1)}, bf16[512,256]{1,0:T(8,128)(2,1)S(1)}, u32[]{:S(2)}, u32[]{:S(2)}) collective-permute-start(bf16[512,256]{1,0:T(8,128)(2,1)S(1)} %get-tuple-element.27), channel_id=1, source_target_pairs={{0,2},{1,3},{2,0},{3,1},{4,6},{5,7},{6,4},{7,5},{8,10},{9,11},{10,... | collective-permute-start | bytes 786440 | tf_op jit(solution)/shard_map/ppermute | solution.py:154
  86.5 14.6 %collective-permute-start.19 = (bf16[512,256]{1,0:T(8,128)(2,1)S(1)}, bf16[512,256]{1,0:T(8,128)(2,1)S(1)}, u32[]{:S(2)}, u32[]{:S(2)}) collective-permute-start(bf16[512,256]{1,0:T(8,128)(2,1)S(1)} %get-tuple-element.25), channel_id=1, source_target_pairs={{0,2},{1,3},{2,0},{3,1},{4,6},{5,7},{6,4},{7,5},{8,10},{9,11},{10,... | collective-permute-start | bytes 786440 | tf_op jit(solution)/shard_map/ppermute | solution.py:154
  93.8 7.3 %collective-permute-start.23 = (bf16[512,256]{1,0:T(8,128)(2,1)S(1)}, bf16[512,256]{1,0:T(8,128)(2,1)S(1)}, u32[]{:S(2)}, u32[]{:S(2)}) collective-permute-start(bf16[512,256]{1,0:T(8,128)(2,1)S(1)} %fusion.13), channel_id=1, source_target_pairs={{12,8},{13,9},{14,10},{15,11},{28,24},{29,25},{30,26},{31,27}} | collective-permute-start | bytes 786440 | tf_op jit(solution)/shard_map/ppermute | solution.py:154
  94.5 9.3 %collective-permute-start.20 = (bf16[512,256]{1,0:T(8,128)(2,1)S(1)}, bf16[512,256]{1,0:T(8,128)(2,1)S(1)}, u32[]{:S(2)}, u32[]{:S(2)}) collective-permute-start(bf16[512,256]{1,0:T(8,128)(2,1)S(1)} %fusion.13), channel_id=1, source_target_pairs={{0,4},{1,5},{2,6},{3,7},{16,20},{17,21},{18,22},{19,23}} | collective-permute-start | bytes 786440 | tf_op jit(solution)/shard_map/ppermute | solution.py:154
  99.6 15.4 %collective-permute-start.18 = (bf16[512,256]{1,0:T(8,128)(2,1)S(1)}, bf16[512,256]{1,0:T(8,128)(2,1)S(1)}, u32[]{:S(2)}, u32[]{:S(2)}) collective-permute-start(bf16[512,256]{1,0:T(8,128)(2,1)S(1)} %get-tuple-element.26), channel_id=1, source_target_pairs={{0,2},{1,3},{2,0},{3,1},{4,6},{5,7},{6,4},{7,5},{8,10},{9,11},{10,... | collective-permute-start | bytes 786440 | tf_op jit(solution)/shard_map/ppermute | solution.py:154
  105.4 18.3 %copy-start.3 = (bf16[768,512]{1,0:T(8,128)(2,1)S(1)}, bf16[768,512]{1,0:T(8,128)(2,1)}, u32[]{:S(2)}) copy-start(bf16[768,512]{1,0:T(8,128)(2,1)} %constant.114.clone.wl) | copy-start | bytes 2359300
  105.4 18.3 %copy-start.4 = (bf16[768,512]{1,0:T(8,128)(2,1)S(1)}, bf16[768,512]{1,0:T(8,128)(2,1)}, u32[]{:S(2)}) copy-start(bf16[768,512]{1,0:T(8,128)(2,1)} %constant.113.clone.wh) | copy-start | bytes 2359300
  105.4 11.1 %collective-permute-start.21 = (bf16[512,256]{1,0:T(8,128)(2,1)S(1)}, bf16[512,256]{1,0:T(8,128)(2,1)S(1)}, u32[]{:S(2)}, u32[]{:S(2)}) collective-permute-start(bf16[512,256]{1,0:T(8,128)(2,1)S(1)} %get-tuple-element.22), channel_id=1, source_target_pairs={{0,4},{1,5},{2,6},{3,7},{4,8},{5,9},{6,10},{7,11},{16,20},{17,21},... | collective-permute-start | bytes 786440 | tf_op jit(solution)/shard_map/ppermute | solution.py:154
  109.9 6.6 %collective-permute-start.24 = (bf16[512,256]{1,0:T(8,128)(2,1)S(1)}, bf16[512,256]{1,0:T(8,128)(2,1)S(1)}, u32[]{:S(2)}, u32[]{:S(2)}) collective-permute-start(bf16[512,256]{1,0:T(8,128)(2,1)S(1)} %get-tuple-element.23), channel_id=1, source_target_pairs={{8,4},{9,5},{10,6},{11,7},{12,8},{13,9},{14,10},{15,11},{24,20},{2... | collective-permute-start | bytes 786440 | tf_op jit(solution)/shard_map/ppermute | solution.py:154
  110.7 13.0 %collective-permute-start.14 = (f32[256,128]{1,0:T(8,128)S(1)}, f32[256,128]{1,0:T(8,128)S(1)}, u32[]{:S(2)}, u32[]{:S(2)}) collective-permute-start(f32[256,128]{1,0:T(8,128)S(1)} %get-tuple-element.28), channel_id=1, source_target_pairs={{1,0},{2,1},{3,2},{4,3},{5,4},{6,5},{7,6},{8,7},{9,8},{10,9},{11,1... | collective-permute-start | bytes 393224 | tf_op jit(solution)/shard_map/ppermute | solution.py:154
  112.0 11.7 %collective-permute-start.13 = (f32[256,128]{1,0:T(8,128)S(1)}, f32[256,128]{1,0:T(8,128)S(1)}, u32[]{:S(2)}, u32[]{:S(2)}) collective-permute-start(f32[256,128]{1,0:T(8,128)S(1)} %get-tuple-element.29), channel_id=1, source_target_pairs={{0,1},{1,2},{2,3},{3,4},{4,5},{5,6},{6,7},{7,8},{8,9},{9,10},{10,1... | collective-permute-start | bytes 393224 | tf_op jit(solution)/shard_map/ppermute | solution.py:154
  115.0 12.8 %collective-permute-start.16 = (bf16[512,256]{1,0:T(8,128)(2,1)S(1)}, bf16[512,256]{1,0:T(8,128)(2,1)S(1)}, u32[]{:S(2)}, u32[]{:S(2)}) collective-permute-start(bf16[512,256]{1,0:T(8,128)(2,1)S(1)} %get-tuple-element.24), channel_id=1, source_target_pairs={{0,2},{1,3},{2,0},{3,1},{4,6},{5,7},{6,4},{7,5},{8,10},{9,11},{10,... | collective-permute-start | bytes 786440 | tf_op jit(solution)/shard_map/ppermute | solution.py:154
  118.2 10.8 %collective-permute-start.22 = (bf16[512,256]{1,0:T(8,128)(2,1)S(1)}, bf16[512,256]{1,0:T(8,128)(2,1)S(1)}, u32[]{:S(2)}, u32[]{:S(2)}) collective-permute-start(bf16[512,256]{1,0:T(8,128)(2,1)S(1)} %get-tuple-element.20), channel_id=1, source_target_pairs={{0,4},{1,5},{2,6},{3,7},{4,8},{5,9},{6,10},{7,11},{8,12},{9,13},{1... | collective-permute-start | bytes 786440 | tf_op jit(solution)/shard_map/ppermute | solution.py:154
  122.4 10.8 %collective-permute-start.25 = (bf16[512,256]{1,0:T(8,128)(2,1)S(1)}, bf16[512,256]{1,0:T(8,128)(2,1)S(1)}, u32[]{:S(2)}, u32[]{:S(2)}) collective-permute-start(bf16[512,256]{1,0:T(8,128)(2,1)S(1)} %get-tuple-element.21), channel_id=1, source_target_pairs={{4,0},{5,1},{6,2},{7,3},{8,4},{9,5},{10,6},{11,7},{12,8},{13,9},{1... | collective-permute-start | bytes 786440 | tf_op jit(solution)/shard_map/ppermute | solution.py:154

commit v2 on v1

v2 whole, which is shorter than its diff:
```python
import functools

import jax
import jax.numpy as jnp
import numpy as np
from jax import lax
from jax.experimental import pallas as pl
from jax.experimental.pallas import tpu as pltpu
from jax.sharding import PartitionSpec as P

BLK = 128
ROW = 4
F32 = jnp.float32
BF16 = jnp.bfloat16
VMEM = pl.BlockSpec(memory_space=pltpu.VMEM)
ANY = pl.BlockSpec(memory_space=pl.ANY)


def split_const(a):
    high = a.astype(jnp.bfloat16)
    low = (a - high.astype(np.float64)).astype(jnp.bfloat16)
    return high, low


@functools.lru_cache(maxsize=None)
def dft_tables(length, outputs, first):
    half = length // 2
    t = np.arange(length)[:, None]
    f = np.arange(half)[None, :]
    angle = 2 * np.pi * ((t * f) % length) / length
    cos, sin = np.cos(angle), np.sin(angle)
    sin[:, 0] = 1 - 2 * (np.arange(length) % 2)
    forward = np.concatenate([cos, sin], axis=1)
    weight = np.full((half,), 2.0 / length)
    weight[0] = 1.0 / length
    inverse = (forward * np.concatenate([weight, weight])[None, :]).T
    inverse = inverse[:, first : first + outputs]
    return split_const(forward) + split_const(inverse)


def dot3(a, b_high, b_low):
    high = a.astype(BF16)
    low = (a - high.astype(F32)).astype(BF16)
    out = jnp.dot(high, b_high, preferred_element_type=F32)
    out += jnp.dot(low, b_high, preferred_element_type=F32)
    out += jnp.dot(high, b_low, preferred_element_type=F32)
    return out


def product(signal, taps, sign):
    half = signal.shape[1] // 2
    xr, xi = signal[:, :half], signal[:, half:]
    kr, ki = taps[:, :half], taps[:, half:]
    first = lax.broadcasted_iota(jnp.int32, kr.shape, 1) == 0
    kr_i = jnp.where(first, ki, kr)
    ki_x = jnp.where(first, 0.0, ki) * sign
    return jnp.concatenate([xr * kr + xi * ki_x, xi * kr_i - xr * ki_x], axis=1)


def smooth_kernel(low, mid, high, taps, fh, fl, wh, wl, out, spectrum):
    width = low.shape[1]
    bins = mid.shape[1]
    k_spec = dot3(taps[...], fh[: taps.shape[1]], fl[: taps.shape[1]])
    spectrum[...] = k_spec
    x_spec = dot3(mid[...], fh[width : width + bins], fl[width : width + bins])
    x_spec += dot3(low[...], fh[:width], fl[:width])
    x_spec += dot3(high[...], fh[width + bins :], fl[width + bins :])
    out[...] = dot3(product(x_spec, k_spec, 1.0), wh[...], wl[...]).astype(out.dtype)


def unsmooth_kernel(low, mid, high, k_spec, fh, fl, wh, wl, out):
    width = low.shape[1]
    bins = mid.shape[1]
    x_spec = dot3(mid[...], fh[width : width + bins], fl[width : width + bins])
    x_spec += dot3(low[...], fh[:width], fl[:width])
    x_spec += dot3(high[...], fh[width + bins :], fl[width + bins :])
    out[...] = dot3(product(x_spec, k_spec[...], -1.0), wh[...], wl[...])


def place_of(ids, e, entries, me, forward):
    chain = lax.axis_size("tm") // ROW
    owner, slot = ids[e], ids[entries + e]
    owner_z, owner_y, owner_c = owner // ROW, (owner // 2) % 2, owner % 2
    z, y = me // ROW, (me // 2) % 2
    step = (owner_z - z) if forward else (z - owner_z)
    turn = jnp.where(step < 0, step + chain, step)
    piece = jnp.where(owner_y == y, 0, chain) + turn
    return owner_c, piece, pl.multiple_of(slot * BLK, BLK)


def pack_kernel(entries, ids, asked, *refs):
    pieces, (out, sem) = refs[:-2], refs[-2:]
    me = ids[2 * entries]

    def copy(piece, e, row):
        return pltpu.make_async_copy(
            piece.at[pl.ds(row, BLK)], out.at[pl.ds(pl.multiple_of(e * BLK, BLK), BLK)], sem.at[e]
        )

    def start(e, _):
        core, piece, row = place_of(asked, e, entries, me, False)
        for q, ref in enumerate(pieces):

            @pl.when(jnp.logical_and(core == me % 2, piece == q))
            def _():
                copy(ref, e, row).start()

        return 0

    def wait(e, _):
        core, _, row = place_of(asked, e, entries, me, False)

        @pl.when(core == me % 2)
        def _():
            copy(pieces[0], e, row).wait()

        return 0

    lax.fori_loop(0, entries, start, 0)
    lax.fori_loop(0, entries, wait, 0)


def session_kernel(entries, group, ids, mask, smoothed, recorded, packed, *refs):
    pieces = refs[:-7]
    grad, grad_low, grad_high, terms, rows, resid, sem = refs[-7:]
    bins = smoothed.shape[1]
    me = ids[2 * entries]

    def copy(source, e, row):
        return pltpu.make_async_copy(source.at[pl.ds(row, BLK)], rows.at[e], sem.at[e])

    def fetch(e, _):
        core, piece, row = place_of(ids, e, entries, me, False)
        for q, ref in enumerate(pieces):

            @pl.when(jnp.logical_and(core == me % 2, piece == q))
            def _():
                copy(ref, e, row).start()

        @pl.when(core != me % 2)
        def _():
            copy(packed, e, pl.multiple_of(e * BLK, BLK)).start()

        return 0

    lax.fori_loop(0, entries, fetch, 0)
    grad[...] = jnp.zeros_like(grad)
    depth = group * BLK

    def step(g, _):
        for i in range(group):
            copy(packed, g * group + i, 0).wait()
        block = rows[pl.ds(g * group, group)].reshape(depth, rows.shape[2])
        predicted = jnp.dot(block, smoothed[...], preferred_element_type=F32)
        for i in range(group):
            e = g * group + i
            for t in range(bins // BLK):
                cut = slice(t * BLK, (t + 1) * BLK)
                weight = mask[e * (bins // BLK) + t].astype(F32)
                part = predicted[i * BLK : (i + 1) * BLK, cut]
                seen = recorded[e, :, cut].astype(F32)
                resid[i * BLK : (i + 1) * BLK, cut] = (weight * (part - seen)).astype(BF16)
        term = lax.dot_general(
            resid[...], smoothed[...], (((1,), (1,)), ((), ())), preferred_element_type=F32
        )
        target = pl.ds(pl.multiple_of(g * depth, depth), depth)
        terms[target] = (term * (1.0 / BLK)).astype(BF16)
        grad[...] += lax.dot_general(
            block, resid[...], (((0,), (0,)), ((), ())), preferred_element_type=F32
        ) * (1.0 / BLK)
        return 0

    lax.fori_loop(0, entries // group, step, 0)
    width = grad_low.shape[1]
    grad_low[...] = grad[:, bins - width :]
    grad_high[...] = grad[:, :width]


def merge_kernel(entries, ids, asked, own, got, *refs):
    outs, sums = refs[:-1], refs[-1]
    me = ids[2 * entries]
    chunk = outs[0].shape[0]
    sums[...] = jnp.zeros_like(sums)

    def add(e, _):
        source = pl.ds(pl.multiple_of(e * BLK, BLK), BLK)
        for names, terms in ((ids, own), (asked, got)):
            core, piece, row = place_of(names, e, entries, me, True)

            @pl.when(core == me % 2)
            def _():
                target = pl.ds(pl.multiple_of(piece * chunk + row, BLK), BLK)
                sums[target] += terms[source].astype(F32)

        return 0

    lax.fori_loop(0, entries, add, 0)
    for q, out in enumerate(outs):
        out[...] = sums[q * chunk : (q + 1) * chunk].astype(out.dtype)


def local(latents, kernel, loadings, recorded, owner_ids, local_ids, recorded_mask):
    latent_dim, bins = latents.shape
    halfwidth = kernel.shape[1] // 2
    count = lax.axis_size("tm")
    chain = count // ROW
    chunk = loadings.shape[0]
    entries = owner_ids.size
    smem = pl.BlockSpec(memory_space=pltpu.SMEM)

    def permute(x, pairs):
        return lax.ppermute(x, "tm", pairs)

    def rotate(x, r):
        return permute(x, [(i, (i + r * ROW) % count) for i in range(count)])

    def flip(x, bit):
        return permute(x, [(i, i ^ bit) for i in range(count)])

    up_one = [(i, i + 1) for i in range(count - 1)]
    down_one = [(i + 1, i) for i in range(count - 1)]

    me = jnp.full((1,), lax.axis_index("tm"), jnp.int32)
    ids = jnp.concatenate([owner_ids.reshape(-1), local_ids.reshape(-1), me])
    asked = flip(ids, 1)

    low = permute(latents[:, bins - halfwidth :], up_one)
    high = permute(latents[:, :halfwidth], down_one)

    pieces = [loadings] + [rotate(loadings, r) for r in range(1, chain)]
    pieces += [flip(piece, 2) for piece in pieces]

    length = bins + 2 * halfwidth
    fh, fl, wh, wl = dft_tables(length, bins, 0)
    mxu = latent_dim * length * (length + bins) * 6
    smoothed, spectrum = pl.pallas_call(
        smooth_kernel,
        out_shape=(
            jax.ShapeDtypeStruct((latent_dim, bins), BF16),
            jax.ShapeDtypeStruct((latent_dim, length), F32),
        ),
        in_specs=[VMEM] * 8,
        out_specs=(VMEM, VMEM),
        compiler_params=pltpu.CompilerParams(vmem_limit_bytes=40 * 2**20),
        cost_estimate=pl.CostEstimate(flops=mxu, bytes_accessed=6 * 2**20, transcendentals=0),
        name="smooth",
    )(low, latents, high, kernel, fh, fl, wh, wl)

    slots = jax.ShapeDtypeStruct((entries * BLK, latent_dim), BF16)
    packed = pl.pallas_call(
        functools.partial(pack_kernel, entries),
        out_shape=slots,
        in_specs=[smem] * 2 + [ANY] * len(pieces),
        out_specs=ANY,
        scratch_shapes=[pltpu.SemaphoreType.DMA((entries,))],
        cost_estimate=pl.CostEstimate(flops=0, bytes_accessed=2 * 2**20, transcendentals=0),
        name="pack",
    )(ids, asked, *pieces)
    packed = flip(packed, 1)

    group = 4
    strip = jax.ShapeDtypeStruct((latent_dim, halfwidth), F32)
    grad, grad_low, grad_high, terms = pl.pallas_call(
        functools.partial(session_kernel, entries, group),
        out_shape=(jax.ShapeDtypeStruct((latent_dim, bins), F32), strip, strip, slots),
        in_specs=[smem] * 2 + [VMEM] * 2 + [ANY] * (1 + len(pieces)),
        out_specs=(VMEM,) * 4,
        scratch_shapes=[
            pltpu.VMEM((entries, BLK, latent_dim), BF16),
            pltpu.VMEM((group * BLK, bins), BF16),
            pltpu.SemaphoreType.DMA((entries,)),
        ],
        compiler_params=pltpu.CompilerParams(vmem_limit_bytes=56 * 2**20),
        cost_estimate=pl.CostEstimate(
            flops=6 * entries * BLK * latent_dim * bins, bytes_accessed=8 * 2**20, transcendentals=0
        ),
        name="session",
    )(
        ids,
        recorded_mask.reshape(-1),
        smoothed,
        recorded.reshape(entries, BLK, bins),
        packed,
        *pieces,
    )

    got = flip(terms, 1)
    grad_low = permute(grad_low, up_one)
    grad_high = permute(grad_high, down_one)
    sums = pl.pallas_call(
        functools.partial(merge_kernel, entries),
        out_shape=(jax.ShapeDtypeStruct((chunk, latent_dim), F32),) * chain
        + (jax.ShapeDtypeStruct((chunk, latent_dim), BF16),) * chain,
        in_specs=[smem] * 2 + [VMEM] * 2,
        out_specs=(VMEM,) * (2 * chain),
        scratch_shapes=[pltpu.VMEM((2 * chain * chunk, latent_dim), F32)],
        compiler_params=pltpu.CompilerParams(vmem_limit_bytes=60 * 2**20),
        cost_estimate=pl.CostEstimate(flops=0, bytes_accessed=5 * 2**20, transcendentals=0),
        name="merge",
    )(ids, asked, terms, got)
    turned = []
    far_first = sorted(range(chain), key=lambda r: -min(r, chain - r))
    for r in far_first:
        total = sums[r] + flip(sums[chain + r], 2).astype(F32)
        if r:
            turned.append(rotate(total.astype(BF16), r))
        else:
            loading_grad = total
    for part in turned:
        loading_grad = loading_grad + part.astype(F32)

    fh, fl, wh, wl = dft_tables(length, bins, 2 * halfwidth)
    latent_grad = pl.pallas_call(
        unsmooth_kernel,
        out_shape=jax.ShapeDtypeStruct((latent_dim, bins), F32),
        in_specs=[VMEM] * 8,
        out_specs=VMEM,
        compiler_params=pltpu.CompilerParams(vmem_limit_bytes=40 * 2**20),
        cost_estimate=pl.CostEstimate(flops=mxu, bytes_accessed=6 * 2**20, transcendentals=0),
        name="unsmooth",
    )(grad_low, grad, grad_high, spectrum, fh, fl, wh, wl)
    return latent_grad, loading_grad


def solution(mesh):
    return jax.shard_map(
        local,
        mesh=mesh,
        in_specs=(
            P(None, ("groups", "tm")),
            P(),
            P(("groups", "tm"), None),
            P(None, None, None, ("groups", "tm")),
            P(("groups", "tm"), None, None),
            P(("groups", "tm"), None, None),
            P(None, None, ("groups", "tm")),
        ),
        out_specs=(P(None, ("groups", "tm")), P(("groups", "tm"), None)),
        check_vma=False,
    )
```

time: 135 us -> 138 us (1.022)
  waiting for transfers between devices: 30.9 us -> 52.1 us
  Pallas kernels: 17.9 us -> 38.8 us
  starting transfers between devices: 48.8 us -> 34.3 us
  other arithmetic: 16.6 us -> 2.22 us
  local copies, waits for them, and re-layouts: 18.9 us -> 8.58 us
    ppermute x26 -> x21, waiting for transfers between devices: 30.9 us -> 52.1 us  [permute(): return lax.ppermute(x, 'tm', pairs)]
    pallas_call x1 -> x3, Pallas kernels: 10.2 us -> 31.1 us  [the longest x1 19.8 us: local(): pl.pallas_call(functools.partial(pack_kernel, entries), out_shape=slots,...]
    ppermute x26 -> x21, starting transfers between devices: 48.8 us -> 34.3 us  [permute(): return lax.ppermute(x, 'tm', pairs)]
    unnamed x3 -> x0, other arithmetic: 6.51 us -> none
    dynamic_slice x5 -> x0, local copies, waits for them, and re-layouts: 5.67 us -> none  [choose(): hit = jnp.asarray([o is d for o in options])[my_z]]
    convert_element_type x5 -> x3, other arithmetic: 6.09 us -> 1.21 us  [local(): turned.append(rotate(total.astype(BF16), r))]
    unnamed x37 -> x43, local copies, waits for them, and re-layouts: 7.97 us -> 5.72 us
    add x3 -> x1, other arithmetic: 2.77 us -> 0.93 us  [local(): loading_grad = loading_grad + part.astype(F32)]
  transfers between devices with their start and end apart: 26 -> 21, of which waited for: 9 -> 11; matrix products, arithmetic and copies ran while one was open for 22% -> 3% of each run, Pallas kernels for 6% -> 6%
where the time goes in v2:
time: 138 us; the launch traced here: 137 us
  waiting for transfers between devices  52.1 us (38%)
  Pallas kernels  38.8 us (28%)
  starting transfers between devices  34.3 us (25%)
  local copies, waits for them, and re-layouts  8.58 us (6%)
  other arithmetic  2.22 us (2%)
    ppermute x21, waiting for transfers between devices, permute(): return lax.ppermute(x, 'tm', pairs)  52.1 us
    ppermute x21, starting transfers between devices, permute(): return lax.ppermute(x, 'tm', pairs)  34.3 us
    pallas_call x1, Pallas kernels, local(): pl.pallas_call(functools.partial(pack_kernel, entries), out_shape=slots,...  19.8 us
    pallas_call x1, Pallas kernels, local(): pl.pallas_call(functools.partial(session_kernel, entries, group), out_sha...  6.76 us
    unnamed x43, local copies, waits for them, and re-layouts  5.72 us
    pallas_call x1, Pallas kernels, local(): pl.pallas_call(functools.partial(merge_kernel, entries), out_shape=(jax.S...  4.57 us
    pallas_call x1, Pallas kernels, local(): pl.pallas_call(unsmooth_kernel, out_shape=jax.ShapeDtypeStruct((latent_di...  4.1 us
    pallas_call x1, Pallas kernels, local(): pl.pallas_call(smooth_kernel, out_shape=(jax.ShapeDtypeStruct((latent_dim...  3.59 us
  transfers between devices with their start and end apart: 21, of which 11 were waited for; matrix products, arithmetic and copies ran while one was open for 3% of the time, Pallas kernels for 6%

profile of v2, /device:TPU:0, one launch (start us, length us, event | category | flops | bytes accessed | tf_op | source)
XLA Modules:
  0.0 136.9 jit_solution(9652287187546843022)
XLA Ops:
  0.6 5.1 %collective-permute-start.5 = (bf16[512,256]{1,0:T(8,128)(2,1)}, bf16[512,256]{1,0:T(8,128)(2,1)}, u32[]{:S(2)}, u32[]{:S(2)}) collective-permute-start(bf16[512,256]{1,0:T(8,128)(2,1)} %refs_0_.3), channel_id=1, source_target_pairs={{0,12},{1,13},{2,14},{3,15},{4,0},{5,1},{6,2},{7,3},{8,4},{9,5},{1... | collective-permute-start | bytes 786440 | tf_op jit(solution)/shard_map/ppermute | solution.py:212
  5.7 0.0 collective-permute-start.4
  5.7 1.0 collective-permute-start.3
  6.7 1.5 %collective-permute-start.6 = (bf16[512,256]{1,0:T(8,128)(2,1)}, bf16[512,256]{1,0:T(8,128)(2,1)}, u32[]{:S(2)}, u32[]{:S(2)}) collective-permute-start(bf16[512,256]{1,0:T(8,128)(2,1)} %refs_0_.3), channel_id=1, source_target_pairs={{0,2},{1,3},{2,0},{3,1},{4,6},{5,7},{6,4},{7,5},{8,10},{9,11},{10,... | collective-permute-start | bytes 786440 | tf_op jit(solution)/shard_map/ppermute | solution.py:212
  8.3 4.5 %collective-permute-done.5.refs_3_ = bf16[512,256]{1,0:T(8,128)(2,1)} collective-permute-done((bf16[512,256]{1,0:T(8,128)(2,1)}, bf16[512,256]{1,0:T(8,128)(2,1)}, u32[]{:S(2)}, u32[]{:S(2)}) %collective-permute-start.5) | collective-permute-done | bytes 262176 | tf_op jit(solution)/shard_map/ppermute | solution.py:212
  12.8 1.5 %collective-permute-start.9 = (bf16[512,256]{1,0:T(8,128)(2,1)}, bf16[512,256]{1,0:T(8,128)(2,1)}, u32[]{:S(2)}, u32[]{:S(2)}) collective-permute-start(bf16[512,256]{1,0:T(8,128)(2,1)} %collective-permute-done.5.refs_3_), channel_id=1, source_target_pairs={{0,2},{1,3},{2,0},{3,1},{4,6},{5,7},{6,4},{7,5},{8,10},{9,11},{10,... | collective-permute-start | bytes 786440 | tf_op jit(solution)/shard_map/ppermute | solution.py:212
  14.3 14.0 %collective-permute-done.4.refs_2_ = bf16[512,256]{1,0:T(8,128)(2,1)} collective-permute-done((bf16[512,256]{1,0:T(8,128)(2,1)}, bf16[512,256]{1,0:T(8,128)(2,1)}, u32[]{:S(2)}, u32[]{:S(2)}) %collective-permute-start.4) | collective-permute-done | bytes 262176 | tf_op jit(solution)/shard_map/ppermute | solution.py:212
  28.4 1.5 %collective-permute-start.8 = (bf16[512,256]{1,0:T(8,128)(2,1)}, bf16[512,256]{1,0:T(8,128)(2,1)}, u32[]{:S(2)}, u32[]{:S(2)}) collective-permute-start(bf16[512,256]{1,0:T(8,128)(2,1)} %collective-permute-done.4.refs_2_), channel_id=1, source_target_pairs={{0,2},{1,3},{2,0},{3,1},{4,6},{5,7},{6,4},{7,5},{8,10},{9,11},{10,... | collective-permute-start | bytes 786440 | tf_op jit(solution)/shard_map/ppermute | solution.py:212
  29.9 0.5 collective-permute-start.7
  30.4 0.8 reshape.16
  31.1 0.8 reshape.17
  31.9 0.1 pad_add_fusion.ids
  32.0 0.0 copy-start.1
  32.0 0.0 copy-start.7
  32.0 0.1 collective-permute-start.2
  32.1 1.1 collective-permute-done.2.asked
  33.2 0.0 collective-permute-done.6.refs_4_
  33.2 0.0 collective-permute-done.9.refs_7_
  33.2 4.7 %collective-permute-done.8.refs_6_ = bf16[512,256]{1,0:T(8,128)(2,1)} collective-permute-done((bf16[512,256]{1,0:T(8,128)(2,1)}, bf16[512,256]{1,0:T(8,128)(2,1)}, u32[]{:S(2)}, u32[]{:S(2)}) %collective-permute-start.8) | collective-permute-done | bytes 262176 | tf_op jit(solution)/shard_map/ppermute | solution.py:212
  37.9 3.5 %collective-permute-done.7.refs_5_ = bf16[512,256]{1,0:T(8,128)(2,1)} collective-permute-done((bf16[512,256]{1,0:T(8,128)(2,1)}, bf16[512,256]{1,0:T(8,128)(2,1)}, u32[]{:S(2)}, u32[]{:S(2)}) %collective-permute-start.7) | collective-permute-done | bytes 262176 | tf_op jit(solution)/shard_map/ppermute | solution.py:212
  41.5 19.8 %pack.1 = bf16[2048,256]{1,0:T(8,128)(2,1)} custom-call(s32[33]{0:T(128)} %copy-done.16, s32[33]{0:T(128)} %copy-done.18, bf16[512,256]{1,0:T(8,128)(2,1)} %refs_0_.3, bf16[512,256]{1,0:T(8,128)(2,1)} %collective-permute-done.3.refs_1_, bf16[512,256]{1,0:T(8,128)(2,1)} %collective-permute-done.4.refs_2_, bf16[512,256]{1,0:T(8,128)(2,1)} %collective-permute-done.5.refs_3_, ...), custom_call_target="tpu_custom_call" | custom-call | bytes 2097152 | tf_op jit(solution)/shard_map/pack/pallas_call | solution.py:250
  61.3 0.1 collective-permute-start.10
  61.4 0.7 fusion
  62.1 1.3 collective-permute-start.1
  63.3 3.0 %collective-permute-start = (f32[256,128]{1,0:T(8,128)S(1)}, f32[256,128]{1,0:T(8,128)S(1)}, u32[]{:S(2)}, u32[]{:S(2)}) collective-permute-start(f32[256,128]{1,0:T(8,128)S(1)} %get-tuple-element.31), channel_id=1, source_target_pairs={{0,1},{1,2},{2,3},{3,4},{4,5},{5,6},{6,7},{7,8},{8,9},{9,10},{10,1... | collective-permute-start | bytes 393224 | tf_op jit(solution)/shard_map/ppermute | solution.py:212
  66.4 0.1 copy.18
  66.5 0.7 reshape.18.mask
  67.2 0.0 collective-permute-done.1.high
  67.2 0.2 collective-permute-done.low
  67.4 0.7 copy-done.8
  68.0 1.0 copy-done.6
  69.1 0.9 copy-done.9
  70.0 1.1 copy-done.10
  71.1 1.1 copy-done.11
  72.2 3.6 %smooth.1 = (bf16[256,512]{1,0:T(8,128)(2,1)S(1)}, f32[256,768]{1,0:T(8,128)S(1)}) custom-call(f32[256,128]{1,0:T(8,128)S(1)} %copy-done.9, f32[256,512]{1,0:T(8,128)S(1)} %copy-done.6, f32[256,128]{1,0:T(8,128)S(1)} %collective-permute-done.1.high, f32[256,256]{1,0:T(8,128)S(1)} %copy-done.7, bf16[768,768]{1,0:T(8,128)(2,1)S(1)} %copy-done.1, ...), custom_call_target="tpu_custom_call" | custom-call | flops 1509949440 | bytes 6291456 | tf_op jit(solution)/shard_map/smooth/pallas_call | solution.py:236
  75.8 0.0 copy-start.12
  75.8 0.7 copy-done.12
  76.5 6.8 %session.1 = (f32[256,512]{1,0:T(8,128)}, f32[256,128]{1,0:T(8,128)}, f32[256,128]{1,0:T(8,128)}, bf16[2048,256]{1,0:T(8,128)(2,1)}) custom-call(s32[33]{0:T(128)} %copy-done.16, s32[64]{0:T(128)} %reshape.18.mask, bf16[256,512]{1,0:T(8,128)(2,1)} %copy-done.12, bf16[16,128,512]{2,1,0:T(8,128)(2,1)} %bitcast.2, ...), custom_call_target="tpu_custom_call" | custom-call | flops 1610612736 | bytes 8388608 | tf_op jit(solution)/shard_map/session/pallas_call | solution.py:263
  83.3 2.7 %collective-permute-start.13 = (bf16[2048,256]{1,0:T(8,128)(2,1)}, bf16[2048,256]{1,0:T(8,128)(2,1)}, u32[]{:S(2)}, u32[]{:S(2)}) collective-permute-start(bf16[2048,256]{1,0:T(8,128)(2,1)} %get-tuple-element.21.own), channel_id=1, source_target_pairs={{0,1},{1,0},{2,3},{3,2},{4,5},{5,4},{6,7},{7,6},{8,9},{9,8},{10,11... | collective-permute-start | bytes 3145736 | tf_op jit(solution)/shard_map/ppermute | solution.py:212
  86.1 2.6 %collective-permute-done.13.got = bf16[2048,256]{1,0:T(8,128)(2,1)} collective-permute-done((bf16[2048,256]{1,0:T(8,128)(2,1)}, bf16[2048,256]{1,0:T(8,128)(2,1)}, u32[]{:S(2)}, u32[]{:S(2)}) %collective-permute-start.13) | collective-permute-done | bytes 1048608 | tf_op jit(solution)/shard_map/ppermute | solution.py:212
  88.7 4.6 %merge.1 = (f32[512,256]{1,0:T(8,128)}, f32[512,256]{1,0:T(8,128)}, f32[512,256]{1,0:T(8,128)}, f32[512,256]{1,0:T(8,128)}, bf16[512,256]{1,0:T(8,128)(2,1)}, /*...) custom-call(s32[33]{0:T(128)} %copy-done.16, s32[33]{0:T(128)} %copy-done.18, ...), custom_call_target="tpu_custom_call" | custom-call | bytes 5242880 | tf_op jit(solution)/shard_map/merge/pallas_call | solution.py:290
  93.3 2.7 %collective-permute-start.15 = (bf16[512,256]{1,0:T(8,128)(2,1)}, bf16[512,256]{1,0:T(8,128)(2,1)S(1)}, u32[]{:S(2)}, u32[]{:S(2)}) collective-permute-start(bf16[512,256]{1,0:T(8,128)(2,1)} %get-tuple-element.25), channel_id=1, source_target_pairs={{0,2},{1,3},{2,0},{3,1},{4,6},{5,7},{6,4},{7,5},{8,10},{9,11},{10,... | collective-permute-start | bytes 786440 | tf_op jit(solution)/shard_map/ppermute | solution.py:212
  96.0 0.1 collective-permute-start.17
  96.1 1.8 %collective-permute-start.11 = (f32[256,128]{1,0:T(8,128)S(1)}, f32[256,128]{1,0:T(8,128)S(1)}, u32[]{:S(2)}, u32[]{:S(2)}) collective-permute-start(f32[256,128]{1,0:T(8,128)S(1)} %copy-done.20), channel_id=1, source_target_pairs={{0,1},{1,2},{2,3},{3,4},{4,5},{5,6},{6,7},{7,8},{8,9},{9,10},{10,1... | collective-permute-start | bytes 393224 | tf_op jit(solution)/shard_map/ppermute | solution.py:212
  97.9 1.3 collective-permute-start.12
  99.2 4.5 %collective-permute-start.14 = (bf16[512,256]{1,0:T(8,128)(2,1)}, bf16[512,256]{1,0:T(8,128)(2,1)S(1)}, u32[]{:S(2)}, u32[]{:S(2)}) collective-permute-start(bf16[512,256]{1,0:T(8,128)(2,1)} %get-tuple-element.23), channel_id=1, source_target_pairs={{0,2},{1,3},{2,0},{3,1},{4,6},{5,7},{6,4},{7,5},{8,10},{9,11},{10,... | collective-permute-start | bytes 786440 | tf_op jit(solution)/shard_map/ppermute | solution.py:212
  103.7 1.7 %collective-permute-start.19 = (bf16[512,256]{1,0:T(8,128)(2,1)}, bf16[512,256]{1,0:T(8,128)(2,1)S(1)}, u32[]{:S(2)}, u32[]{:S(2)}) collective-permute-start(bf16[512,256]{1,0:T(8,128)(2,1)} %get-tuple-element.29), channel_id=1, source_target_pairs={{0,2},{1,3},{2,0},{3,1},{4,6},{5,7},{6,4},{7,5},{8,10},{9,11},{10,... | collective-permute-start | bytes 786440 | tf_op jit(solution)/shard_map/ppermute | solution.py:212
  105.4 1.1 add_convert_fusion.2
  106.5 0.0 copy-start.2
  106.5 0.0 copy-start.3
  106.5 0.0 copy-start.4
  106.5 3.5 %collective-permute-done.17 = bf16[512,256]{1,0:T(8,128)(2,1)S(1)} collective-permute-done((bf16[512,256]{1,0:T(8,128)(2,1)}, bf16[512,256]{1,0:T(8,128)(2,1)S(1)}, u32[]{:S(2)}, u32[]{:S(2)}) %collective-permute-start.17) | collective-permute-done | bytes 262176 | tf_op jit(solution)/shard_map/ppermute | solution.py:212
  110.0 0.0 collective-permute-start.16
  110.0 0.1 add_convert_fusion.1
  110.1 11.2 %collective-permute-done.19 = bf16[512,256]{1,0:T(8,128)(2,1)S(1)} collective-permute-done((bf16[512,256]{1,0:T(8,128)(2,1)}, bf16[512,256]{1,0:T(8,128)(2,1)S(1)}, u32[]{:S(2)}, u32[]{:S(2)}) %collective-permute-start.19) | collective-permute-done | bytes 262176 | tf_op jit(solution)/shard_map/ppermute | solution.py:212
  121.3 2.4 %collective-permute-start.18 = (bf16[512,256]{1,0:T(8,128)(2,1)S(1)}, bf16[512,256]{1,0:T(8,128)(2,1)S(1)}, u32[]{:S(2)}, u32[]{:S(2)}) collective-permute-start(bf16[512,256]{1,0:T(8,128)(2,1)S(1)} %add_convert_fusion.1), channel_id=1, source_target_pairs={{0,4},{1,5},{2,6},{3,7},{4,8},{5,9},{6,10},{7,11},{8,12},{9,13},{1... | collective-permute-start | bytes 786440 | tf_op jit(solution)/shard_map/ppermute | solution.py:212
  123.7 0.1 add_convert_fusion
  123.7 0.0 collective-permute-done.11.low
  123.7 1.5 %collective-permute-start.20 = (bf16[512,256]{1,0:T(8,128)(2,1)S(1)}, bf16[512,256]{1,0:T(8,128)(2,1)S(1)}, u32[]{:S(2)}, u32[]{:S(2)}) collective-permute-start(bf16[512,256]{1,0:T(8,128)(2,1)S(1)} %add_convert_fusion), channel_id=1, source_target_pairs={{0,12},{1,13},{2,14},{3,15},{4,0},{5,1},{6,2},{7,3},{8,4},{9,5},{1... | collective-permute-start | bytes 786440 | tf_op jit(solution)/shard_map/ppermute | solution.py:212
  125.2 0.0 collective-permute-done.12.high
  125.2 4.1 %unsmooth.1 = f32[256,512]{1,0:T(8,128)} custom-call(f32[256,128]{1,0:T(8,128)S(1)} %collective-permute-done.11.low, f32[256,512]{1,0:T(8,128)S(1)} %copy-done.4, f32[256,128]{1,0:T(8,128)S(1)} %collective-permute-done.12.high, f32[256,768]{1,0:T(8,128)S(1)} %get-tuple-element.20.k_spec, bf16[768,768]{1,0:T(8,128)(2,1)S(1)} %copy-done.1, ...), custom_call_target="tpu_custom_call" | custom-call | flops 1509949440 | bytes 6291456 | tf_op jit(solution)/shard_map/unsmooth/pallas_call | solution.py:313
  129.3 2.9 %collective-permute-done.18 = bf16[512,256]{1,0:T(8,128)(2,1)S(1)} collective-permute-done((bf16[512,256]{1,0:T(8,128)(2,1)S(1)}, bf16[512,256]{1,0:T(8,128)(2,1)S(1)}, u32[]{:S(2)}, u32[]{:S(2)}) %collective-permute-start.18) | collective-permute-done | bytes 262176 | tf_op jit(solution)/shard_map/ppermute | solution.py:212
  132.3 3.7 %collective-permute-done.20 = bf16[512,256]{1,0:T(8,128)(2,1)S(1)} collective-permute-done((bf16[512,256]{1,0:T(8,128)(2,1)S(1)}, bf16[512,256]{1,0:T(8,128)(2,1)S(1)}, u32[]{:S(2)}, u32[]{:S(2)}) %collective-permute-start.20) | collective-permute-done | bytes 262176 | tf_op jit(solution)/shard_map/ppermute | solution.py:212
  136.0 0.9 convert_add_fusion
  (35 shorter events, 0.1 us)
Async XLA Ops:
  0.6 12.2 %collective-permute-start.5 = (bf16[512,256]{1,0:T(8,128)(2,1)}, bf16[512,256]{1,0:T(8,128)(2,1)}, u32[]{:S(2)}, u32[]{:S(2)}) collective-permute-start(bf16[512,256]{1,0:T(8,128)(2,1)} %refs_0_.3), channel_id=1, source_target_pairs={{0,12},{1,13},{2,14},{3,15},{4,0},{5,1},{6,2},{7,3},{8,4},{9,5},{1... | collective-permute-start | bytes 786440 | tf_op jit(solution)/shard_map/ppermute | solution.py:212
  5.7 22.6 %collective-permute-start.4 = (bf16[512,256]{1,0:T(8,128)(2,1)}, bf16[512,256]{1,0:T(8,128)(2,1)}, u32[]{:S(2)}, u32[]{:S(2)}) collective-permute-start(bf16[512,256]{1,0:T(8,128)(2,1)} %refs_0_.3), channel_id=1, source_target_pairs={{0,8},{1,9},{2,10},{3,11},{4,12},{5,13},{6,14},{7,15},{8,0},{9,1},... | collective-permute-start | bytes 786440 | tf_op jit(solution)/shard_map/ppermute | solution.py:212
  5.7 24.1 %collective-permute-start.3 = (bf16[512,256]{1,0:T(8,128)(2,1)}, bf16[512,256]{1,0:T(8,128)(2,1)}, u32[]{:S(2)}, u32[]{:S(2)}) collective-permute-start(bf16[512,256]{1,0:T(8,128)(2,1)} %refs_0_.3), channel_id=1, source_target_pairs={{0,4},{1,5},{2,6},{3,7},{4,8},{5,9},{6,10},{7,11},{8,12},{9,13},{1... | collective-permute-start | bytes 786440 | tf_op jit(solution)/shard_map/ppermute | solution.py:212
  6.7 26.5 %collective-permute-start.6 = (bf16[512,256]{1,0:T(8,128)(2,1)}, bf16[512,256]{1,0:T(8,128)(2,1)}, u32[]{:S(2)}, u32[]{:S(2)}) collective-permute-start(bf16[512,256]{1,0:T(8,128)(2,1)} %refs_0_.3), channel_id=1, source_target_pairs={{0,2},{1,3},{2,0},{3,1},{4,6},{5,7},{6,4},{7,5},{8,10},{9,11},{10,... | collective-permute-start | bytes 786440 | tf_op jit(solution)/shard_map/ppermute | solution.py:212
  12.8 20.4 %collective-permute-start.9 = (bf16[512,256]{1,0:T(8,128)(2,1)}, bf16[512,256]{1,0:T(8,128)(2,1)}, u32[]{:S(2)}, u32[]{:S(2)}) collective-permute-start(bf16[512,256]{1,0:T(8,128)(2,1)} %collective-permute-done.5.refs_3_), channel_id=1, source_target_pairs={{0,2},{1,3},{2,0},{3,1},{4,6},{5,7},{6,4},{7,5},{8,10},{9,11},{10,... | collective-permute-start | bytes 786440 | tf_op jit(solution)/shard_map/ppermute | solution.py:212
  28.4 9.6 %collective-permute-start.8 = (bf16[512,256]{1,0:T(8,128)(2,1)}, bf16[512,256]{1,0:T(8,128)(2,1)}, u32[]{:S(2)}, u32[]{:S(2)}) collective-permute-start(bf16[512,256]{1,0:T(8,128)(2,1)} %collective-permute-done.4.refs_2_), channel_id=1, source_target_pairs={{0,2},{1,3},{2,0},{3,1},{4,6},{5,7},{6,4},{7,5},{8,10},{9,11},{10,... | collective-permute-start | bytes 786440 | tf_op jit(solution)/shard_map/ppermute | solution.py:212
  29.9 11.6 %collective-permute-start.7 = (bf16[512,256]{1,0:T(8,128)(2,1)}, bf16[512,256]{1,0:T(8,128)(2,1)}, u32[]{:S(2)}, u32[]{:S(2)}) collective-permute-start(bf16[512,256]{1,0:T(8,128)(2,1)} %collective-permute-done.3.refs_1_), channel_id=1, source_target_pairs={{0,2},{1,3},{2,0},{3,1},{4,6},{5,7},{6,4},{7,5},{8,10},{9,11},{10,... | collective-permute-start | bytes 786440 | tf_op jit(solution)/shard_map/ppermute | solution.py:212
  32.0 9.5 %copy-start.16 = (s32[33]{0:T(128)}, s32[33]{0:T(128)S(1)}, u32[]{:S(2)}) copy-start(s32[33]{0:T(128)S(1)} %pad_add_fusion.ids) | copy-start | bytes 400
  32.0 29.4 %copy-start.5 = (f32[256,512]{1,0:T(8,128)S(1)}, f32[256,512]{1,0:T(8,128)}, u32[]{:S(2)}) copy-start(f32[256,512]{1,0:T(8,128)} %mid.1) | copy-start | bytes 1572868
  32.0 34.4 %copy-start.17 = (s32[2,8,4]{1,2,0:T(4,128)S(1)}, s32[2,8,4]{1,2,0:T(4,128)}, u32[]{:S(2)}) copy-start(s32[2,8,4]{1,2,0:T(4,128)} %param.21) | copy-start | bytes 772
  32.0 36.0 %copy-start = (bf16[768,768]{1,0:T(8,128)(2,1)S(1)}, bf16[768,768]{1,0:T(8,128)(2,1)}, u32[]{:S(2)}) copy-start(bf16[768,768]{1,0:T(8,128)(2,1)} %constant.17.clone.fl) | copy-start | bytes 3538948
  32.0 36.0 %copy-start.1 = (bf16[768,768]{1,0:T(8,128)(2,1)S(1)}, bf16[768,768]{1,0:T(8,128)(2,1)}, u32[]{:S(2)}) copy-start(bf16[768,768]{1,0:T(8,128)(2,1)} %constant.16.clone.fh) | copy-start | bytes 3538948
  32.0 36.0 %copy-start.7 = (f32[256,256]{1,0:T(8,128)S(1)}, f32[256,256]{1,0:T(8,128)}, u32[]{:S(2)}) copy-start(f32[256,256]{1,0:T(8,128)} %taps.1) | copy-start | bytes 786436
  32.0 1.2 collective-permute-start.2
  33.2 8.3 %copy-start.18 = (s32[33]{0:T(128)}, s32[33]{0:T(128)S(1)}, u32[]{:S(2)}) copy-start(s32[33]{0:T(128)S(1)} %collective-permute-done.2.asked) | copy-start | bytes 400
  61.3 15.2 %collective-permute-start.10 = (bf16[2048,256]{1,0:T(8,128)(2,1)}, bf16[2048,256]{1,0:T(8,128)(2,1)}, u32[]{:S(2)}, u32[]{:S(2)}) collective-permute-start(bf16[2048,256]{1,0:T(8,128)(2,1)} %pack.1), channel_id=1, source_target_pairs={{0,1},{1,0},{2,3},{3,2},{4,5},{5,4},{6,7},{7,6},{8,9},{9,8},{10,11... | collective-permute-start | bytes 3145736 | tf_op jit(solution)/shard_map/ppermute | solution.py:212
  62.1 5.1 %collective-permute-start.1 = (f32[256,128]{1,0:T(8,128)}, f32[256,128]{1,0:T(8,128)S(1)}, u32[]{:S(2)}, u32[]{:S(2)}) collective-permute-start(f32[256,128]{1,0:T(8,128)} %get-tuple-element.30), channel_id=1, source_target_pairs={{1,0},{2,1},{3,2},{4,3},{5,4},{6,5},{7,6},{8,7},{9,8},{10,9},{11,1... | collective-permute-start | bytes 393224 | tf_op jit(solution)/shard_map/ppermute | solution.py:212
  63.3 4.0 %collective-permute-start = (f32[256,128]{1,0:T(8,128)S(1)}, f32[256,128]{1,0:T(8,128)S(1)}, u32[]{:S(2)}, u32[]{:S(2)}) collective-permute-start(f32[256,128]{1,0:T(8,128)S(1)} %get-tuple-element.31), channel_id=1, source_target_pairs={{0,1},{1,2},{2,3},{3,4},{4,5},{5,6},{6,7},{7,8},{8,9},{9,10},{10,1... | collective-permute-start | bytes 393224 | tf_op jit(solution)/shard_map/ppermute | solution.py:212
  67.4 0.7 copy-start.8
  68.0 1.0 copy-start.6
  69.1 0.9 copy-start.9
  70.0 1.1 copy-start.10
  71.1 1.1 copy-start.11
  75.8 0.7 copy-start.12
  83.3 12.8 %copy-start.20 = (f32[256,128]{1,0:T(8,128)S(1)}, f32[256,128]{1,0:T(8,128)}, u32[]{:S(2)}) copy-start(f32[256,128]{1,0:T(8,128)} %get-tuple-element.17) | copy-start | bytes 393220
  83.3 14.6 %copy-start.19 = (f32[256,128]{1,0:T(8,128)S(1)}, f32[256,128]{1,0:T(8,128)}, u32[]{:S(2)}) copy-start(f32[256,128]{1,0:T(8,128)} %get-tuple-element.19) | copy-start | bytes 393220
  83.3 5.4 %collective-permute-start.13 = (bf16[2048,256]{1,0:T(8,128)(2,1)}, bf16[2048,256]{1,0:T(8,128)(2,1)}, u32[]{:S(2)}, u32[]{:S(2)}) collective-permute-start(bf16[2048,256]{1,0:T(8,128)(2,1)} %get-tuple-element.21.own), channel_id=1, source_target_pairs={{0,1},{1,0},{2,3},{3,2},{4,5},{5,4},{6,7},{7,6},{8,9},{9,8},{10,11... | collective-permute-start | bytes 3145736 | tf_op jit(solution)/shard_map/ppermute | solution.py:212
  93.3 16.7 %copy-start.14 = (f32[512,256]{1,0:T(8,128)S(1)}, f32[512,256]{1,0:T(8,128)}, u32[]{:S(2)}) copy-start(f32[512,256]{1,0:T(8,128)} %get-tuple-element.26) | copy-start | bytes 1572868
  93.3 30.4 %copy-start.13 = (f32[512,256]{1,0:T(8,128)S(1)}, f32[512,256]{1,0:T(8,128)}, u32[]{:S(2)}) copy-start(f32[512,256]{1,0:T(8,128)} %get-tuple-element.28) | copy-start | bytes 1572868
  93.3 10.4 %collective-permute-start.15 = (bf16[512,256]{1,0:T(8,128)(2,1)}, bf16[512,256]{1,0:T(8,128)(2,1)S(1)}, u32[]{:S(2)}, u32[]{:S(2)}) collective-permute-start(bf16[512,256]{1,0:T(8,128)(2,1)} %get-tuple-element.25), channel_id=1, source_target_pairs={{0,2},{1,3},{2,0},{3,1},{4,6},{5,7},{6,4},{7,5},{8,10},{9,11},{10,... | collective-permute-start | bytes 786440 | tf_op jit(solution)/shard_map/ppermute | solution.py:212
  96.0 14.0 %collective-permute-start.17 = (bf16[512,256]{1,0:T(8,128)(2,1)}, bf16[512,256]{1,0:T(8,128)(2,1)S(1)}, u32[]{:S(2)}, u32[]{:S(2)}) collective-permute-start(bf16[512,256]{1,0:T(8,128)(2,1)} %get-tuple-element.27), channel_id=1, source_target_pairs={{0,2},{1,3},{2,0},{3,1},{4,6},{5,7},{6,4},{7,5},{8,10},{9,11},{10,... | collective-permute-start | bytes 786440 | tf_op jit(solution)/shard_map/ppermute | solution.py:212
  96.1 27.6 %collective-permute-start.11 = (f32[256,128]{1,0:T(8,128)S(1)}, f32[256,128]{1,0:T(8,128)S(1)}, u32[]{:S(2)}, u32[]{:S(2)}) collective-permute-start(f32[256,128]{1,0:T(8,128)S(1)} %copy-done.20), channel_id=1, source_target_pairs={{0,1},{1,2},{2,3},{3,4},{4,5},{5,6},{6,7},{7,8},{8,9},{9,10},{10,1... | collective-permute-start | bytes 393224 | tf_op jit(solution)/shard_map/ppermute | solution.py:212
  97.9 27.3 %collective-permute-start.12 = (f32[256,128]{1,0:T(8,128)S(1)}, f32[256,128]{1,0:T(8,128)S(1)}, u32[]{:S(2)}, u32[]{:S(2)}) collective-permute-start(f32[256,128]{1,0:T(8,128)S(1)} %copy-done.19), channel_id=1, source_target_pairs={{1,0},{2,1},{3,2},{4,3},{5,4},{6,5},{7,6},{8,7},{9,8},{10,9},{11,1... | collective-permute-start | bytes 393224 | tf_op jit(solution)/shard_map/ppermute | solution.py:212
  99.2 30.1 %collective-permute-start.14 = (bf16[512,256]{1,0:T(8,128)(2,1)}, bf16[512,256]{1,0:T(8,128)(2,1)S(1)}, u32[]{:S(2)}, u32[]{:S(2)}) collective-permute-start(bf16[512,256]{1,0:T(8,128)(2,1)} %get-tuple-element.23), channel_id=1, source_target_pairs={{0,2},{1,3},{2,0},{3,1},{4,6},{5,7},{6,4},{7,5},{8,10},{9,11},{10,... | collective-permute-start | bytes 786440 | tf_op jit(solution)/shard_map/ppermute | solution.py:212
  103.7 17.6 %collective-permute-start.19 = (bf16[512,256]{1,0:T(8,128)(2,1)}, bf16[512,256]{1,0:T(8,128)(2,1)S(1)}, u32[]{:S(2)}, u32[]{:S(2)}) collective-permute-start(bf16[512,256]{1,0:T(8,128)(2,1)} %get-tuple-element.29), channel_id=1, source_target_pairs={{0,2},{1,3},{2,0},{3,1},{4,6},{5,7},{6,4},{7,5},{8,10},{9,11},{10,... | collective-permute-start | bytes 786440 | tf_op jit(solution)/shard_map/ppermute | solution.py:212
  106.5 18.7 %copy-start.2 = (bf16[768,512]{1,0:T(8,128)(2,1)S(1)}, bf16[768,512]{1,0:T(8,128)(2,1)}, u32[]{:S(2)}) copy-start(bf16[768,512]{1,0:T(8,128)(2,1)} %constant.21.clone.wl) | copy-start | bytes 2359300
  106.5 18.7 %copy-start.3 = (bf16[768,512]{1,0:T(8,128)(2,1)S(1)}, bf16[768,512]{1,0:T(8,128)(2,1)}, u32[]{:S(2)}) copy-start(bf16[768,512]{1,0:T(8,128)(2,1)} %constant.20.clone.wh) | copy-start | bytes 2359300
  106.5 18.7 %copy-start.4 = (f32[256,512]{1,0:T(8,128)S(1)}, f32[256,512]{1,0:T(8,128)}, u32[]{:S(2)}) copy-start(f32[256,512]{1,0:T(8,128)} %get-tuple-element.18.mid) | copy-start | bytes 1572868
  110.0 19.3 %collective-permute-start.16 = (bf16[512,256]{1,0:T(8,128)(2,1)S(1)}, bf16[512,256]{1,0:T(8,128)(2,1)S(1)}, u32[]{:S(2)}, u32[]{:S(2)}) collective-permute-start(bf16[512,256]{1,0:T(8,128)(2,1)S(1)} %add_convert_fusion.2), channel_id=1, source_target_pairs={{0,8},{1,9},{2,10},{3,11},{4,12},{5,13},{6,14},{7,15},{8,0},{9,1},... | collective-permute-start | bytes 786440 | tf_op jit(solution)/shard_map/ppermute | solution.py:212
  121.3 11.0 %collective-permute-start.18 = (bf16[512,256]{1,0:T(8,128)(2,1)S(1)}, bf16[512,256]{1,0:T(8,128)(2,1)S(1)}, u32[]{:S(2)}, u32[]{:S(2)}) collective-permute-start(bf16[512,256]{1,0:T(8,128)(2,1)S(1)} %add_convert_fusion.1), channel_id=1, source_target_pairs={{0,4},{1,5},{2,6},{3,7},{4,8},{5,9},{6,10},{7,11},{8,12},{9,13},{1... | collective-permute-start | bytes 786440 | tf_op jit(solution)/shard_map/ppermute | solution.py:212
  123.7 12.2 %collective-permute-start.20 = (bf16[512,256]{1,0:T(8,128)(2,1)S(1)}, bf16[512,256]{1,0:T(8,128)(2,1)S(1)}, u32[]{:S(2)}, u32[]{:S(2)}) collective-permute-start(bf16[512,256]{1,0:T(8,128)(2,1)S(1)} %add_convert_fusion), channel_id=1, source_target_pairs={{0,12},{1,13},{2,14},{3,15},{4,0},{5,1},{6,2},{7,3},{8,4},{9,5},{1... | collective-permute-start | bytes 786440 | tf_op jit(solution)/shard_map/ppermute | solution.py:212
  125.2 10.8 %copy-start.15 = (f32[512,256]{1,0:T(8,128)S(1)}, f32[512,256]{1,0:T(8,128)}, u32[]{:S(2)}) copy-start(f32[512,256]{1,0:T(8,128)} %get-tuple-element.22) | copy-start | bytes 1572868

commit v3 on v2

--- a/solution.py
+++ b/solution.py
@@ -88,7 +88,7 @@
     return owner_c, piece, pl.multiple_of(slot * BLK, BLK)
 
 
-def pack_kernel(entries, ids, asked, *refs):
+def pack_kernel(entries, late, ids, asked, *refs):
     pieces, (out, sem) = refs[:-2], refs[-2:]
     me = ids[2 * entries]
 
@@ -99,7 +99,9 @@
 
     def start(e, _):
         core, piece, row = place_of(asked, e, entries, me, False)
-        for q, ref in enumerate(pieces):
+        for q, ref in enumerate(pieces[:late] + (None,) + pieces[late:]):
+            if q == late:
+                continue
 
             @pl.when(jnp.logical_and(core == me % 2, piece == q))
             def _():
@@ -108,9 +110,9 @@
         return 0
 
     def wait(e, _):
-        core, _, row = place_of(asked, e, entries, me, False)
-
-        @pl.when(core == me % 2)
+        core, piece, row = place_of(asked, e, entries, me, False)
+
+        @pl.when(jnp.logical_and(core == me % 2, piece != late))
         def _():
             copy(pieces[0], e, row).wait()
 
@@ -120,7 +122,9 @@
     lax.fori_loop(0, entries, wait, 0)
 
 
-def session_kernel(entries, group, ids, mask, smoothed, recorded, packed, *refs):
+def session_kernel(
+    entries, group, late, ids, mask, smoothed, recorded, packed, late_theirs, *refs
+):
     pieces = refs[:-7]
     grad, grad_low, grad_high, terms, rows, resid, sem = refs[-7:]
     bins = smoothed.shape[1]
@@ -137,9 +141,13 @@
             def _():
                 copy(ref, e, row).start()
 
-        @pl.when(core != me % 2)
+        @pl.when(jnp.logical_and(core != me % 2, piece != late))
         def _():
             copy(packed, e, pl.multiple_of(e * BLK, BLK)).start()
+
+        @pl.when(jnp.logical_and(core != me % 2, piece == late))
+        def _():
+            copy(late_theirs, e, row).start()
 
         return 0
 
@@ -176,7 +184,7 @@
     grad_high[...] = grad[:, :width]
 
 
-def merge_kernel(entries, ids, asked, own, got, *refs):
+def merge_kernel(entries, late, only_late, ids, asked, own, got, *refs):
     outs, sums = refs[:-1], refs[-1]
     me = ids[2 * entries]
     chunk = outs[0].shape[0]
@@ -187,9 +195,14 @@
         for names, terms in ((ids, own), (asked, got)):
             core, piece, row = place_of(names, e, entries, me, True)
 
-            @pl.when(core == me % 2)
+            if only_late:
+                wanted, index = piece == late, 0
+            else:
+                wanted, index = piece != late, jnp.where(piece < late, piece, piece - 1)
+
+            @pl.when(jnp.logical_and(core == me % 2, wanted))
             def _():
-                target = pl.ds(pl.multiple_of(piece * chunk + row, BLK), BLK)
+                target = pl.ds(pl.multiple_of(index * chunk + row, BLK), BLK)
                 sums[target] += terms[source].astype(F32)
 
         return 0
@@ -227,8 +240,14 @@
     low = permute(latents[:, bins - halfwidth :], up_one)
     high = permute(latents[:, :halfwidth], down_one)
 
-    pieces = [loadings] + [rotate(loadings, r) for r in range(1, chain)]
-    pieces += [flip(piece, 2) for piece in pieces]
+    half = chain // 2
+    late = chain + half
+    straight = [loadings] * chain
+    for r in range(1, half):
+        straight[r] = rotate(straight[r - 1], 1)
+        straight[-r] = rotate(straight[1 - r], -1)
+    straight[half] = rotate(straight[half - 1], 1)
+    across = [flip(straight[r], 2) if r != half else None for r in range(chain)]
 
     length = bins + 2 * halfwidth
     fh, fl, wh, wl = dft_tables(length, bins, 0)
@@ -247,23 +266,30 @@
     )(low, latents, high, kernel, fh, fl, wh, wl)
 
     slots = jax.ShapeDtypeStruct((entries * BLK, latent_dim), BF16)
+    ids, asked, smoothed, mask = lax.optimization_barrier(
+        (ids, asked, smoothed, recorded_mask.reshape(-1))
+    )
+    across[half] = flip(straight[half], 2)
+    early = straight + across[:half] + across[half + 1 :]
     packed = pl.pallas_call(
-        functools.partial(pack_kernel, entries),
+        functools.partial(pack_kernel, entries, late),
         out_shape=slots,
-        in_specs=[smem] * 2 + [ANY] * len(pieces),
-        out_specs=ANY,
+        in_specs=[smem] * 2 + [ANY] * len(early),
+        out_specs=VMEM,
         scratch_shapes=[pltpu.SemaphoreType.DMA((entries,))],
         cost_estimate=pl.CostEstimate(flops=0, bytes_accessed=2 * 2**20, transcendentals=0),
         name="pack",
-    )(ids, asked, *pieces)
+    )(ids, asked, *early)
     packed = flip(packed, 1)
+    late_theirs = flip(across[half], 1)
+    pieces = straight + across
 
     group = 4
     strip = jax.ShapeDtypeStruct((latent_dim, halfwidth), F32)
     grad, grad_low, grad_high, terms = pl.pallas_call(
-        functools.partial(session_kernel, entries, group),
+        functools.partial(session_kernel, entries, group, late),
         out_shape=(jax.ShapeDtypeStruct((latent_dim, bins), F32), strip, strip, slots),
-        in_specs=[smem] * 2 + [VMEM] * 2 + [ANY] * (1 + len(pieces)),
+        in_specs=[smem] * 2 + [VMEM] * 2 + [ANY] * (2 + len(pieces)),
         out_specs=(VMEM,) * 4,
         scratch_shapes=[
             pltpu.VMEM((entries, BLK, latent_dim), BF16),
@@ -277,37 +303,49 @@
         name="session",
     )(
         ids,
-        recorded_mask.reshape(-1),
+        mask,
         smoothed,
         recorded.reshape(entries, BLK, bins),
         packed,
+        late_theirs,
         *pieces,
     )
 
     got = flip(terms, 1)
     grad_low = permute(grad_low, up_one)
     grad_high = permute(grad_high, down_one)
-    sums = pl.pallas_call(
-        functools.partial(merge_kernel, entries),
-        out_shape=(jax.ShapeDtypeStruct((chunk, latent_dim), F32),) * chain
-        + (jax.ShapeDtypeStruct((chunk, latent_dim), BF16),) * chain,
-        in_specs=[smem] * 2 + [VMEM] * 2,
-        out_specs=(VMEM,) * (2 * chain),
-        scratch_shapes=[pltpu.VMEM((2 * chain * chunk, latent_dim), F32)],
-        compiler_params=pltpu.CompilerParams(vmem_limit_bytes=60 * 2**20),
-        cost_estimate=pl.CostEstimate(flops=0, bytes_accessed=5 * 2**20, transcendentals=0),
-        name="merge",
-    )(ids, asked, terms, got)
-    turned = []
-    far_first = sorted(range(chain), key=lambda r: -min(r, chain - r))
-    for r in far_first:
-        total = sums[r] + flip(sums[chain + r], 2).astype(F32)
-        if r:
-            turned.append(rotate(total.astype(BF16), r))
-        else:
-            loading_grad = total
-    for part in turned:
-        loading_grad = loading_grad + part.astype(F32)
+
+    def merge(only_late, out_shape):
+        return pl.pallas_call(
+            functools.partial(merge_kernel, entries, late, only_late),
+            out_shape=out_shape,
+            in_specs=[smem] * 2 + [VMEM] * 2,
+            out_specs=(VMEM,) * len(out_shape),
+            scratch_shapes=[pltpu.VMEM((len(out_shape) * chunk, latent_dim), F32)],
+            compiler_params=pltpu.CompilerParams(vmem_limit_bytes=60 * 2**20),
+            cost_estimate=pl.CostEstimate(flops=0, bytes_accessed=5 * 2**20, transcendentals=0),
+            name="merge",
+        )(ids, asked, terms, got)
+
+    wide = jax.ShapeDtypeStruct((chunk, latent_dim), F32)
+    narrow = jax.ShapeDtypeStruct((chunk, latent_dim), BF16)
+    (sent,) = merge(True, (narrow,))
+    back = flip(sent, 2)
+    sums = merge(False, (wide,) * chain + (narrow,) * (chain - 1))
+    other = {half: back}
+    for r in sorted(range(chain), key=lambda r: -min(r, chain - r)):
+        if r != half:
+            other[r] = flip(sums[chain + r - (r > half)], 2)
+    totals = [sums[r] + other[r].astype(F32) for r in range(chain)]
+    rise = totals[half]
+    for r in range(half - 1, -1, -1):
+        rise = totals[r] + rotate(rise.astype(BF16), 1).astype(F32)
+    loading_grad = rise
+    if half > 1:
+        fall = totals[half + 1]
+        for r in range(half + 2, chain):
+            fall = totals[r] + rotate(fall.astype(BF16), -1).astype(F32)
+        loading_grad = loading_grad + rotate(fall.astype(BF16), -1).astype(F32)
 
     fh, fl, wh, wl = dft_tables(length, bins, 2 * halfwidth)
     latent_grad = pl.pallas_call(

time: 138 us -> 104 us (0.75)
  waiting for transfers between devices: 52.1 us -> 30.5 us
  Pallas kernels: 38.8 us -> 25.7 us
  starting transfers between devices: 34.3 us -> 26.4 us
  local copies, waits for them, and re-layouts: 8.58 us -> 14.9 us
  other arithmetic: 2.22 us -> 4.51 us
    ppermute x21 -> x22, waiting for transfers between devices: 52.1 us -> 30.5 us  [permute(): return lax.ppermute(x, 'tm', pairs)]
    pallas_call x3 -> x4, Pallas kernels: 31.1 us -> 18 us  [the longest x2 7.93 us: merge(): pl.pallas_call(functools.partial(merge_kernel, entries, late, only_late),...]
    ppermute x21 -> x22, starting transfers between devices: 34.3 us -> 26.4 us  [permute(): return lax.ppermute(x, 'tm', pairs)]
    unnamed x43 -> x55, local copies, waits for them, and re-layouts: 5.72 us -> 11.9 us
    convert_element_type x3, other arithmetic: 1.21 us -> 3.54 us  [the longest x2 2.29 us: local(): rise = totals[r] + rotate(rise.astype(BF16), 1).astype(F32)]
  transfers between devices with their start and end apart: 21 -> 22, of which waited for: 11 -> 10; matrix products, arithmetic and copies ran while one was open for 3% -> 7% of each run, Pallas kernels for 6% -> 12%
where the time goes in v3:
time: 104 us; the launch traced here: 103 us
  waiting for transfers between devices  30.5 us (29%)
  starting transfers between devices  26.4 us (25%)
  Pallas kernels  25.7 us (25%)
  local copies, waits for them, and re-layouts  14.9 us (14%)
  other arithmetic  4.51 us (4%)
    ppermute x22, waiting for transfers between devices, permute(): return lax.ppermute(x, 'tm', pairs)  30.5 us
    ppermute x22, starting transfers between devices, permute(): return lax.ppermute(x, 'tm', pairs)  26.4 us
    unnamed x55, local copies, waits for them, and re-layouts  11.9 us
    pallas_call x2, Pallas kernels, merge(): pl.pallas_call(functools.partial(merge_kernel, entries, late, only_late),...  7.93 us
    pallas_call x1, Pallas kernels, local(): pl.pallas_call(functools.partial(session_kernel, entries, group, late), o...  6.76 us
    pallas_call x1, Pallas kernels, local(): pl.pallas_call(unsmooth_kernel, out_shape=jax.ShapeDtypeStruct((latent_di...  4.1 us
    pallas_call x1, Pallas kernels, local(): pl.pallas_call(smooth_kernel, out_shape=(jax.ShapeDtypeStruct((latent_dim...  3.59 us
    pallas_call x1, Pallas kernels, local(): pl.pallas_call(functools.partial(pack_kernel, entries, late), out_shape=s...  3.34 us
  transfers between devices with their start and end apart: 22, of which 10 were waited for; matrix products, arithmetic and copies ran while one was open for 7% of the time, Pallas kernels for 12%

profile of v3, /device:TPU:0, one launch (start us, length us, event | category | flops | bytes accessed | tf_op | source)
XLA Modules:
  0.0 103.0 jit_solution(4191073785986595577)
XLA Ops:
  0.6 5.1 %collective-permute-start.5 = (bf16[512,256]{1,0:T(8,128)(2,1)}, bf16[512,256]{1,0:T(8,128)(2,1)S(1)}, u32[]{:S(2)}, u32[]{:S(2)}) collective-permute-start(bf16[512,256]{1,0:T(8,128)(2,1)} %refs_0_.3), channel_id=1, source_target_pairs={{0,12},{1,13},{2,14},{3,15},{4,0},{5,1},{6,2},{7,3},{8,4},{9,5},{1... | collective-permute-start | bytes 786440 | tf_op jit(solution)/shard_map/ppermute | solution.py:225
  5.7 1.0 fusion
  6.7 1.3 %collective-permute-start.2 = (f32[256,128]{1,0:T(8,128)S(1)}, f32[256,128]{1,0:T(8,128)S(1)}, u32[]{:S(2)}, u32[]{:S(2)}) collective-permute-start(f32[256,128]{1,0:T(8,128)S(1)} %get-tuple-element.36), channel_id=1, source_target_pairs={{1,0},{2,1},{3,2},{4,3},{5,4},{6,5},{7,6},{8,7},{9,8},{10,9},{11,1... | collective-permute-start | bytes 393224 | tf_op jit(solution)/shard_map/ppermute | solution.py:225
  8.0 3.0 %collective-permute-start.1 = (f32[256,128]{1,0:T(8,128)S(1)}, f32[256,128]{1,0:T(8,128)S(1)}, u32[]{:S(2)}, u32[]{:S(2)}) collective-permute-start(f32[256,128]{1,0:T(8,128)S(1)} %get-tuple-element.37), channel_id=1, source_target_pairs={{0,1},{1,2},{2,3},{3,4},{4,5},{5,6},{6,7},{7,8},{8,9},{9,10},{10,1... | collective-permute-start | bytes 393224 | tf_op jit(solution)/shard_map/ppermute | solution.py:225
  11.1 1.6 %collective-permute-start.6 = (bf16[512,256]{1,0:T(8,128)(2,1)}, bf16[512,256]{1,0:T(8,128)(2,1)S(1)}, u32[]{:S(2)}, u32[]{:S(2)}) collective-permute-start(bf16[512,256]{1,0:T(8,128)(2,1)} %refs_0_.3), channel_id=1, source_target_pairs={{0,2},{1,3},{2,0},{3,1},{4,6},{5,7},{6,4},{7,5},{8,10},{9,11},{10,... | collective-permute-start | bytes 786440 | tf_op jit(solution)/shard_map/ppermute | solution.py:225
  12.7 0.1 collective-permute-done.5.refs_3_
  12.8 1.5 %collective-permute-start.8 = (bf16[512,256]{1,0:T(8,128)(2,1)S(1)}, bf16[512,256]{1,0:T(8,128)(2,1)S(1)}, u32[]{:S(2)}, u32[]{:S(2)}) collective-permute-start(bf16[512,256]{1,0:T(8,128)(2,1)S(1)} %collective-permute-done.5.refs_3_), channel_id=1, source_target_pairs={{0,2},{1,3},{2,0},{3,1},{4,6},{5,7},{6,4},{7,5},{8,10},{9,11},{10,... | collective-permute-start | bytes 786440 | tf_op jit(solution)/shard_map/ppermute | solution.py:225
  14.3 3.9 %collective-permute-done.3.refs_1_ = bf16[512,256]{1,0:T(8,128)(2,1)S(1)} collective-permute-done((bf16[512,256]{1,0:T(8,128)(2,1)}, bf16[512,256]{1,0:T(8,128)(2,1)S(1)}, u32[]{:S(2)}, u32[]{:S(2)}) %collective-permute-start.3) | collective-permute-done | bytes 262176 | tf_op jit(solution)/shard_map/ppermute | solution.py:225
  18.1 1.8 %collective-permute-start.7 = (bf16[512,256]{1,0:T(8,128)(2,1)S(1)}, bf16[512,256]{1,0:T(8,128)(2,1)S(1)}, u32[]{:S(2)}, u32[]{:S(2)}) collective-permute-start(bf16[512,256]{1,0:T(8,128)(2,1)S(1)} %collective-permute-done.3.refs_1_), channel_id=1, source_target_pairs={{0,2},{1,3},{2,0},{3,1},{4,6},{5,7},{6,4},{7,5},{8,10},{9,11},{10,... | collective-permute-start | bytes 786440 | tf_op jit(solution)/shard_map/ppermute | solution.py:225
  19.9 0.0 collective-permute-done.2.high
  19.9 2.4 %collective-permute-start.4 = (bf16[512,256]{1,0:T(8,128)(2,1)S(1)}, bf16[512,256]{1,0:T(8,128)(2,1)S(1)}, u32[]{:S(2)}, u32[]{:S(2)}) collective-permute-start(bf16[512,256]{1,0:T(8,128)(2,1)S(1)} %collective-permute-done.3.refs_1_), channel_id=1, source_target_pairs={{0,4},{1,5},{2,6},{3,7},{4,8},{5,9},{6,10},{7,11},{8,12},{9,13},{1... | collective-permute-start | bytes 786440 | tf_op jit(solution)/shard_map/ppermute | solution.py:225
  22.3 0.8 reshape.16
  23.0 0.8 reshape.17
  23.8 0.8 copy.18
  24.6 0.6 reshape.18.mask
  25.1 0.1 pad_add_fusion.ids
  25.2 0.0 collective-permute-start
  25.3 0.0 copy-start
  25.3 1.3 %copy-done = bf16[768,768]{1,0:T(8,128)(2,1)S(1)} copy-done((bf16[768,768]{1,0:T(8,128)(2,1)S(1)}, bf16[768,768]{1,0:T(8,128)(2,1)}, u32[]{:S(2)}) %copy-start) | copy-done | bytes 1179672
  26.5 1.3 %copy-done.2 = bf16[768,768]{1,0:T(8,128)(2,1)S(1)} copy-done((bf16[768,768]{1,0:T(8,128)(2,1)S(1)}, bf16[768,768]{1,0:T(8,128)(2,1)}, u32[]{:S(2)}) %copy-start.2) | copy-done | bytes 1179672
  27.8 1.0 %copy-done.7 = f32[256,512]{1,0:T(8,128)S(1)} copy-done((f32[256,512]{1,0:T(8,128)S(1)}, f32[256,512]{1,0:T(8,128)}, u32[]{:S(2)}) %copy-start.7) | copy-done | bytes 524312
  28.8 0.9 copy-done.8
  29.8 1.1 %copy-done.9 = bf16[768,512]{1,0:T(8,128)(2,1)S(1)} copy-done((bf16[768,512]{1,0:T(8,128)(2,1)S(1)}, bf16[768,512]{1,0:T(8,128)(2,1)}, u32[]{:S(2)}) %copy-start.9) | copy-done | bytes 786456
  30.9 1.1 %copy-done.10 = bf16[768,512]{1,0:T(8,128)(2,1)S(1)} copy-done((bf16[768,512]{1,0:T(8,128)(2,1)S(1)}, bf16[768,512]{1,0:T(8,128)(2,1)}, u32[]{:S(2)}) %copy-start.10) | copy-done | bytes 786456
  32.1 3.6 %smooth.1 = (bf16[256,512]{1,0:T(8,128)(2,1)S(1)}, f32[256,768]{1,0:T(8,128)S(1)}) custom-call(f32[256,128]{1,0:T(8,128)S(1)} %collective-permute-done.1.low, f32[256,512]{1,0:T(8,128)S(1)} %copy-done.7, f32[256,128]{1,0:T(8,128)S(1)} %collective-permute-done.2.high, f32[256,256]{1,0:T(8,128)S(1)} %copy-done.8, bf16[768,768]{1,0:T(8,128)(2,1)S(1)} %copy-done.2, ...), custom_call_target="tpu_custom_call" | custom-call | flops 1509949440 | bytes 6291456 | tf_op jit(solution)/shard_map/smooth/pallas_call | solution.py:255
  35.7 0.0 copy-start.11
  35.7 0.7 copy-done.11
  36.4 0.0 collective-permute-done.asked
  36.5 0.5 copy-done.21
  37.0 0.1 copy-done.16
  37.1 0.1 copy-done.17
  37.2 0.1 copy-done.18
  37.3 0.7 copy-done.19
  38.0 3.3 %pack.1 = bf16[2048,256]{1,0:T(8,128)(2,1)} custom-call(s32[33]{0:T(128)} %copy-done.20, s32[33]{0:T(128)} %copy-done.21, bf16[512,256]{1,0:T(8,128)(2,1)} %refs_0_.3, bf16[512,256]{1,0:T(8,128)(2,1)} %copy-done.15, bf16[512,256]{1,0:T(8,128)(2,1)} %copy-done.19, bf16[512,256]{1,0:T(8,128)(2,1)} %copy-done.14, bf16[512,256]{1,0:T(8,128)(2,1)} %copy-done.16, ...), custom_call_target="tpu_custom_call" | custom-call | bytes 2097152 | tf_op jit(solution)/shard_map/pack/pallas_call | solution.py:274
  41.3 0.6 collective-permute-start.9
  41.9 8.5 %collective-permute-done.10.refs_6_ = bf16[512,256]{1,0:T(8,128)(2,1)S(1)} collective-permute-done((bf16[512,256]{1,0:T(8,128)(2,1)}, bf16[512,256]{1,0:T(8,128)(2,1)S(1)}, u32[]{:S(2)}, u32[]{:S(2)}) %collective-permute-start.10) | collective-permute-done | bytes 262176 | tf_op jit(solution)/shard_map/ppermute | solution.py:225
  50.4 1.5 %collective-permute-done.11.late_theirs = bf16[512,256]{1,0:T(8,128)(2,1)S(1)} collective-permute-done((bf16[512,256]{1,0:T(8,128)(2,1)S(1)}, bf16[512,256]{1,0:T(8,128)(2,1)S(1)}, u32[]{:S(2)}, u32[]{:S(2)}) %collective-permute-start.11) | collective-permute-done | bytes 262176 | tf_op jit(solution)/shard_map/ppermute | solution.py:225
  51.9 0.7 copy-done.24
  52.7 0.3 copy-done.22
  53.0 6.8 %session.1 = (f32[256,512]{1,0:T(8,128)}, f32[256,128]{1,0:T(8,128)}, f32[256,128]{1,0:T(8,128)}, bf16[2048,256]{1,0:T(8,128)(2,1)}) custom-call(s32[33]{0:T(128)} %copy-done.20, s32[64]{0:T(128)} %reshape.18.mask, bf16[256,512]{1,0:T(8,128)(2,1)} %copy-done.11, bf16[16,128,512]{2,1,0:T(8,128)(2,1)} %bitcast.2, bf16[2048,256]{1,0:T(8,128)(2,1)} %copy-done.22, ...), custom_call_target="tpu_custom_call" | custom-call | flops 1610612736 | bytes 8388608 | tf_op jit(solution)/shard_map/session/pallas_call | solution.py:289
  59.8 0.2 collective-permute-start.14
  60.0 2.7 %collective-permute-done.14.got = bf16[2048,256]{1,0:T(8,128)(2,1)S(1)} collective-permute-done((bf16[2048,256]{1,0:T(8,128)(2,1)}, bf16[2048,256]{1,0:T(8,128)(2,1)S(1)}, u32[]{:S(2)}, u32[]{:S(2)}) %collective-permute-start.14) | collective-permute-done | bytes 1048608 | tf_op jit(solution)/shard_map/ppermute | solution.py:225
  62.7 1.0 copy-done.12
  63.7 3.3 %merge.3 = bf16[512,256]{1,0:T(8,128)(2,1)} custom-call(s32[33]{0:T(128)} %copy-done.20, s32[33]{0:T(128)} %copy-done.21, bf16[2048,256]{1,0:T(8,128)(2,1)} %get-tuple-element.28.own, bf16[2048,256]{1,0:T(8,128)(2,1)} %copy-done.12), custom_call_target="tpu_custom_call" | custom-call | bytes 5242880 | tf_op jit(solution)/shard_map/merge/pallas_call | solution.py:319
  67.0 0.3 collective-permute-start.17
  67.3 4.6 %merge.2 = (f32[512,256]{1,0:T(8,128)}, f32[512,256]{1,0:T(8,128)}, f32[512,256]{1,0:T(8,128)}, f32[512,256]{1,0:T(8,128)}, bf16[512,256]{1,0:T(8,128)(2,1)}, /*...) custom-call(s32[33]{0:T(128)} %copy-done.20, s32[33]{0:T(128)} %copy-done.21, bf16[2048,256]{1,0:T(8,128)(2,1)} %get-tuple-element.28.own, ...), custom_call_target="tpu_custom_call" | custom-call | bytes 5242880 | tf_op jit(solution)/shard_map/merge/pallas_call | solution.py:319
  71.9 1.8 %collective-permute-start.20 = (bf16[512,256]{1,0:T(8,128)(2,1)}, bf16[512,256]{1,0:T(8,128)(2,1)S(1)}, u32[]{:S(2)}, u32[]{:S(2)}) collective-permute-start(bf16[512,256]{1,0:T(8,128)(2,1)} %get-tuple-element.35), channel_id=1, source_target_pairs={{0,2},{1,3},{2,0},{3,1},{4,6},{5,7},{6,4},{7,5},{8,10},{9,11},{10,... | collective-permute-start | bytes 786440 | tf_op jit(solution)/shard_map/ppermute | solution.py:225
  73.7 0.3 collective-permute-start.16
  73.9 2.4 %collective-permute-done.17 = bf16[512,256]{1,0:T(8,128)(2,1)S(1)} collective-permute-done((bf16[512,256]{1,0:T(8,128)(2,1)}, bf16[512,256]{1,0:T(8,128)(2,1)S(1)}, u32[]{:S(2)}, u32[]{:S(2)}) %collective-permute-start.17) | collective-permute-done | bytes 262176 | tf_op jit(solution)/shard_map/ppermute | solution.py:225
  76.3 1.2 %add_convert_fusion.2 = bf16[512,256]{1,0:T(8,128)(2,1)S(1)} fusion(f32[512,256]{1,0:T(8,128)} %get-tuple-element.33, bf16[512,256]{1,0:T(8,128)(2,1)S(1)} %collective-permute-done.17), kind=kLoop, calls=%fused_computation.3 | loop fusion | flops 393216 | bytes 1048576 | tf_op jit(solution)/shard_map/convert_element_type | solution.py:342
  77.5 0.1 collective-permute-start.18
  77.6 1.3 %collective-permute-start.12 = (f32[256,128]{1,0:T(8,128)S(1)}, f32[256,128]{1,0:T(8,128)S(1)}, u32[]{:S(2)}, u32[]{:S(2)}) collective-permute-start(f32[256,128]{1,0:T(8,128)S(1)} %copy-done.26), channel_id=1, source_target_pairs={{0,1},{1,2},{2,3},{3,4},{4,5},{5,6},{6,7},{7,8},{8,9},{9,10},{10,1... | collective-permute-start | bytes 393224 | tf_op jit(solution)/shard_map/ppermute | solution.py:225
  78.9 1.3 %collective-permute-start.13 = (f32[256,128]{1,0:T(8,128)S(1)}, f32[256,128]{1,0:T(8,128)S(1)}, u32[]{:S(2)}, u32[]{:S(2)}) collective-permute-start(f32[256,128]{1,0:T(8,128)S(1)} %copy-done.25), channel_id=1, source_target_pairs={{1,0},{2,1},{3,2},{4,3},{5,4},{6,5},{7,6},{8,7},{9,8},{10,9},{11,1... | collective-permute-start | bytes 393224 | tf_op jit(solution)/shard_map/ppermute | solution.py:225
  80.2 1.8 %collective-permute-done.20 = bf16[512,256]{1,0:T(8,128)(2,1)S(1)} collective-permute-done((bf16[512,256]{1,0:T(8,128)(2,1)}, bf16[512,256]{1,0:T(8,128)(2,1)S(1)}, u32[]{:S(2)}, u32[]{:S(2)}) %collective-permute-start.20) | collective-permute-done | bytes 262176 | tf_op jit(solution)/shard_map/ppermute | solution.py:225
  82.0 1.1 %collective-permute-start.15 = (bf16[512,256]{1,0:T(8,128)(2,1)}, bf16[512,256]{1,0:T(8,128)(2,1)S(1)}, u32[]{:S(2)}, u32[]{:S(2)}) collective-permute-start(bf16[512,256]{1,0:T(8,128)(2,1)} %get-tuple-element.30), channel_id=1, source_target_pairs={{0,2},{1,3},{2,0},{3,1},{4,6},{5,7},{6,4},{7,5},{8,10},{9,11},{10,... | collective-permute-start | bytes 786440 | tf_op jit(solution)/shard_map/ppermute | solution.py:225
  83.1 1.2 %add_convert_fusion = bf16[512,256]{1,0:T(8,128)(2,1)S(1)} fusion(f32[512,256]{1,0:T(8,128)} %get-tuple-element.34, bf16[512,256]{1,0:T(8,128)(2,1)S(1)} %collective-permute-done.20), kind=kLoop, calls=%fused_computation.1 | loop fusion | flops 393216 | bytes 1048576 | tf_op jit(solution)/shard_map/convert_element_type | solution.py:348
  84.3 3.3 %collective-permute-done.16 = bf16[512,256]{1,0:T(8,128)(2,1)S(1)} collective-permute-done((bf16[512,256]{1,0:T(8,128)(2,1)}, bf16[512,256]{1,0:T(8,128)(2,1)S(1)}, u32[]{:S(2)}, u32[]{:S(2)}) %collective-permute-start.16) | collective-permute-done | bytes 262176 | tf_op jit(solution)/shard_map/ppermute | solution.py:225
  87.6 2.8 %collective-permute-start.21 = (bf16[512,256]{1,0:T(8,128)(2,1)S(1)}, bf16[512,256]{1,0:T(8,128)(2,1)S(1)}, u32[]{:S(2)}, u32[]{:S(2)}) collective-permute-start(bf16[512,256]{1,0:T(8,128)(2,1)S(1)} %add_convert_fusion), channel_id=1, source_target_pairs={{0,12},{1,13},{2,14},{3,15},{4,0},{5,1},{6,2},{7,3},{8,4},{9,5},{1... | collective-permute-start | bytes 786440 | tf_op jit(solution)/shard_map/ppermute | solution.py:225
  90.4 1.1 %add_convert_fusion.1 = bf16[512,256]{1,0:T(8,128)(2,1)S(1)} fusion(bf16[512,256]{1,0:T(8,128)(2,1)S(1)} %collective-permute-done.18, f32[512,256]{1,0:T(8,128)} %get-tuple-element.31, bf16[512,256]{1,0:T(8,128)(2,1)S(1)} %collective-permute-done.16), kind=kLoop, calls=%fused_computation.2 | loop fusion | flops 655360 | bytes 1310720 | tf_op jit(solution)/shard_map/convert_element_type | solution.py:342
  91.5 0.1 collective-permute-start.19
  91.6 4.1 %unsmooth.1 = f32[256,512]{1,0:T(8,128)} custom-call(f32[256,128]{1,0:T(8,128)S(1)} %collective-permute-done.12.low, f32[256,512]{1,0:T(8,128)S(1)} %copy-done.6, f32[256,128]{1,0:T(8,128)S(1)} %collective-permute-done.13.high, f32[256,768]{1,0:T(8,128)S(1)} %get-tuple-element.27.k_spec, bf16[768,768]{1,0:T(8,128)(2,1)S(1)} %copy-done.3, ...), custom_call_target="tpu_custom_call" | custom-call | flops 1509949440 | bytes 6291456 | tf_op jit(solution)/shard_map/unsmooth/pallas_call | solution.py:351
  95.7 1.4 %collective-permute-done.21 = bf16[512,256]{1,0:T(8,128)(2,1)S(1)} collective-permute-done((bf16[512,256]{1,0:T(8,128)(2,1)S(1)}, bf16[512,256]{1,0:T(8,128)(2,1)S(1)}, u32[]{:S(2)}, u32[]{:S(2)}) %collective-permute-start.21) | collective-permute-done | bytes 262176 | tf_op jit(solution)/shard_map/ppermute | solution.py:225
  97.1 4.9 %collective-permute-done.19 = bf16[512,256]{1,0:T(8,128)(2,1)S(1)} collective-permute-done((bf16[512,256]{1,0:T(8,128)(2,1)S(1)}, bf16[512,256]{1,0:T(8,128)(2,1)S(1)}, u32[]{:S(2)}, u32[]{:S(2)}) %collective-permute-start.19) | collective-permute-done | bytes 262176 | tf_op jit(solution)/shard_map/ppermute | solution.py:225
  102.1 0.9 convert_add_fusion
  (50 shorter events, 0.1 us)
Async XLA Ops:
  0.6 12.1 %collective-permute-start.5 = (bf16[512,256]{1,0:T(8,128)(2,1)}, bf16[512,256]{1,0:T(8,128)(2,1)S(1)}, u32[]{:S(2)}, u32[]{:S(2)}) collective-permute-start(bf16[512,256]{1,0:T(8,128)(2,1)} %refs_0_.3), channel_id=1, source_target_pairs={{0,12},{1,13},{2,14},{3,15},{4,0},{5,1},{6,2},{7,3},{8,4},{9,5},{1... | collective-permute-start | bytes 786440 | tf_op jit(solution)/shard_map/ppermute | solution.py:225
  5.7 12.4 %collective-permute-start.3 = (bf16[512,256]{1,0:T(8,128)(2,1)}, bf16[512,256]{1,0:T(8,128)(2,1)S(1)}, u32[]{:S(2)}, u32[]{:S(2)}) collective-permute-start(bf16[512,256]{1,0:T(8,128)(2,1)} %refs_0_.3), channel_id=1, source_target_pairs={{0,4},{1,5},{2,6},{3,7},{4,8},{5,9},{6,10},{7,11},{8,12},{9,13},{1... | collective-permute-start | bytes 786440 | tf_op jit(solution)/shard_map/ppermute | solution.py:225
  6.7 13.2 %collective-permute-start.2 = (f32[256,128]{1,0:T(8,128)S(1)}, f32[256,128]{1,0:T(8,128)S(1)}, u32[]{:S(2)}, u32[]{:S(2)}) collective-permute-start(f32[256,128]{1,0:T(8,128)S(1)} %get-tuple-element.36), channel_id=1, source_target_pairs={{1,0},{2,1},{3,2},{4,3},{5,4},{6,5},{7,6},{8,7},{9,8},{10,9},{11,1... | collective-permute-start | bytes 393224 | tf_op jit(solution)/shard_map/ppermute | solution.py:225
  8.0 17.2 %collective-permute-start.1 = (f32[256,128]{1,0:T(8,128)S(1)}, f32[256,128]{1,0:T(8,128)S(1)}, u32[]{:S(2)}, u32[]{:S(2)}) collective-permute-start(f32[256,128]{1,0:T(8,128)S(1)} %get-tuple-element.37), channel_id=1, source_target_pairs={{0,1},{1,2},{2,3},{3,4},{4,5},{5,6},{6,7},{7,8},{8,9},{9,10},{10,1... | collective-permute-start | bytes 393224 | tf_op jit(solution)/shard_map/ppermute | solution.py:225
  11.1 25.3 %collective-permute-start.6 = (bf16[512,256]{1,0:T(8,128)(2,1)}, bf16[512,256]{1,0:T(8,128)(2,1)S(1)}, u32[]{:S(2)}, u32[]{:S(2)}) collective-permute-start(bf16[512,256]{1,0:T(8,128)(2,1)} %refs_0_.3), channel_id=1, source_target_pairs={{0,2},{1,3},{2,0},{3,1},{4,6},{5,7},{6,4},{7,5},{8,10},{9,11},{10,... | collective-permute-start | bytes 786440 | tf_op jit(solution)/shard_map/ppermute | solution.py:225
  12.8 22.9 %copy-start.14 = (bf16[512,256]{1,0:T(8,128)(2,1)}, bf16[512,256]{1,0:T(8,128)(2,1)S(1)}, u32[]{:S(2)}) copy-start(bf16[512,256]{1,0:T(8,128)(2,1)S(1)} %collective-permute-done.5.refs_3_) | copy-start | bytes 786436
  12.8 23.7 %collective-permute-start.8 = (bf16[512,256]{1,0:T(8,128)(2,1)S(1)}, bf16[512,256]{1,0:T(8,128)(2,1)S(1)}, u32[]{:S(2)}, u32[]{:S(2)}) collective-permute-start(bf16[512,256]{1,0:T(8,128)(2,1)S(1)} %collective-permute-done.5.refs_3_), channel_id=1, source_target_pairs={{0,2},{1,3},{2,0},{3,1},{4,6},{5,7},{6,4},{7,5},{8,10},{9,11},{10,... | collective-permute-start | bytes 786440 | tf_op jit(solution)/shard_map/ppermute | solution.py:225
  18.1 17.5 %copy-start.15 = (bf16[512,256]{1,0:T(8,128)(2,1)}, bf16[512,256]{1,0:T(8,128)(2,1)S(1)}, u32[]{:S(2)}) copy-start(bf16[512,256]{1,0:T(8,128)(2,1)S(1)} %collective-permute-done.3.refs_1_) | copy-start | bytes 786436
  18.1 18.3 %collective-permute-start.7 = (bf16[512,256]{1,0:T(8,128)(2,1)S(1)}, bf16[512,256]{1,0:T(8,128)(2,1)S(1)}, u32[]{:S(2)}, u32[]{:S(2)}) collective-permute-start(bf16[512,256]{1,0:T(8,128)(2,1)S(1)} %collective-permute-done.3.refs_1_), channel_id=1, source_target_pairs={{0,2},{1,3},{2,0},{3,1},{4,6},{5,7},{6,4},{7,5},{8,10},{9,11},{10,... | collective-permute-start | bytes 786440 | tf_op jit(solution)/shard_map/ppermute | solution.py:225
  19.9 16.6 %collective-permute-start.4 = (bf16[512,256]{1,0:T(8,128)(2,1)S(1)}, bf16[512,256]{1,0:T(8,128)(2,1)S(1)}, u32[]{:S(2)}, u32[]{:S(2)}) collective-permute-start(bf16[512,256]{1,0:T(8,128)(2,1)S(1)} %collective-permute-done.3.refs_1_), channel_id=1, source_target_pairs={{0,4},{1,5},{2,6},{3,7},{4,8},{5,9},{6,10},{7,11},{8,12},{9,13},{1... | collective-permute-start | bytes 786440 | tf_op jit(solution)/shard_map/ppermute | solution.py:225
  25.2 10.5 %copy-start.20 = (s32[33]{0:T(128)}, s32[33]{0:T(128)S(1)}, u32[]{:S(2)}) copy-start(s32[33]{0:T(128)S(1)} %pad_add_fusion.ids) | copy-start | bytes 400
  25.2 11.2 %collective-permute-start = (s32[33]{0:T(128)S(1)}, s32[33]{0:T(128)S(1)}, u32[]{:S(2)}, u32[]{:S(2)}) collective-permute-start(s32[33]{0:T(128)S(1)} %pad_add_fusion.ids), channel_id=1, source_target_pairs={{0,1},{1,0},{2,3},{3,2},{4,5},{5,4},{6,7},{7,6},{8,9},{9,8},{10,11... | collective-permute-start | bytes 404 | tf_op jit(solution)/shard_map/ppermute | solution.py:225
  25.3 1.3 %copy-start = (bf16[768,768]{1,0:T(8,128)(2,1)S(1)}, bf16[768,768]{1,0:T(8,128)(2,1)}, u32[]{:S(2)}) copy-start(bf16[768,768]{1,0:T(8,128)(2,1)} %constant.17.clone.fl) | copy-start | bytes 3538948
  26.5 1.3 %copy-start.2 = (bf16[768,768]{1,0:T(8,128)(2,1)S(1)}, bf16[768,768]{1,0:T(8,128)(2,1)}, u32[]{:S(2)}) copy-start(bf16[768,768]{1,0:T(8,128)(2,1)} %constant.16.clone.fh) | copy-start | bytes 3538948
  27.8 1.0 %copy-start.7 = (f32[256,512]{1,0:T(8,128)S(1)}, f32[256,512]{1,0:T(8,128)}, u32[]{:S(2)}) copy-start(f32[256,512]{1,0:T(8,128)} %mid.1) | copy-start | bytes 1572868
  28.8 0.9 copy-start.8
  29.8 1.1 %copy-start.9 = (bf16[768,512]{1,0:T(8,128)(2,1)S(1)}, bf16[768,512]{1,0:T(8,128)(2,1)}, u32[]{:S(2)}) copy-start(bf16[768,512]{1,0:T(8,128)(2,1)} %constant.19.clone.wl) | copy-start | bytes 2359300
  30.9 1.1 %copy-start.10 = (bf16[768,512]{1,0:T(8,128)(2,1)S(1)}, bf16[768,512]{1,0:T(8,128)(2,1)}, u32[]{:S(2)}) copy-start(bf16[768,512]{1,0:T(8,128)(2,1)} %constant.18.clone.wh) | copy-start | bytes 2359300
  35.7 0.7 copy-start.11
  36.4 0.6 copy-start.21
  36.4 0.7 copy-start.16
  36.4 0.8 copy-start.17
  36.4 0.8 copy-start.18
  37.3 0.7 copy-start.19
  41.3 10.6 %collective-permute-start.9 = (bf16[2048,256]{1,0:T(8,128)(2,1)}, bf16[2048,256]{1,0:T(8,128)(2,1)S(1)}, u32[]{:S(2)}, u32[]{:S(2)}) collective-permute-start(bf16[2048,256]{1,0:T(8,128)(2,1)} %pack.1), channel_id=1, source_target_pairs={{0,1},{1,0},{2,3},{3,2},{4,5},{5,4},{6,7},{7,6},{8,9},{9,8},{10,11... | collective-permute-start | bytes 3145736 | tf_op jit(solution)/shard_map/ppermute | solution.py:225
  41.9 8.5 %collective-permute-start.10 = (bf16[512,256]{1,0:T(8,128)(2,1)}, bf16[512,256]{1,0:T(8,128)(2,1)S(1)}, u32[]{:S(2)}, u32[]{:S(2)}) collective-permute-start(bf16[512,256]{1,0:T(8,128)(2,1)} %copy-done.19), channel_id=1, source_target_pairs={{0,2},{1,3},{2,0},{3,1},{4,6},{5,7},{6,4},{7,5},{8,10},{9,11},{10,... | collective-permute-start | bytes 786440 | tf_op jit(solution)/shard_map/ppermute | solution.py:225
  50.4 1.5 %copy-start.23 = (bf16[512,256]{1,0:T(8,128)(2,1)}, bf16[512,256]{1,0:T(8,128)(2,1)S(1)}, u32[]{:S(2)}) copy-start(bf16[512,256]{1,0:T(8,128)(2,1)S(1)} %collective-permute-done.10.refs_6_) | copy-start | bytes 786436
  50.4 1.5 %collective-permute-start.11 = (bf16[512,256]{1,0:T(8,128)(2,1)S(1)}, bf16[512,256]{1,0:T(8,128)(2,1)S(1)}, u32[]{:S(2)}, u32[]{:S(2)}) collective-permute-start(bf16[512,256]{1,0:T(8,128)(2,1)S(1)} %collective-permute-done.10.refs_6_), channel_id=1, source_target_pairs={{0,1},{1,0},{2,3},{3,2},{4,5},{5,4},{6,7},{7,6},{8,9},{9,8},{10,11... | collective-permute-start | bytes 786440 | tf_op jit(solution)/shard_map/ppermute | solution.py:225
  51.9 0.7 copy-start.24
  51.9 1.1 %copy-start.22 = (bf16[2048,256]{1,0:T(8,128)(2,1)}, bf16[2048,256]{1,0:T(8,128)(2,1)S(1)}, u32[]{:S(2)}) copy-start(bf16[2048,256]{1,0:T(8,128)(2,1)S(1)} %collective-permute-done.9.packed) | copy-start | bytes 3145732
  59.8 2.9 %collective-permute-start.14 = (bf16[2048,256]{1,0:T(8,128)(2,1)}, bf16[2048,256]{1,0:T(8,128)(2,1)S(1)}, u32[]{:S(2)}, u32[]{:S(2)}) collective-permute-start(bf16[2048,256]{1,0:T(8,128)(2,1)} %get-tuple-element.28.own), channel_id=1, source_target_pairs={{0,1},{1,0},{2,3},{3,2},{4,5},{5,4},{6,7},{7,6},{8,9},{9,8},{10,11... | collective-permute-start | bytes 3145736 | tf_op jit(solution)/shard_map/ppermute | solution.py:225
  62.7 1.0 copy-start.12
  67.0 10.6 %copy-start.26 = (f32[256,128]{1,0:T(8,128)S(1)}, f32[256,128]{1,0:T(8,128)}, u32[]{:S(2)}) copy-start(f32[256,128]{1,0:T(8,128)} %get-tuple-element.24) | copy-start | bytes 393220
  67.0 11.9 %copy-start.25 = (f32[256,128]{1,0:T(8,128)S(1)}, f32[256,128]{1,0:T(8,128)}, u32[]{:S(2)}) copy-start(f32[256,128]{1,0:T(8,128)} %get-tuple-element.26) | copy-start | bytes 393220
  67.0 9.4 %collective-permute-start.17 = (bf16[512,256]{1,0:T(8,128)(2,1)}, bf16[512,256]{1,0:T(8,128)(2,1)S(1)}, u32[]{:S(2)}, u32[]{:S(2)}) collective-permute-start(bf16[512,256]{1,0:T(8,128)(2,1)} %merge.3), channel_id=1, source_target_pairs={{0,2},{1,3},{2,0},{3,1},{4,6},{5,7},{6,4},{7,5},{8,10},{9,11},{10,... | collective-permute-start | bytes 786440 | tf_op jit(solution)/shard_map/ppermute | solution.py:225
  67.3 24.3 %copy-start.5 = (bf16[768,512]{1,0:T(8,128)(2,1)S(1)}, bf16[768,512]{1,0:T(8,128)(2,1)}, u32[]{:S(2)}) copy-start(bf16[768,512]{1,0:T(8,128)(2,1)} %constant.20.clone.wh) | copy-start | bytes 2359300
  67.3 24.3 %copy-start.6 = (f32[256,512]{1,0:T(8,128)S(1)}, f32[256,512]{1,0:T(8,128)}, u32[]{:S(2)}) copy-start(f32[256,512]{1,0:T(8,128)} %get-tuple-element.25.mid) | copy-start | bytes 1572868
  71.9 10.1 %collective-permute-start.20 = (bf16[512,256]{1,0:T(8,128)(2,1)}, bf16[512,256]{1,0:T(8,128)(2,1)S(1)}, u32[]{:S(2)}, u32[]{:S(2)}) collective-permute-start(bf16[512,256]{1,0:T(8,128)(2,1)} %get-tuple-element.35), channel_id=1, source_target_pairs={{0,2},{1,3},{2,0},{3,1},{4,6},{5,7},{6,4},{7,5},{8,10},{9,11},{10,... | collective-permute-start | bytes 786440 | tf_op jit(solution)/shard_map/ppermute | solution.py:225
  73.7 13.9 %collective-permute-start.16 = (bf16[512,256]{1,0:T(8,128)(2,1)}, bf16[512,256]{1,0:T(8,128)(2,1)S(1)}, u32[]{:S(2)}, u32[]{:S(2)}) collective-permute-start(bf16[512,256]{1,0:T(8,128)(2,1)} %get-tuple-element.32), channel_id=1, source_target_pairs={{0,2},{1,3},{2,0},{3,1},{4,6},{5,7},{6,4},{7,5},{8,10},{9,11},{10,... | collective-permute-start | bytes 786440 | tf_op jit(solution)/shard_map/ppermute | solution.py:225
  76.3 15.3 %copy-start.4 = (bf16[768,512]{1,0:T(8,128)(2,1)S(1)}, bf16[768,512]{1,0:T(8,128)(2,1)}, u32[]{:S(2)}) copy-start(bf16[768,512]{1,0:T(8,128)(2,1)} %constant.21.clone.wl) | copy-start | bytes 2359300
  77.5 12.8 %collective-permute-start.18 = (bf16[512,256]{1,0:T(8,128)(2,1)S(1)}, bf16[512,256]{1,0:T(8,128)(2,1)S(1)}, u32[]{:S(2)}, u32[]{:S(2)}) collective-permute-start(bf16[512,256]{1,0:T(8,128)(2,1)S(1)} %add_convert_fusion.2), channel_id=1, source_target_pairs={{0,4},{1,5},{2,6},{3,7},{4,8},{5,9},{6,10},{7,11},{8,12},{9,13},{1... | collective-permute-start | bytes 786440 | tf_op jit(solution)/shard_map/ppermute | solution.py:225
  77.6 14.0 %collective-permute-start.12 = (f32[256,128]{1,0:T(8,128)S(1)}, f32[256,128]{1,0:T(8,128)S(1)}, u32[]{:S(2)}, u32[]{:S(2)}) collective-permute-start(f32[256,128]{1,0:T(8,128)S(1)} %copy-done.26), channel_id=1, source_target_pairs={{0,1},{1,2},{2,3},{3,4},{4,5},{5,6},{6,7},{7,8},{8,9},{9,10},{10,1... | collective-permute-start | bytes 393224 | tf_op jit(solution)/shard_map/ppermute | solution.py:225
  78.9 12.7 %collective-permute-start.13 = (f32[256,128]{1,0:T(8,128)S(1)}, f32[256,128]{1,0:T(8,128)S(1)}, u32[]{:S(2)}, u32[]{:S(2)}) collective-permute-start(f32[256,128]{1,0:T(8,128)S(1)} %copy-done.25), channel_id=1, source_target_pairs={{1,0},{2,1},{3,2},{4,3},{5,4},{6,5},{7,6},{8,7},{9,8},{10,9},{11,1... | collective-permute-start | bytes 393224 | tf_op jit(solution)/shard_map/ppermute | solution.py:225
  82.0 13.8 %collective-permute-start.15 = (bf16[512,256]{1,0:T(8,128)(2,1)}, bf16[512,256]{1,0:T(8,128)(2,1)S(1)}, u32[]{:S(2)}, u32[]{:S(2)}) collective-permute-start(bf16[512,256]{1,0:T(8,128)(2,1)} %get-tuple-element.30), channel_id=1, source_target_pairs={{0,2},{1,3},{2,0},{3,1},{4,6},{5,7},{6,4},{7,5},{8,10},{9,11},{10,... | collective-permute-start | bytes 786440 | tf_op jit(solution)/shard_map/ppermute | solution.py:225
  83.1 8.6 %copy-start.1 = (bf16[768,768]{1,0:T(8,128)(2,1)S(1)}, bf16[768,768]{1,0:T(8,128)(2,1)}, u32[]{:S(2)}) copy-start(bf16[768,768]{1,0:T(8,128)(2,1)} %constant.17.clone.fl) | copy-start | bytes 3538948
  83.1 8.6 %copy-start.3 = (bf16[768,768]{1,0:T(8,128)(2,1)S(1)}, bf16[768,768]{1,0:T(8,128)(2,1)}, u32[]{:S(2)}) copy-start(bf16[768,768]{1,0:T(8,128)(2,1)} %constant.16.clone.fh) | copy-start | bytes 3538948
  87.6 9.5 %collective-permute-start.21 = (bf16[512,256]{1,0:T(8,128)(2,1)S(1)}, bf16[512,256]{1,0:T(8,128)(2,1)S(1)}, u32[]{:S(2)}, u32[]{:S(2)}) collective-permute-start(bf16[512,256]{1,0:T(8,128)(2,1)S(1)} %add_convert_fusion), channel_id=1, source_target_pairs={{0,12},{1,13},{2,14},{3,15},{4,0},{5,1},{6,2},{7,3},{8,4},{9,5},{1... | collective-permute-start | bytes 786440 | tf_op jit(solution)/shard_map/ppermute | solution.py:225
  91.5 10.6 %collective-permute-start.19 = (bf16[512,256]{1,0:T(8,128)(2,1)S(1)}, bf16[512,256]{1,0:T(8,128)(2,1)S(1)}, u32[]{:S(2)}, u32[]{:S(2)}) collective-permute-start(bf16[512,256]{1,0:T(8,128)(2,1)S(1)} %add_convert_fusion.1), channel_id=1, source_target_pairs={{0,4},{1,5},{2,6},{3,7},{4,8},{5,9},{6,10},{7,11},{8,12},{9,13},{1... | collective-permute-start | bytes 786440 | tf_op jit(solution)/shard_map/ppermute | solution.py:225
  91.6 10.4 %copy-start.13 = (f32[512,256]{1,0:T(8,128)S(1)}, f32[512,256]{1,0:T(8,128)}, u32[]{:S(2)}) copy-start(f32[512,256]{1,0:T(8,128)} %get-tuple-element.29) | copy-start | bytes 1572868

commit v4 on v3

v4 whole, which is shorter than its diff:
```python
import functools

import jax
import jax.numpy as jnp
import numpy as np
from jax import lax
from jax.experimental import pallas as pl
from jax.experimental.pallas import tpu as pltpu
from jax.sharding import PartitionSpec as P

BLK = 128
ROW = 4
VMEM_LIMIT = 60 * 2**20
F32 = jnp.float32
BF16 = jnp.bfloat16
VMEM = pl.BlockSpec(memory_space=pltpu.VMEM)
HBM = pl.BlockSpec(memory_space=pltpu.HBM)


def split_const(a):
    high = a.astype(jnp.bfloat16)
    low = (a - high.astype(np.float64)).astype(jnp.bfloat16)
    return high, low


@functools.lru_cache(maxsize=None)
def dft_tables(length, outputs, first):
    half = length // 2
    t = np.arange(length)[:, None]
    f = np.arange(half)[None, :]
    angle = 2 * np.pi * ((t * f) % length) / length
    cos, sin = np.cos(angle), np.sin(angle)
    sin[:, 0] = 1 - 2 * (np.arange(length) % 2)
    forward = np.concatenate([cos, sin], axis=1)
    weight = np.full((half,), 2.0 / length)
    weight[0] = 1.0 / length
    inverse = (forward * np.concatenate([weight, weight])[None, :]).T
    inverse = inverse[:, first : first + outputs]
    return split_const(forward) + split_const(inverse)


def parts(a):
    high = a.astype(BF16)
    return high, (a - high.astype(F32)).astype(BF16)


def dot3(a, b_high, b_low):
    high, low = a
    out = jnp.dot(high, b_high, preferred_element_type=F32)
    out += jnp.dot(low, b_high, preferred_element_type=F32)
    out += jnp.dot(high, b_low, preferred_element_type=F32)
    return out


def product(signal, taps, sign):
    half = signal.shape[1] // 2
    xr, xi = signal[:, :half], signal[:, half:]
    kr, ki = taps[:, :half], taps[:, half:]
    first = lax.broadcasted_iota(jnp.int32, kr.shape, 1) == 0
    kr_i = jnp.where(first, ki, kr)
    ki_x = jnp.where(first, 0.0, ki) * sign
    return jnp.concatenate([xr * kr + xi * ki_x, xi * kr_i - xr * ki_x], axis=1)


def with_halo(mid, core_side, far_side, fh, fl):
    width = core_side[0].shape[1]
    bins = mid.shape[1]
    even = lax.rem(lax.axis_index("tm"), 2) == 0
    out = dot3(parts(mid), fh[width : width + bins], fl[width : width + bins])
    for side, later in ((core_side, even), (far_side, jnp.logical_not(even))):
        rows = pl.ds(pl.multiple_of(jnp.where(later, width + bins, 0), BLK), width)
        out += dot3(side, fh[rows], fl[rows])
    return out


def load(sources, targets, sem):
    copies = [
        pltpu.make_async_copy(s, t, sem.at[i]) for i, (s, t) in enumerate(zip(sources, targets))
    ]
    for copy in copies:
        copy.start()
    return copies


def smooth_kernel(mid, core_side, far_side, taps, *refs):
    tables, (out, spectrum), held, sem = refs[:4], refs[4:6], refs[6:10], refs[10]
    copies = load(tables, held, sem)
    fh, fl, wh, wl = held
    copies[0].wait()
    copies[1].wait()
    count = taps.shape[1]
    k_spec = dot3(parts(taps[...]), fh[:count], fl[:count])
    spectrum[...] = k_spec
    x_spec = with_halo(mid[...], parts(core_side[...]), parts(far_side[...]), fh, fl)
    copies[2].wait()
    copies[3].wait()
    out[...] = dot3(parts(product(x_spec, k_spec, 1.0)), wh[...], wl[...]).astype(out.dtype)


def unsmooth_kernel(mid, core_terms, far_side, k_spec, *refs):
    tables, out, held, sem = refs[:4], refs[4], refs[5:10], refs[10]
    first = core_terms.shape[0] - far_side.shape[0]
    copies = load(tables + (core_terms.at[pl.ds(first, far_side.shape[0])],), held, sem)
    fh, fl, wh, wl, core_side = held
    width = far_side.shape[1] // 2
    for i in (0, 1, 4):
        copies[i].wait()
    x_spec = with_halo(
        mid[...],
        (core_side[:, :width], core_side[:, width:]),
        (far_side[:, :width], far_side[:, width:]),
        fh,
        fl,
    )
    copies[2].wait()
    copies[3].wait()
    out[...] = dot3(parts(product(x_spec, k_spec[...], -1.0)), wh[...], wl[...])


def place_of(ids, e, blocks, forward):
    me = lax.axis_index("tm")
    chain = lax.axis_size("tm") // ROW
    top = ids.shape[1]
    code = ids[e // top, e % top]
    owner, slot = code // blocks, code % blocks
    step = owner // ROW - me // ROW
    step = step if forward else -step
    turn = jnp.where(step < 0, step + chain, step)
    piece = jnp.where((owner // 2) % 2 == (me // 2) % 2, 0, chain) + turn
    return owner % 2 == me % 2, piece, pl.multiple_of(slot * BLK, BLK)


def pack_kernel(entries, late, asked, *refs):
    pieces, (out, sem) = refs[:-2], refs[-2:]
    blocks = pieces[0].shape[0] // BLK

    def copy(piece, e, row):
        return pltpu.make_async_copy(
            piece.at[pl.ds(row, BLK)], out.at[pl.ds(pl.multiple_of(e * BLK, BLK), BLK)], sem.at[e]
        )

    def start(e, _):
        core, piece, row = place_of(asked, e, blocks, False)
        for q, ref in enumerate(pieces[:late] + (None,) + pieces[late:]):
            if q == late:
                continue

            @pl.when(jnp.logical_and(core, piece == q))
            def _():
                copy(ref, e, row).start()

        return 0

    def wait(e, _):
        core, piece, row = place_of(asked, e, blocks, False)

        @pl.when(jnp.logical_and(core, piece != late))
        def _():
            copy(pieces[0], e, row).wait()

        return 0

    lax.fori_loop(0, entries, start, 0)
    lax.fori_loop(0, entries, wait, 0)


def session_kernel(
    entries, group, late, ids, mask, smoothed, recorded, packed, late_theirs, *refs
):
    pieces = refs[:-6]
    grad, far_side, terms, rows, resid, sem = refs[-6:]
    blocks = pieces[0].shape[0] // BLK
    bins = smoothed.shape[1]
    top = ids.shape[1]

    def copy(source, e, row):
        return pltpu.make_async_copy(source.at[pl.ds(row, BLK)], rows.at[e], sem.at[e])

    def fetch(e, _):
        core, piece, row = place_of(ids, e, blocks, False)
        for q, ref in enumerate(pieces):

            @pl.when(jnp.logical_and(core, piece == q))
            def _():
                copy(ref, e, row).start()

        @pl.when(jnp.logical_and(jnp.logical_not(core), piece != late))
        def _():
            copy(packed, e, pl.multiple_of(e * BLK, BLK)).start()

        @pl.when(jnp.logical_and(jnp.logical_not(core), piece == late))
        def _():
            copy(late_theirs, e, row).start()

        return 0

    lax.fori_loop(0, entries, fetch, 0)
    grad[...] = jnp.zeros_like(grad)
    depth = group * BLK

    def step(g, _):
        for i in range(group):
            copy(packed, g * group + i, 0).wait()
        block = rows[pl.ds(g * group, group)].reshape(depth, rows.shape[2])
        predicted = jnp.dot(block, smoothed[...], preferred_element_type=F32)
        for i in range(group):
            e = g * group + i
            for t in range(bins // BLK):
                cut = slice(t * BLK, (t + 1) * BLK)
                weight = mask[e // top, t, e % top].astype(F32)
                part = predicted[i * BLK : (i + 1) * BLK, cut]
                seen = recorded[e, :, cut].astype(F32)
                resid[i * BLK : (i + 1) * BLK, cut] = (weight * (part - seen)).astype(BF16)
        term = lax.dot_general(
            resid[...], smoothed[...], (((1,), (1,)), ((), ())), preferred_element_type=F32
        )
        target = pl.ds(pl.multiple_of(g * depth, depth), depth)
        terms[target] = (term * (1.0 / BLK)).astype(BF16)
        grad[...] += lax.dot_general(
            block, resid[...], (((0,), (0,)), ((), ())), preferred_element_type=F32
        ) * (1.0 / BLK)
        return 0

    lax.fori_loop(0, entries // group, step, 0)
    width = far_side.shape[1] // 2
    even = lax.rem(lax.axis_index("tm"), 2) == 0
    later, earlier = grad[:, bins - width :], grad[:, :width]
    core_edge, far_edge = jnp.where(even, later, earlier), jnp.where(even, earlier, later)
    target = pl.ds(entries * BLK, far_side.shape[0])
    terms[target] = jnp.concatenate(parts(core_edge), axis=1)
    far_side[...] = jnp.concatenate(parts(far_edge), axis=1)


def merge_late_kernel(entries, late, ids, asked, own, got, out, slots, sums, sem):
    blocks = out.shape[0] // BLK

    def each(act):
        def body(e, _):
            for i, (names, terms) in enumerate(((ids, own), (asked, got))):
                core, piece, row = place_of(names, e, blocks, True)

                @pl.when(jnp.logical_and(core, piece == late))
                def _():
                    k = e * 2 + i
                    source = pl.ds(pl.multiple_of(e * BLK, BLK), BLK)
                    act(pltpu.make_async_copy(terms.at[source], slots.at[k], sem.at[k]), k, row)

            return 0

        lax.fori_loop(0, entries, body, 0)

    def start(copy, k, row):
        copy.start()

    def add(copy, k, row):
        copy.wait()
        sums[pl.ds(row, BLK)] += slots[k].astype(F32)

    each(start)
    sums[...] = jnp.zeros_like(sums)
    each(add)
    out[...] = sums[...].astype(out.dtype)


def merge_kernel(entries, late, ids, asked, own, got, *refs):
    outs, sums = refs[:-1], refs[-1]
    chunk = outs[0].shape[0]
    sums[...] = jnp.zeros_like(sums)

    def add(e, _):
        source = pl.ds(pl.multiple_of(e * BLK, BLK), BLK)
        for names, terms in ((ids, own), (asked, got)):
            core, piece, row = place_of(names, e, chunk // BLK, True)
            index = jnp.where(piece < late, piece, piece - 1)

            @pl.when(jnp.logical_and(core, piece != late))
            def _():
                target = pl.ds(pl.multiple_of(index * chunk + row, BLK), BLK)
                sums[target] += terms[source].astype(F32)

        return 0

    lax.fori_loop(0, entries, add, 0)
    for q, out in enumerate(outs):
        out[...] = sums[q * chunk : (q + 1) * chunk].astype(out.dtype)


def local(latents, kernel, loadings, recorded, owner_ids, local_ids, recorded_mask):
    latent_dim, bins = latents.shape
    halfwidth = kernel.shape[1] // 2
    count = lax.axis_size("tm")
    chain = count // ROW
    chunk = loadings.shape[0]
    entries = owner_ids.size
    smem = pl.BlockSpec(memory_space=pltpu.SMEM)

    def permute(x, pairs):
        return lax.ppermute(x, "tm", pairs)

    def rotate(x, r):
        return permute(x, [(i, (i + r * ROW) % count) for i in range(count)])

    def flip(x, bit):
        return permute(x, [(i, i ^ bit) for i in range(count)])

    odd_even = [(i, i + 1) for i in range(1, count - 1, 2)]
    odd_even += [(target, source) for source, target in odd_even]

    ids = owner_ids[0] * (chunk // BLK) + local_ids[0]
    asked = flip(ids, 1)
    mask = jnp.transpose(recorded_mask, (0, 2, 1))

    even = lax.axis_index("tm") % 2 == 0
    later, earlier = latents[:, bins - halfwidth :], latents[:, :halfwidth]
    core_side = flip(jnp.where(even, later, earlier), 1)
    far_side = permute(jnp.where(even, earlier, later), odd_even)

    half = chain // 2
    late = chain + half
    straight = [loadings] * chain
    for r in range(1, half):
        straight[r] = rotate(straight[r - 1], 1)
        straight[-r] = rotate(straight[1 - r], -1)
    across = [flip(loadings, 2)] + [None] * (chain - 1)
    if half > 1:
        straight[1], across[0] = lax.optimization_barrier((straight[1], across[0]))
    straight[half] = rotate(straight[half - 1], 1)
    for r in range(1, chain):
        if r != half:
            across[r] = flip(straight[r], 2)

    length = bins + 2 * halfwidth
    tables = dft_tables(length, bins, 0)
    held = [pltpu.VMEM(t.shape, BF16) for t in tables]
    mxu = latent_dim * length * (length + bins) * 6
    smoothed, spectrum = pl.pallas_call(
        smooth_kernel,
        out_shape=(
            jax.ShapeDtypeStruct((latent_dim, bins), BF16),
            jax.ShapeDtypeStruct((latent_dim, length), F32),
        ),
        in_specs=[VMEM] * 4 + [HBM] * 4,
        out_specs=(VMEM, VMEM),
        scratch_shapes=held + [pltpu.SemaphoreType.DMA((4,))],
        compiler_params=pltpu.CompilerParams(vmem_limit_bytes=VMEM_LIMIT),
        cost_estimate=pl.CostEstimate(flops=mxu, bytes_accessed=6 * 2**20, transcendentals=0),
        name="smooth",
    )(latents, core_side, far_side, kernel, *tables)

    slots = jax.ShapeDtypeStruct((entries * BLK, latent_dim), BF16)
    ids, asked, smoothed, mask = lax.optimization_barrier(
        (ids, asked, smoothed, mask)
    )
    across[half] = flip(straight[half], 2)
    early = straight + across[:half] + across[half + 1 :]
    packed = pl.pallas_call(
        functools.partial(pack_kernel, entries, late),
        out_shape=slots,
        in_specs=[smem] + [HBM] * len(early),
        out_specs=VMEM,
        scratch_shapes=[pltpu.SemaphoreType.DMA((entries,))],
        compiler_params=pltpu.CompilerParams(vmem_limit_bytes=VMEM_LIMIT),
        cost_estimate=pl.CostEstimate(flops=0, bytes_accessed=2 * 2**20, transcendentals=0),
        name="pack",
    )(asked, *early)
    packed = flip(packed, 1)
    late_theirs = flip(across[half], 1)
    pieces = straight + across

    group = 4
    extended = jax.ShapeDtypeStruct((entries * BLK + latent_dim, latent_dim), BF16)
    grad, far_side, terms = pl.pallas_call(
        functools.partial(session_kernel, entries, group, late),
        out_shape=(
            jax.ShapeDtypeStruct((latent_dim, bins), F32),
            jax.ShapeDtypeStruct((latent_dim, 2 * halfwidth), BF16),
            extended,
        ),
        in_specs=[smem] * 2 + [VMEM] * 2 + [HBM] * (2 + len(pieces)),
        out_specs=(VMEM,) * 3,
        scratch_shapes=[
            pltpu.VMEM((entries, BLK, latent_dim), BF16),
            pltpu.VMEM((group * BLK, bins), BF16),
            pltpu.SemaphoreType.DMA((entries,)),
        ],
        compiler_params=pltpu.CompilerParams(vmem_limit_bytes=VMEM_LIMIT),
        cost_estimate=pl.CostEstimate(
            flops=6 * entries * BLK * latent_dim * bins, bytes_accessed=8 * 2**20, transcendentals=0
        ),
        name="session",
    )(
        ids,
        mask,
        smoothed,
        recorded.reshape(entries, BLK, bins),
        packed,
        late_theirs,
        *pieces,
    )

    got = flip(terms, 1)
    far_side = permute(far_side, odd_even)
    narrow = jax.ShapeDtypeStruct((chunk, latent_dim), BF16)
    sent = pl.pallas_call(
        functools.partial(merge_late_kernel, entries, late),
        out_shape=narrow,
        in_specs=[smem] * 2 + [HBM] * 2,
        out_specs=VMEM,
        scratch_shapes=[
            pltpu.VMEM((2 * entries, BLK, latent_dim), BF16),
            pltpu.VMEM((chunk, latent_dim), F32),
            pltpu.SemaphoreType.DMA((2 * entries,)),
        ],
        compiler_params=pltpu.CompilerParams(vmem_limit_bytes=VMEM_LIMIT),
        cost_estimate=pl.CostEstimate(flops=0, bytes_accessed=2**20, transcendentals=0),
        name="merge_late",
    )(ids, asked, terms, got)
    back = flip(sent, 2)
    got, far_side = lax.optimization_barrier((got, far_side))
    wide = jax.ShapeDtypeStruct((chunk, latent_dim), F32)
    out_shape = (wide,) * chain + (narrow,) * (chain - 1)
    sums = pl.pallas_call(
        functools.partial(merge_kernel, entries, late),
        out_shape=out_shape,
        in_specs=[smem] * 2 + [VMEM] * 2,
        out_specs=(VMEM,) * len(out_shape),
        scratch_shapes=[pltpu.VMEM((len(out_shape) * chunk, latent_dim), F32)],
        compiler_params=pltpu.CompilerParams(vmem_limit_bytes=VMEM_LIMIT),
        cost_estimate=pl.CostEstimate(flops=0, bytes_accessed=5 * 2**20, transcendentals=0),
        name="merge",
    )(ids, asked, terms, got)
    other = {half: back}
    for r in sorted(range(chain), key=lambda r: -min(r, chain - r)):
        if r != half:
            other[r] = flip(sums[chain + r - (r > half)], 2)
    totals = [sums[r] + other[r].astype(F32) for r in range(chain)]
    rise = totals[half]
    for r in range(half - 1, -1, -1):
        rise = totals[r] + rotate(rise.astype(BF16), 1).astype(F32)
    loading_grad = rise
    if half > 1:
        fall = totals[half + 1]
        for r in range(half + 2, chain):
            fall = totals[r] + rotate(fall.astype(BF16), -1).astype(F32)
        loading_grad = loading_grad + rotate(fall.astype(BF16), -1).astype(F32)

    tables = dft_tables(length, bins, 2 * halfwidth)
    latent_grad = pl.pallas_call(
        unsmooth_kernel,
        out_shape=jax.ShapeDtypeStruct((latent_dim, bins), F32),
        in_specs=[VMEM, HBM, VMEM, VMEM] + [HBM] * 4,
        out_specs=VMEM,
        scratch_shapes=held
        + [pltpu.VMEM((latent_dim, 2 * halfwidth), BF16), pltpu.SemaphoreType.DMA((5,))],
        compiler_params=pltpu.CompilerParams(vmem_limit_bytes=VMEM_LIMIT),
        cost_estimate=pl.CostEstimate(flops=mxu, bytes_accessed=6 * 2**20, transcendentals=0),
        name="unsmooth",
    )(grad, got, far_side, spectrum, *tables)
    return latent_grad, loading_grad


def solution(mesh):
    return jax.shard_map(
        local,
        mesh=mesh,
        in_specs=(
            P(None, ("groups", "tm")),
            P(),
            P(("groups", "tm"), None),
            P(None, None, None, ("groups", "tm")),
            P(("groups", "tm"), None, None),
            P(("groups", "tm"), None, None),
            P(None, None, ("groups", "tm")),
        ),
        out_specs=(P(None, ("groups", "tm")), P(("groups", "tm"), None)),
        check_vma=False,
    )
```

time: 104 us -> 104 us (level)
  local copies, waits for them, and re-layouts: 14.9 us -> 4.8 us
  Pallas kernels: 25.7 us -> 34.3 us
  starting transfers between devices: 26.4 us -> 31.8 us
  waiting for transfers between devices: 30.5 us -> 27.7 us
    unnamed x55 -> x38, local copies, waits for them, and re-layouts: 11.9 us -> 4.8 us
    ppermute x22 -> x21, starting transfers between devices: 26.4 us -> 31.8 us  [permute(): return lax.ppermute(x, 'tm', pairs)]
    pallas_call x1, Pallas kernels: 3.59 us -> 7.24 us  [local(): pl.pallas_call(smooth_kernel, out_shape=(jax.ShapeDtypeStruct((latent_dim...]
    pallas_call x1, Pallas kernels: 4.1 us -> 7.7 us  [local(): pl.pallas_call(unsmooth_kernel, out_shape=jax.ShapeDtypeStruct((latent_di...]
    ppermute x22 -> x21, waiting for transfers between devices: 30.5 us -> 27.7 us  [permute(): return lax.ppermute(x, 'tm', pairs)]
    reshape x3 -> x0, local copies, waits for them, and re-layouts: 2.09 us -> none  [the longest x2 1.52 us: local(): ids = jnp.concatenate([owner_ids.reshape(-1), local_ids.reshape(-1), me])]
    convert_element_type x1, other arithmetic: 1.25 us -> 0.07 us  [local(): loading_grad = loading_grad + rotate(fall.astype(BF16), -1).astype(F32)]
    pallas_call x2, Pallas kernels: 7.93 us -> 9.05 us  [the longest x1 4.97 us: local(): pl.pallas_call(functools.partial(merge_kernel, entries, late), out_shape=...]
  transfers between devices with their start and end apart: 22 -> 21, of which waited for: 10 -> 7; matrix products, arithmetic and copies ran while one was open for 7% -> 3% of each run, Pallas kernels for 12% -> 19%
where the time goes in v4:
time: 104 us; the launch traced here: 103 us
  Pallas kernels  34.3 us (33%)
  starting transfers between devices  31.8 us (31%)
  waiting for transfers between devices  27.7 us (27%)
  local copies, waits for them, and re-layouts  4.8 us (5%)
  other arithmetic  3.83 us (4%)
    ppermute x21, starting transfers between devices, permute(): return lax.ppermute(x, 'tm', pairs)  31.8 us
    ppermute x21, waiting for transfers between devices, permute(): return lax.ppermute(x, 'tm', pairs)  27.7 us
    pallas_call x1, Pallas kernels, local(): pl.pallas_call(unsmooth_kernel, out_shape=jax.ShapeDtypeStruct((latent_di...  7.7 us
    pallas_call x1, Pallas kernels, local(): pl.pallas_call(smooth_kernel, out_shape=(jax.ShapeDtypeStruct((latent_dim...  7.24 us
    pallas_call x1, Pallas kernels, local(): pl.pallas_call(functools.partial(session_kernel, entries, group, late), o...  6.9 us
    pallas_call x1, Pallas kernels, local(): pl.pallas_call(functools.partial(merge_kernel, entries, late), out_shape=...  4.97 us
    unnamed x38, local copies, waits for them, and re-layouts  4.8 us
    pallas_call x1, Pallas kernels, local(): pl.pallas_call(functools.partial(merge_late_kernel, entries, late), out_s...  4.08 us
  transfers between devices with their start and end apart: 21, of which 7 were waited for; matrix products, arithmetic and copies ran while one was open for 3% of the time, Pallas kernels for 19%

profile of v4, /device:TPU:0, one launch (start us, length us, event | category | flops | bytes accessed | tf_op | source)
XLA Modules:
  0.0 103.3 jit_solution(16288675103502311237)
XLA Ops:
  0.6 3.0 %collective-permute-start.4 = (bf16[512,256]{1,0:T(8,128)(2,1)}, bf16[512,256]{1,0:T(8,128)(2,1)S(1)}, u32[]{:S(2)}, u32[]{:S(2)}) collective-permute-start(bf16[512,256]{1,0:T(8,128)(2,1)} %refs_0_.5), channel_id=1, source_target_pairs={{0,2},{1,3},{2,0},{3,1},{4,6},{5,7},{6,4},{7,5},{8,10},{9,11},{10,... | collective-permute-start | bytes 786440 | tf_op jit(solution)/shard_map/ppermute | solution.py:298
  3.7 1.6 %collective-permute-start.3 = (bf16[512,256]{1,0:T(8,128)(2,1)}, bf16[512,256]{1,0:T(8,128)(2,1)S(1)}, u32[]{:S(2)}, u32[]{:S(2)}) collective-permute-start(bf16[512,256]{1,0:T(8,128)(2,1)} %refs_0_.5), channel_id=1, source_target_pairs={{0,4},{1,5},{2,6},{3,7},{4,8},{5,9},{6,10},{7,11},{8,12},{9,13},{1... | collective-permute-start | bytes 786440 | tf_op jit(solution)/shard_map/ppermute | solution.py:298
  5.2 2.2 %collective-permute-start.6 = (bf16[512,256]{1,0:T(8,128)(2,1)}, bf16[512,256]{1,0:T(8,128)(2,1)S(1)}, u32[]{:S(2)}, u32[]{:S(2)}) collective-permute-start(bf16[512,256]{1,0:T(8,128)(2,1)} %refs_0_.5), channel_id=1, source_target_pairs={{0,12},{1,13},{2,14},{3,15},{4,0},{5,1},{6,2},{7,3},{8,4},{9,5},{1... | collective-permute-start | bytes 786440 | tf_op jit(solution)/shard_map/ppermute | solution.py:298
  7.5 1.0 slice_select_fusion
  8.5 0.7 collective-permute-start.2
  9.2 1.7 %collective-permute-start.1 = (f32[256,128]{1,0:T(8,128)S(1)}, f32[256,128]{1,0:T(8,128)S(1)}, u32[]{:S(2)}, u32[]{:S(2)}) collective-permute-start(f32[256,128]{1,0:T(8,128)S(1)} %get-tuple-element.43), channel_id=1, source_target_pairs={{0,1},{1,0},{2,3},{3,2},{4,5},{5,4},{6,7},{7,6},{8,9},{9,8},{10,11... | collective-permute-start | bytes 393224 | tf_op jit(solution)/shard_map/ppermute | solution.py:298
  10.9 0.0 collective-permute-done.4.refs_4_
  10.9 4.1 %collective-permute-done.3.refs_1_ = bf16[512,256]{1,0:T(8,128)(2,1)S(1)} collective-permute-done((bf16[512,256]{1,0:T(8,128)(2,1)}, bf16[512,256]{1,0:T(8,128)(2,1)S(1)}, u32[]{:S(2)}, u32[]{:S(2)}) %collective-permute-start.3) | collective-permute-done | bytes 262176 | tf_op jit(solution)/shard_map/ppermute | solution.py:298
  14.9 0.3 collective-permute-start.7
  15.2 0.0 collective-permute-start.5
  15.2 4.0 %collective-permute-done.6.refs_3_ = bf16[512,256]{1,0:T(8,128)(2,1)S(1)} collective-permute-done((bf16[512,256]{1,0:T(8,128)(2,1)}, bf16[512,256]{1,0:T(8,128)(2,1)S(1)}, u32[]{:S(2)}, u32[]{:S(2)}) %collective-permute-start.6) | collective-permute-done | bytes 262176 | tf_op jit(solution)/shard_map/ppermute | solution.py:298
  19.3 0.3 collective-permute-start.8
  19.6 0.7 add_bitcast_fusion.ids
  20.3 0.0 collective-permute-done.2.far_side
  20.3 0.1 collective-permute-start
  20.4 0.0 collective-permute-done.1.core_side
  20.4 0.6 copy-done.16
  20.9 0.7 copy-done.17
  21.6 7.2 %smooth.1 = (bf16[256,512]{1,0:T(8,128)(2,1)}, f32[256,768]{1,0:T(8,128)}) custom-call(f32[256,512]{1,0:T(8,128)} %mid.1, f32[256,128]{1,0:T(8,128)} %copy-done.17, f32[256,128]{1,0:T(8,128)} %copy-done.16, f32[256,256]{1,0:T(8,128)} %taps.1, bf16[768,768]{1,0:T(8,128)(2,1)} %constant.32.clone.refs_0_, bf16[768,768]{1,0:T(8,128)(2,1)} %constant.33.clone.refs_1_, ...), custom_call_target="tpu_custom_call" | custom-call | flops 1509949440 | bytes 6291456 | tf_op jit(solution)/shard_map/smooth/pallas_call | solution.py:336
  28.9 0.0 collective-permute-done.asked
  28.9 0.0 collective-permute-done.8.refs_6_.refs_7_
  28.9 0.0 collective-permute-done.7.refs_5_
  28.9 0.0 collective-permute-done.5.refs_2_
  28.9 0.5 copy-done.11
  29.4 0.2 copy-done.9
  29.6 0.1 copy-done.7
  29.7 0.7 copy-done.8
  30.4 3.5 %pack.1 = bf16[2048,256]{1,0:T(8,128)(2,1)} custom-call(s32[2,8]{1,0:T(2,128)} %copy-done.11, bf16[512,256]{1,0:T(8,128)(2,1)} %refs_0_.5, bf16[512,256]{1,0:T(8,128)(2,1)} %copy-done.5, bf16[512,256]{1,0:T(8,128)(2,1)} %copy-done.8, bf16[512,256]{1,0:T(8,128)(2,1)} %copy-done.6, bf16[512,256]{1,0:T(8,128)(2,1)} %copy-done.4, bf16[512,256]{1,0:T(8,128)(2,1)} %copy-done.7, ...), custom_call_target="tpu_custom_call" | custom-call | bytes 2097152 | tf_op jit(solution)/shard_map/pack/pallas_call | solution.py:356
  33.9 0.1 collective-permute-start.9
  33.9 3.5 %collective-permute-start.10 = (bf16[512,256]{1,0:T(8,128)(2,1)}, bf16[512,256]{1,0:T(8,128)(2,1)S(1)}, u32[]{:S(2)}, u32[]{:S(2)}) collective-permute-start(bf16[512,256]{1,0:T(8,128)(2,1)} %copy-done.8), channel_id=1, source_target_pairs={{0,2},{1,3},{2,0},{3,1},{4,6},{5,7},{6,4},{7,5},{8,10},{9,11},{10,... | collective-permute-start | bytes 786440 | tf_op jit(solution)/shard_map/ppermute | solution.py:298
  37.4 6.8 %collective-permute-done.10.refs_6_ = bf16[512,256]{1,0:T(8,128)(2,1)S(1)} collective-permute-done((bf16[512,256]{1,0:T(8,128)(2,1)}, bf16[512,256]{1,0:T(8,128)(2,1)S(1)}, u32[]{:S(2)}, u32[]{:S(2)}) %collective-permute-start.10) | collective-permute-done | bytes 262176 | tf_op jit(solution)/shard_map/ppermute | solution.py:298
  44.2 0.0 collective-permute-start.11
  44.2 1.5 %collective-permute-done.11.late_theirs = bf16[512,256]{1,0:T(8,128)(2,1)S(1)} collective-permute-done((bf16[512,256]{1,0:T(8,128)(2,1)S(1)}, bf16[512,256]{1,0:T(8,128)(2,1)S(1)}, u32[]{:S(2)}, u32[]{:S(2)}) %collective-permute-start.11) | collective-permute-done | bytes 262176 | tf_op jit(solution)/shard_map/ppermute | solution.py:298
  45.7 0.0 collective-permute-done.9.packed
  45.7 0.7 copy-done.15
  46.4 0.4 copy-done.13
  46.8 6.9 %session.1 = (f32[256,512]{1,0:T(8,128)}, bf16[256,256]{1,0:T(8,128)(2,1)}, bf16[2304,256]{1,0:T(8,128)(2,1)}) custom-call(s32[2,8]{1,0:T(2,128)} %copy-done.12, s32[2,4,8]{2,1,0:T(4,128)} %bitcast.5, bf16[256,512]{1,0:T(8,128)(2,1)} %get-tuple-element.25.smoothed, bf16[16,128,512]{2,1,0:T(8,128)(2,1)} %bitcast.4, bf16[2048,256]{1,0:T(8,128)(2,1)} %copy-done.13, ...), custom_call_target="tpu_custom_call" | custom-call | flops 1610612736 | bytes 8388608 | tf_op jit(solution)/shard_map/session/pallas_call | solution.py:372
  53.7 0.2 collective-permute-start.12
  53.9 2.9 %collective-permute-done.12.core_terms.got = bf16[2304,256]{1,0:T(8,128)(2,1)S(1)} collective-permute-done((bf16[2304,256]{1,0:T(8,128)(2,1)}, bf16[2304,256]{1,0:T(8,128)(2,1)S(1)}, u32[]{:S(2)}, u32[]{:S(2)}) %collective-permute-start.12) | collective-permute-done | bytes 1179680 | tf_op jit(solution)/shard_map/ppermute | solution.py:298
  56.8 1.0 copy-done
  57.9 4.1 %merge_late.1 = bf16[512,256]{1,0:T(8,128)(2,1)} custom-call(s32[2,8]{1,0:T(2,128)} %copy-done.12, s32[2,8]{1,0:T(2,128)} %copy-done.11, bf16[2304,256]{1,0:T(8,128)(2,1)} %get-tuple-element.30.own, bf16[2304,256]{1,0:T(8,128)(2,1)} %copy-done), custom_call_target="tpu_custom_call" | custom-call | bytes 1048576 | tf_op jit(solution)/shard_map/merge_late/pallas_call | solution.py:404
  61.9 1.8 %collective-permute-start.16 = (bf16[512,256]{1,0:T(8,128)(2,1)}, bf16[512,256]{1,0:T(8,128)(2,1)S(1)}, u32[]{:S(2)}, u32[]{:S(2)}) collective-permute-start(bf16[512,256]{1,0:T(8,128)(2,1)} %merge_late.1), channel_id=1, source_target_pairs={{0,2},{1,3},{2,0},{3,1},{4,6},{5,7},{6,4},{7,5},{8,10},{9,11},{10,... | collective-permute-start | bytes 786440 | tf_op jit(solution)/shard_map/ppermute | solution.py:298
  63.7 0.7 collective-permute-start.13
  64.4 0.0 collective-permute-done.13.far_side
  64.4 5.0 %merge.1 = (f32[512,256]{1,0:T(8,128)}, f32[512,256]{1,0:T(8,128)}, f32[512,256]{1,0:T(8,128)}, f32[512,256]{1,0:T(8,128)}, bf16[512,256]{1,0:T(8,128)(2,1)}, /*...) custom-call(s32[2,8]{1,0:T(2,128)} %copy-done.12, s32[2,8]{1,0:T(2,128)} %copy-done.11, ...), custom_call_target="tpu_custom_call" | custom-call | bytes 5242880 | tf_op jit(solution)/shard_map/merge/pallas_call | solution.py:422
  69.4 0.0 copy-start.2
  69.4 10.8 %collective-permute-start.19 = (bf16[512,256]{1,0:T(8,128)(2,1)}, bf16[512,256]{1,0:T(8,128)(2,1)S(1)}, u32[]{:S(2)}, u32[]{:S(2)}) collective-permute-start(bf16[512,256]{1,0:T(8,128)(2,1)} %get-tuple-element.41), channel_id=1, source_target_pairs={{0,2},{1,3},{2,0},{3,1},{4,6},{5,7},{6,4},{7,5},{8,10},{9,11},{10,... | collective-permute-start | bytes 786440 | tf_op jit(solution)/shard_map/ppermute | solution.py:298
  80.2 0.1 collective-permute-start.15
  80.3 0.0 collective-permute-done.16
  80.3 1.1 %add_convert_fusion.2 = bf16[512,256]{1,0:T(8,128)(2,1)S(1)} fusion(f32[512,256]{1,0:T(8,128)} %get-tuple-element.39, bf16[512,256]{1,0:T(8,128)(2,1)S(1)} %collective-permute-done.16), kind=kLoop, calls=%fused_computation.3 | loop fusion | flops 393216 | bytes 1048576 | tf_op jit(solution)/shard_map/convert_element_type | solution.py:439
  81.4 1.4 %collective-permute-start.17 = (bf16[512,256]{1,0:T(8,128)(2,1)S(1)}, bf16[512,256]{1,0:T(8,128)(2,1)S(1)}, u32[]{:S(2)}, u32[]{:S(2)}) collective-permute-start(bf16[512,256]{1,0:T(8,128)(2,1)S(1)} %add_convert_fusion.2), channel_id=1, source_target_pairs={{0,4},{1,5},{2,6},{3,7},{4,8},{5,9},{6,10},{7,11},{8,12},{9,13},{1... | collective-permute-start | bytes 786440 | tf_op jit(solution)/shard_map/ppermute | solution.py:298
  82.8 1.9 %collective-permute-start.14 = (bf16[512,256]{1,0:T(8,128)(2,1)}, bf16[512,256]{1,0:T(8,128)(2,1)S(1)}, u32[]{:S(2)}, u32[]{:S(2)}) collective-permute-start(bf16[512,256]{1,0:T(8,128)(2,1)} %get-tuple-element.36), channel_id=1, source_target_pairs={{0,2},{1,3},{2,0},{3,1},{4,6},{5,7},{6,4},{7,5},{8,10},{9,11},{10,... | collective-permute-start | bytes 786440 | tf_op jit(solution)/shard_map/ppermute | solution.py:298
  84.8 2.8 %collective-permute-done.19 = bf16[512,256]{1,0:T(8,128)(2,1)S(1)} collective-permute-done((bf16[512,256]{1,0:T(8,128)(2,1)}, bf16[512,256]{1,0:T(8,128)(2,1)S(1)}, u32[]{:S(2)}, u32[]{:S(2)}) %collective-permute-start.19) | collective-permute-done | bytes 262176 | tf_op jit(solution)/shard_map/ppermute | solution.py:298
  87.6 0.1 add_convert_fusion
  87.7 0.1 collective-permute-start.20
  87.7 5.5 %collective-permute-done.15 = bf16[512,256]{1,0:T(8,128)(2,1)S(1)} collective-permute-done((bf16[512,256]{1,0:T(8,128)(2,1)}, bf16[512,256]{1,0:T(8,128)(2,1)S(1)}, u32[]{:S(2)}, u32[]{:S(2)}) %collective-permute-start.15) | collective-permute-done | bytes 262176 | tf_op jit(solution)/shard_map/ppermute | solution.py:298
  93.2 0.0 collective-permute-done.17
  93.2 0.1 add_convert_fusion.1
  93.3 1.4 %collective-permute-start.18 = (bf16[512,256]{1,0:T(8,128)(2,1)S(1)}, bf16[512,256]{1,0:T(8,128)(2,1)S(1)}, u32[]{:S(2)}, u32[]{:S(2)}) collective-permute-start(bf16[512,256]{1,0:T(8,128)(2,1)S(1)} %add_convert_fusion.1), channel_id=1, source_target_pairs={{0,4},{1,5},{2,6},{3,7},{4,8},{5,9},{6,10},{7,11},{8,12},{9,13},{1... | collective-permute-start | bytes 786440 | tf_op jit(solution)/shard_map/ppermute | solution.py:298
  94.7 7.7 %unsmooth.1 = f32[256,512]{1,0:T(8,128)} custom-call(f32[256,512]{1,0:T(8,128)} %get-tuple-element.29.mid, bf16[2304,256]{1,0:T(8,128)(2,1)} %copy-done, bf16[256,256]{1,0:T(8,128)(2,1)} %copy-done.10, f32[256,768]{1,0:T(8,128)} %get-tuple-element.34.k_spec, bf16[768,768]{1,0:T(8,128)(2,1)} %constant.32.clone.refs_0_, ...), custom_call_target="tpu_custom_call" | custom-call | flops 1509949440 | bytes 6291456 | tf_op jit(solution)/shard_map/unsmooth/pallas_call | solution.py:448
  102.4 0.0 collective-permute-done.14
  102.4 0.0 collective-permute-done.20
  102.4 0.0 collective-permute-done.18
  102.4 0.9 convert_add_fusion
  (28 shorter events, 0.1 us)
Async XLA Ops:
  0.6 10.2 %collective-permute-start.4 = (bf16[512,256]{1,0:T(8,128)(2,1)}, bf16[512,256]{1,0:T(8,128)(2,1)S(1)}, u32[]{:S(2)}, u32[]{:S(2)}) collective-permute-start(bf16[512,256]{1,0:T(8,128)(2,1)} %refs_0_.5), channel_id=1, source_target_pairs={{0,2},{1,3},{2,0},{3,1},{4,6},{5,7},{6,4},{7,5},{8,10},{9,11},{10,... | collective-permute-start | bytes 786440 | tf_op jit(solution)/shard_map/ppermute | solution.py:298
  3.7 11.3 %collective-permute-start.3 = (bf16[512,256]{1,0:T(8,128)(2,1)}, bf16[512,256]{1,0:T(8,128)(2,1)S(1)}, u32[]{:S(2)}, u32[]{:S(2)}) collective-permute-start(bf16[512,256]{1,0:T(8,128)(2,1)} %refs_0_.5), channel_id=1, source_target_pairs={{0,4},{1,5},{2,6},{3,7},{4,8},{5,9},{6,10},{7,11},{8,12},{9,13},{1... | collective-permute-start | bytes 786440 | tf_op jit(solution)/shard_map/ppermute | solution.py:298
  5.2 14.0 %collective-permute-start.6 = (bf16[512,256]{1,0:T(8,128)(2,1)}, bf16[512,256]{1,0:T(8,128)(2,1)S(1)}, u32[]{:S(2)}, u32[]{:S(2)}) collective-permute-start(bf16[512,256]{1,0:T(8,128)(2,1)} %refs_0_.5), channel_id=1, source_target_pairs={{0,12},{1,13},{2,14},{3,15},{4,0},{5,1},{6,2},{7,3},{8,4},{9,5},{1... | collective-permute-start | bytes 786440 | tf_op jit(solution)/shard_map/ppermute | solution.py:298
  8.5 11.8 %collective-permute-start.2 = (f32[256,128]{1,0:T(8,128)S(1)}, f32[256,128]{1,0:T(8,128)S(1)}, u32[]{:S(2)}, u32[]{:S(2)}) collective-permute-start(f32[256,128]{1,0:T(8,128)S(1)} %get-tuple-element.42), channel_id=1, source_target_pairs={{1,2},{3,4},{5,6},{7,8},{9,10},{11,12},{13,14},{2,1},{4,3},{6,5},{... | collective-permute-start | bytes 393224 | tf_op jit(solution)/shard_map/ppermute | solution.py:298
  9.2 11.2 %collective-permute-start.1 = (f32[256,128]{1,0:T(8,128)S(1)}, f32[256,128]{1,0:T(8,128)S(1)}, u32[]{:S(2)}, u32[]{:S(2)}) collective-permute-start(f32[256,128]{1,0:T(8,128)S(1)} %get-tuple-element.43), channel_id=1, source_target_pairs={{0,1},{1,0},{2,3},{3,2},{4,5},{5,4},{6,7},{7,6},{8,9},{9,8},{10,11... | collective-permute-start | bytes 393224 | tf_op jit(solution)/shard_map/ppermute | solution.py:298
  10.9 18.0 %copy-start.4 = (bf16[512,256]{1,0:T(8,128)(2,1)}, bf16[512,256]{1,0:T(8,128)(2,1)S(1)}, u32[]{:S(2)}) copy-start(bf16[512,256]{1,0:T(8,128)(2,1)S(1)} %collective-permute-done.4.refs_4_) | copy-start | bytes 786436
  14.9 13.9 %copy-start.5 = (bf16[512,256]{1,0:T(8,128)(2,1)}, bf16[512,256]{1,0:T(8,128)(2,1)S(1)}, u32[]{:S(2)}) copy-start(bf16[512,256]{1,0:T(8,128)(2,1)S(1)} %collective-permute-done.3.refs_1_) | copy-start | bytes 786436
  14.9 14.0 %collective-permute-start.7 = (bf16[512,256]{1,0:T(8,128)(2,1)S(1)}, bf16[512,256]{1,0:T(8,128)(2,1)S(1)}, u32[]{:S(2)}, u32[]{:S(2)}) collective-permute-start(bf16[512,256]{1,0:T(8,128)(2,1)S(1)} %collective-permute-done.3.refs_1_), channel_id=1, source_target_pairs={{0,2},{1,3},{2,0},{3,1},{4,6},{5,7},{6,4},{7,5},{8,10},{9,11},{10,... | collective-permute-start | bytes 786440 | tf_op jit(solution)/shard_map/ppermute | solution.py:298
  15.2 13.7 %collective-permute-start.5 = (bf16[512,256]{1,0:T(8,128)(2,1)S(1)}, bf16[512,256]{1,0:T(8,128)(2,1)S(1)}, u32[]{:S(2)}, u32[]{:S(2)}) collective-permute-start(bf16[512,256]{1,0:T(8,128)(2,1)S(1)} %collective-permute-done.3.refs_1_), channel_id=1, source_target_pairs={{0,4},{1,5},{2,6},{3,7},{4,8},{5,9},{6,10},{7,11},{8,12},{9,13},{1... | collective-permute-start | bytes 786440 | tf_op jit(solution)/shard_map/ppermute | solution.py:298
  19.3 9.6 %copy-start.6 = (bf16[512,256]{1,0:T(8,128)(2,1)}, bf16[512,256]{1,0:T(8,128)(2,1)S(1)}, u32[]{:S(2)}) copy-start(bf16[512,256]{1,0:T(8,128)(2,1)S(1)} %collective-permute-done.6.refs_3_) | copy-start | bytes 786436
  19.3 9.6 %collective-permute-start.8 = (bf16[512,256]{1,0:T(8,128)(2,1)S(1)}, bf16[512,256]{1,0:T(8,128)(2,1)S(1)}, u32[]{:S(2)}, u32[]{:S(2)}) collective-permute-start(bf16[512,256]{1,0:T(8,128)(2,1)S(1)} %collective-permute-done.6.refs_3_), channel_id=1, source_target_pairs={{0,2},{1,3},{2,0},{3,1},{4,6},{5,7},{6,4},{7,5},{8,10},{9,11},{10,... | collective-permute-start | bytes 786440 | tf_op jit(solution)/shard_map/ppermute | solution.py:298
  20.3 8.6 %copy-start.12 = (s32[2,8]{1,0:T(2,128)}, s32[2,8]{1,0:T(2,128)S(1)}, u32[]{:S(2)}) copy-start(s32[2,8]{1,0:T(2,128)S(1)} %add_bitcast_fusion.ids) | copy-start | bytes 196
  20.3 0.6 copy-start.16
  20.3 8.6 %collective-permute-start = (s32[2,8]{1,0:T(2,128)S(1)}, s32[2,8]{1,0:T(2,128)S(1)}, u32[]{:S(2)}, u32[]{:S(2)}) collective-permute-start(s32[2,8]{1,0:T(2,128)S(1)} %add_bitcast_fusion.ids), channel_id=1, source_target_pairs={{0,1},{1,0},{2,3},{3,2},{4,5},{5,4},{6,7},{7,6},{8,9},{9,8},{10,11... | collective-permute-start | bytes 200 | tf_op jit(solution)/shard_map/ppermute | solution.py:298
  20.9 0.7 copy-start.17
  28.9 0.5 copy-start.11
  28.9 0.7 copy-start.9
  28.9 0.8 copy-start.7
  29.7 0.7 copy-start.8
  33.9 11.9 %collective-permute-start.9 = (bf16[2048,256]{1,0:T(8,128)(2,1)}, bf16[2048,256]{1,0:T(8,128)(2,1)S(1)}, u32[]{:S(2)}, u32[]{:S(2)}) collective-permute-start(bf16[2048,256]{1,0:T(8,128)(2,1)} %pack.1), channel_id=1, source_target_pairs={{0,1},{1,0},{2,3},{3,2},{4,5},{5,4},{6,7},{7,6},{8,9},{9,8},{10,11... | collective-permute-start | bytes 3145736 | tf_op jit(solution)/shard_map/ppermute | solution.py:298
  33.9 10.2 %collective-permute-start.10 = (bf16[512,256]{1,0:T(8,128)(2,1)}, bf16[512,256]{1,0:T(8,128)(2,1)S(1)}, u32[]{:S(2)}, u32[]{:S(2)}) collective-permute-start(bf16[512,256]{1,0:T(8,128)(2,1)} %copy-done.8), channel_id=1, source_target_pairs={{0,2},{1,3},{2,0},{3,1},{4,6},{5,7},{6,4},{7,5},{8,10},{9,11},{10,... | collective-permute-start | bytes 786440 | tf_op jit(solution)/shard_map/ppermute | solution.py:298
  44.2 1.5 %copy-start.14 = (bf16[512,256]{1,0:T(8,128)(2,1)}, bf16[512,256]{1,0:T(8,128)(2,1)S(1)}, u32[]{:S(2)}) copy-start(bf16[512,256]{1,0:T(8,128)(2,1)S(1)} %collective-permute-done.10.refs_6_) | copy-start | bytes 786436
  44.2 1.5 %collective-permute-start.11 = (bf16[512,256]{1,0:T(8,128)(2,1)S(1)}, bf16[512,256]{1,0:T(8,128)(2,1)S(1)}, u32[]{:S(2)}, u32[]{:S(2)}) collective-permute-start(bf16[512,256]{1,0:T(8,128)(2,1)S(1)} %collective-permute-done.10.refs_6_), channel_id=1, source_target_pairs={{0,1},{1,0},{2,3},{3,2},{4,5},{5,4},{6,7},{7,6},{8,9},{9,8},{10,11... | collective-permute-start | bytes 786440 | tf_op jit(solution)/shard_map/ppermute | solution.py:298
  45.7 0.7 copy-start.15
  45.7 1.1 %copy-start.13 = (bf16[2048,256]{1,0:T(8,128)(2,1)}, bf16[2048,256]{1,0:T(8,128)(2,1)S(1)}, u32[]{:S(2)}) copy-start(bf16[2048,256]{1,0:T(8,128)(2,1)S(1)} %collective-permute-done.9.packed) | copy-start | bytes 3145732
  53.7 10.0 %copy-start.18 = (bf16[256,256]{1,0:T(8,128)(2,1)S(1)}, bf16[256,256]{1,0:T(8,128)(2,1)}, u32[]{:S(2)}) copy-start(bf16[256,256]{1,0:T(8,128)(2,1)} %get-tuple-element.31) | copy-start | bytes 393220
  53.7 3.1 %collective-permute-start.12 = (bf16[2304,256]{1,0:T(8,128)(2,1)}, bf16[2304,256]{1,0:T(8,128)(2,1)S(1)}, u32[]{:S(2)}, u32[]{:S(2)}) collective-permute-start(bf16[2304,256]{1,0:T(8,128)(2,1)} %get-tuple-element.30.own), channel_id=1, source_target_pairs={{0,1},{1,0},{2,3},{3,2},{4,5},{5,4},{6,7},{7,6},{8,9},{9,8},{10,11... | collective-permute-start | bytes 3538952 | tf_op jit(solution)/shard_map/ppermute | solution.py:298
  56.8 1.0 copy-start
  61.9 18.3 %collective-permute-start.16 = (bf16[512,256]{1,0:T(8,128)(2,1)}, bf16[512,256]{1,0:T(8,128)(2,1)S(1)}, u32[]{:S(2)}, u32[]{:S(2)}) collective-permute-start(bf16[512,256]{1,0:T(8,128)(2,1)} %merge_late.1), channel_id=1, source_target_pairs={{0,2},{1,3},{2,0},{3,1},{4,6},{5,7},{6,4},{7,5},{8,10},{9,11},{10,... | collective-permute-start | bytes 786440 | tf_op jit(solution)/shard_map/ppermute | solution.py:298
  63.7 0.7 collective-permute-start.13
  64.4 5.0 %copy-start.10 = (bf16[256,256]{1,0:T(8,128)(2,1)}, bf16[256,256]{1,0:T(8,128)(2,1)S(1)}, u32[]{:S(2)}) copy-start(bf16[256,256]{1,0:T(8,128)(2,1)S(1)} %collective-permute-done.13.far_side) | copy-start | bytes 393220
  69.4 18.2 %copy-start.3 = (f32[512,256]{1,0:T(8,128)S(1)}, f32[512,256]{1,0:T(8,128)}, u32[]{:S(2)}) copy-start(f32[512,256]{1,0:T(8,128)} %get-tuple-element.40) | copy-start | bytes 1572868
  69.4 23.8 %copy-start.2 = (f32[512,256]{1,0:T(8,128)S(1)}, f32[512,256]{1,0:T(8,128)}, u32[]{:S(2)}) copy-start(f32[512,256]{1,0:T(8,128)} %get-tuple-element.37) | copy-start | bytes 1572868
  69.4 18.2 %collective-permute-start.19 = (bf16[512,256]{1,0:T(8,128)(2,1)}, bf16[512,256]{1,0:T(8,128)(2,1)S(1)}, u32[]{:S(2)}, u32[]{:S(2)}) collective-permute-start(bf16[512,256]{1,0:T(8,128)(2,1)} %get-tuple-element.41), channel_id=1, source_target_pairs={{0,2},{1,3},{2,0},{3,1},{4,6},{5,7},{6,4},{7,5},{8,10},{9,11},{10,... | collective-permute-start | bytes 786440 | tf_op jit(solution)/shard_map/ppermute | solution.py:298
  80.2 13.0 %collective-permute-start.15 = (bf16[512,256]{1,0:T(8,128)(2,1)}, bf16[512,256]{1,0:T(8,128)(2,1)S(1)}, u32[]{:S(2)}, u32[]{:S(2)}) collective-permute-start(bf16[512,256]{1,0:T(8,128)(2,1)} %get-tuple-element.38), channel_id=1, source_target_pairs={{0,2},{1,3},{2,0},{3,1},{4,6},{5,7},{6,4},{7,5},{8,10},{9,11},{10,... | collective-permute-start | bytes 786440 | tf_op jit(solution)/shard_map/ppermute | solution.py:298
  81.4 11.9 %collective-permute-start.17 = (bf16[512,256]{1,0:T(8,128)(2,1)S(1)}, bf16[512,256]{1,0:T(8,128)(2,1)S(1)}, u32[]{:S(2)}, u32[]{:S(2)}) collective-permute-start(bf16[512,256]{1,0:T(8,128)(2,1)S(1)} %add_convert_fusion.2), channel_id=1, source_target_pairs={{0,4},{1,5},{2,6},{3,7},{4,8},{5,9},{6,10},{7,11},{8,12},{9,13},{1... | collective-permute-start | bytes 786440 | tf_op jit(solution)/shard_map/ppermute | solution.py:298
  82.8 19.6 %collective-permute-start.14 = (bf16[512,256]{1,0:T(8,128)(2,1)}, bf16[512,256]{1,0:T(8,128)(2,1)S(1)}, u32[]{:S(2)}, u32[]{:S(2)}) collective-permute-start(bf16[512,256]{1,0:T(8,128)(2,1)} %get-tuple-element.36), channel_id=1, source_target_pairs={{0,2},{1,3},{2,0},{3,1},{4,6},{5,7},{6,4},{7,5},{8,10},{9,11},{10,... | collective-permute-start | bytes 786440 | tf_op jit(solution)/shard_map/ppermute | solution.py:298
  87.7 14.7 %collective-permute-start.20 = (bf16[512,256]{1,0:T(8,128)(2,1)S(1)}, bf16[512,256]{1,0:T(8,128)(2,1)S(1)}, u32[]{:S(2)}, u32[]{:S(2)}) collective-permute-start(bf16[512,256]{1,0:T(8,128)(2,1)S(1)} %add_convert_fusion), channel_id=1, source_target_pairs={{0,12},{1,13},{2,14},{3,15},{4,0},{5,1},{6,2},{7,3},{8,4},{9,5},{1... | collective-permute-start | bytes 786440 | tf_op jit(solution)/shard_map/ppermute | solution.py:298
  93.3 9.1 %collective-permute-start.18 = (bf16[512,256]{1,0:T(8,128)(2,1)S(1)}, bf16[512,256]{1,0:T(8,128)(2,1)S(1)}, u32[]{:S(2)}, u32[]{:S(2)}) collective-permute-start(bf16[512,256]{1,0:T(8,128)(2,1)S(1)} %add_convert_fusion.1), channel_id=1, source_target_pairs={{0,4},{1,5},{2,6},{3,7},{4,8},{5,9},{6,10},{7,11},{8,12},{9,13},{1... | collective-permute-start | bytes 786440 | tf_op jit(solution)/shard_map/ppermute | solution.py:298
  94.7 7.7 %copy-start.1 = (f32[512,256]{1,0:T(8,128)S(1)}, f32[512,256]{1,0:T(8,128)}, u32[]{:S(2)}) copy-start(f32[512,256]{1,0:T(8,128)} %get-tuple-element.35) | copy-start | bytes 1572868

commit v5 on v4

v5 whole, which is shorter than its diff:
```python
import functools

import jax
import jax.numpy as jnp
import numpy as np
from jax import lax
from jax.experimental import pallas as pl
from jax.experimental.pallas import tpu as pltpu
from jax.sharding import PartitionSpec as P

BLK = 128
ROW = 4
MIB = 2**20
F32 = jnp.float32
BF16 = jnp.bfloat16
VMEM = pl.BlockSpec(memory_space=pltpu.VMEM)
HBM = pl.BlockSpec(memory_space=pltpu.HBM)


def split_const(a):
    high = a.astype(jnp.bfloat16)
    low = (a - high.astype(np.float64)).astype(jnp.bfloat16)
    return high, low


@functools.lru_cache(maxsize=None)
def dft_tables(size):
    t = np.arange(size)[:, None]
    g = np.arange(size)[None, :]
    half = size // 2
    angle = 2 * np.pi * ((t * g[:, :half]) % size) / size
    cos, sin = np.cos(angle), np.sin(angle)
    sin[:, 0] = 1 - 2 * (np.arange(size) % 2)
    real = np.concatenate([cos, sin], axis=1)
    angle = 2 * np.pi * ((t * (3 * g + 1)) % (3 * size)) / (3 * size)
    cos, sin = np.cos(angle), np.sin(angle)
    weight = np.full((size,), 2.0)
    weight[0] = weight[half] = 1.0
    scale = 1.0 / (3 * size)
    tables = [real, cos, sin, (real * weight).T * scale, cos.T * 2 * scale, sin.T * 2 * scale]
    return np.concatenate([part for table in tables for part in split_const(table)])


def parts(a):
    high = a.astype(BF16)
    return high, (a - high.astype(F32)).astype(BF16)


def times(a, tables, index):
    rows, size = a.shape
    high, low = parts(a)
    t_high = tables[2 * index * size : (2 * index + 1) * size]
    t_low = tables[(2 * index + 1) * size : (2 * index + 2) * size]
    out = jnp.dot(jnp.concatenate([high, low]), t_high, preferred_element_type=F32)
    return out[:rows] + out[rows:] + jnp.dot(high, t_low, preferred_element_type=F32)


ROOT = 0.75**0.5


def spectrum_of(thirds, tables):
    first, second, third = thirds
    rows = first.shape[0]
    base = times(first + second + third, tables, 0)
    y = jnp.concatenate([first - 0.5 * (second + third), ROOT * (third - second)])
    cos, sin = times(y, tables, 1), times(y, tables, 2)
    return base, cos[:rows] + sin[rows:], cos[rows:] - sin[:rows]


def filtered(signal, taps, sign, tables, wanted):
    (xb, xr, xi), (kb, kr, ki) = signal, taps
    rows, size = xb.shape
    half = size // 2
    first = lax.broadcasted_iota(jnp.int32, (rows, half), 1) == 0
    kc, ks = kb[:, :half], kb[:, half:]
    kc_s = jnp.where(first, ks, kc)
    ks_x = jnp.where(first, 0.0, ks) * sign
    xc, xs = xb[:, :half], xb[:, half:]
    base = times(jnp.concatenate([xc * kc + xs * ks_x, xs * kc_s - xc * ks_x], axis=1), tables, 3)
    ki = ki * sign
    z = jnp.concatenate([xr * kr + xi * ki, xi * kr - xr * ki])
    cos, sin = times(z, tables, 4), times(z, tables, 5)
    vr, vi = cos[:rows] - sin[rows:], sin[:rows] + cos[rows:]
    each = (base + vr, base - 0.5 * vr - ROOT * vi, base - 0.5 * vr + ROOT * vi)
    return jnp.concatenate([each[m] for m in wanted], axis=1)


def thirds_of(mid, core_side, far_side):
    width = core_side.shape[1]
    size = 2 * width
    even = lax.rem(lax.axis_index("tm"), 2) == 0
    low, high = jnp.where(even, far_side, core_side), jnp.where(even, core_side, far_side)
    last = mid.shape[1] - width
    return (
        jnp.concatenate([low, mid[:, :width]], axis=1),
        mid[:, width : width + size],
        jnp.concatenate([mid[:, last:], high], axis=1),
    )


def smooth_kernel(mid, core_side, far_side, taps, table, out, *refs):
    spectrum, held, sem = refs[:3], refs[3], refs[4]
    copy = pltpu.make_async_copy(table, held, sem)
    copy.start()
    thirds = thirds_of(mid[...], core_side[...], far_side[...])
    copy.wait()
    base = times(taps[...], held, 0)
    kr, ki = times(taps[...], held, 1), -times(taps[...], held, 2)
    for ref, value in zip(spectrum, (base, kr, ki)):
        ref[...] = value
    signal = spectrum_of(thirds, held)
    out[...] = filtered(signal, (base, kr, ki), 1.0, held, (0, 1)).astype(out.dtype)


def unsmooth_kernel(mid, core_side, far_side, base, kr, ki, table, out, held, sem):
    copy = pltpu.make_async_copy(table, held, sem)
    copy.start()
    width = far_side.shape[1] // 2
    first = core_side.shape[0] - far_side.shape[0]
    core = core_side[first:, :width].astype(F32) + core_side[first:, width:].astype(F32)
    far = far_side[:, :width].astype(F32) + far_side[:, width:].astype(F32)
    thirds = thirds_of(mid[...], core, far)
    copy.wait()
    signal = spectrum_of(thirds, held)
    out[...] = filtered(signal, (base[...], kr[...], ki[...]), -1.0, held, (1, 2))


def divide(a, n):
    return a >> (n.bit_length() - 1) if n & (n - 1) == 0 else a // n


def remainder(a, n):
    return a & (n - 1) if n & (n - 1) == 0 else a % n


def place_of(ids, e, me, blocks, forward):
    chain = lax.axis_size("tm") // ROW
    top = ids.shape[1]
    code = ids[divide(e, top), remainder(e, top)]
    owner, slot = divide(code, blocks), remainder(code, blocks)
    step = divide(owner, ROW) - divide(me, ROW)
    step = step if forward else -step
    turn = jnp.where(step < 0, step + chain, step)
    differ = owner ^ me
    piece = jnp.where(differ & 2 == 0, 0, chain) + turn
    return differ & 1 == 0, piece, pl.multiple_of(slot * BLK, BLK)


def pick(refs, index, act):
    if len(refs) == 1:
        act(refs[0])
        return
    half = len(refs) // 2
    lax.cond(
        index < half,
        lambda: pick(refs[:half], index, act),
        lambda: pick(refs[half:], index - half, act),
    )


def pack_kernel(entries, late, asked, *refs):
    pieces, out = refs[:-1], refs[-1]
    blocks = pieces[0].shape[0] // BLK
    me = lax.axis_index("tm")

    def body(e, _):
        core, piece, row = place_of(asked, e, me, blocks, False)
        target = pl.ds(pl.multiple_of(e * BLK, BLK), BLK)

        @pl.when(jnp.logical_and(core, piece != late))
        def _():
            def act(ref):
                out[target] = ref[pl.ds(row, BLK)]

            pick(pieces, jnp.where(piece < late, piece, piece - 1), act)

        return 0

    lax.fori_loop(0, entries, body, 0)


def session_kernel(
    entries, group, late, ids, mask, smoothed, recorded, packed, late_theirs, *refs
):
    pieces = refs[:-5]
    grad, far_side, terms, rows, resid = refs[-5:]
    blocks = pieces[0].shape[0] // BLK
    bins = smoothed.shape[1]
    top = ids.shape[1]
    me = lax.axis_index("tm")
    grad[...] = jnp.zeros_like(grad)
    depth = group * BLK

    def step(g, _):
        for i in range(group):
            e = g * group + i
            core, piece, row = place_of(ids, e, me, blocks, False)

            def own():
                def act(ref):
                    rows[i * BLK : (i + 1) * BLK] = ref[pl.ds(row, BLK)]

                pick(pieces, piece, act)

            def other():
                @pl.when(piece == late)
                def _():
                    rows[i * BLK : (i + 1) * BLK] = late_theirs[pl.ds(row, BLK)]

                @pl.when(piece != late)
                def _():
                    source = pl.ds(pl.multiple_of(e * BLK, BLK), BLK)
                    rows[i * BLK : (i + 1) * BLK] = packed[source]

            lax.cond(core, own, other)
        block = rows[...]
        predicted = jnp.dot(block, smoothed[...], preferred_element_type=F32)
        for i in range(group):
            e = g * group + i
            for t in range(bins // BLK):
                cut = slice(t * BLK, (t + 1) * BLK)
                weight = mask[divide(e, top), t, remainder(e, top)].astype(F32)
                part = predicted[i * BLK : (i + 1) * BLK, cut]
                seen = recorded[e, :, cut].astype(F32)
                resid[i * BLK : (i + 1) * BLK, cut] = (weight * (part - seen)).astype(BF16)
        term = lax.dot_general(
            resid[...], smoothed[...], (((1,), (1,)), ((), ())), preferred_element_type=F32
        )
        target = pl.ds(pl.multiple_of(g * depth, depth), depth)
        terms[target] = (term * (1.0 / BLK)).astype(BF16)
        grad[...] += lax.dot_general(
            block, resid[...], (((0,), (0,)), ((), ())), preferred_element_type=F32
        ) * (1.0 / BLK)
        return 0

    lax.fori_loop(0, entries // group, step, 0)
    width = far_side.shape[1] // 2
    even = me & 1 == 0
    later, earlier = grad[:, bins - width :], grad[:, :width]
    core_edge, far_edge = jnp.where(even, later, earlier), jnp.where(even, earlier, later)
    target = pl.ds(entries * BLK, far_side.shape[0])
    terms[target] = jnp.concatenate(parts(core_edge), axis=1)
    far_side[...] = jnp.concatenate(parts(far_edge), axis=1)


def merge_late_kernel(entries, late, ids, asked, own, got, out, sums):
    blocks = out.shape[0] // BLK
    me = lax.axis_index("tm")
    sums[...] = jnp.zeros_like(sums)

    def add(e, _):
        source = pl.ds(pl.multiple_of(e * BLK, BLK), BLK)
        for names, terms in ((ids, own), (asked, got)):
            core, piece, row = place_of(names, e, me, blocks, True)

            @pl.when(jnp.logical_and(core, piece == late))
            def _():
                sums[pl.ds(row, BLK)] += terms[source].astype(F32)

        return 0

    lax.fori_loop(0, entries, add, 0)
    out[...] = sums[...].astype(out.dtype)


def merge_kernel(entries, late, ids, asked, own, got, *refs):
    chain = len(refs) // 2
    kept, outs, sums = refs[:chain], refs[chain:-1], refs[-1]
    chunk = kept[0].shape[0]
    me = lax.axis_index("tm")
    for ref in kept:
        ref[...] = jnp.zeros_like(ref)
    sums[...] = jnp.zeros_like(sums)

    def add(e, _):
        source = pl.ds(pl.multiple_of(e * BLK, BLK), BLK)
        for names, terms in ((ids, own), (asked, got)):
            core, piece, row = place_of(names, e, me, chunk // BLK, True)
            index = jnp.where(piece < late, piece - chain, piece - 1 - chain)

            @pl.when(jnp.logical_and(core, piece < chain))
            def _():
                def act(ref):
                    ref[pl.ds(row, BLK)] += terms[source].astype(F32)

                pick(kept, piece, act)

            @pl.when(jnp.logical_and(core, jnp.logical_and(piece >= chain, piece != late)))
            def _():
                sums[pl.ds(pl.multiple_of(index * chunk + row, BLK), BLK)] += terms[source].astype(F32)

        return 0

    lax.fori_loop(0, entries, add, 0)
    for q, out in enumerate(outs):
        out[...] = sums[q * chunk : (q + 1) * chunk].astype(out.dtype)


def local(latents, kernel, loadings, recorded, owner_ids, local_ids, recorded_mask):
    latent_dim, bins = latents.shape
    halfwidth = kernel.shape[1] // 2
    count = lax.axis_size("tm")
    chain = count // ROW
    chunk = loadings.shape[0]
    entries = owner_ids.size
    piece_bytes = count * chunk * latent_dim
    smem = pl.BlockSpec(memory_space=pltpu.SMEM)

    def permute(x, pairs):
        return lax.ppermute(x, "tm", pairs)

    def rotate(x, r):
        return permute(x, [(i, (i + r * ROW) % count) for i in range(count)])

    def flip(x, bit):
        return permute(x, [(i, i ^ bit) for i in range(count)])

    odd_even = [(i, i + 1) for i in range(1, count - 1, 2)]
    odd_even += [(target, source) for source, target in odd_even]

    ids = owner_ids[0] * (chunk // BLK) + local_ids[0]
    asked = flip(ids, 1)
    mask = jnp.transpose(recorded_mask, (0, 2, 1))

    even = lax.axis_index("tm") % 2 == 0
    later, earlier = latents[:, bins - halfwidth :], latents[:, :halfwidth]
    core_side = flip(jnp.where(even, later, earlier), 1)
    far_side = permute(jnp.where(even, earlier, later), odd_even)

    half = chain // 2
    late = chain + half
    straight = [loadings] * chain
    for r in range(1, half):
        straight[r] = rotate(straight[r - 1], 1)
        straight[-r] = rotate(straight[1 - r], -1)
    across = [flip(loadings, 2)] + [None] * (chain - 1)
    if half > 1:
        straight[1], across[0] = lax.optimization_barrier((straight[1], across[0]))
    straight[half] = rotate(straight[half - 1], 1)
    for r in range(1, chain):
        if r != half:
            across[r] = flip(straight[r], 2)

    table = dft_tables(2 * halfwidth)
    table_scratch = [pltpu.VMEM(table.shape, BF16), pltpu.SemaphoreType.DMA(())]
    mxu = 40 * 2 * latent_dim * (2 * halfwidth) ** 2
    square = jax.ShapeDtypeStruct((latent_dim, 2 * halfwidth), F32)
    smoothed, *spectrum = pl.pallas_call(
        smooth_kernel,
        out_shape=(jax.ShapeDtypeStruct((latent_dim, bins), BF16),) + (square,) * 3,
        in_specs=[VMEM] * 4 + [HBM],
        out_specs=(VMEM,) * 4,
        scratch_shapes=table_scratch,
        compiler_params=pltpu.CompilerParams(vmem_limit_bytes=16 * MIB),
        cost_estimate=pl.CostEstimate(flops=mxu, bytes_accessed=4 * 2**20, transcendentals=0),
        name="smooth",
    )(latents, core_side, far_side, kernel, table)

    slots = jax.ShapeDtypeStruct((entries * BLK, latent_dim), BF16)
    ids, asked, smoothed, mask = lax.optimization_barrier(
        (ids, asked, smoothed, mask)
    )
    across[half] = flip(straight[half], 2)
    early = straight + across[:half] + across[half + 1 :]
    packed = pl.pallas_call(
        functools.partial(pack_kernel, entries, late),
        out_shape=slots,
        in_specs=[smem] + [VMEM] * len(early),
        out_specs=VMEM,
        compiler_params=pltpu.CompilerParams(vmem_limit_bytes=4 * MIB + 3 * piece_bytes),
        cost_estimate=pl.CostEstimate(flops=0, bytes_accessed=2 * 2**20, transcendentals=0),
        name="pack",
    )(asked, *early)
    packed = flip(packed, 1)
    late_theirs = flip(across[half], 1)
    pieces = straight + across

    group = 4
    extended = jax.ShapeDtypeStruct((entries * BLK + latent_dim, latent_dim), BF16)
    grad, far_side, terms = pl.pallas_call(
        functools.partial(session_kernel, entries, group, late),
        out_shape=(
            jax.ShapeDtypeStruct((latent_dim, bins), F32),
            jax.ShapeDtypeStruct((latent_dim, 2 * halfwidth), BF16),
            extended,
        ),
        in_specs=[smem] * 2 + [VMEM] * (4 + len(pieces)),
        out_specs=(VMEM,) * 3,
        scratch_shapes=[
            pltpu.VMEM((group * BLK, latent_dim), BF16),
            pltpu.VMEM((group * BLK, bins), BF16),
        ],
        compiler_params=pltpu.CompilerParams(vmem_limit_bytes=12 * MIB + 6 * piece_bytes),
        cost_estimate=pl.CostEstimate(
            flops=6 * entries * BLK * latent_dim * bins, bytes_accessed=8 * 2**20, transcendentals=0
        ),
        name="session",
    )(
        ids,
        mask,
        smoothed,
        recorded.reshape(entries, BLK, bins),
        packed,
        late_theirs,
        *pieces,
    )

    got = flip(terms, 1)
    narrow = jax.ShapeDtypeStruct((chunk, latent_dim), BF16)
    sent = pl.pallas_call(
        functools.partial(merge_late_kernel, entries, late),
        out_shape=narrow,
        in_specs=[smem] * 2 + [VMEM] * 2,
        out_specs=VMEM,
        scratch_shapes=[pltpu.VMEM((chunk, latent_dim), F32)],
        compiler_params=pltpu.CompilerParams(vmem_limit_bytes=4 * MIB + 3 * piece_bytes),
        cost_estimate=pl.CostEstimate(flops=0, bytes_accessed=2**20, transcendentals=0),
        name="merge_late",
    )(ids, asked, terms, got)
    back = flip(sent, 2)
    far_side, back = lax.optimization_barrier((far_side, back))
    far_side = permute(far_side, odd_even)
    wide = jax.ShapeDtypeStruct((chunk, latent_dim), F32)
    merged = pl.pallas_call(
        functools.partial(merge_kernel, entries, late),
        out_shape=(wide,) * chain + (narrow,) * (chain - 1),
        in_specs=[smem] * 2 + [VMEM] * 2,
        out_specs=(VMEM,) * (2 * chain - 1),
        scratch_shapes=[pltpu.VMEM(((chain - 1) * chunk, latent_dim), F32)],
        compiler_params=pltpu.CompilerParams(vmem_limit_bytes=4 * MIB + 6 * piece_bytes),
        cost_estimate=pl.CostEstimate(flops=0, bytes_accessed=5 * 2**20, transcendentals=0),
        name="merge",
    )(ids, asked, terms, got)
    other = {half: back}
    for r in sorted(range(chain), key=lambda r: -min(r, chain - r)):
        if r != half:
            other[r] = flip(merged[chain + r - (r > half)], 2)
    totals = [merged[r] + other[r].astype(F32) for r in range(chain)]
    rise = totals[half]
    for r in range(half - 1, -1, -1):
        rise = totals[r] + rotate(rise.astype(BF16), 1).astype(F32)
    loading_grad = rise
    if half > 1:
        fall = totals[half + 1]
        for r in range(half + 2, chain):
            fall = totals[r] + rotate(fall.astype(BF16), -1).astype(F32)
        loading_grad = loading_grad + rotate(fall.astype(BF16), -1).astype(F32)

    latent_grad = pl.pallas_call(
        unsmooth_kernel,
        out_shape=jax.ShapeDtypeStruct((latent_dim, bins), F32),
        in_specs=[VMEM] * 6 + [HBM],
        out_specs=VMEM,
        scratch_shapes=table_scratch,
        compiler_params=pltpu.CompilerParams(vmem_limit_bytes=16 * MIB),
        cost_estimate=pl.CostEstimate(flops=mxu, bytes_accessed=4 * 2**20, transcendentals=0),
        name="unsmooth",
    )(grad, got, far_side, *spectrum, table)
    return latent_grad, loading_grad


def solution(mesh):
    return jax.shard_map(
        local,
        mesh=mesh,
        in_specs=(
            P(None, ("groups", "tm")),
            P(),
            P(("groups", "tm"), None),
            P(None, None, None, ("groups", "tm")),
            P(("groups", "tm"), None, None),
            P(("groups", "tm"), None, None),
            P(None, None, ("groups", "tm")),
        ),
        out_specs=(P(None, ("groups", "tm")), P(("groups", "tm"), None)),
        check_vma=False,
    )
```

time: 104 us -> 85.1 us (0.82)
  the two profiles are of different devices: /device:TPU:0 before, /device:TPU:18 now
where the time goes in v5:
time: 85.1 us; the launch traced here: 84.8 us
  waiting for transfers between devices  42.4 us (50%)
  starting transfers between devices  22 us (26%)
  Pallas kernels  13.4 us (16%)
  local copies, waits for them, and re-layouts  3.41 us (4%)
  other arithmetic  2.79 us (3%)
    ppermute x21, waiting for transfers between devices, permute(): return lax.ppermute(x, 'tm', pairs)  42.4 us
    ppermute x21, starting transfers between devices, permute(): return lax.ppermute(x, 'tm', pairs)  22 us
    pallas_call x1, Pallas kernels, local(): pl.pallas_call(functools.partial(session_kernel, entries, group, late), o...  3.95 us
    unnamed x14, local copies, waits for them, and re-layouts  3.41 us
    pallas_call x1, Pallas kernels, local(): pl.pallas_call(unsmooth_kernel, out_shape=jax.ShapeDtypeStruct((latent_di...  2.69 us
    pallas_call x1, Pallas kernels, local(): pl.pallas_call(smooth_kernel, out_shape=(jax.ShapeDtypeStruct((latent_dim...  2.56 us
    pallas_call x1, Pallas kernels, local(): pl.pallas_call(functools.partial(merge_kernel, entries, late), out_shape=...  1.91 us
  transfers between devices with their start and end apart: 21, of which 9 were waited for; matrix products, arithmetic and copies ran while one was open for 2% of the time, Pallas kernels for 8%

profile of v5, /device:TPU:18, one launch (start us, length us, event | category | flops | bytes accessed | tf_op | source)
XLA Modules:
  0.0 84.8 jit_solution(12474275609143266418)
XLA Ops:
  0.6 1.6 %collective-permute-start.4 = (bf16[512,256]{1,0:T(8,128)(2,1)}, bf16[512,256]{1,0:T(8,128)(2,1)S(1)}, u32[]{:S(2)}, u32[]{:S(2)}) collective-permute-start(bf16[512,256]{1,0:T(8,128)(2,1)} %refs_0_.3), channel_id=1, source_target_pairs={{0,2},{1,3},{2,0},{3,1},{4,6},{5,7},{6,4},{7,5},{8,10},{9,11},{10,... | collective-permute-start | bytes 786440 | tf_op jit(solution)/shard_map/ppermute | solution.py:310
  2.2 1.6 %collective-permute-start.3 = (bf16[512,256]{1,0:T(8,128)(2,1)}, bf16[512,256]{1,0:T(8,128)(2,1)S(1)}, u32[]{:S(2)}, u32[]{:S(2)}) collective-permute-start(bf16[512,256]{1,0:T(8,128)(2,1)} %refs_0_.3), channel_id=1, source_target_pairs={{0,4},{1,5},{2,6},{3,7},{4,8},{5,9},{6,10},{7,11},{8,12},{9,13},{1... | collective-permute-start | bytes 786440 | tf_op jit(solution)/shard_map/ppermute | solution.py:310
  3.8 0.4 collective-permute-start.6
  4.2 1.0 %slice_select_fusion = (f32[256,128]{1,0:T(8,128)S(1)}, f32[256,128]{1,0:T(8,128)S(1)}) fusion(f32[256,512]{1,0:T(8,128)} %mid.1, pred[]{:T(512)S(6)} %eq.5), kind=kLoop, calls=%fused_computation.4 | loop fusion | flops 65536 | bytes 524289 | tf_op jit(solution)/shard_map/jit(_where)/select_n | solution.py:328
  5.2 1.9 %collective-permute-start.2 = (f32[256,128]{1,0:T(8,128)S(1)}, f32[256,128]{1,0:T(8,128)S(1)}, u32[]{:S(2)}, u32[]{:S(2)}) collective-permute-start(f32[256,128]{1,0:T(8,128)S(1)} %get-tuple-element.46), channel_id=1, source_target_pairs={{1,2},{3,4},{5,6},{7,8},{9,10},{11,12},{13,14},{2,1},{4,3},{6,5},{... | collective-permute-start | bytes 393224 | tf_op jit(solution)/shard_map/ppermute | solution.py:310
  7.2 0.7 collective-permute-start.1
  7.8 1.1 %collective-permute-done.4.refs_4_ = bf16[512,256]{1,0:T(8,128)(2,1)S(1)} collective-permute-done((bf16[512,256]{1,0:T(8,128)(2,1)}, bf16[512,256]{1,0:T(8,128)(2,1)S(1)}, u32[]{:S(2)}, u32[]{:S(2)}) %collective-permute-start.4) | collective-permute-done | bytes 262176 | tf_op jit(solution)/shard_map/ppermute | solution.py:310
  9.0 5.4 %collective-permute-done.3.refs_1_ = bf16[512,256]{1,0:T(8,128)(2,1)S(1)} collective-permute-done((bf16[512,256]{1,0:T(8,128)(2,1)}, bf16[512,256]{1,0:T(8,128)(2,1)S(1)}, u32[]{:S(2)}, u32[]{:S(2)}) %collective-permute-start.3) | collective-permute-done | bytes 262176 | tf_op jit(solution)/shard_map/ppermute | solution.py:310
  14.4 1.1 %collective-permute-start.7 = (bf16[512,256]{1,0:T(8,128)(2,1)S(1)}, bf16[512,256]{1,0:T(8,128)(2,1)S(1)}, u32[]{:S(2)}, u32[]{:S(2)}) collective-permute-start(bf16[512,256]{1,0:T(8,128)(2,1)S(1)} %collective-permute-done.3.refs_1_), channel_id=1, source_target_pairs={{0,2},{1,3},{2,0},{3,1},{4,6},{5,7},{6,4},{7,5},{8,10},{9,11},{10,... | collective-permute-start | bytes 786440 | tf_op jit(solution)/shard_map/ppermute | solution.py:310
  15.5 1.8 %collective-permute-start.5 = (bf16[512,256]{1,0:T(8,128)(2,1)S(1)}, bf16[512,256]{1,0:T(8,128)(2,1)S(1)}, u32[]{:S(2)}, u32[]{:S(2)}) collective-permute-start(bf16[512,256]{1,0:T(8,128)(2,1)S(1)} %collective-permute-done.3.refs_1_), channel_id=1, source_target_pairs={{0,4},{1,5},{2,6},{3,7},{4,8},{5,9},{6,10},{7,11},{8,12},{9,13},{1... | collective-permute-start | bytes 786440 | tf_op jit(solution)/shard_map/ppermute | solution.py:310
  17.3 0.0 collective-permute-done.6.refs_3_
  17.3 0.9 %collective-permute-start.8 = (bf16[512,256]{1,0:T(8,128)(2,1)S(1)}, bf16[512,256]{1,0:T(8,128)(2,1)S(1)}, u32[]{:S(2)}, u32[]{:S(2)}) collective-permute-start(bf16[512,256]{1,0:T(8,128)(2,1)S(1)} %collective-permute-done.6.refs_3_), channel_id=1, source_target_pairs={{0,2},{1,3},{2,0},{3,1},{4,6},{5,7},{6,4},{7,5},{8,10},{9,11},{10,... | collective-permute-start | bytes 786440 | tf_op jit(solution)/shard_map/ppermute | solution.py:310
  18.2 0.7 add_bitcast_fusion.ids
  18.9 0.0 collective-permute-done.2.far_side
  18.9 0.1 collective-permute-start
  18.9 0.0 collective-permute-done.1.core_side
  18.9 0.0 copy-start.1
  19.0 1.0 %copy-done.1 = f32[256,512]{1,0:T(8,128)S(1)} copy-done((f32[256,512]{1,0:T(8,128)S(1)}, f32[256,512]{1,0:T(8,128)}, u32[]{:S(2)}) %copy-start.1) | copy-done | bytes 524312
  20.0 0.9 %copy-done.3 = f32[256,256]{1,0:T(8,128)S(1)} copy-done((f32[256,256]{1,0:T(8,128)S(1)}, f32[256,256]{1,0:T(8,128)}, u32[]{:S(2)}) %copy-start.3) | copy-done | bytes 262168
  20.9 1.4 %copy-done.5 = bf16[3072,256]{1,0:T(8,128)(2,1)S(1)} copy-done((bf16[3072,256]{1,0:T(8,128)(2,1)S(1)}, bf16[3072,256]{1,0:T(8,128)(2,1)}, u32[]{:S(2)}) %copy-start.5) | copy-done | bytes 1572888
  22.4 2.6 %smooth.1 = (bf16[256,512]{1,0:T(8,128)(2,1)S(1)}, f32[256,256]{1,0:T(8,128)S(1)}, f32[256,256]{1,0:T(8,128)S(1)}, f32[256,256]{1,0:T(8,128)S(1)}) custom-call(f32[256,512]{1,0:T(8,128)S(1)} %copy-done.1, f32[256,128]{1,0:T(8,128)S(1)} %collective-permute-done.1.core_side, f32[256,128]{1,0:T(8,128)S(1)} %collective-permute-done.2.far_side, ...), custom_call_target="tpu_custom_call" | custom-call | flops 1342177280 | bytes 4194304 | tf_op jit(solution)/shard_map/smooth/pallas_call | solution.py:348
  24.9 0.0 copy-start.2
  24.9 0.0 copy-start.4
  24.9 0.0 collective-permute-done.asked
  25.0 1.4 %collective-permute-done.8.refs_6_.refs_7_ = bf16[512,256]{1,0:T(8,128)(2,1)S(1)} collective-permute-done((bf16[512,256]{1,0:T(8,128)(2,1)S(1)}, bf16[512,256]{1,0:T(8,128)(2,1)S(1)}, u32[]{:S(2)}, u32[]{:S(2)}) %collective-permute-start.8) | collective-permute-done | bytes 262176 | tf_op jit(solution)/shard_map/ppermute | solution.py:310
  26.4 0.0 collective-permute-done.7.refs_5_
  26.4 0.0 collective-permute-done.5.refs_2_
  26.4 0.0 copy-done
  26.4 1.0 %pack.1 = bf16[2048,256]{1,0:T(8,128)(2,1)S(1)} custom-call(s32[2,8]{1,0:T(2,128)S(1)} %collective-permute-done.asked, bf16[512,256]{1,0:T(8,128)(2,1)S(1)} %copy-done, bf16[512,256]{1,0:T(8,128)(2,1)S(1)} %collective-permute-done.3.refs_1_, bf16[512,256]{1,0:T(8,128)(2,1)S(1)} %collective-permute-done.5.refs_2_, ...), custom_call_target="tpu_custom_call" | custom-call | bytes 2097152 | tf_op jit(solution)/shard_map/pack/pallas_call | solution.py:365
  27.4 0.1 collective-permute-start.9
  27.5 1.9 %collective-permute-start.10 = (bf16[512,256]{1,0:T(8,128)(2,1)S(1)}, bf16[512,256]{1,0:T(8,128)(2,1)S(1)}, u32[]{:S(2)}, u32[]{:S(2)}) collective-permute-start(bf16[512,256]{1,0:T(8,128)(2,1)S(1)} %collective-permute-done.5.refs_2_), channel_id=1, source_target_pairs={{0,2},{1,3},{2,0},{3,1},{4,6},{5,7},{6,4},{7,5},{8,10},{9,11},{10,... | collective-permute-start | bytes 786440 | tf_op jit(solution)/shard_map/ppermute | solution.py:310
  29.4 6.9 %collective-permute-done.10.refs_6_ = bf16[512,256]{1,0:T(8,128)(2,1)S(1)} collective-permute-done((bf16[512,256]{1,0:T(8,128)(2,1)S(1)}, bf16[512,256]{1,0:T(8,128)(2,1)S(1)}, u32[]{:S(2)}, u32[]{:S(2)}) %collective-permute-start.10) | collective-permute-done | bytes 262176 | tf_op jit(solution)/shard_map/ppermute | solution.py:310
  36.3 0.0 collective-permute-start.11
  36.3 1.5 %collective-permute-done.11.late_theirs = bf16[512,256]{1,0:T(8,128)(2,1)S(1)} collective-permute-done((bf16[512,256]{1,0:T(8,128)(2,1)S(1)}, bf16[512,256]{1,0:T(8,128)(2,1)S(1)}, u32[]{:S(2)}, u32[]{:S(2)}) %collective-permute-start.11) | collective-permute-done | bytes 262176 | tf_op jit(solution)/shard_map/ppermute | solution.py:310
  37.9 0.0 collective-permute-done.9.packed
  37.9 0.0 copy-done.2
  37.9 0.0 copy-done.4
  37.9 4.0 %session.1 = (f32[256,512]{1,0:T(8,128)S(1)}, bf16[256,256]{1,0:T(8,128)(2,1)S(1)}, bf16[2304,256]{1,0:T(8,128)(2,1)S(1)}) custom-call(s32[2,8]{1,0:T(2,128)S(1)} %add_bitcast_fusion.ids, s32[2,4,8]{2,1,0:T(4,128)S(1)} %bitcast.5, bf16[256,512]{1,0:T(8,128)(2,1)S(1)} %get-tuple-element.27.smoothed, bf16[16,128,512]{2,1,0:T(8,128)(2,1)S(1)} %bitcast.4, ...), custom_call_target="tpu_custom_call" | custom-call | flops 1610612736 | bytes 8388608 | tf_op jit(solution)/shard_map/session/pallas_call | solution.py:380
  41.8 0.2 collective-permute-start.12
  42.0 2.7 %collective-permute-done.12.got.core_side = bf16[2304,256]{1,0:T(8,128)(2,1)S(1)} collective-permute-done((bf16[2304,256]{1,0:T(8,128)(2,1)S(1)}, bf16[2304,256]{1,0:T(8,128)(2,1)S(1)}, u32[]{:S(2)}, u32[]{:S(2)}) %collective-permute-start.12) | collective-permute-done | bytes 1179680 | tf_op jit(solution)/shard_map/ppermute | solution.py:310
  44.8 1.2 %merge_late.1 = bf16[512,256]{1,0:T(8,128)(2,1)S(1)} custom-call(s32[2,8]{1,0:T(2,128)S(1)} %add_bitcast_fusion.ids, s32[2,8]{1,0:T(2,128)S(1)} %collective-permute-done.asked, bf16[2304,256]{1,0:T(8,128)(2,1)S(1)} %get-tuple-element.32.own, bf16[2304,256]{1,0:T(8,128)(2,1)S(1)} %collective-permute-done.12.got.core_side), custom_call_target="tpu_custom_call" | custom-call | bytes 1048576 | tf_op jit(solution)/shard_map/merge_late/pallas_call | solution.py:410
  46.0 1.8 %collective-permute-start.13 = (bf16[512,256]{1,0:T(8,128)(2,1)S(1)}, bf16[512,256]{1,0:T(8,128)(2,1)S(1)}, u32[]{:S(2)}, u32[]{:S(2)}) collective-permute-start(bf16[512,256]{1,0:T(8,128)(2,1)S(1)} %merge_late.1), channel_id=1, source_target_pairs={{0,2},{1,3},{2,0},{3,1},{4,6},{5,7},{6,4},{7,5},{8,10},{9,11},{10,... | collective-permute-start | bytes 786440 | tf_op jit(solution)/shard_map/ppermute | solution.py:310
  47.8 1.9 %merge.1 = (f32[512,256]{1,0:T(8,128)S(1)}, f32[512,256]{1,0:T(8,128)S(1)}, f32[512,256]{1,0:T(8,128)S(1)}, f32[512,256]{1,0:T(8,128)S(1)}, bf16[512,256]{1,0:T(...) custom-call(s32[2,8]{1,0:T(2,128)S(1)} %add_bitcast_fusion.ids, ...), custom_call_target="tpu_custom_call" | custom-call | bytes 5242880 | tf_op jit(solution)/shard_map/merge/pallas_call | solution.py:424
  49.7 0.4 collective-permute-start.16
  50.1 1.7 %collective-permute-start.19 = (bf16[512,256]{1,0:T(8,128)(2,1)S(1)}, bf16[512,256]{1,0:T(8,128)(2,1)S(1)}, u32[]{:S(2)}, u32[]{:S(2)}) collective-permute-start(bf16[512,256]{1,0:T(8,128)(2,1)S(1)} %get-tuple-element.45), channel_id=1, source_target_pairs={{0,2},{1,3},{2,0},{3,1},{4,6},{5,7},{6,4},{7,5},{8,10},{9,11},{10,... | collective-permute-start | bytes 786440 | tf_op jit(solution)/shard_map/ppermute | solution.py:310
  51.8 3.4 %collective-permute-done.13 = bf16[512,256]{1,0:T(8,128)(2,1)S(1)} collective-permute-done((bf16[512,256]{1,0:T(8,128)(2,1)S(1)}, bf16[512,256]{1,0:T(8,128)(2,1)S(1)}, u32[]{:S(2)}, u32[]{:S(2)}) %collective-permute-start.13) | collective-permute-done | bytes 262176 | tf_op jit(solution)/shard_map/ppermute | solution.py:310
  55.2 0.1 add_convert_fusion.2
  55.2 0.7 collective-permute-start.17
  55.9 1.2 %collective-permute-start.15 = (bf16[512,256]{1,0:T(8,128)(2,1)S(1)}, bf16[512,256]{1,0:T(8,128)(2,1)S(1)}, u32[]{:S(2)}, u32[]{:S(2)}) collective-permute-start(bf16[512,256]{1,0:T(8,128)(2,1)S(1)} %get-tuple-element.39), channel_id=1, source_target_pairs={{0,2},{1,3},{2,0},{3,1},{4,6},{5,7},{6,4},{7,5},{8,10},{9,11},{10,... | collective-permute-start | bytes 786440 | tf_op jit(solution)/shard_map/ppermute | solution.py:310
  57.1 9.3 %collective-permute-done.19 = bf16[512,256]{1,0:T(8,128)(2,1)S(1)} collective-permute-done((bf16[512,256]{1,0:T(8,128)(2,1)S(1)}, bf16[512,256]{1,0:T(8,128)(2,1)S(1)}, u32[]{:S(2)}, u32[]{:S(2)}) %collective-permute-start.19) | collective-permute-done | bytes 262176 | tf_op jit(solution)/shard_map/ppermute | solution.py:310
  66.4 0.1 add_convert_fusion
  66.5 0.4 collective-permute-start.20
  66.9 0.0 collective-permute-done.16
  66.9 0.0 collective-permute-done.17
  66.9 0.1 add_convert_fusion.1
  67.0 1.7 %collective-permute-start.18 = (bf16[512,256]{1,0:T(8,128)(2,1)S(1)}, bf16[512,256]{1,0:T(8,128)(2,1)S(1)}, u32[]{:S(2)}, u32[]{:S(2)}) collective-permute-start(bf16[512,256]{1,0:T(8,128)(2,1)S(1)} %add_convert_fusion.1), channel_id=1, source_target_pairs={{0,4},{1,5},{2,6},{3,7},{4,8},{5,9},{6,10},{7,11},{8,12},{9,13},{1... | collective-permute-start | bytes 786440 | tf_op jit(solution)/shard_map/ppermute | solution.py:310
  68.7 1.9 %collective-permute-start.14 = (bf16[256,256]{1,0:T(8,128)(2,1)S(1)}, bf16[256,256]{1,0:T(8,128)(2,1)S(1)}, u32[]{:S(2)}, u32[]{:S(2)}) collective-permute-start(bf16[256,256]{1,0:T(8,128)(2,1)S(1)} %get-tuple-element.34), channel_id=1, source_target_pairs={{1,2},{3,4},{5,6},{7,8},{9,10},{11,12},{13,14},{2,1},{4,3},{6,5},{... | collective-permute-start | bytes 393224 | tf_op jit(solution)/shard_map/ppermute | solution.py:310
  70.6 10.5 %collective-permute-done.14.far_side = bf16[256,256]{1,0:T(8,128)(2,1)S(1)} collective-permute-done((bf16[256,256]{1,0:T(8,128)(2,1)S(1)}, bf16[256,256]{1,0:T(8,128)(2,1)S(1)}, u32[]{:S(2)}, u32[]{:S(2)}) %collective-permute-start.14) | collective-permute-done | bytes 131104 | tf_op jit(solution)/shard_map/ppermute | solution.py:310
  81.1 0.0 copy-done.6
  81.1 2.7 %unsmooth.1 = f32[256,512]{1,0:T(8,128)} custom-call(f32[256,512]{1,0:T(8,128)S(1)} %get-tuple-element.31.mid, bf16[2304,256]{1,0:T(8,128)(2,1)S(1)} %collective-permute-done.12.got.core_side, bf16[256,256]{1,0:T(8,128)(2,1)S(1)} %collective-permute-done.14.far_side, f32[256,256]{1,0:T(8,128)S(1)} %get-tuple-element.35.base, ...), custom_call_target="tpu_custom_call" | custom-call | flops 1342177280 | bytes 4194304 | tf_op jit(solution)/shard_map/unsmooth/pallas_call | solution.py:449
  83.8 0.0 collective-permute-done.15
  83.9 0.0 collective-permute-done.20
  83.9 0.0 collective-permute-done.18
  83.9 0.9 %convert_add_fusion = f32[512,256]{1,0:T(8,128)} fusion(bf16[512,256]{1,0:T(8,128)(2,1)S(1)} %collective-permute-done.20, bf16[512,256]{1,0:T(8,128)(2,1)S(1)} %collective-permute-done.18, f32[512,256]{1,0:T(8,128)S(1)} %get-tuple-element.38, bf16[512,256]{1,0:T(8,128)(2,1)S(1)} %collective-permute-done.15), kind=kLoop, calls=%fused_computation | loop fusion | flops 786432 | bytes 1835008 | tf_op jit(solution)/shard_map/add | solution.py:447
  (4 shorter events, 0.0 us)
Async XLA Ops:
  0.6 8.3 %collective-permute-start.4 = (bf16[512,256]{1,0:T(8,128)(2,1)}, bf16[512,256]{1,0:T(8,128)(2,1)S(1)}, u32[]{:S(2)}, u32[]{:S(2)}) collective-permute-start(bf16[512,256]{1,0:T(8,128)(2,1)} %refs_0_.3), channel_id=1, source_target_pairs={{0,2},{1,3},{2,0},{3,1},{4,6},{5,7},{6,4},{7,5},{8,10},{9,11},{10,... | collective-permute-start | bytes 786440 | tf_op jit(solution)/shard_map/ppermute | solution.py:310
  2.2 12.2 %collective-permute-start.3 = (bf16[512,256]{1,0:T(8,128)(2,1)}, bf16[512,256]{1,0:T(8,128)(2,1)S(1)}, u32[]{:S(2)}, u32[]{:S(2)}) collective-permute-start(bf16[512,256]{1,0:T(8,128)(2,1)} %refs_0_.3), channel_id=1, source_target_pairs={{0,4},{1,5},{2,6},{3,7},{4,8},{5,9},{6,10},{7,11},{8,12},{9,13},{1... | collective-permute-start | bytes 786440 | tf_op jit(solution)/shard_map/ppermute | solution.py:310
  3.8 13.5 %collective-permute-start.6 = (bf16[512,256]{1,0:T(8,128)(2,1)}, bf16[512,256]{1,0:T(8,128)(2,1)S(1)}, u32[]{:S(2)}, u32[]{:S(2)}) collective-permute-start(bf16[512,256]{1,0:T(8,128)(2,1)} %refs_0_.3), channel_id=1, source_target_pairs={{0,12},{1,13},{2,14},{3,15},{4,0},{5,1},{6,2},{7,3},{8,4},{9,5},{1... | collective-permute-start | bytes 786440 | tf_op jit(solution)/shard_map/ppermute | solution.py:310
  5.2 13.6 %collective-permute-start.2 = (f32[256,128]{1,0:T(8,128)S(1)}, f32[256,128]{1,0:T(8,128)S(1)}, u32[]{:S(2)}, u32[]{:S(2)}) collective-permute-start(f32[256,128]{1,0:T(8,128)S(1)} %get-tuple-element.46), channel_id=1, source_target_pairs={{1,2},{3,4},{5,6},{7,8},{9,10},{11,12},{13,14},{2,1},{4,3},{6,5},{... | collective-permute-start | bytes 393224 | tf_op jit(solution)/shard_map/ppermute | solution.py:310
  7.2 11.8 %collective-permute-start.1 = (f32[256,128]{1,0:T(8,128)S(1)}, f32[256,128]{1,0:T(8,128)S(1)}, u32[]{:S(2)}, u32[]{:S(2)}) collective-permute-start(f32[256,128]{1,0:T(8,128)S(1)} %get-tuple-element.47), channel_id=1, source_target_pairs={{0,1},{1,0},{2,3},{3,2},{4,5},{5,4},{6,7},{7,6},{8,9},{9,8},{10,11... | collective-permute-start | bytes 393224 | tf_op jit(solution)/shard_map/ppermute | solution.py:310
  14.4 12.0 %collective-permute-start.7 = (bf16[512,256]{1,0:T(8,128)(2,1)S(1)}, bf16[512,256]{1,0:T(8,128)(2,1)S(1)}, u32[]{:S(2)}, u32[]{:S(2)}) collective-permute-start(bf16[512,256]{1,0:T(8,128)(2,1)S(1)} %collective-permute-done.3.refs_1_), channel_id=1, source_target_pairs={{0,2},{1,3},{2,0},{3,1},{4,6},{5,7},{6,4},{7,5},{8,10},{9,11},{10,... | collective-permute-start | bytes 786440 | tf_op jit(solution)/shard_map/ppermute | solution.py:310
  15.5 10.9 %collective-permute-start.5 = (bf16[512,256]{1,0:T(8,128)(2,1)S(1)}, bf16[512,256]{1,0:T(8,128)(2,1)S(1)}, u32[]{:S(2)}, u32[]{:S(2)}) collective-permute-start(bf16[512,256]{1,0:T(8,128)(2,1)S(1)} %collective-permute-done.3.refs_1_), channel_id=1, source_target_pairs={{0,4},{1,5},{2,6},{3,7},{4,8},{5,9},{6,10},{7,11},{8,12},{9,13},{1... | collective-permute-start | bytes 786440 | tf_op jit(solution)/shard_map/ppermute | solution.py:310
  17.3 9.1 %collective-permute-start.8 = (bf16[512,256]{1,0:T(8,128)(2,1)S(1)}, bf16[512,256]{1,0:T(8,128)(2,1)S(1)}, u32[]{:S(2)}, u32[]{:S(2)}) collective-permute-start(bf16[512,256]{1,0:T(8,128)(2,1)S(1)} %collective-permute-done.6.refs_3_), channel_id=1, source_target_pairs={{0,2},{1,3},{2,0},{3,1},{4,6},{5,7},{6,4},{7,5},{8,10},{9,11},{10,... | collective-permute-start | bytes 786440 | tf_op jit(solution)/shard_map/ppermute | solution.py:310
  18.9 7.5 %copy-start = (bf16[512,256]{1,0:T(8,128)(2,1)S(1)}, bf16[512,256]{1,0:T(8,128)(2,1)}, u32[]{:S(2)}) copy-start(bf16[512,256]{1,0:T(8,128)(2,1)} %refs_0_.3) | copy-start | bytes 786436
  18.9 6.1 %collective-permute-start = (s32[2,8]{1,0:T(2,128)S(1)}, s32[2,8]{1,0:T(2,128)S(1)}, u32[]{:S(2)}, u32[]{:S(2)}) collective-permute-start(s32[2,8]{1,0:T(2,128)S(1)} %add_bitcast_fusion.ids), channel_id=1, source_target_pairs={{0,1},{1,0},{2,3},{3,2},{4,5},{5,4},{6,7},{7,6},{8,9},{9,8},{10,11... | collective-permute-start | bytes 200 | tf_op jit(solution)/shard_map/ppermute | solution.py:310
  18.9 1.0 %copy-start.1 = (f32[256,512]{1,0:T(8,128)S(1)}, f32[256,512]{1,0:T(8,128)}, u32[]{:S(2)}) copy-start(f32[256,512]{1,0:T(8,128)} %mid.1) | copy-start | bytes 1572868
  20.0 0.9 %copy-start.3 = (f32[256,256]{1,0:T(8,128)S(1)}, f32[256,256]{1,0:T(8,128)}, u32[]{:S(2)}) copy-start(f32[256,256]{1,0:T(8,128)} %taps.1) | copy-start | bytes 786436
  20.9 1.4 %copy-start.5 = (bf16[3072,256]{1,0:T(8,128)(2,1)S(1)}, bf16[3072,256]{1,0:T(8,128)(2,1)}, u32[]{:S(2)}) copy-start(bf16[3072,256]{1,0:T(8,128)(2,1)} %constant.22.clone.table) | copy-start | bytes 4718596
  24.9 13.0 %copy-start.2 = (bf16[2,8,128,512]{3,2,1,0:T(8,128)(2,1)S(1)}, bf16[2,8,128,512]{3,2,1,0:T(8,128)(2,1)}, u32[]{:S(2)}) copy-start(bf16[2,8,128,512]{3,2,1,0:T(8,128)(2,1)} %param.11) | copy-start | bytes 6291460
  24.9 12.9 %copy-start.4 = (s32[2,8,4]{1,2,0:T(4,128)S(1)}, s32[2,8,4]{1,2,0:T(4,128)}, u32[]{:S(2)}) copy-start(s32[2,8,4]{1,2,0:T(4,128)} %param.14) | copy-start | bytes 772
  27.4 10.4 %collective-permute-start.9 = (bf16[2048,256]{1,0:T(8,128)(2,1)S(1)}, bf16[2048,256]{1,0:T(8,128)(2,1)S(1)}, u32[]{:S(2)}, u32[]{:S(2)}) collective-permute-start(bf16[2048,256]{1,0:T(8,128)(2,1)S(1)} %pack.1), channel_id=1, source_target_pairs={{0,1},{1,0},{2,3},{3,2},{4,5},{5,4},{6,7},{7,6},{8,9},{9,8},{10,11... | collective-permute-start | bytes 3145736 | tf_op jit(solution)/shard_map/ppermute | solution.py:310
  27.5 8.8 %collective-permute-start.10 = (bf16[512,256]{1,0:T(8,128)(2,1)S(1)}, bf16[512,256]{1,0:T(8,128)(2,1)S(1)}, u32[]{:S(2)}, u32[]{:S(2)}) collective-permute-start(bf16[512,256]{1,0:T(8,128)(2,1)S(1)} %collective-permute-done.5.refs_2_), channel_id=1, source_target_pairs={{0,2},{1,3},{2,0},{3,1},{4,6},{5,7},{6,4},{7,5},{8,10},{9,11},{10,... | collective-permute-start | bytes 786440 | tf_op jit(solution)/shard_map/ppermute | solution.py:310
  36.3 1.5 %collective-permute-start.11 = (bf16[512,256]{1,0:T(8,128)(2,1)S(1)}, bf16[512,256]{1,0:T(8,128)(2,1)S(1)}, u32[]{:S(2)}, u32[]{:S(2)}) collective-permute-start(bf16[512,256]{1,0:T(8,128)(2,1)S(1)} %collective-permute-done.10.refs_6_), channel_id=1, source_target_pairs={{0,1},{1,0},{2,3},{3,2},{4,5},{5,4},{6,7},{7,6},{8,9},{9,8},{10,11... | collective-permute-start | bytes 786440 | tf_op jit(solution)/shard_map/ppermute | solution.py:310
  41.8 2.9 %collective-permute-start.12 = (bf16[2304,256]{1,0:T(8,128)(2,1)S(1)}, bf16[2304,256]{1,0:T(8,128)(2,1)S(1)}, u32[]{:S(2)}, u32[]{:S(2)}) collective-permute-start(bf16[2304,256]{1,0:T(8,128)(2,1)S(1)} %get-tuple-element.32.own), channel_id=1, source_target_pairs={{0,1},{1,0},{2,3},{3,2},{4,5},{5,4},{6,7},{7,6},{8,9},{9,8},{10,11... | collective-permute-start | bytes 3538952 | tf_op jit(solution)/shard_map/ppermute | solution.py:310
  46.0 9.2 %collective-permute-start.13 = (bf16[512,256]{1,0:T(8,128)(2,1)S(1)}, bf16[512,256]{1,0:T(8,128)(2,1)S(1)}, u32[]{:S(2)}, u32[]{:S(2)}) collective-permute-start(bf16[512,256]{1,0:T(8,128)(2,1)S(1)} %merge_late.1), channel_id=1, source_target_pairs={{0,2},{1,3},{2,0},{3,1},{4,6},{5,7},{6,4},{7,5},{8,10},{9,11},{10,... | collective-permute-start | bytes 786440 | tf_op jit(solution)/shard_map/ppermute | solution.py:310
  49.7 17.2 %collective-permute-start.16 = (bf16[512,256]{1,0:T(8,128)(2,1)S(1)}, bf16[512,256]{1,0:T(8,128)(2,1)S(1)}, u32[]{:S(2)}, u32[]{:S(2)}) collective-permute-start(bf16[512,256]{1,0:T(8,128)(2,1)S(1)} %get-tuple-element.41), channel_id=1, source_target_pairs={{0,2},{1,3},{2,0},{3,1},{4,6},{5,7},{6,4},{7,5},{8,10},{9,11},{10,... | collective-permute-start | bytes 786440 | tf_op jit(solution)/shard_map/ppermute | solution.py:310
  50.1 16.4 %collective-permute-start.19 = (bf16[512,256]{1,0:T(8,128)(2,1)S(1)}, bf16[512,256]{1,0:T(8,128)(2,1)S(1)}, u32[]{:S(2)}, u32[]{:S(2)}) collective-permute-start(bf16[512,256]{1,0:T(8,128)(2,1)S(1)} %get-tuple-element.45), channel_id=1, source_target_pairs={{0,2},{1,3},{2,0},{3,1},{4,6},{5,7},{6,4},{7,5},{8,10},{9,11},{10,... | collective-permute-start | bytes 786440 | tf_op jit(solution)/shard_map/ppermute | solution.py:310
  55.2 26.0 %copy-start.6 = (bf16[3072,256]{1,0:T(8,128)(2,1)S(1)}, bf16[3072,256]{1,0:T(8,128)(2,1)}, u32[]{:S(2)}) copy-start(bf16[3072,256]{1,0:T(8,128)(2,1)} %constant.22.clone.table) | copy-start | bytes 4718596
  55.2 11.6 %collective-permute-start.17 = (bf16[512,256]{1,0:T(8,128)(2,1)S(1)}, bf16[512,256]{1,0:T(8,128)(2,1)S(1)}, u32[]{:S(2)}, u32[]{:S(2)}) collective-permute-start(bf16[512,256]{1,0:T(8,128)(2,1)S(1)} %add_convert_fusion.2), channel_id=1, source_target_pairs={{0,4},{1,5},{2,6},{3,7},{4,8},{5,9},{6,10},{7,11},{8,12},{9,13},{1... | collective-permute-start | bytes 786440 | tf_op jit(solution)/shard_map/ppermute | solution.py:310
  55.9 27.9 %collective-permute-start.15 = (bf16[512,256]{1,0:T(8,128)(2,1)S(1)}, bf16[512,256]{1,0:T(8,128)(2,1)S(1)}, u32[]{:S(2)}, u32[]{:S(2)}) collective-permute-start(bf16[512,256]{1,0:T(8,128)(2,1)S(1)} %get-tuple-element.39), channel_id=1, source_target_pairs={{0,2},{1,3},{2,0},{3,1},{4,6},{5,7},{6,4},{7,5},{8,10},{9,11},{10,... | collective-permute-start | bytes 786440 | tf_op jit(solution)/shard_map/ppermute | solution.py:310
  66.5 17.4 %collective-permute-start.20 = (bf16[512,256]{1,0:T(8,128)(2,1)S(1)}, bf16[512,256]{1,0:T(8,128)(2,1)S(1)}, u32[]{:S(2)}, u32[]{:S(2)}) collective-permute-start(bf16[512,256]{1,0:T(8,128)(2,1)S(1)} %add_convert_fusion), channel_id=1, source_target_pairs={{0,12},{1,13},{2,14},{3,15},{4,0},{5,1},{6,2},{7,3},{8,4},{9,5},{1... | collective-permute-start | bytes 786440 | tf_op jit(solution)/shard_map/ppermute | solution.py:310
  67.0 16.9 %collective-permute-start.18 = (bf16[512,256]{1,0:T(8,128)(2,1)S(1)}, bf16[512,256]{1,0:T(8,128)(2,1)S(1)}, u32[]{:S(2)}, u32[]{:S(2)}) collective-permute-start(bf16[512,256]{1,0:T(8,128)(2,1)S(1)} %add_convert_fusion.1), channel_id=1, source_target_pairs={{0,4},{1,5},{2,6},{3,7},{4,8},{5,9},{6,10},{7,11},{8,12},{9,13},{1... | collective-permute-start | bytes 786440 | tf_op jit(solution)/shard_map/ppermute | solution.py:310
  68.7 12.4 %collective-permute-start.14 = (bf16[256,256]{1,0:T(8,128)(2,1)S(1)}, bf16[256,256]{1,0:T(8,128)(2,1)S(1)}, u32[]{:S(2)}, u32[]{:S(2)}) collective-permute-start(bf16[256,256]{1,0:T(8,128)(2,1)S(1)} %get-tuple-element.34), channel_id=1, source_target_pairs={{1,2},{3,4},{5,6},{7,8},{9,10},{11,12},{13,14},{2,1},{4,3},{6,5},{... | collective-permute-start | bytes 393224 | tf_op jit(solution)/shard_map/ppermute | solution.py:310

commit v6 on v5

--- a/solution.py
+++ b/solution.py
@@ -158,13 +158,13 @@
     )
 
 
-def pack_kernel(entries, late, asked, *refs):
+def pack_kernel(first, entries, late, asked, *refs):
     pieces, out = refs[:-1], refs[-1]
     blocks = pieces[0].shape[0] // BLK
     me = lax.axis_index("tm")
 
     def body(e, _):
-        core, piece, row = place_of(asked, e, me, blocks, False)
+        core, piece, row = place_of(asked, first + e, me, blocks, False)
         target = pl.ds(pl.multiple_of(e * BLK, BLK), BLK)
 
         @pl.when(jnp.logical_and(core, piece != late))
@@ -180,7 +180,7 @@
 
 
 def session_kernel(
-    entries, group, late, ids, mask, smoothed, recorded, packed, late_theirs, *refs
+    entries, group, late, ids, mask, smoothed, recorded, packed, packed_rest, late_theirs, *refs
 ):
     pieces = refs[:-5]
     grad, far_side, terms, rows, resid = refs[-5:]
@@ -209,8 +209,11 @@
 
                 @pl.when(piece != late)
                 def _():
-                    source = pl.ds(pl.multiple_of(e * BLK, BLK), BLK)
-                    rows[i * BLK : (i + 1) * BLK] = packed[source]
+                    def act(ref):
+                        source = pl.ds(pl.multiple_of(remainder(e, entries // 2) * BLK, BLK), BLK)
+                        rows[i * BLK : (i + 1) * BLK] = ref[source]
+
+                    pick((packed, packed_rest), divide(e, entries // 2), act)
 
             lax.cond(core, own, other)
         block = rows[...]
@@ -341,6 +344,9 @@
         if r != half:
             across[r] = flip(straight[r], 2)
 
+    core_side, far_side, straight[half] = lax.optimization_barrier(
+        (core_side, far_side, straight[half])
+    )
     table = dft_tables(2 * halfwidth)
     table_scratch = [pltpu.VMEM(table.shape, BF16), pltpu.SemaphoreType.DMA(())]
     mxu = 40 * 2 * latent_dim * (2 * halfwidth) ** 2
@@ -357,22 +363,24 @@
     )(latents, core_side, far_side, kernel, table)
 
     slots = jax.ShapeDtypeStruct((entries * BLK, latent_dim), BF16)
-    ids, asked, smoothed, mask = lax.optimization_barrier(
-        (ids, asked, smoothed, mask)
-    )
     across[half] = flip(straight[half], 2)
     early = straight + across[:half] + across[half + 1 :]
-    packed = pl.pallas_call(
-        functools.partial(pack_kernel, entries, late),
-        out_shape=slots,
-        in_specs=[smem] + [VMEM] * len(early),
-        out_specs=VMEM,
-        compiler_params=pltpu.CompilerParams(vmem_limit_bytes=4 * MIB + 3 * piece_bytes),
-        cost_estimate=pl.CostEstimate(flops=0, bytes_accessed=2 * 2**20, transcendentals=0),
-        name="pack",
-    )(asked, *early)
-    packed = flip(packed, 1)
-    late_theirs = flip(across[half], 1)
+
+    def pack(first, total):
+        return pl.pallas_call(
+            functools.partial(pack_kernel, first, total, late),
+            out_shape=jax.ShapeDtypeStruct((total * BLK, latent_dim), BF16),
+            in_specs=[smem] + [VMEM] * len(early),
+            out_specs=VMEM,
+            compiler_params=pltpu.CompilerParams(vmem_limit_bytes=4 * MIB + 3 * piece_bytes),
+            cost_estimate=pl.CostEstimate(flops=0, bytes_accessed=2**20, transcendentals=0),
+            name="pack",
+        )(asked, *early)
+
+    asked, smoothed, mask = lax.optimization_barrier((asked, smoothed, mask))
+    packed = [flip(pack(first, entries // 2), 1) for first in (0, entries // 2)]
+    last, smoothed = lax.optimization_barrier((across[half], smoothed))
+    late_theirs = flip(last, 1)
     pieces = straight + across
 
     group = 4
@@ -384,7 +392,7 @@
             jax.ShapeDtypeStruct((latent_dim, 2 * halfwidth), BF16),
             extended,
         ),
-        in_specs=[smem] * 2 + [VMEM] * (4 + len(pieces)),
+        in_specs=[smem] * 2 + [VMEM] * (5 + len(pieces)),
         out_specs=(VMEM,) * 3,
         scratch_shapes=[
             pltpu.VMEM((group * BLK, latent_dim), BF16),
@@ -400,7 +408,7 @@
         mask,
         smoothed,
         recorded.reshape(entries, BLK, bins),
-        packed,
+        *packed,
         late_theirs,
         *pieces,
     )
@@ -418,7 +426,6 @@
         name="merge_late",
     )(ids, asked, terms, got)
     back = flip(sent, 2)
-    far_side, back = lax.optimization_barrier((far_side, back))
     far_side = permute(far_side, odd_even)
     wide = jax.ShapeDtypeStruct((chunk, latent_dim), F32)
     merged = pl.pallas_call(
@@ -431,10 +438,16 @@
         cost_estimate=pl.CostEstimate(flops=0, bytes_accessed=5 * 2**20, transcendentals=0),
         name="merge",
     )(ids, asked, terms, got)
-    other = {half: back}
-    for r in sorted(range(chain), key=lambda r: -min(r, chain - r)):
-        if r != half:
-            other[r] = flip(merged[chain + r - (r > half)], 2)
+    merged = list(merged)
+    far_side, *merged = lax.optimization_barrier((far_side, *merged))
+    crossed = {r: merged[chain + r - (r > half)] for r in range(chain) if r != half}
+    first = [r for r in range(half + 1, chain)]
+    other = {r: flip(crossed[r], 2) for r in first}
+    rest = [r for r in crossed if r not in first]
+    back, *held = lax.optimization_barrier((back, *(crossed[r] for r in rest)))
+    other[half] = back
+    for r, part in zip(rest, held):
+        other[r] = flip(part, 2)
     totals = [merged[r] + other[r].astype(F32) for r in range(chain)]
     rise = totals[half]
     for r in range(half - 1, -1, -1):

time: 85.1 us -> 88.2 us (1.036)
  the two profiles are of different devices: /device:TPU:18 before, /device:TPU:0 now
where the time goes in v6:
time: 88.2 us; the launch traced here: 87.9 us
  waiting for transfers between devices  33.5 us (38%)
  starting transfers between devices  33.4 us (38%)
  Pallas kernels  13.9 us (16%)
  local copies, waits for them, and re-layouts  3.42 us (4%)
  other arithmetic  2.79 us (3%)
    ppermute x22, waiting for transfers between devices, permute(): return lax.ppermute(x, 'tm', pairs)  33.5 us
    ppermute x22, starting transfers between devices, permute(): return lax.ppermute(x, 'tm', pairs)  33.4 us
    pallas_call x1, Pallas kernels, local(): pl.pallas_call(functools.partial(session_kernel, entries, group, late), o...  4 us
    unnamed x14, local copies, waits for them, and re-layouts  3.42 us
    pallas_call x1, Pallas kernels, local(): pl.pallas_call(unsmooth_kernel, out_shape=jax.ShapeDtypeStruct((latent_di...  2.67 us
    pallas_call x1, Pallas kernels, local(): pl.pallas_call(smooth_kernel, out_shape=(jax.ShapeDtypeStruct((latent_dim...  2.56 us
    pallas_call x1, Pallas kernels, local(): pl.pallas_call(functools.partial(merge_kernel, entries, late), out_shape=...  1.9 us
  transfers between devices with their start and end apart: 22, of which 11 were waited for; matrix products, arithmetic and copies ran while one was open for 2% of the time, Pallas kernels for 10%

profile of v6, /device:TPU:0, one launch (start us, length us, event | category | flops | bytes accessed | tf_op | source)
XLA Modules:
  0.0 87.9 jit_solution(8699588073534876036)
XLA Ops:
  0.6 3.0 %collective-permute-start.4 = (bf16[512,256]{1,0:T(8,128)(2,1)}, bf16[512,256]{1,0:T(8,128)(2,1)S(1)}, u32[]{:S(2)}, u32[]{:S(2)}) collective-permute-start(bf16[512,256]{1,0:T(8,128)(2,1)} %refs_0_.5), channel_id=1, source_target_pairs={{0,2},{1,3},{2,0},{3,1},{4,6},{5,7},{6,4},{7,5},{8,10},{9,11},{10,... | collective-permute-start | bytes 786440 | tf_op jit(solution)/shard_map/ppermute | solution.py:313
  3.7 1.6 %collective-permute-start.3 = (bf16[512,256]{1,0:T(8,128)(2,1)}, bf16[512,256]{1,0:T(8,128)(2,1)S(1)}, u32[]{:S(2)}, u32[]{:S(2)}) collective-permute-start(bf16[512,256]{1,0:T(8,128)(2,1)} %refs_0_.5), channel_id=1, source_target_pairs={{0,4},{1,5},{2,6},{3,7},{4,8},{5,9},{6,10},{7,11},{8,12},{9,13},{1... | collective-permute-start | bytes 786440 | tf_op jit(solution)/shard_map/ppermute | solution.py:313
  5.2 2.2 %collective-permute-start.7 = (bf16[512,256]{1,0:T(8,128)(2,1)}, bf16[512,256]{1,0:T(8,128)(2,1)S(1)}, u32[]{:S(2)}, u32[]{:S(2)}) collective-permute-start(bf16[512,256]{1,0:T(8,128)(2,1)} %refs_0_.5), channel_id=1, source_target_pairs={{0,12},{1,13},{2,14},{3,15},{4,0},{5,1},{6,2},{7,3},{8,4},{9,5},{1... | collective-permute-start | bytes 786440 | tf_op jit(solution)/shard_map/ppermute | solution.py:313
  7.5 2.7 %collective-permute-done.4.refs_4_ = bf16[512,256]{1,0:T(8,128)(2,1)S(1)} collective-permute-done((bf16[512,256]{1,0:T(8,128)(2,1)}, bf16[512,256]{1,0:T(8,128)(2,1)S(1)}, u32[]{:S(2)}, u32[]{:S(2)}) %collective-permute-start.4) | collective-permute-done | bytes 262176 | tf_op jit(solution)/shard_map/ppermute | solution.py:313
  10.2 4.8 %collective-permute-done.3.refs_1_ = bf16[512,256]{1,0:T(8,128)(2,1)S(1)} collective-permute-done((bf16[512,256]{1,0:T(8,128)(2,1)}, bf16[512,256]{1,0:T(8,128)(2,1)S(1)}, u32[]{:S(2)}, u32[]{:S(2)}) %collective-permute-start.3) | collective-permute-done | bytes 262176 | tf_op jit(solution)/shard_map/ppermute | solution.py:313
  14.9 0.0 collective-permute-start.5
  14.9 1.0 %slice_select_fusion = (f32[256,128]{1,0:T(8,128)S(1)}, f32[256,128]{1,0:T(8,128)S(1)}) fusion(f32[256,512]{1,0:T(8,128)} %mid.1, pred[]{:T(512)S(6)} %eq.5), kind=kLoop, calls=%fused_computation.4 | loop fusion | flops 65536 | bytes 524289 | tf_op jit(solution)/shard_map/jit(_where)/select_n | solution.py:331
  15.9 0.7 collective-permute-start.2
  16.6 1.7 %collective-permute-start.1 = (f32[256,128]{1,0:T(8,128)S(1)}, f32[256,128]{1,0:T(8,128)S(1)}, u32[]{:S(2)}, u32[]{:S(2)}) collective-permute-start(f32[256,128]{1,0:T(8,128)S(1)} %get-tuple-element.73), channel_id=1, source_target_pairs={{0,1},{1,0},{2,3},{3,2},{4,5},{5,4},{6,7},{7,6},{8,9},{9,8},{10,11... | collective-permute-start | bytes 393224 | tf_op jit(solution)/shard_map/ppermute | solution.py:313
  18.3 5.3 %collective-permute-start.8 = (bf16[512,256]{1,0:T(8,128)(2,1)S(1)}, bf16[512,256]{1,0:T(8,128)(2,1)S(1)}, u32[]{:S(2)}, u32[]{:S(2)}) collective-permute-start(bf16[512,256]{1,0:T(8,128)(2,1)S(1)} %collective-permute-done.3.refs_1_), channel_id=1, source_target_pairs={{0,2},{1,3},{2,0},{3,1},{4,6},{5,7},{6,4},{7,5},{8,10},{9,11},{10,... | collective-permute-start | bytes 786440 | tf_op jit(solution)/shard_map/ppermute | solution.py:313
  23.7 0.0 collective-permute-done.7.refs_3_
  23.7 0.0 collective-permute-start.9
  23.7 0.7 add_bitcast_fusion.ids
  24.4 0.0 collective-permute-done.2.far_side
  24.4 0.1 collective-permute-start
  24.5 0.0 collective-permute-done.1.core_side
  24.5 0.4 collective-permute-done.5.refs_2_
  24.9 2.7 %collective-permute-start.6 = (bf16[512,256]{1,0:T(8,128)(2,1)S(1)}, bf16[512,256]{1,0:T(8,128)(2,1)S(1)}, u32[]{:S(2)}, u32[]{:S(2)}) collective-permute-start(bf16[512,256]{1,0:T(8,128)(2,1)S(1)} %collective-permute-done.5.refs_2_), channel_id=1, source_target_pairs={{0,2},{1,3},{2,0},{3,1},{4,6},{5,7},{6,4},{7,5},{8,10},{9,11},{10,... | collective-permute-start | bytes 786440 | tf_op jit(solution)/shard_map/ppermute | solution.py:313
  27.6 1.0 %copy-done.1 = f32[256,512]{1,0:T(8,128)S(1)} copy-done((f32[256,512]{1,0:T(8,128)S(1)}, f32[256,512]{1,0:T(8,128)}, u32[]{:S(2)}) %copy-start.1) | copy-done | bytes 524312
  28.7 0.9 %copy-done.3 = f32[256,256]{1,0:T(8,128)S(1)} copy-done((f32[256,256]{1,0:T(8,128)S(1)}, f32[256,256]{1,0:T(8,128)}, u32[]{:S(2)}) %copy-start.3) | copy-done | bytes 262168
  29.6 1.4 %copy-done.5 = bf16[3072,256]{1,0:T(8,128)(2,1)S(1)} copy-done((bf16[3072,256]{1,0:T(8,128)(2,1)S(1)}, bf16[3072,256]{1,0:T(8,128)(2,1)}, u32[]{:S(2)}) %copy-start.5) | copy-done | bytes 1572888
  31.0 2.6 %smooth.1 = (bf16[256,512]{1,0:T(8,128)(2,1)S(1)}, f32[256,256]{1,0:T(8,128)S(1)}, f32[256,256]{1,0:T(8,128)S(1)}, f32[256,256]{1,0:T(8,128)S(1)}) custom-call(f32[256,512]{1,0:T(8,128)S(1)} %copy-done.1, f32[256,128]{1,0:T(8,128)S(1)} %collective-permute-done.1.core_side, f32[256,128]{1,0:T(8,128)S(1)} %collective-permute-done.2.far_side, ...), custom_call_target="tpu_custom_call" | custom-call | flops 1342177280 | bytes 4194304 | tf_op jit(solution)/shard_map/smooth/pallas_call | solution.py:354
  33.6 0.0 collective-permute-done.asked
  33.6 2.9 %collective-permute-done.9.refs_6_.refs_7_ = bf16[512,256]{1,0:T(8,128)(2,1)S(1)} collective-permute-done((bf16[512,256]{1,0:T(8,128)(2,1)S(1)}, bf16[512,256]{1,0:T(8,128)(2,1)S(1)}, u32[]{:S(2)}, u32[]{:S(2)}) %collective-permute-start.9) | collective-permute-done | bytes 262176 | tf_op jit(solution)/shard_map/ppermute | solution.py:313
  36.5 0.0 collective-permute-done.8.refs_5_
  36.5 0.0 copy-done
  36.5 0.8 pack.2
  37.3 0.0 copy-start.2
  37.3 0.0 copy-start.4
  37.3 0.1 collective-permute-start.10
  37.4 0.8 pack.3
  38.3 0.5 collective-permute-start.11
  38.8 3.2 %collective-permute-done.6.refs_6_ = bf16[512,256]{1,0:T(8,128)(2,1)S(1)} collective-permute-done((bf16[512,256]{1,0:T(8,128)(2,1)S(1)}, bf16[512,256]{1,0:T(8,128)(2,1)S(1)}, u32[]{:S(2)}, u32[]{:S(2)}) %collective-permute-start.6) | collective-permute-done | bytes 262176 | tf_op jit(solution)/shard_map/ppermute | solution.py:313
  42.0 0.0 collective-permute-start.12
  42.0 1.5 %collective-permute-done.12.late_theirs = bf16[512,256]{1,0:T(8,128)(2,1)S(1)} collective-permute-done((bf16[512,256]{1,0:T(8,128)(2,1)S(1)}, bf16[512,256]{1,0:T(8,128)(2,1)S(1)}, u32[]{:S(2)}, u32[]{:S(2)}) %collective-permute-start.12) | collective-permute-done | bytes 262176 | tf_op jit(solution)/shard_map/ppermute | solution.py:313
  43.5 0.0 collective-permute-done.10.packed
  43.5 0.0 collective-permute-done.11.packed_rest
  43.6 4.0 %session.1 = (f32[256,512]{1,0:T(8,128)S(1)}, bf16[256,256]{1,0:T(8,128)(2,1)S(1)}, bf16[2304,256]{1,0:T(8,128)(2,1)S(1)}) custom-call(s32[2,8]{1,0:T(2,128)S(1)} %add_bitcast_fusion.ids, s32[2,4,8]{2,1,0:T(4,128)S(1)} %bitcast.5, bf16[256,512]{1,0:T(8,128)(2,1)S(1)} %get-tuple-element.44.smoothed, bf16[16,128,512]{2,1,0:T(8,128)(2,1)S(1)} %bitcast.4, ...), custom_call_target="tpu_custom_call" | custom-call | flops 1610612736 | bytes 8388608 | tf_op jit(solution)/shard_map/session/pallas_call | solution.py:388
  47.6 0.2 collective-permute-start.13
  47.8 2.7 %collective-permute-done.13.got.core_side = bf16[2304,256]{1,0:T(8,128)(2,1)S(1)} collective-permute-done((bf16[2304,256]{1,0:T(8,128)(2,1)S(1)}, bf16[2304,256]{1,0:T(8,128)(2,1)S(1)}, u32[]{:S(2)}, u32[]{:S(2)}) %collective-permute-start.13) | collective-permute-done | bytes 1179680 | tf_op jit(solution)/shard_map/ppermute | solution.py:313
  50.5 1.2 %merge_late.1 = bf16[512,256]{1,0:T(8,128)(2,1)S(1)} custom-call(s32[2,8]{1,0:T(2,128)S(1)} %add_bitcast_fusion.ids, s32[2,8]{1,0:T(2,128)S(1)} %collective-permute-done.asked, bf16[2304,256]{1,0:T(8,128)(2,1)S(1)} %get-tuple-element.49.own, bf16[2304,256]{1,0:T(8,128)(2,1)S(1)} %collective-permute-done.13.got.core_side), custom_call_target="tpu_custom_call" | custom-call | bytes 1048576 | tf_op jit(solution)/shard_map/merge_late/pallas_call | solution.py:418
  51.7 2.5 %collective-permute-start.15 = (bf16[512,256]{1,0:T(8,128)(2,1)S(1)}, bf16[512,256]{1,0:T(8,128)(2,1)S(1)}, u32[]{:S(2)}, u32[]{:S(2)}) collective-permute-start(bf16[512,256]{1,0:T(8,128)(2,1)S(1)} %merge_late.1), channel_id=1, source_target_pairs={{0,2},{1,3},{2,0},{3,1},{4,6},{5,7},{6,4},{7,5},{8,10},{9,11},{10,... | collective-permute-start | bytes 786440 | tf_op jit(solution)/shard_map/ppermute | solution.py:313
  54.2 0.7 collective-permute-start.14
  54.9 1.9 %merge.1 = (f32[512,256]{1,0:T(8,128)S(1)}, f32[512,256]{1,0:T(8,128)S(1)}, f32[512,256]{1,0:T(8,128)S(1)}, f32[512,256]{1,0:T(8,128)S(1)}, bf16[512,256]{1,0:T(...) custom-call(s32[2,8]{1,0:T(2,128)S(1)} %add_bitcast_fusion.ids, ...), custom_call_target="tpu_custom_call" | custom-call | bytes 5242880 | tf_op jit(solution)/shard_map/merge/pallas_call | solution.py:431
  56.8 0.0 collective-permute-done.14.far_side
  56.8 0.0 copy-start.6
  56.8 8.6 %collective-permute-start.20 = (bf16[512,256]{1,0:T(8,128)(2,1)S(1)}, bf16[512,256]{1,0:T(8,128)(2,1)S(1)}, u32[]{:S(2)}, u32[]{:S(2)}) collective-permute-start(bf16[512,256]{1,0:T(8,128)(2,1)S(1)} %get-tuple-element.71), channel_id=1, source_target_pairs={{0,2},{1,3},{2,0},{3,1},{4,6},{5,7},{6,4},{7,5},{8,10},{9,11},{10,... | collective-permute-start | bytes 786440 | tf_op jit(solution)/shard_map/ppermute | solution.py:313
  65.4 0.0 collective-permute-done.15
  65.4 0.1 collective-permute-start.17
  65.5 0.1 add_convert_fusion.2
  65.5 0.7 collective-permute-start.18
  66.3 2.0 %collective-permute-start.16 = (bf16[512,256]{1,0:T(8,128)(2,1)S(1)}, bf16[512,256]{1,0:T(8,128)(2,1)S(1)}, u32[]{:S(2)}, u32[]{:S(2)}) collective-permute-start(bf16[512,256]{1,0:T(8,128)(2,1)S(1)} %get-tuple-element.65), channel_id=1, source_target_pairs={{0,2},{1,3},{2,0},{3,1},{4,6},{5,7},{6,4},{7,5},{8,10},{9,11},{10,... | collective-permute-start | bytes 786440 | tf_op jit(solution)/shard_map/ppermute | solution.py:313
  68.2 4.4 %collective-permute-done.20 = bf16[512,256]{1,0:T(8,128)(2,1)S(1)} collective-permute-done((bf16[512,256]{1,0:T(8,128)(2,1)S(1)}, bf16[512,256]{1,0:T(8,128)(2,1)S(1)}, u32[]{:S(2)}, u32[]{:S(2)}) %collective-permute-start.20) | collective-permute-done | bytes 262176 | tf_op jit(solution)/shard_map/ppermute | solution.py:313
  72.6 0.1 add_convert_fusion
  72.7 0.1 collective-permute-start.21
  72.7 5.5 %collective-permute-done.17 = bf16[512,256]{1,0:T(8,128)(2,1)S(1)} collective-permute-done((bf16[512,256]{1,0:T(8,128)(2,1)S(1)}, bf16[512,256]{1,0:T(8,128)(2,1)S(1)}, u32[]{:S(2)}, u32[]{:S(2)}) %collective-permute-start.17) | collective-permute-done | bytes 262176 | tf_op jit(solution)/shard_map/ppermute | solution.py:313
  78.2 0.0 collective-permute-done.18
  78.2 0.1 add_convert_fusion.1
  78.3 0.7 collective-permute-start.19
  79.0 2.7 %unsmooth.1 = f32[256,512]{1,0:T(8,128)} custom-call(f32[256,512]{1,0:T(8,128)S(1)} %get-tuple-element.48.mid, bf16[2304,256]{1,0:T(8,128)(2,1)S(1)} %collective-permute-done.13.got.core_side, bf16[256,256]{1,0:T(8,128)(2,1)S(1)} %collective-permute-done.14.far_side, f32[256,256]{1,0:T(8,128)S(1)} %get-tuple-element.59.base, ...), custom_call_target="tpu_custom_call" | custom-call | flops 1342177280 | bytes 4194304 | tf_op jit(solution)/shard_map/unsmooth/pallas_call | solution.py:462
  81.7 0.8 collective-permute-done.16
  82.5 0.0 collective-permute-done.21
  82.5 4.5 %collective-permute-done.19 = bf16[512,256]{1,0:T(8,128)(2,1)S(1)} collective-permute-done((bf16[512,256]{1,0:T(8,128)(2,1)S(1)}, bf16[512,256]{1,0:T(8,128)(2,1)S(1)}, u32[]{:S(2)}, u32[]{:S(2)}) %collective-permute-start.19) | collective-permute-done | bytes 262176 | tf_op jit(solution)/shard_map/ppermute | solution.py:313
  87.0 0.9 %convert_add_fusion = f32[512,256]{1,0:T(8,128)} fusion(bf16[512,256]{1,0:T(8,128)(2,1)S(1)} %collective-permute-done.21, bf16[512,256]{1,0:T(8,128)(2,1)S(1)} %collective-permute-done.19, f32[512,256]{1,0:T(8,128)S(1)} %get-tuple-element.62, bf16[512,256]{1,0:T(8,128)(2,1)S(1)} %collective-permute-done.16), kind=kLoop, calls=%fused_computation | loop fusion | flops 786432 | bytes 1835008 | tf_op jit(solution)/shard_map/add | solution.py:460
  (7 shorter events, 0.0 us)
Async XLA Ops:
  0.6 9.6 %collective-permute-start.4 = (bf16[512,256]{1,0:T(8,128)(2,1)}, bf16[512,256]{1,0:T(8,128)(2,1)S(1)}, u32[]{:S(2)}, u32[]{:S(2)}) collective-permute-start(bf16[512,256]{1,0:T(8,128)(2,1)} %refs_0_.5), channel_id=1, source_target_pairs={{0,2},{1,3},{2,0},{3,1},{4,6},{5,7},{6,4},{7,5},{8,10},{9,11},{10,... | collective-permute-start | bytes 786440 | tf_op jit(solution)/shard_map/ppermute | solution.py:313
  3.7 11.3 %collective-permute-start.3 = (bf16[512,256]{1,0:T(8,128)(2,1)}, bf16[512,256]{1,0:T(8,128)(2,1)S(1)}, u32[]{:S(2)}, u32[]{:S(2)}) collective-permute-start(bf16[512,256]{1,0:T(8,128)(2,1)} %refs_0_.5), channel_id=1, source_target_pairs={{0,4},{1,5},{2,6},{3,7},{4,8},{5,9},{6,10},{7,11},{8,12},{9,13},{1... | collective-permute-start | bytes 786440 | tf_op jit(solution)/shard_map/ppermute | solution.py:313
  5.2 18.4 %collective-permute-start.7 = (bf16[512,256]{1,0:T(8,128)(2,1)}, bf16[512,256]{1,0:T(8,128)(2,1)S(1)}, u32[]{:S(2)}, u32[]{:S(2)}) collective-permute-start(bf16[512,256]{1,0:T(8,128)(2,1)} %refs_0_.5), channel_id=1, source_target_pairs={{0,12},{1,13},{2,14},{3,15},{4,0},{5,1},{6,2},{7,3},{8,4},{9,5},{1... | collective-permute-start | bytes 786440 | tf_op jit(solution)/shard_map/ppermute | solution.py:313
  14.9 10.0 %collective-permute-start.5 = (bf16[512,256]{1,0:T(8,128)(2,1)S(1)}, bf16[512,256]{1,0:T(8,128)(2,1)S(1)}, u32[]{:S(2)}, u32[]{:S(2)}) collective-permute-start(bf16[512,256]{1,0:T(8,128)(2,1)S(1)} %collective-permute-done.3.refs_1_), channel_id=1, source_target_pairs={{0,4},{1,5},{2,6},{3,7},{4,8},{5,9},{6,10},{7,11},{8,12},{9,13},{1... | collective-permute-start | bytes 786440 | tf_op jit(solution)/shard_map/ppermute | solution.py:313
  15.9 8.5 %collective-permute-start.2 = (f32[256,128]{1,0:T(8,128)S(1)}, f32[256,128]{1,0:T(8,128)S(1)}, u32[]{:S(2)}, u32[]{:S(2)}) collective-permute-start(f32[256,128]{1,0:T(8,128)S(1)} %get-tuple-element.72), channel_id=1, source_target_pairs={{1,2},{3,4},{5,6},{7,8},{9,10},{11,12},{13,14},{2,1},{4,3},{6,5},{... | collective-permute-start | bytes 393224 | tf_op jit(solution)/shard_map/ppermute | solution.py:313
  16.6 7.9 %collective-permute-start.1 = (f32[256,128]{1,0:T(8,128)S(1)}, f32[256,128]{1,0:T(8,128)S(1)}, u32[]{:S(2)}, u32[]{:S(2)}) collective-permute-start(f32[256,128]{1,0:T(8,128)S(1)} %get-tuple-element.73), channel_id=1, source_target_pairs={{0,1},{1,0},{2,3},{3,2},{4,5},{5,4},{6,7},{7,6},{8,9},{9,8},{10,11... | collective-permute-start | bytes 393224 | tf_op jit(solution)/shard_map/ppermute | solution.py:313
  18.3 18.2 %collective-permute-start.8 = (bf16[512,256]{1,0:T(8,128)(2,1)S(1)}, bf16[512,256]{1,0:T(8,128)(2,1)S(1)}, u32[]{:S(2)}, u32[]{:S(2)}) collective-permute-start(bf16[512,256]{1,0:T(8,128)(2,1)S(1)} %collective-permute-done.3.refs_1_), channel_id=1, source_target_pairs={{0,2},{1,3},{2,0},{3,1},{4,6},{5,7},{6,4},{7,5},{8,10},{9,11},{10,... | collective-permute-start | bytes 786440 | tf_op jit(solution)/shard_map/ppermute | solution.py:313
  23.7 12.9 %collective-permute-start.9 = (bf16[512,256]{1,0:T(8,128)(2,1)S(1)}, bf16[512,256]{1,0:T(8,128)(2,1)S(1)}, u32[]{:S(2)}, u32[]{:S(2)}) collective-permute-start(bf16[512,256]{1,0:T(8,128)(2,1)S(1)} %collective-permute-done.7.refs_3_), channel_id=1, source_target_pairs={{0,2},{1,3},{2,0},{3,1},{4,6},{5,7},{6,4},{7,5},{8,10},{9,11},{10,... | collective-permute-start | bytes 786440 | tf_op jit(solution)/shard_map/ppermute | solution.py:313
  24.4 12.1 %copy-start = (bf16[512,256]{1,0:T(8,128)(2,1)S(1)}, bf16[512,256]{1,0:T(8,128)(2,1)}, u32[]{:S(2)}) copy-start(bf16[512,256]{1,0:T(8,128)(2,1)} %refs_0_.5) | copy-start | bytes 786436
  24.4 9.2 %collective-permute-start = (s32[2,8]{1,0:T(2,128)S(1)}, s32[2,8]{1,0:T(2,128)S(1)}, u32[]{:S(2)}, u32[]{:S(2)}) collective-permute-start(s32[2,8]{1,0:T(2,128)S(1)} %add_bitcast_fusion.ids), channel_id=1, source_target_pairs={{0,1},{1,0},{2,3},{3,2},{4,5},{5,4},{6,7},{7,6},{8,9},{9,8},{10,11... | collective-permute-start | bytes 200 | tf_op jit(solution)/shard_map/ppermute | solution.py:313
  24.9 17.1 %collective-permute-start.6 = (bf16[512,256]{1,0:T(8,128)(2,1)S(1)}, bf16[512,256]{1,0:T(8,128)(2,1)S(1)}, u32[]{:S(2)}, u32[]{:S(2)}) collective-permute-start(bf16[512,256]{1,0:T(8,128)(2,1)S(1)} %collective-permute-done.5.refs_2_), channel_id=1, source_target_pairs={{0,2},{1,3},{2,0},{3,1},{4,6},{5,7},{6,4},{7,5},{8,10},{9,11},{10,... | collective-permute-start | bytes 786440 | tf_op jit(solution)/shard_map/ppermute | solution.py:313
  27.6 1.0 %copy-start.1 = (f32[256,512]{1,0:T(8,128)S(1)}, f32[256,512]{1,0:T(8,128)}, u32[]{:S(2)}) copy-start(f32[256,512]{1,0:T(8,128)} %mid.1) | copy-start | bytes 1572868
  28.7 0.9 %copy-start.3 = (f32[256,256]{1,0:T(8,128)S(1)}, f32[256,256]{1,0:T(8,128)}, u32[]{:S(2)}) copy-start(f32[256,256]{1,0:T(8,128)} %taps.1) | copy-start | bytes 786436
  29.6 1.4 %copy-start.5 = (bf16[3072,256]{1,0:T(8,128)(2,1)S(1)}, bf16[3072,256]{1,0:T(8,128)(2,1)}, u32[]{:S(2)}) copy-start(bf16[3072,256]{1,0:T(8,128)(2,1)} %constant.22.clone.table) | copy-start | bytes 4718596
  37.3 6.2 %copy-start.2 = (bf16[2,8,128,512]{3,2,1,0:T(8,128)(2,1)S(1)}, bf16[2,8,128,512]{3,2,1,0:T(8,128)(2,1)}, u32[]{:S(2)}) copy-start(bf16[2,8,128,512]{3,2,1,0:T(8,128)(2,1)} %param.11) | copy-start | bytes 6291460
  37.3 6.2 %copy-start.4 = (s32[2,8,4]{1,2,0:T(4,128)S(1)}, s32[2,8,4]{1,2,0:T(4,128)}, u32[]{:S(2)}) copy-start(s32[2,8,4]{1,2,0:T(4,128)} %param.14) | copy-start | bytes 772
  37.3 6.2 %collective-permute-start.10 = (bf16[1024,256]{1,0:T(8,128)(2,1)S(1)}, bf16[1024,256]{1,0:T(8,128)(2,1)S(1)}, u32[]{:S(2)}, u32[]{:S(2)}) collective-permute-start(bf16[1024,256]{1,0:T(8,128)(2,1)S(1)} %pack.2), channel_id=1, source_target_pairs={{0,1},{1,0},{2,3},{3,2},{4,5},{5,4},{6,7},{7,6},{8,9},{9,8},{10,11... | collective-permute-start | bytes 1572872 | tf_op jit(solution)/shard_map/ppermute | solution.py:313
  38.3 5.3 %collective-permute-start.11 = (bf16[1024,256]{1,0:T(8,128)(2,1)S(1)}, bf16[1024,256]{1,0:T(8,128)(2,1)S(1)}, u32[]{:S(2)}, u32[]{:S(2)}) collective-permute-start(bf16[1024,256]{1,0:T(8,128)(2,1)S(1)} %pack.3), channel_id=1, source_target_pairs={{0,1},{1,0},{2,3},{3,2},{4,5},{5,4},{6,7},{7,6},{8,9},{9,8},{10,11... | collective-permute-start | bytes 1572872 | tf_op jit(solution)/shard_map/ppermute | solution.py:313
  42.0 1.5 %collective-permute-start.12 = (bf16[512,256]{1,0:T(8,128)(2,1)S(1)}, bf16[512,256]{1,0:T(8,128)(2,1)S(1)}, u32[]{:S(2)}, u32[]{:S(2)}) collective-permute-start(bf16[512,256]{1,0:T(8,128)(2,1)S(1)} %collective-permute-done.6.refs_6_), channel_id=1, source_target_pairs={{0,1},{1,0},{2,3},{3,2},{4,5},{5,4},{6,7},{7,6},{8,9},{9,8},{10,11... | collective-permute-start | bytes 786440 | tf_op jit(solution)/shard_map/ppermute | solution.py:313
  47.6 2.9 %collective-permute-start.13 = (bf16[2304,256]{1,0:T(8,128)(2,1)S(1)}, bf16[2304,256]{1,0:T(8,128)(2,1)S(1)}, u32[]{:S(2)}, u32[]{:S(2)}) collective-permute-start(bf16[2304,256]{1,0:T(8,128)(2,1)S(1)} %get-tuple-element.49.own), channel_id=1, source_target_pairs={{0,1},{1,0},{2,3},{3,2},{4,5},{5,4},{6,7},{7,6},{8,9},{9,8},{10,11... | collective-permute-start | bytes 3538952 | tf_op jit(solution)/shard_map/ppermute | solution.py:313
  51.7 13.7 %collective-permute-start.15 = (bf16[512,256]{1,0:T(8,128)(2,1)S(1)}, bf16[512,256]{1,0:T(8,128)(2,1)S(1)}, u32[]{:S(2)}, u32[]{:S(2)}) collective-permute-start(bf16[512,256]{1,0:T(8,128)(2,1)S(1)} %merge_late.1), channel_id=1, source_target_pairs={{0,2},{1,3},{2,0},{3,1},{4,6},{5,7},{6,4},{7,5},{8,10},{9,11},{10,... | collective-permute-start | bytes 786440 | tf_op jit(solution)/shard_map/ppermute | solution.py:313
  54.2 2.6 %collective-permute-start.14 = (bf16[256,256]{1,0:T(8,128)(2,1)S(1)}, bf16[256,256]{1,0:T(8,128)(2,1)S(1)}, u32[]{:S(2)}, u32[]{:S(2)}) collective-permute-start(bf16[256,256]{1,0:T(8,128)(2,1)S(1)} %get-tuple-element.50), channel_id=1, source_target_pairs={{1,2},{3,4},{5,6},{7,8},{9,10},{11,12},{13,14},{2,1},{4,3},{6,5},{... | collective-permute-start | bytes 393224 | tf_op jit(solution)/shard_map/ppermute | solution.py:313
  56.8 22.2 %copy-start.6 = (bf16[3072,256]{1,0:T(8,128)(2,1)S(1)}, bf16[3072,256]{1,0:T(8,128)(2,1)}, u32[]{:S(2)}) copy-start(bf16[3072,256]{1,0:T(8,128)(2,1)} %constant.22.clone.table) | copy-start | bytes 4718596
  56.8 15.8 %collective-permute-start.20 = (bf16[512,256]{1,0:T(8,128)(2,1)S(1)}, bf16[512,256]{1,0:T(8,128)(2,1)S(1)}, u32[]{:S(2)}, u32[]{:S(2)}) collective-permute-start(bf16[512,256]{1,0:T(8,128)(2,1)S(1)} %get-tuple-element.71), channel_id=1, source_target_pairs={{0,2},{1,3},{2,0},{3,1},{4,6},{5,7},{6,4},{7,5},{8,10},{9,11},{10,... | collective-permute-start | bytes 786440 | tf_op jit(solution)/shard_map/ppermute | solution.py:313
  65.4 12.8 %collective-permute-start.17 = (bf16[512,256]{1,0:T(8,128)(2,1)S(1)}, bf16[512,256]{1,0:T(8,128)(2,1)S(1)}, u32[]{:S(2)}, u32[]{:S(2)}) collective-permute-start(bf16[512,256]{1,0:T(8,128)(2,1)S(1)} %get-tuple-element.67), channel_id=1, source_target_pairs={{0,2},{1,3},{2,0},{3,1},{4,6},{5,7},{6,4},{7,5},{8,10},{9,11},{10,... | collective-permute-start | bytes 786440 | tf_op jit(solution)/shard_map/ppermute | solution.py:313
  65.5 12.7 %collective-permute-start.18 = (bf16[512,256]{1,0:T(8,128)(2,1)S(1)}, bf16[512,256]{1,0:T(8,128)(2,1)S(1)}, u32[]{:S(2)}, u32[]{:S(2)}) collective-permute-start(bf16[512,256]{1,0:T(8,128)(2,1)S(1)} %add_convert_fusion.2), channel_id=1, source_target_pairs={{0,4},{1,5},{2,6},{3,7},{4,8},{5,9},{6,10},{7,11},{8,12},{9,13},{1... | collective-permute-start | bytes 786440 | tf_op jit(solution)/shard_map/ppermute | solution.py:313
  66.3 16.2 %collective-permute-start.16 = (bf16[512,256]{1,0:T(8,128)(2,1)S(1)}, bf16[512,256]{1,0:T(8,128)(2,1)S(1)}, u32[]{:S(2)}, u32[]{:S(2)}) collective-permute-start(bf16[512,256]{1,0:T(8,128)(2,1)S(1)} %get-tuple-element.65), channel_id=1, source_target_pairs={{0,2},{1,3},{2,0},{3,1},{4,6},{5,7},{6,4},{7,5},{8,10},{9,11},{10,... | collective-permute-start | bytes 786440 | tf_op jit(solution)/shard_map/ppermute | solution.py:313
  72.7 9.8 %collective-permute-start.21 = (bf16[512,256]{1,0:T(8,128)(2,1)S(1)}, bf16[512,256]{1,0:T(8,128)(2,1)S(1)}, u32[]{:S(2)}, u32[]{:S(2)}) collective-permute-start(bf16[512,256]{1,0:T(8,128)(2,1)S(1)} %add_convert_fusion), channel_id=1, source_target_pairs={{0,12},{1,13},{2,14},{3,15},{4,0},{5,1},{6,2},{7,3},{8,4},{9,5},{1... | collective-permute-start | bytes 786440 | tf_op jit(solution)/shard_map/ppermute | solution.py:313
  78.3 8.7 %collective-permute-start.19 = (bf16[512,256]{1,0:T(8,128)(2,1)S(1)}, bf16[512,256]{1,0:T(8,128)(2,1)S(1)}, u32[]{:S(2)}, u32[]{:S(2)}) collective-permute-start(bf16[512,256]{1,0:T(8,128)(2,1)S(1)} %add_convert_fusion.1), channel_id=1, source_target_pairs={{0,4},{1,5},{2,6},{3,7},{4,8},{5,9},{6,10},{7,11},{8,12},{9,13},{1... | collective-permute-start | bytes 786440 | tf_op jit(solution)/shard_map/ppermute | solution.py:313

commit v7 on v6

--- a/solution.py
+++ b/solution.py
@@ -112,14 +112,23 @@
     out[...] = filtered(signal, (base, kr, ki), 1.0, held, (0, 1)).astype(out.dtype)
 
 
-def unsmooth_kernel(mid, core_side, far_side, base, kr, ki, table, out, held, sem):
+def unsmooth_kernel(mid, got, back, rise, fall, base, kr, ki, table, out, held, sem):
     copy = pltpu.make_async_copy(table, held, sem)
     copy.start()
-    width = far_side.shape[1] // 2
-    first = core_side.shape[0] - far_side.shape[0]
-    core = core_side[first:, :width].astype(F32) + core_side[first:, width:].astype(F32)
-    far = far_side[:, :width].astype(F32) + far_side[:, width:].astype(F32)
-    thirds = thirds_of(mid[...], core, far)
+    rows = mid.shape[0]
+    width = got.shape[1] // 2
+    me = lax.axis_index("tm")
+    count = lax.axis_size("tm")
+    first = got.shape[0] - 2 * rows
+    core = got[first : first + rows]
+    near, below, above = (ref[ref.shape[0] - rows :] for ref in (back, rise, fall))
+    equal = (me >> 1) & 1 == me & 1
+    far = jnp.where(equal, jnp.where(me & 1 == 0, below, above), near).astype(F32)
+    far = jnp.where(jnp.logical_or(me == 0, me == count - 1), 0.0, far)
+    core = core.astype(F32)
+    thirds = thirds_of(
+        mid[...], core[:, :width] + core[:, width:], far[:, :width] + far[:, width:]
+    )
     copy.wait()
     signal = spectrum_of(thirds, held)
     out[...] = filtered(signal, (base[...], kr[...], ki[...]), -1.0, held, (1, 2))
@@ -182,8 +191,8 @@
 def session_kernel(
     entries, group, late, ids, mask, smoothed, recorded, packed, packed_rest, late_theirs, *refs
 ):
-    pieces = refs[:-5]
-    grad, far_side, terms, rows, resid = refs[-5:]
+    pieces = refs[:-4]
+    grad, terms, rows, resid = refs[-4:]
     blocks = pieces[0].shape[0] // BLK
     bins = smoothed.shape[1]
     top = ids.shape[1]
@@ -237,17 +246,18 @@
         return 0
 
     lax.fori_loop(0, entries // group, step, 0)
-    width = far_side.shape[1] // 2
+    latent_dim, width = grad.shape[0], rows.shape[1] // 2
     even = me & 1 == 0
     later, earlier = grad[:, bins - width :], grad[:, :width]
     core_edge, far_edge = jnp.where(even, later, earlier), jnp.where(even, earlier, later)
-    target = pl.ds(entries * BLK, far_side.shape[0])
-    terms[target] = jnp.concatenate(parts(core_edge), axis=1)
-    far_side[...] = jnp.concatenate(parts(far_edge), axis=1)
+    for k, edge in enumerate((core_edge, far_edge)):
+        target = pl.ds(entries * BLK + k * latent_dim, latent_dim)
+        terms[target] = jnp.concatenate(parts(edge), axis=1)
 
 
 def merge_late_kernel(entries, late, ids, asked, own, got, out, sums):
-    blocks = out.shape[0] // BLK
+    chunk = sums.shape[0]
+    blocks = chunk // BLK
     me = lax.axis_index("tm")
     sums[...] = jnp.zeros_like(sums)
 
@@ -263,7 +273,8 @@
         return 0
 
     lax.fori_loop(0, entries, add, 0)
-    out[...] = sums[...].astype(out.dtype)
+    out[:chunk] = sums[...].astype(out.dtype)
+    out[chunk:] = got[got.shape[0] - (out.shape[0] - chunk) :]
 
 
 def merge_kernel(entries, late, ids, asked, own, got, *refs):
@@ -297,6 +308,12 @@
     lax.fori_loop(0, entries, add, 0)
     for q, out in enumerate(outs):
         out[...] = sums[q * chunk : (q + 1) * chunk].astype(out.dtype)
+
+
+def hop_kernel(total, came, back, out):
+    chunk = total.shape[0]
+    out[:chunk] = (total[...] + came[:chunk].astype(F32)).astype(out.dtype)
+    out[chunk:] = back[chunk:]
 
 
 def local(latents, kernel, loadings, recorded, owner_ids, local_ids, recorded_mask):
@@ -344,9 +361,6 @@
         if r != half:
             across[r] = flip(straight[r], 2)
 
-    core_side, far_side, straight[half] = lax.optimization_barrier(
-        (core_side, far_side, straight[half])
-    )
     table = dft_tables(2 * halfwidth)
     table_scratch = [pltpu.VMEM(table.shape, BF16), pltpu.SemaphoreType.DMA(())]
     mxu = 40 * 2 * latent_dim * (2 * halfwidth) ** 2
@@ -384,16 +398,15 @@
     pieces = straight + across
 
     group = 4
-    extended = jax.ShapeDtypeStruct((entries * BLK + latent_dim, latent_dim), BF16)
-    grad, far_side, terms = pl.pallas_call(
+    extended = jax.ShapeDtypeStruct((entries * BLK + 2 * latent_dim, latent_dim), BF16)
+    grad, terms = pl.pallas_call(
         functools.partial(session_kernel, entries, group, late),
         out_shape=(
             jax.ShapeDtypeStruct((latent_dim, bins), F32),
-            jax.ShapeDtypeStruct((latent_dim, 2 * halfwidth), BF16),
             extended,
         ),
         in_specs=[smem] * 2 + [VMEM] * (5 + len(pieces)),
-        out_specs=(VMEM,) * 3,
+        out_specs=(VMEM,) * 2,
         scratch_shapes=[
             pltpu.VMEM((group * BLK, latent_dim), BF16),
             pltpu.VMEM((group * BLK, bins), BF16),
@@ -417,7 +430,7 @@
     narrow = jax.ShapeDtypeStruct((chunk, latent_dim), BF16)
     sent = pl.pallas_call(
         functools.partial(merge_late_kernel, entries, late),
-        out_shape=narrow,
+        out_shape=jax.ShapeDtypeStruct((chunk + latent_dim, latent_dim), BF16),
         in_specs=[smem] * 2 + [VMEM] * 2,
         out_specs=VMEM,
         scratch_shapes=[pltpu.VMEM((chunk, latent_dim), F32)],
@@ -425,9 +438,9 @@
         cost_estimate=pl.CostEstimate(flops=0, bytes_accessed=2**20, transcendentals=0),
         name="merge_late",
     )(ids, asked, terms, got)
+    wide = jax.ShapeDtypeStruct((chunk, latent_dim), F32)
+    sent, ids = lax.optimization_barrier((sent, ids))
     back = flip(sent, 2)
-    far_side = permute(far_side, odd_even)
-    wide = jax.ShapeDtypeStruct((chunk, latent_dim), F32)
     merged = pl.pallas_call(
         functools.partial(merge_kernel, entries, late),
         out_shape=(wide,) * chain + (narrow,) * (chain - 1),
@@ -438,37 +451,40 @@
         cost_estimate=pl.CostEstimate(flops=0, bytes_accessed=5 * 2**20, transcendentals=0),
         name="merge",
     )(ids, asked, terms, got)
-    merged = list(merged)
-    far_side, *merged = lax.optimization_barrier((far_side, *merged))
     crossed = {r: merged[chain + r - (r > half)] for r in range(chain) if r != half}
-    first = [r for r in range(half + 1, chain)]
-    other = {r: flip(crossed[r], 2) for r in first}
-    rest = [r for r in crossed if r not in first]
-    back, *held = lax.optimization_barrier((back, *(crossed[r] for r in rest)))
-    other[half] = back
-    for r, part in zip(rest, held):
-        other[r] = flip(part, 2)
-    totals = [merged[r] + other[r].astype(F32) for r in range(chain)]
-    rise = totals[half]
-    for r in range(half - 1, -1, -1):
-        rise = totals[r] + rotate(rise.astype(BF16), 1).astype(F32)
-    loading_grad = rise
-    if half > 1:
-        fall = totals[half + 1]
-        for r in range(half + 2, chain):
-            fall = totals[r] + rotate(fall.astype(BF16), -1).astype(F32)
-        loading_grad = loading_grad + rotate(fall.astype(BF16), -1).astype(F32)
+    other = {r: flip(part, 2) for r, part in crossed.items()}
+
+    def hop(total, came):
+        return pl.pallas_call(
+            hop_kernel,
+            out_shape=jax.ShapeDtypeStruct(back.shape, BF16),
+            in_specs=[VMEM] * 3,
+            out_specs=VMEM,
+            compiler_params=pltpu.CompilerParams(vmem_limit_bytes=8 * MIB),
+            cost_estimate=pl.CostEstimate(flops=2 * 10**9, bytes_accessed=MIB, transcendentals=0),
+            name="hop",
+        )(total, came, back)
+
+    rise = hop(merged[half], back)
+    totals = {r: merged[r] + other[r].astype(F32) for r in other}
+    rise_side = rise = rotate(rise, 1)
+    for r in range(half - 1, 0, -1):
+        rise = rotate((totals[r] + rise[:chunk].astype(F32)).astype(BF16), 1)
+    fall_side = fall = rotate(hop(merged[half + 1], other[half + 1]), -1)
+    for r in range(half + 2, chain):
+        fall = rotate((totals[r] + fall[:chunk].astype(F32)).astype(BF16), -1)
+    loading_grad = totals[0] + rise[:chunk].astype(F32) + fall[:chunk].astype(F32)
 
     latent_grad = pl.pallas_call(
         unsmooth_kernel,
         out_shape=jax.ShapeDtypeStruct((latent_dim, bins), F32),
-        in_specs=[VMEM] * 6 + [HBM],
+        in_specs=[VMEM] * 8 + [HBM],
         out_specs=VMEM,
         scratch_shapes=table_scratch,
         compiler_params=pltpu.CompilerParams(vmem_limit_bytes=16 * MIB),
         cost_estimate=pl.CostEstimate(flops=mxu, bytes_accessed=4 * 2**20, transcendentals=0),
         name="unsmooth",
-    )(grad, got, far_side, *spectrum, table)
+    )(grad, got, back, rise_side, fall_side, *spectrum, table)
     return latent_grad, loading_grad
 
 

time: 88.2 us -> 84.8 us (0.961)
  starting transfers between devices: 33.4 us -> 21.8 us
  waiting for transfers between devices: 33.5 us -> 41.6 us
    ppermute x22 -> x21, starting transfers between devices: 33.4 us -> 21.8 us  [permute(): return lax.ppermute(x, 'tm', pairs)]
    ppermute x22 -> x21, waiting for transfers between devices: 33.5 us -> 41.6 us  [permute(): return lax.ppermute(x, 'tm', pairs)]
  transfers between devices with their start and end apart: 22 -> 21, of which waited for: 11 -> 11; matrix products, arithmetic and copies ran while one was open for 2% -> 2% of each run, Pallas kernels for 10% -> 11%
where the time goes in v7:
time: 84.8 us; the launch traced here: 84.5 us
  waiting for transfers between devices  41.6 us (49%)
  starting transfers between devices  21.8 us (26%)
  Pallas kernels  14.1 us (17%)
  local copies, waits for them, and re-layouts  3.41 us (4%)
  other arithmetic  2.7 us (3%)
    ppermute x21, waiting for transfers between devices, permute(): return lax.ppermute(x, 'tm', pairs)  41.6 us
    ppermute x21, starting transfers between devices, permute(): return lax.ppermute(x, 'tm', pairs)  21.8 us
    pallas_call x1, Pallas kernels, local(): pl.pallas_call(functools.partial(session_kernel, entries, group, late), o...  4 us
    unnamed x14, local copies, waits for them, and re-layouts  3.41 us
    pallas_call x1, Pallas kernels, local(): pl.pallas_call(unsmooth_kernel, out_shape=jax.ShapeDtypeStruct((latent_di...  2.7 us
    pallas_call x1, Pallas kernels, local(): pl.pallas_call(smooth_kernel, out_shape=(jax.ShapeDtypeStruct((latent_dim...  2.55 us
    pallas_call x1, Pallas kernels, local(): pl.pallas_call(functools.partial(merge_kernel, entries, late), out_shape=...  1.95 us
  transfers between devices with their start and end apart: 21, of which 11 were waited for; matrix products, arithmetic and copies ran while one was open for 2% of the time, Pallas kernels for 11%

profile of v7, /device:TPU:0, one launch (start us, length us, event | category | flops | bytes accessed | tf_op | source)
XLA Modules:
  0.0 84.5 jit_solution(12847687609831426444)
XLA Ops:
  0.6 3.0 %collective-permute-start.4 = (bf16[512,256]{1,0:T(8,128)(2,1)}, bf16[512,256]{1,0:T(8,128)(2,1)S(1)}, u32[]{:S(2)}, u32[]{:S(2)}) collective-permute-start(bf16[512,256]{1,0:T(8,128)(2,1)} %refs_0_.5), channel_id=1, source_target_pairs={{0,2},{1,3},{2,0},{3,1},{4,6},{5,7},{6,4},{7,5},{8,10},{9,11},{10,... | collective-permute-start | bytes 786440 | tf_op jit(solution)/shard_map/ppermute | solution.py:330
  3.7 1.6 %collective-permute-start.3 = (bf16[512,256]{1,0:T(8,128)(2,1)}, bf16[512,256]{1,0:T(8,128)(2,1)S(1)}, u32[]{:S(2)}, u32[]{:S(2)}) collective-permute-start(bf16[512,256]{1,0:T(8,128)(2,1)} %refs_0_.5), channel_id=1, source_target_pairs={{0,4},{1,5},{2,6},{3,7},{4,8},{5,9},{6,10},{7,11},{8,12},{9,13},{1... | collective-permute-start | bytes 786440 | tf_op jit(solution)/shard_map/ppermute | solution.py:330
  5.2 2.2 %collective-permute-start.7 = (bf16[512,256]{1,0:T(8,128)(2,1)}, bf16[512,256]{1,0:T(8,128)(2,1)S(1)}, u32[]{:S(2)}, u32[]{:S(2)}) collective-permute-start(bf16[512,256]{1,0:T(8,128)(2,1)} %refs_0_.5), channel_id=1, source_target_pairs={{0,12},{1,13},{2,14},{3,15},{4,0},{5,1},{6,2},{7,3},{8,4},{9,5},{1... | collective-permute-start | bytes 786440 | tf_op jit(solution)/shard_map/ppermute | solution.py:330
  7.5 1.0 %slice_select_fusion = (f32[256,128]{1,0:T(8,128)S(1)}, f32[256,128]{1,0:T(8,128)S(1)}) fusion(f32[256,512]{1,0:T(8,128)} %mid.1, pred[]{:T(512)S(6)} %eq.5), kind=kLoop, calls=%fused_computation.2 | loop fusion | flops 65536 | bytes 524289 | tf_op jit(solution)/shard_map/jit(_where)/select_n | solution.py:348
  8.5 0.7 collective-permute-start.2
  9.2 1.7 %collective-permute-start.1 = (f32[256,128]{1,0:T(8,128)S(1)}, f32[256,128]{1,0:T(8,128)S(1)}, u32[]{:S(2)}, u32[]{:S(2)}) collective-permute-start(f32[256,128]{1,0:T(8,128)S(1)} %get-tuple-element.47), channel_id=1, source_target_pairs={{0,1},{1,0},{2,3},{3,2},{4,5},{5,4},{6,7},{7,6},{8,9},{9,8},{10,11... | collective-permute-start | bytes 393224 | tf_op jit(solution)/shard_map/ppermute | solution.py:330
  10.9 0.0 collective-permute-done.4.refs_4_
  10.9 4.1 %collective-permute-done.3.refs_1_ = bf16[512,256]{1,0:T(8,128)(2,1)S(1)} collective-permute-done((bf16[512,256]{1,0:T(8,128)(2,1)}, bf16[512,256]{1,0:T(8,128)(2,1)S(1)}, u32[]{:S(2)}, u32[]{:S(2)}) %collective-permute-start.3) | collective-permute-done | bytes 262176 | tf_op jit(solution)/shard_map/ppermute | solution.py:330
  14.9 0.3 collective-permute-start.8
  15.2 0.0 collective-permute-start.5
  15.2 4.0 %collective-permute-done.7.refs_3_ = bf16[512,256]{1,0:T(8,128)(2,1)S(1)} collective-permute-done((bf16[512,256]{1,0:T(8,128)(2,1)}, bf16[512,256]{1,0:T(8,128)(2,1)S(1)}, u32[]{:S(2)}, u32[]{:S(2)}) %collective-permute-start.7) | collective-permute-done | bytes 262176 | tf_op jit(solution)/shard_map/ppermute | solution.py:330
  19.3 0.3 collective-permute-start.9
  19.6 0.7 add_bitcast_fusion.ids
  20.3 0.0 collective-permute-done.2.far_side
  20.3 0.0 collective-permute-start
  20.3 0.0 collective-permute-done.1.core_side
  20.3 0.0 copy-start
  20.3 1.4 %copy-done = bf16[3072,256]{1,0:T(8,128)(2,1)S(1)} copy-done((bf16[3072,256]{1,0:T(8,128)(2,1)S(1)}, bf16[3072,256]{1,0:T(8,128)(2,1)}, u32[]{:S(2)}) %copy-start) | copy-done | bytes 1572888
  21.7 1.0 %copy-done.3 = f32[256,512]{1,0:T(8,128)S(1)} copy-done((f32[256,512]{1,0:T(8,128)S(1)}, f32[256,512]{1,0:T(8,128)}, u32[]{:S(2)}) %copy-start.3) | copy-done | bytes 524312
  22.7 0.9 %copy-done.5 = f32[256,256]{1,0:T(8,128)S(1)} copy-done((f32[256,256]{1,0:T(8,128)S(1)}, f32[256,256]{1,0:T(8,128)}, u32[]{:S(2)}) %copy-start.5) | copy-done | bytes 262168
  23.7 2.5 %smooth.1 = (bf16[256,512]{1,0:T(8,128)(2,1)S(1)}, f32[256,256]{1,0:T(8,128)S(1)}, f32[256,256]{1,0:T(8,128)S(1)}, f32[256,256]{1,0:T(8,128)S(1)}) custom-call(f32[256,512]{1,0:T(8,128)S(1)} %copy-done.3, f32[256,128]{1,0:T(8,128)S(1)} %collective-permute-done.1.core_side, f32[256,128]{1,0:T(8,128)S(1)} %collective-permute-done.2.far_side, ...), custom_call_target="tpu_custom_call" | custom-call | flops 1342177280 | bytes 4194304 | tf_op jit(solution)/shard_map/smooth/pallas_call | solution.py:368
  26.2 0.0 collective-permute-done.asked
  26.3 0.0 collective-permute-done.5.refs_2_
  26.3 3.4 %collective-permute-start.6 = (bf16[512,256]{1,0:T(8,128)(2,1)S(1)}, bf16[512,256]{1,0:T(8,128)(2,1)S(1)}, u32[]{:S(2)}, u32[]{:S(2)}) collective-permute-start(bf16[512,256]{1,0:T(8,128)(2,1)S(1)} %collective-permute-done.5.refs_2_), channel_id=1, source_target_pairs={{0,2},{1,3},{2,0},{3,1},{4,6},{5,7},{6,4},{7,5},{8,10},{9,11},{10,... | collective-permute-start | bytes 786440 | tf_op jit(solution)/shard_map/ppermute | solution.py:330
  29.7 0.0 collective-permute-done.9.refs_6_.refs_7_
  29.7 0.0 collective-permute-done.8.refs_5_
  29.7 0.0 copy-done.2
  29.7 0.8 pack.2
  30.5 0.0 copy-start.4
  30.5 0.0 copy-start.6
  30.5 0.1 collective-permute-start.10
  30.6 0.8 pack.3
  31.4 0.6 collective-permute-start.11
  32.0 4.2 %collective-permute-done.6.refs_6_ = bf16[512,256]{1,0:T(8,128)(2,1)S(1)} collective-permute-done((bf16[512,256]{1,0:T(8,128)(2,1)S(1)}, bf16[512,256]{1,0:T(8,128)(2,1)S(1)}, u32[]{:S(2)}, u32[]{:S(2)}) %collective-permute-start.6) | collective-permute-done | bytes 262176 | tf_op jit(solution)/shard_map/ppermute | solution.py:330
  36.2 0.0 collective-permute-start.12
  36.2 1.5 %collective-permute-done.12.late_theirs = bf16[512,256]{1,0:T(8,128)(2,1)S(1)} collective-permute-done((bf16[512,256]{1,0:T(8,128)(2,1)S(1)}, bf16[512,256]{1,0:T(8,128)(2,1)S(1)}, u32[]{:S(2)}, u32[]{:S(2)}) %collective-permute-start.12) | collective-permute-done | bytes 262176 | tf_op jit(solution)/shard_map/ppermute | solution.py:330
  37.7 0.0 collective-permute-done.10.packed
  37.7 0.0 collective-permute-done.11.packed_rest
  37.7 0.0 copy-done.4
  37.7 0.0 copy-done.6
  37.7 4.0 %session.1 = (f32[256,512]{1,0:T(8,128)S(1)}, bf16[2560,256]{1,0:T(8,128)(2,1)S(1)}) custom-call(s32[2,8]{1,0:T(2,128)S(1)} %add_bitcast_fusion.ids, s32[2,4,8]{2,1,0:T(4,128)S(1)} %bitcast.5, bf16[256,512]{1,0:T(8,128)(2,1)S(1)} %get-tuple-element.28.smoothed, bf16[16,128,512]{2,1,0:T(8,128)(2,1)S(1)} %bitcast.4, ...), custom_call_target="tpu_custom_call" | custom-call | flops 1610612736 | bytes 8388608 | tf_op jit(solution)/shard_map/session/pallas_call | solution.py:402
  41.8 0.2 collective-permute-start.13
  41.9 2.9 %collective-permute-done.13.got = bf16[2560,256]{1,0:T(8,128)(2,1)S(1)} collective-permute-done((bf16[2560,256]{1,0:T(8,128)(2,1)S(1)}, bf16[2560,256]{1,0:T(8,128)(2,1)S(1)}, u32[]{:S(2)}, u32[]{:S(2)}) %collective-permute-start.13) | collective-permute-done | bytes 1310752 | tf_op jit(solution)/shard_map/ppermute | solution.py:330
  44.9 1.2 %merge_late.1 = bf16[768,256]{1,0:T(8,128)(2,1)S(1)} custom-call(s32[2,8]{1,0:T(2,128)S(1)} %add_bitcast_fusion.ids, s32[2,8]{1,0:T(2,128)S(1)} %collective-permute-done.asked, bf16[2560,256]{1,0:T(8,128)(2,1)S(1)} %get-tuple-element.33.own, bf16[2560,256]{1,0:T(8,128)(2,1)S(1)} %collective-permute-done.13.got), custom_call_target="tpu_custom_call" | custom-call | bytes 1048576 | tf_op jit(solution)/shard_map/merge_late/pallas_call | solution.py:431
  46.1 1.8 %collective-permute-start.14 = (bf16[768,256]{1,0:T(8,128)(2,1)S(1)}, bf16[768,256]{1,0:T(8,128)(2,1)S(1)}, u32[]{:S(2)}, u32[]{:S(2)}) collective-permute-start(bf16[768,256]{1,0:T(8,128)(2,1)S(1)} %merge_late.1), channel_id=1, source_target_pairs={{0,2},{1,3},{2,0},{3,1},{4,6},{5,7},{6,4},{7,5},{8,10},{9,11},{10,... | collective-permute-start | bytes 1179656 | tf_op jit(solution)/shard_map/ppermute | solution.py:330
  47.9 2.0 %merge.1 = (f32[512,256]{1,0:T(8,128)S(1)}, f32[512,256]{1,0:T(8,128)S(1)}, f32[512,256]{1,0:T(8,128)S(1)}, f32[512,256]{1,0:T(8,128)S(1)}, bf16[512,256]{1,0:T(...) custom-call(s32[2,8]{1,0:T(2,128)S(1)} %add_bitcast_fusion.ids, ...), custom_call_target="tpu_custom_call" | custom-call | bytes 5242880 | tf_op jit(solution)/shard_map/merge/pallas_call | solution.py:444
  49.9 0.3 collective-permute-start.16
  50.2 7.9 %collective-permute-done.14.came.back = bf16[768,256]{1,0:T(8,128)(2,1)S(1)} collective-permute-done((bf16[768,256]{1,0:T(8,128)(2,1)S(1)}, bf16[768,256]{1,0:T(8,128)(2,1)S(1)}, u32[]{:S(2)}, u32[]{:S(2)}) %collective-permute-start.14) | collective-permute-done | bytes 393248 | tf_op jit(solution)/shard_map/ppermute | solution.py:330
  58.2 1.5 %collective-permute-start.15 = (bf16[768,256]{1,0:T(8,128)(2,1)S(1)}, bf16[768,256]{1,0:T(8,128)(2,1)S(1)}, u32[]{:S(2)}, u32[]{:S(2)}) collective-permute-start(bf16[768,256]{1,0:T(8,128)(2,1)S(1)} %hop.2), channel_id=1, source_target_pairs={{0,4},{1,5},{2,6},{3,7},{4,8},{5,9},{6,10},{7,11},{8,12},{9,13},{1... | collective-permute-start | bytes 1179656 | tf_op jit(solution)/shard_map/ppermute | solution.py:330
  59.7 1.7 %collective-permute-start.19 = (bf16[512,256]{1,0:T(8,128)(2,1)S(1)}, bf16[512,256]{1,0:T(8,128)(2,1)S(1)}, u32[]{:S(2)}, u32[]{:S(2)}) collective-permute-start(bf16[512,256]{1,0:T(8,128)(2,1)S(1)} %get-tuple-element.45), channel_id=1, source_target_pairs={{0,2},{1,3},{2,0},{3,1},{4,6},{5,7},{6,4},{7,5},{8,10},{9,11},{10,... | collective-permute-start | bytes 786440 | tf_op jit(solution)/shard_map/ppermute | solution.py:330
  61.4 0.3 collective-permute-start.18
  61.7 2.0 %collective-permute-done.16.came = bf16[512,256]{1,0:T(8,128)(2,1)S(1)} collective-permute-done((bf16[512,256]{1,0:T(8,128)(2,1)S(1)}, bf16[512,256]{1,0:T(8,128)(2,1)S(1)}, u32[]{:S(2)}, u32[]{:S(2)}) %collective-permute-start.16) | collective-permute-done | bytes 262176 | tf_op jit(solution)/shard_map/ppermute | solution.py:330
  63.7 0.1 hop.3
  63.8 2.0 %collective-permute-start.17 = (bf16[768,256]{1,0:T(8,128)(2,1)S(1)}, bf16[768,256]{1,0:T(8,128)(2,1)S(1)}, u32[]{:S(2)}, u32[]{:S(2)}) collective-permute-start(bf16[768,256]{1,0:T(8,128)(2,1)S(1)} %hop.3), channel_id=1, source_target_pairs={{0,12},{1,13},{2,14},{3,15},{4,0},{5,1},{6,2},{7,3},{8,4},{9,5},{1... | collective-permute-start | bytes 1179656 | tf_op jit(solution)/shard_map/ppermute | solution.py:330
  65.8 3.6 %collective-permute-done.19 = bf16[512,256]{1,0:T(8,128)(2,1)S(1)} collective-permute-done((bf16[512,256]{1,0:T(8,128)(2,1)S(1)}, bf16[512,256]{1,0:T(8,128)(2,1)S(1)}, u32[]{:S(2)}, u32[]{:S(2)}) %collective-permute-start.19) | collective-permute-done | bytes 262176 | tf_op jit(solution)/shard_map/ppermute | solution.py:330
  69.3 2.7 %collective-permute-done.15.rise = bf16[768,256]{1,0:T(8,128)(2,1)S(1)} collective-permute-done((bf16[768,256]{1,0:T(8,128)(2,1)S(1)}, bf16[768,256]{1,0:T(8,128)(2,1)S(1)}, u32[]{:S(2)}, u32[]{:S(2)}) %collective-permute-start.15) | collective-permute-done | bytes 393248 | tf_op jit(solution)/shard_map/ppermute | solution.py:330
  72.1 0.1 add_convert_fusion
  72.2 0.1 collective-permute-start.20
  72.2 8.3 %collective-permute-done.17.fall = bf16[768,256]{1,0:T(8,128)(2,1)S(1)} collective-permute-done((bf16[768,256]{1,0:T(8,128)(2,1)S(1)}, bf16[768,256]{1,0:T(8,128)(2,1)S(1)}, u32[]{:S(2)}, u32[]{:S(2)}) %collective-permute-start.17) | collective-permute-done | bytes 393248 | tf_op jit(solution)/shard_map/ppermute | solution.py:330
  80.5 0.0 copy-done.1
  80.5 2.7 %unsmooth.1 = f32[256,512]{1,0:T(8,128)} custom-call(f32[256,512]{1,0:T(8,128)S(1)} %get-tuple-element.32.mid, bf16[2560,256]{1,0:T(8,128)(2,1)S(1)} %collective-permute-done.13.got, bf16[768,256]{1,0:T(8,128)(2,1)S(1)} %collective-permute-done.14.came.back, bf16[768,256]{1,0:T(8,128)(2,1)S(1)} %collective-permute-done.15.rise, ...), custom_call_target="tpu_custom_call" | custom-call | flops 1342177280 | bytes 4194304 | tf_op jit(solution)/shard_map/unsmooth/pallas_call | solution.py:478
  83.2 0.0 collective-permute-done.18
  83.2 0.4 collective-permute-done.20
  83.6 0.9 %convert_add_fusion = f32[512,256]{1,0:T(8,128)} fusion(bf16[512,256]{1,0:T(8,128)(2,1)S(1)} %collective-permute-done.20, f32[512,256]{1,0:T(8,128)S(1)} %get-tuple-element.42, bf16[512,256]{1,0:T(8,128)(2,1)S(1)} %collective-permute-done.18, bf16[768,256]{1,0:T(8,128)(2,1)S(1)} %collective-permute-done.17.fall), kind=kLoop, calls=%fused_computation | loop fusion | flops 786432 | bytes 1835008 | tf_op jit(solution)/shard_map/add | solution.py:476
  (5 shorter events, 0.1 us)
Async XLA Ops:
  0.6 10.2 %collective-permute-start.4 = (bf16[512,256]{1,0:T(8,128)(2,1)}, bf16[512,256]{1,0:T(8,128)(2,1)S(1)}, u32[]{:S(2)}, u32[]{:S(2)}) collective-permute-start(bf16[512,256]{1,0:T(8,128)(2,1)} %refs_0_.5), channel_id=1, source_target_pairs={{0,2},{1,3},{2,0},{3,1},{4,6},{5,7},{6,4},{7,5},{8,10},{9,11},{10,... | collective-permute-start | bytes 786440 | tf_op jit(solution)/shard_map/ppermute | solution.py:330
  3.7 11.3 %collective-permute-start.3 = (bf16[512,256]{1,0:T(8,128)(2,1)}, bf16[512,256]{1,0:T(8,128)(2,1)S(1)}, u32[]{:S(2)}, u32[]{:S(2)}) collective-permute-start(bf16[512,256]{1,0:T(8,128)(2,1)} %refs_0_.5), channel_id=1, source_target_pairs={{0,4},{1,5},{2,6},{3,7},{4,8},{5,9},{6,10},{7,11},{8,12},{9,13},{1... | collective-permute-start | bytes 786440 | tf_op jit(solution)/shard_map/ppermute | solution.py:330
  5.2 14.0 %collective-permute-start.7 = (bf16[512,256]{1,0:T(8,128)(2,1)}, bf16[512,256]{1,0:T(8,128)(2,1)S(1)}, u32[]{:S(2)}, u32[]{:S(2)}) collective-permute-start(bf16[512,256]{1,0:T(8,128)(2,1)} %refs_0_.5), channel_id=1, source_target_pairs={{0,12},{1,13},{2,14},{3,15},{4,0},{5,1},{6,2},{7,3},{8,4},{9,5},{1... | collective-permute-start | bytes 786440 | tf_op jit(solution)/shard_map/ppermute | solution.py:330
  8.5 11.8 %collective-permute-start.2 = (f32[256,128]{1,0:T(8,128)S(1)}, f32[256,128]{1,0:T(8,128)S(1)}, u32[]{:S(2)}, u32[]{:S(2)}) collective-permute-start(f32[256,128]{1,0:T(8,128)S(1)} %get-tuple-element.46), channel_id=1, source_target_pairs={{1,2},{3,4},{5,6},{7,8},{9,10},{11,12},{13,14},{2,1},{4,3},{6,5},{... | collective-permute-start | bytes 393224 | tf_op jit(solution)/shard_map/ppermute | solution.py:330
  9.2 11.1 %collective-permute-start.1 = (f32[256,128]{1,0:T(8,128)S(1)}, f32[256,128]{1,0:T(8,128)S(1)}, u32[]{:S(2)}, u32[]{:S(2)}) collective-permute-start(f32[256,128]{1,0:T(8,128)S(1)} %get-tuple-element.47), channel_id=1, source_target_pairs={{0,1},{1,0},{2,3},{3,2},{4,5},{5,4},{6,7},{7,6},{8,9},{9,8},{10,11... | collective-permute-start | bytes 393224 | tf_op jit(solution)/shard_map/ppermute | solution.py:330
  14.9 14.8 %collective-permute-start.8 = (bf16[512,256]{1,0:T(8,128)(2,1)S(1)}, bf16[512,256]{1,0:T(8,128)(2,1)S(1)}, u32[]{:S(2)}, u32[]{:S(2)}) collective-permute-start(bf16[512,256]{1,0:T(8,128)(2,1)S(1)} %collective-permute-done.3.refs_1_), channel_id=1, source_target_pairs={{0,2},{1,3},{2,0},{3,1},{4,6},{5,7},{6,4},{7,5},{8,10},{9,11},{10,... | collective-permute-start | bytes 786440 | tf_op jit(solution)/shard_map/ppermute | solution.py:330
  15.2 11.0 %collective-permute-start.5 = (bf16[512,256]{1,0:T(8,128)(2,1)S(1)}, bf16[512,256]{1,0:T(8,128)(2,1)S(1)}, u32[]{:S(2)}, u32[]{:S(2)}) collective-permute-start(bf16[512,256]{1,0:T(8,128)(2,1)S(1)} %collective-permute-done.3.refs_1_), channel_id=1, source_target_pairs={{0,4},{1,5},{2,6},{3,7},{4,8},{5,9},{6,10},{7,11},{8,12},{9,13},{1... | collective-permute-start | bytes 786440 | tf_op jit(solution)/shard_map/ppermute | solution.py:330
  19.3 10.4 %collective-permute-start.9 = (bf16[512,256]{1,0:T(8,128)(2,1)S(1)}, bf16[512,256]{1,0:T(8,128)(2,1)S(1)}, u32[]{:S(2)}, u32[]{:S(2)}) collective-permute-start(bf16[512,256]{1,0:T(8,128)(2,1)S(1)} %collective-permute-done.7.refs_3_), channel_id=1, source_target_pairs={{0,2},{1,3},{2,0},{3,1},{4,6},{5,7},{6,4},{7,5},{8,10},{9,11},{10,... | collective-permute-start | bytes 786440 | tf_op jit(solution)/shard_map/ppermute | solution.py:330
  20.3 6.0 %collective-permute-start = (s32[2,8]{1,0:T(2,128)S(1)}, s32[2,8]{1,0:T(2,128)S(1)}, u32[]{:S(2)}, u32[]{:S(2)}) collective-permute-start(s32[2,8]{1,0:T(2,128)S(1)} %add_bitcast_fusion.ids), channel_id=1, source_target_pairs={{0,1},{1,0},{2,3},{3,2},{4,5},{5,4},{6,7},{7,6},{8,9},{9,8},{10,11... | collective-permute-start | bytes 200 | tf_op jit(solution)/shard_map/ppermute | solution.py:330
  20.3 1.4 %copy-start = (bf16[3072,256]{1,0:T(8,128)(2,1)S(1)}, bf16[3072,256]{1,0:T(8,128)(2,1)}, u32[]{:S(2)}) copy-start(bf16[3072,256]{1,0:T(8,128)(2,1)} %constant.22.clone.table) | copy-start | bytes 4718596
  21.7 1.0 %copy-start.3 = (f32[256,512]{1,0:T(8,128)S(1)}, f32[256,512]{1,0:T(8,128)}, u32[]{:S(2)}) copy-start(f32[256,512]{1,0:T(8,128)} %mid.1) | copy-start | bytes 1572868
  22.7 0.9 %copy-start.5 = (f32[256,256]{1,0:T(8,128)S(1)}, f32[256,256]{1,0:T(8,128)}, u32[]{:S(2)}) copy-start(f32[256,256]{1,0:T(8,128)} %taps.1) | copy-start | bytes 786436
  23.7 6.0 %copy-start.2 = (bf16[512,256]{1,0:T(8,128)(2,1)S(1)}, bf16[512,256]{1,0:T(8,128)(2,1)}, u32[]{:S(2)}) copy-start(bf16[512,256]{1,0:T(8,128)(2,1)} %refs_0_.5) | copy-start | bytes 786436
  26.3 9.9 %collective-permute-start.6 = (bf16[512,256]{1,0:T(8,128)(2,1)S(1)}, bf16[512,256]{1,0:T(8,128)(2,1)S(1)}, u32[]{:S(2)}, u32[]{:S(2)}) collective-permute-start(bf16[512,256]{1,0:T(8,128)(2,1)S(1)} %collective-permute-done.5.refs_2_), channel_id=1, source_target_pairs={{0,2},{1,3},{2,0},{3,1},{4,6},{5,7},{6,4},{7,5},{8,10},{9,11},{10,... | collective-permute-start | bytes 786440 | tf_op jit(solution)/shard_map/ppermute | solution.py:330
  30.5 7.2 %copy-start.4 = (bf16[2,8,128,512]{3,2,1,0:T(8,128)(2,1)S(1)}, bf16[2,8,128,512]{3,2,1,0:T(8,128)(2,1)}, u32[]{:S(2)}) copy-start(bf16[2,8,128,512]{3,2,1,0:T(8,128)(2,1)} %param.11) | copy-start | bytes 6291460
  30.5 7.2 %copy-start.6 = (s32[2,8,4]{1,2,0:T(4,128)S(1)}, s32[2,8,4]{1,2,0:T(4,128)}, u32[]{:S(2)}) copy-start(s32[2,8,4]{1,2,0:T(4,128)} %param.14) | copy-start | bytes 772
  30.5 7.2 %collective-permute-start.10 = (bf16[1024,256]{1,0:T(8,128)(2,1)S(1)}, bf16[1024,256]{1,0:T(8,128)(2,1)S(1)}, u32[]{:S(2)}, u32[]{:S(2)}) collective-permute-start(bf16[1024,256]{1,0:T(8,128)(2,1)S(1)} %pack.2), channel_id=1, source_target_pairs={{0,1},{1,0},{2,3},{3,2},{4,5},{5,4},{6,7},{7,6},{8,9},{9,8},{10,11... | collective-permute-start | bytes 1572872 | tf_op jit(solution)/shard_map/ppermute | solution.py:330
  31.4 6.3 %collective-permute-start.11 = (bf16[1024,256]{1,0:T(8,128)(2,1)S(1)}, bf16[1024,256]{1,0:T(8,128)(2,1)S(1)}, u32[]{:S(2)}, u32[]{:S(2)}) collective-permute-start(bf16[1024,256]{1,0:T(8,128)(2,1)S(1)} %pack.3), channel_id=1, source_target_pairs={{0,1},{1,0},{2,3},{3,2},{4,5},{5,4},{6,7},{7,6},{8,9},{9,8},{10,11... | collective-permute-start | bytes 1572872 | tf_op jit(solution)/shard_map/ppermute | solution.py:330
  36.2 1.5 %collective-permute-start.12 = (bf16[512,256]{1,0:T(8,128)(2,1)S(1)}, bf16[512,256]{1,0:T(8,128)(2,1)S(1)}, u32[]{:S(2)}, u32[]{:S(2)}) collective-permute-start(bf16[512,256]{1,0:T(8,128)(2,1)S(1)} %collective-permute-done.6.refs_6_), channel_id=1, source_target_pairs={{0,1},{1,0},{2,3},{3,2},{4,5},{5,4},{6,7},{7,6},{8,9},{9,8},{10,11... | collective-permute-start | bytes 786440 | tf_op jit(solution)/shard_map/ppermute | solution.py:330
  41.8 3.1 %collective-permute-start.13 = (bf16[2560,256]{1,0:T(8,128)(2,1)S(1)}, bf16[2560,256]{1,0:T(8,128)(2,1)S(1)}, u32[]{:S(2)}, u32[]{:S(2)}) collective-permute-start(bf16[2560,256]{1,0:T(8,128)(2,1)S(1)} %get-tuple-element.33.own), channel_id=1, source_target_pairs={{0,1},{1,0},{2,3},{3,2},{4,5},{5,4},{6,7},{7,6},{8,9},{9,8},{10,11... | collective-permute-start | bytes 3932168 | tf_op jit(solution)/shard_map/ppermute | solution.py:330
  46.1 12.0 %collective-permute-start.14 = (bf16[768,256]{1,0:T(8,128)(2,1)S(1)}, bf16[768,256]{1,0:T(8,128)(2,1)S(1)}, u32[]{:S(2)}, u32[]{:S(2)}) collective-permute-start(bf16[768,256]{1,0:T(8,128)(2,1)S(1)} %merge_late.1), channel_id=1, source_target_pairs={{0,2},{1,3},{2,0},{3,1},{4,6},{5,7},{6,4},{7,5},{8,10},{9,11},{10,... | collective-permute-start | bytes 1179656 | tf_op jit(solution)/shard_map/ppermute | solution.py:330
  49.9 13.9 %collective-permute-start.16 = (bf16[512,256]{1,0:T(8,128)(2,1)S(1)}, bf16[512,256]{1,0:T(8,128)(2,1)S(1)}, u32[]{:S(2)}, u32[]{:S(2)}) collective-permute-start(bf16[512,256]{1,0:T(8,128)(2,1)S(1)} %get-tuple-element.38), channel_id=1, source_target_pairs={{0,2},{1,3},{2,0},{3,1},{4,6},{5,7},{6,4},{7,5},{8,10},{9,11},{10,... | collective-permute-start | bytes 786440 | tf_op jit(solution)/shard_map/ppermute | solution.py:330
  58.2 13.9 %collective-permute-start.15 = (bf16[768,256]{1,0:T(8,128)(2,1)S(1)}, bf16[768,256]{1,0:T(8,128)(2,1)S(1)}, u32[]{:S(2)}, u32[]{:S(2)}) collective-permute-start(bf16[768,256]{1,0:T(8,128)(2,1)S(1)} %hop.2), channel_id=1, source_target_pairs={{0,4},{1,5},{2,6},{3,7},{4,8},{5,9},{6,10},{7,11},{8,12},{9,13},{1... | collective-permute-start | bytes 1179656 | tf_op jit(solution)/shard_map/ppermute | solution.py:330
  59.7 9.7 %collective-permute-start.19 = (bf16[512,256]{1,0:T(8,128)(2,1)S(1)}, bf16[512,256]{1,0:T(8,128)(2,1)S(1)}, u32[]{:S(2)}, u32[]{:S(2)}) collective-permute-start(bf16[512,256]{1,0:T(8,128)(2,1)S(1)} %get-tuple-element.45), channel_id=1, source_target_pairs={{0,2},{1,3},{2,0},{3,1},{4,6},{5,7},{6,4},{7,5},{8,10},{9,11},{10,... | collective-permute-start | bytes 786440 | tf_op jit(solution)/shard_map/ppermute | solution.py:330
  61.4 21.8 %collective-permute-start.18 = (bf16[512,256]{1,0:T(8,128)(2,1)S(1)}, bf16[512,256]{1,0:T(8,128)(2,1)S(1)}, u32[]{:S(2)}, u32[]{:S(2)}) collective-permute-start(bf16[512,256]{1,0:T(8,128)(2,1)S(1)} %get-tuple-element.43), channel_id=1, source_target_pairs={{0,2},{1,3},{2,0},{3,1},{4,6},{5,7},{6,4},{7,5},{8,10},{9,11},{10,... | collective-permute-start | bytes 786440 | tf_op jit(solution)/shard_map/ppermute | solution.py:330
  63.7 16.8 %copy-start.1 = (bf16[3072,256]{1,0:T(8,128)(2,1)S(1)}, bf16[3072,256]{1,0:T(8,128)(2,1)}, u32[]{:S(2)}) copy-start(bf16[3072,256]{1,0:T(8,128)(2,1)} %constant.22.clone.table) | copy-start | bytes 4718596
  63.8 16.7 %collective-permute-start.17 = (bf16[768,256]{1,0:T(8,128)(2,1)S(1)}, bf16[768,256]{1,0:T(8,128)(2,1)S(1)}, u32[]{:S(2)}, u32[]{:S(2)}) collective-permute-start(bf16[768,256]{1,0:T(8,128)(2,1)S(1)} %hop.3), channel_id=1, source_target_pairs={{0,12},{1,13},{2,14},{3,15},{4,0},{5,1},{6,2},{7,3},{8,4},{9,5},{1... | collective-permute-start | bytes 1179656 | tf_op jit(solution)/shard_map/ppermute | solution.py:330
  72.2 11.4 %collective-permute-start.20 = (bf16[512,256]{1,0:T(8,128)(2,1)S(1)}, bf16[512,256]{1,0:T(8,128)(2,1)S(1)}, u32[]{:S(2)}, u32[]{:S(2)}) collective-permute-start(bf16[512,256]{1,0:T(8,128)(2,1)S(1)} %add_convert_fusion), channel_id=1, source_target_pairs={{0,4},{1,5},{2,6},{3,7},{4,8},{5,9},{6,10},{7,11},{8,12},{9,13},{1... | collective-permute-start | bytes 786440 | tf_op jit(solution)/shard_map/ppermute | solution.py:330

commit v8 on v6

--- a/solution.py
+++ b/solution.py
@@ -112,14 +112,15 @@
     out[...] = filtered(signal, (base, kr, ki), 1.0, held, (0, 1)).astype(out.dtype)
 
 
-def unsmooth_kernel(mid, core_side, far_side, base, kr, ki, table, out, held, sem):
+def unsmooth_kernel(mid, got, far_side, base, kr, ki, table, out, held, sem):
     copy = pltpu.make_async_copy(table, held, sem)
     copy.start()
     width = far_side.shape[1] // 2
-    first = core_side.shape[0] - far_side.shape[0]
-    core = core_side[first:, :width].astype(F32) + core_side[first:, width:].astype(F32)
-    far = far_side[:, :width].astype(F32) + far_side[:, width:].astype(F32)
-    thirds = thirds_of(mid[...], core, far)
+    core = got[got.shape[0] - far_side.shape[0] :].astype(F32)
+    far = far_side[...].astype(F32)
+    thirds = thirds_of(
+        mid[...], core[:, :width] + core[:, width:], far[:, :width] + far[:, width:]
+    )
     copy.wait()
     signal = spectrum_of(thirds, held)
     out[...] = filtered(signal, (base[...], kr[...], ki[...]), -1.0, held, (1, 2))
@@ -237,12 +238,11 @@
         return 0
 
     lax.fori_loop(0, entries // group, step, 0)
-    width = far_side.shape[1] // 2
+    latent_dim, width = grad.shape[0], rows.shape[1] // 2
     even = me & 1 == 0
     later, earlier = grad[:, bins - width :], grad[:, :width]
     core_edge, far_edge = jnp.where(even, later, earlier), jnp.where(even, earlier, later)
-    target = pl.ds(entries * BLK, far_side.shape[0])
-    terms[target] = jnp.concatenate(parts(core_edge), axis=1)
+    terms[pl.ds(entries * BLK, latent_dim)] = jnp.concatenate(parts(core_edge), axis=1)
     far_side[...] = jnp.concatenate(parts(far_edge), axis=1)
 
 
@@ -297,6 +297,14 @@
     lax.fori_loop(0, entries, add, 0)
     for q, out in enumerate(outs):
         out[...] = sums[q * chunk : (q + 1) * chunk].astype(out.dtype)
+
+
+def hop_kernel(total, *refs):
+    out = refs[-1]
+    value = total[...]
+    for came in refs[:-1]:
+        value += came[...].astype(F32)
+    out[...] = value.astype(out.dtype)
 
 
 def local(latents, kernel, loadings, recorded, owner_ids, local_ids, recorded_mask):
@@ -344,9 +352,6 @@
         if r != half:
             across[r] = flip(straight[r], 2)
 
-    core_side, far_side, straight[half] = lax.optimization_barrier(
-        (core_side, far_side, straight[half])
-    )
     table = dft_tables(2 * halfwidth)
     table_scratch = [pltpu.VMEM(table.shape, BF16), pltpu.SemaphoreType.DMA(())]
     mxu = 40 * 2 * latent_dim * (2 * halfwidth) ** 2
@@ -357,7 +362,7 @@
         in_specs=[VMEM] * 4 + [HBM],
         out_specs=(VMEM,) * 4,
         scratch_shapes=table_scratch,
-        compiler_params=pltpu.CompilerParams(vmem_limit_bytes=16 * MIB),
+        compiler_params=pltpu.CompilerParams(vmem_limit_bytes=52 * MIB),
         cost_estimate=pl.CostEstimate(flops=mxu, bytes_accessed=4 * 2**20, transcendentals=0),
         name="smooth",
     )(latents, core_side, far_side, kernel, table)
@@ -425,9 +430,9 @@
         cost_estimate=pl.CostEstimate(flops=0, bytes_accessed=2**20, transcendentals=0),
         name="merge_late",
     )(ids, asked, terms, got)
+    wide = jax.ShapeDtypeStruct((chunk, latent_dim), F32)
+    sent, ids = lax.optimization_barrier((sent, ids))
     back = flip(sent, 2)
-    far_side = permute(far_side, odd_even)
-    wide = jax.ShapeDtypeStruct((chunk, latent_dim), F32)
     merged = pl.pallas_call(
         functools.partial(merge_kernel, entries, late),
         out_shape=(wide,) * chain + (narrow,) * (chain - 1),
@@ -438,26 +443,31 @@
         cost_estimate=pl.CostEstimate(flops=0, bytes_accessed=5 * 2**20, transcendentals=0),
         name="merge",
     )(ids, asked, terms, got)
-    merged = list(merged)
-    far_side, *merged = lax.optimization_barrier((far_side, *merged))
     crossed = {r: merged[chain + r - (r > half)] for r in range(chain) if r != half}
-    first = [r for r in range(half + 1, chain)]
-    other = {r: flip(crossed[r], 2) for r in first}
-    rest = [r for r in crossed if r not in first]
-    back, *held = lax.optimization_barrier((back, *(crossed[r] for r in rest)))
-    other[half] = back
-    for r, part in zip(rest, held):
-        other[r] = flip(part, 2)
-    totals = [merged[r] + other[r].astype(F32) for r in range(chain)]
-    rise = totals[half]
-    for r in range(half - 1, -1, -1):
-        rise = totals[r] + rotate(rise.astype(BF16), 1).astype(F32)
-    loading_grad = rise
-    if half > 1:
-        fall = totals[half + 1]
-        for r in range(half + 2, chain):
-            fall = totals[r] + rotate(fall.astype(BF16), -1).astype(F32)
-        loading_grad = loading_grad + rotate(fall.astype(BF16), -1).astype(F32)
+    other = {r: flip(part, 2) for r, part in crossed.items()}
+
+    def hop(total, *came):
+        return pl.pallas_call(
+            hop_kernel,
+            out_shape=narrow,
+            in_specs=[VMEM] * (1 + len(came)),
+            out_specs=VMEM,
+            compiler_params=pltpu.CompilerParams(vmem_limit_bytes=8 * MIB),
+            cost_estimate=pl.CostEstimate(flops=10**9, bytes_accessed=MIB, transcendentals=0),
+            name="hop",
+        )(total, *came)
+
+    rise = hop(merged[half], back)
+    rise, far_side = lax.optimization_barrier((rise, far_side))
+    far_side = permute(far_side, odd_even)
+    other[half + 1], far_side = lax.optimization_barrier((other[half + 1], far_side))
+    rise = rotate(rise, 1)
+    for r in range(half - 1, 0, -1):
+        rise = rotate(hop(merged[r], other[r], rise), 1)
+    fall = rotate(hop(merged[half + 1], other[half + 1]), -1)
+    for r in range(half + 2, chain):
+        fall = rotate(hop(merged[r], other[r], fall), -1)
+    loading_grad = merged[0] + other[0].astype(F32) + rise.astype(F32) + fall.astype(F32)
 
     latent_grad = pl.pallas_call(
         unsmooth_kernel,

time: 88.2 us -> 81.4 us (0.923)
  the two profiles are of different devices: /device:TPU:0 before, /device:TPU:1 now
where the time goes in v8:
time: 81.4 us; the launch traced here: 81.1 us
  starting transfers between devices  29.8 us (37%)
  waiting for transfers between devices  29.1 us (36%)
  Pallas kernels  16.5 us (20%)
  other arithmetic  2.62 us (3%)
  local copies, waits for them, and re-layouts  2.21 us (3%)
  between operations  0.82 us (1%)
    ppermute x22, starting transfers between devices, permute(): return lax.ppermute(x, 'tm', pairs)  29.8 us
    ppermute x22, waiting for transfers between devices, permute(): return lax.ppermute(x, 'tm', pairs)  29.1 us
    pallas_call x1, Pallas kernels, local(): pl.pallas_call(smooth_kernel, out_shape=(jax.ShapeDtypeStruct((latent_dim...  4.83 us
    pallas_call x1, Pallas kernels, local(): pl.pallas_call(functools.partial(session_kernel, entries, group, late), o...  4.01 us
    pallas_call x1, Pallas kernels, local(): pl.pallas_call(unsmooth_kernel, out_shape=jax.ShapeDtypeStruct((latent_di...  2.67 us
    unnamed x10, local copies, waits for them, and re-layouts  2.21 us
    pallas_call x1, Pallas kernels, local(): pl.pallas_call(functools.partial(merge_kernel, entries, late), out_shape=...  1.93 us
  transfers between devices with their start and end apart: 22, of which 9 were waited for; matrix products, arithmetic and copies ran while one was open for 2% of the time, Pallas kernels for 14%

profile of v8, /device:TPU:1, one launch (start us, length us, event | category | flops | bytes accessed | tf_op | source)
XLA Modules:
  0.0 81.1 jit_solution(16379558855693323460)
XLA Ops:
  0.6 2.1 %collective-permute-start.4 = (bf16[512,256]{1,0:T(8,128)(2,1)}, bf16[512,256]{1,0:T(8,128)(2,1)S(1)}, u32[]{:S(2)}, u32[]{:S(2)}) collective-permute-start(bf16[512,256]{1,0:T(8,128)(2,1)} %refs_0_.5), channel_id=1, source_target_pairs={{0,2},{1,3},{2,0},{3,1},{4,6},{5,7},{6,4},{7,5},{8,10},{9,11},{10,... | collective-permute-start | bytes 786440 | tf_op jit(solution)/shard_map/ppermute | solution.py:321
  2.8 1.3 %collective-permute-start.3 = (bf16[512,256]{1,0:T(8,128)(2,1)}, bf16[512,256]{1,0:T(8,128)(2,1)S(1)}, u32[]{:S(2)}, u32[]{:S(2)}) collective-permute-start(bf16[512,256]{1,0:T(8,128)(2,1)} %refs_0_.5), channel_id=1, source_target_pairs={{0,4},{1,5},{2,6},{3,7},{4,8},{5,9},{6,10},{7,11},{8,12},{9,13},{1... | collective-permute-start | bytes 786440 | tf_op jit(solution)/shard_map/ppermute | solution.py:321
  4.1 2.0 %collective-permute-start.7 = (bf16[512,256]{1,0:T(8,128)(2,1)}, bf16[512,256]{1,0:T(8,128)(2,1)S(1)}, u32[]{:S(2)}, u32[]{:S(2)}) collective-permute-start(bf16[512,256]{1,0:T(8,128)(2,1)} %refs_0_.5), channel_id=1, source_target_pairs={{0,12},{1,13},{2,14},{3,15},{4,0},{5,1},{6,2},{7,3},{8,4},{9,5},{1... | collective-permute-start | bytes 786440 | tf_op jit(solution)/shard_map/ppermute | solution.py:321
  6.1 1.0 %slice_select_fusion = (f32[256,128]{1,0:T(8,128)S(1)}, f32[256,128]{1,0:T(8,128)S(1)}) fusion(f32[256,512]{1,0:T(8,128)} %mid.1, pred[]{:T(512)S(6)} %eq.5), kind=kLoop, calls=%fused_computation.1 | loop fusion | flops 65536 | bytes 524289 | tf_op jit(solution)/shard_map/jit(_where)/select_n | solution.py:339
  7.1 3.3 %collective-permute-start.2 = (f32[256,128]{1,0:T(8,128)S(1)}, f32[256,128]{1,0:T(8,128)S(1)}, u32[]{:S(2)}, u32[]{:S(2)}) collective-permute-start(f32[256,128]{1,0:T(8,128)S(1)} %get-tuple-element.56), channel_id=1, source_target_pairs={{1,2},{3,4},{5,6},{7,8},{9,10},{11,12},{13,14},{2,1},{4,3},{6,5},{... | collective-permute-start | bytes 393224 | tf_op jit(solution)/shard_map/ppermute | solution.py:321
  10.3 0.1 collective-permute-start.1
  10.4 0.0 collective-permute-done.4.refs_4_
  10.4 1.4 %collective-permute-done.3.refs_1_ = bf16[512,256]{1,0:T(8,128)(2,1)S(1)} collective-permute-done((bf16[512,256]{1,0:T(8,128)(2,1)}, bf16[512,256]{1,0:T(8,128)(2,1)S(1)}, u32[]{:S(2)}, u32[]{:S(2)}) %collective-permute-start.3) | collective-permute-done | bytes 262176 | tf_op jit(solution)/shard_map/ppermute | solution.py:321
  11.9 0.4 collective-permute-start.8
  12.3 0.2 collective-permute-start.5
  12.5 5.0 %collective-permute-done.7.refs_3_ = bf16[512,256]{1,0:T(8,128)(2,1)S(1)} collective-permute-done((bf16[512,256]{1,0:T(8,128)(2,1)}, bf16[512,256]{1,0:T(8,128)(2,1)S(1)}, u32[]{:S(2)}, u32[]{:S(2)}) %collective-permute-start.7) | collective-permute-done | bytes 262176 | tf_op jit(solution)/shard_map/ppermute | solution.py:321
  17.4 0.2 collective-permute-start.9
  17.7 0.7 add_bitcast_fusion.ids
  18.4 0.0 collective-permute-done.2.far_side
  18.4 2.0 %collective-permute-start = (s32[2,8]{1,0:T(2,128)S(1)}, s32[2,8]{1,0:T(2,128)S(1)}, u32[]{:S(2)}, u32[]{:S(2)}) collective-permute-start(s32[2,8]{1,0:T(2,128)S(1)} %add_bitcast_fusion.ids), channel_id=1, source_target_pairs={{0,1},{1,0},{2,3},{3,2},{4,5},{5,4},{6,7},{7,6},{8,9},{9,8},{10,11... | collective-permute-start | bytes 200 | tf_op jit(solution)/shard_map/ppermute | solution.py:321
  20.4 0.0 collective-permute-done.1.core_side
  20.4 0.9 %copy-done.2 = f32[256,256]{1,0:T(8,128)S(1)} copy-done((f32[256,256]{1,0:T(8,128)S(1)}, f32[256,256]{1,0:T(8,128)}, u32[]{:S(2)}) %copy-start.2) | copy-done | bytes 262168
  21.3 4.8 %smooth.1 = (bf16[256,512]{1,0:T(8,128)(2,1)S(1)}, f32[256,256]{1,0:T(8,128)S(1)}, f32[256,256]{1,0:T(8,128)S(1)}, f32[256,256]{1,0:T(8,128)S(1)}) custom-call(f32[256,512]{1,0:T(8,128)} %mid.1, f32[256,128]{1,0:T(8,128)S(1)} %collective-permute-done.1.core_side, f32[256,128]{1,0:T(8,128)S(1)} %collective-permute-done.2.far_side, f32[256,256]{1,0:T(8,128)S(1)} %copy-done.2, ...), custom_call_target="tpu_custom_call" | custom-call | flops 1342177280 | bytes 4194304 | tf_op jit(solution)/shard_map/smooth/pallas_call | solution.py:359
  26.2 0.0 collective-permute-done.asked
  26.2 0.0 collective-permute-done.5.refs_2_
  26.2 2.6 %collective-permute-start.6 = (bf16[512,256]{1,0:T(8,128)(2,1)S(1)}, bf16[512,256]{1,0:T(8,128)(2,1)S(1)}, u32[]{:S(2)}, u32[]{:S(2)}) collective-permute-start(bf16[512,256]{1,0:T(8,128)(2,1)S(1)} %collective-permute-done.5.refs_2_), channel_id=1, source_target_pairs={{0,2},{1,3},{2,0},{3,1},{4,6},{5,7},{6,4},{7,5},{8,10},{9,11},{10,... | collective-permute-start | bytes 786440 | tf_op jit(solution)/shard_map/ppermute | solution.py:321
  28.8 0.0 collective-permute-done.9.refs_6_.refs_7_
  28.8 0.0 collective-permute-done.8.refs_5_
  28.8 0.0 copy-done
  28.8 0.8 %pack.2 = bf16[1024,256]{1,0:T(8,128)(2,1)S(1)} custom-call(s32[2,8]{1,0:T(2,128)S(1)} %collective-permute-done.asked, bf16[512,256]{1,0:T(8,128)(2,1)S(1)} %copy-done, bf16[512,256]{1,0:T(8,128)(2,1)S(1)} %collective-permute-done.3.refs_1_, bf16[512,256]{1,0:T(8,128)(2,1)S(1)} %collective-permute-done.5.refs_2_, ...), custom_call_target="tpu_custom_call" | custom-call | bytes 1048576 | tf_op jit(solution)/shard_map/pack/pallas_call | solution.py:375
  29.7 0.0 copy-start.1
  29.7 0.0 copy-start.3
  29.7 0.8 %collective-permute-start.10 = (bf16[1024,256]{1,0:T(8,128)(2,1)S(1)}, bf16[1024,256]{1,0:T(8,128)(2,1)S(1)}, u32[]{:S(2)}, u32[]{:S(2)}) collective-permute-start(bf16[1024,256]{1,0:T(8,128)(2,1)S(1)} %pack.2), channel_id=1, source_target_pairs={{0,1},{1,0},{2,3},{3,2},{4,5},{5,4},{6,7},{7,6},{8,9},{9,8},{10,11... | collective-permute-start | bytes 1572872 | tf_op jit(solution)/shard_map/ppermute | solution.py:321
  30.5 0.8 pack.3
  31.3 0.1 collective-permute-start.11
  31.4 3.7 %collective-permute-done.6.refs_6_ = bf16[512,256]{1,0:T(8,128)(2,1)S(1)} collective-permute-done((bf16[512,256]{1,0:T(8,128)(2,1)S(1)}, bf16[512,256]{1,0:T(8,128)(2,1)S(1)}, u32[]{:S(2)}, u32[]{:S(2)}) %collective-permute-start.6) | collective-permute-done | bytes 262176 | tf_op jit(solution)/shard_map/ppermute | solution.py:321
  35.0 1.0 %collective-permute-start.12 = (bf16[512,256]{1,0:T(8,128)(2,1)S(1)}, bf16[512,256]{1,0:T(8,128)(2,1)S(1)}, u32[]{:S(2)}, u32[]{:S(2)}) collective-permute-start(bf16[512,256]{1,0:T(8,128)(2,1)S(1)} %collective-permute-done.6.refs_6_), channel_id=1, source_target_pairs={{0,1},{1,0},{2,3},{3,2},{4,5},{5,4},{6,7},{7,6},{8,9},{9,8},{10,11... | collective-permute-start | bytes 786440 | tf_op jit(solution)/shard_map/ppermute | solution.py:321
  36.1 1.2 %collective-permute-done.12.late_theirs = bf16[512,256]{1,0:T(8,128)(2,1)S(1)} collective-permute-done((bf16[512,256]{1,0:T(8,128)(2,1)S(1)}, bf16[512,256]{1,0:T(8,128)(2,1)S(1)}, u32[]{:S(2)}, u32[]{:S(2)}) %collective-permute-start.12) | collective-permute-done | bytes 262176 | tf_op jit(solution)/shard_map/ppermute | solution.py:321
  37.2 0.0 collective-permute-done.10.packed
  37.2 0.0 collective-permute-done.11.packed_rest
  37.2 0.0 copy-done.1
  37.2 0.0 copy-done.3
  37.3 4.0 %session.1 = (f32[256,512]{1,0:T(8,128)S(1)}, bf16[256,256]{1,0:T(8,128)(2,1)S(1)}, bf16[2304,256]{1,0:T(8,128)(2,1)S(1)}) custom-call(s32[2,8]{1,0:T(2,128)S(1)} %add_bitcast_fusion.ids, s32[2,4,8]{2,1,0:T(4,128)S(1)} %bitcast.5, bf16[256,512]{1,0:T(8,128)(2,1)S(1)} %get-tuple-element.33.smoothed, bf16[16,128,512]{2,1,0:T(8,128)(2,1)S(1)} %bitcast.4, ...), custom_call_target="tpu_custom_call" | custom-call | flops 1610612736 | bytes 8388608 | tf_op jit(solution)/shard_map/session/pallas_call | solution.py:393
  41.3 0.4 collective-permute-start.13
  41.7 2.5 %collective-permute-done.13.got = bf16[2304,256]{1,0:T(8,128)(2,1)S(1)} collective-permute-done((bf16[2304,256]{1,0:T(8,128)(2,1)S(1)}, bf16[2304,256]{1,0:T(8,128)(2,1)S(1)}, u32[]{:S(2)}, u32[]{:S(2)}) %collective-permute-start.13) | collective-permute-done | bytes 1179680 | tf_op jit(solution)/shard_map/ppermute | solution.py:321
  44.2 1.2 %merge_late.1 = bf16[512,256]{1,0:T(8,128)(2,1)S(1)} custom-call(s32[2,8]{1,0:T(2,128)S(1)} %add_bitcast_fusion.ids, s32[2,8]{1,0:T(2,128)S(1)} %collective-permute-done.asked, bf16[2304,256]{1,0:T(8,128)(2,1)S(1)} %get-tuple-element.38.own, bf16[2304,256]{1,0:T(8,128)(2,1)S(1)} %collective-permute-done.13.got), custom_call_target="tpu_custom_call" | custom-call | bytes 1048576 | tf_op jit(solution)/shard_map/merge_late/pallas_call | solution.py:423
  45.4 1.5 %collective-permute-start.15 = (bf16[512,256]{1,0:T(8,128)(2,1)S(1)}, bf16[512,256]{1,0:T(8,128)(2,1)S(1)}, u32[]{:S(2)}, u32[]{:S(2)}) collective-permute-start(bf16[512,256]{1,0:T(8,128)(2,1)S(1)} %merge_late.1), channel_id=1, source_target_pairs={{0,2},{1,3},{2,0},{3,1},{4,6},{5,7},{6,4},{7,5},{8,10},{9,11},{10,... | collective-permute-start | bytes 786440 | tf_op jit(solution)/shard_map/ppermute | solution.py:321
  46.9 1.9 %merge.1 = (f32[512,256]{1,0:T(8,128)S(1)}, f32[512,256]{1,0:T(8,128)S(1)}, f32[512,256]{1,0:T(8,128)S(1)}, f32[512,256]{1,0:T(8,128)S(1)}, bf16[512,256]{1,0:T(...) custom-call(s32[2,8]{1,0:T(2,128)S(1)} %add_bitcast_fusion.ids, ...), custom_call_target="tpu_custom_call" | custom-call | bytes 5242880 | tf_op jit(solution)/shard_map/merge/pallas_call | solution.py:436
  48.9 0.1 collective-permute-start.14
  49.0 1.4 %collective-permute-start.18 = (bf16[512,256]{1,0:T(8,128)(2,1)S(1)}, bf16[512,256]{1,0:T(8,128)(2,1)S(1)}, u32[]{:S(2)}, u32[]{:S(2)}) collective-permute-start(bf16[512,256]{1,0:T(8,128)(2,1)S(1)} %get-tuple-element.52), channel_id=1, source_target_pairs={{0,2},{1,3},{2,0},{3,1},{4,6},{5,7},{6,4},{7,5},{8,10},{9,11},{10,... | collective-permute-start | bytes 786440 | tf_op jit(solution)/shard_map/ppermute | solution.py:321
  50.4 2.6 %collective-permute-done.15.refs_0_ = bf16[512,256]{1,0:T(8,128)(2,1)S(1)} collective-permute-done((bf16[512,256]{1,0:T(8,128)(2,1)S(1)}, bf16[512,256]{1,0:T(8,128)(2,1)S(1)}, u32[]{:S(2)}, u32[]{:S(2)}) %collective-permute-start.15) | collective-permute-done | bytes 262176 | tf_op jit(solution)/shard_map/ppermute | solution.py:321
  53.0 0.1 hop.3
  53.1 1.3 %collective-permute-start.19 = (bf16[512,256]{1,0:T(8,128)(2,1)S(1)}, bf16[512,256]{1,0:T(8,128)(2,1)S(1)}, u32[]{:S(2)}, u32[]{:S(2)}) collective-permute-start(bf16[512,256]{1,0:T(8,128)(2,1)S(1)} %hop.3), channel_id=1, source_target_pairs={{0,4},{1,5},{2,6},{3,7},{4,8},{5,9},{6,10},{7,11},{8,12},{9,13},{1... | collective-permute-start | bytes 786440 | tf_op jit(solution)/shard_map/ppermute | solution.py:321
  54.3 5.5 %collective-permute-start.16 = (bf16[256,256]{1,0:T(8,128)(2,1)S(1)}, bf16[256,256]{1,0:T(8,128)(2,1)S(1)}, u32[]{:S(2)}, u32[]{:S(2)}) collective-permute-start(bf16[256,256]{1,0:T(8,128)(2,1)S(1)} %get-tuple-element.44), channel_id=1, source_target_pairs={{1,2},{3,4},{5,6},{7,8},{9,10},{11,12},{13,14},{2,1},{4,3},{6,5},{... | collective-permute-start | bytes 393224 | tf_op jit(solution)/shard_map/ppermute | solution.py:321
  59.8 0.2 collective-permute-start.17
  60.0 0.0 collective-permute-done.14.refs_0_
  60.0 8.7 %collective-permute-done.16.far_side = bf16[256,256]{1,0:T(8,128)(2,1)S(1)} collective-permute-done((bf16[256,256]{1,0:T(8,128)(2,1)S(1)}, bf16[256,256]{1,0:T(8,128)(2,1)S(1)}, u32[]{:S(2)}, u32[]{:S(2)}) %collective-permute-start.16) | collective-permute-done | bytes 131104 | tf_op jit(solution)/shard_map/ppermute | solution.py:321
  68.6 0.1 hop.5
  68.7 3.2 %collective-permute-start.21 = (bf16[512,256]{1,0:T(8,128)(2,1)S(1)}, bf16[512,256]{1,0:T(8,128)(2,1)S(1)}, u32[]{:S(2)}, u32[]{:S(2)}) collective-permute-start(bf16[512,256]{1,0:T(8,128)(2,1)S(1)} %hop.5), channel_id=1, source_target_pairs={{0,12},{1,13},{2,14},{3,15},{4,0},{5,1},{6,2},{7,3},{8,4},{9,5},{1... | collective-permute-start | bytes 786440 | tf_op jit(solution)/shard_map/ppermute | solution.py:321
  71.9 0.0 collective-permute-done.18.refs_0_
  71.9 0.0 collective-permute-done.19.refs_1_
  71.9 0.1 hop.4
  72.0 0.1 collective-permute-start.20
  72.0 1.2 %copy-done.4 = bf16[3072,256]{1,0:T(8,128)(2,1)S(1)} copy-done((bf16[3072,256]{1,0:T(8,128)(2,1)S(1)}, bf16[3072,256]{1,0:T(8,128)(2,1)}, u32[]{:S(2)}) %copy-start.4) | copy-done | bytes 1572888
  73.3 2.7 %unsmooth.1 = f32[256,512]{1,0:T(8,128)} custom-call(f32[256,512]{1,0:T(8,128)S(1)} %get-tuple-element.37.mid, bf16[2304,256]{1,0:T(8,128)(2,1)S(1)} %collective-permute-done.13.got, bf16[256,256]{1,0:T(8,128)(2,1)S(1)} %collective-permute-done.16.far_side, f32[256,256]{1,0:T(8,128)S(1)} %get-tuple-element.46.base, f32[256,256]{1,0:T(8,128)S(1)} %get-tuple-element.47.kr, ...), custom_call_target="tpu_custom_call" | custom-call | flops 1342177280 | bytes 4194304 | tf_op jit(solution)/shard_map/unsmooth/pallas_call | solution.py:472
  76.0 0.0 collective-permute-done.17
  76.0 1.4 %collective-permute-done.21 = bf16[512,256]{1,0:T(8,128)(2,1)S(1)} collective-permute-done((bf16[512,256]{1,0:T(8,128)(2,1)S(1)}, bf16[512,256]{1,0:T(8,128)(2,1)S(1)}, u32[]{:S(2)}, u32[]{:S(2)}) %collective-permute-start.21) | collective-permute-done | bytes 262176 | tf_op jit(solution)/shard_map/ppermute | solution.py:321
  77.3 2.8 %collective-permute-done.20 = bf16[512,256]{1,0:T(8,128)(2,1)S(1)} collective-permute-done((bf16[512,256]{1,0:T(8,128)(2,1)S(1)}, bf16[512,256]{1,0:T(8,128)(2,1)S(1)}, u32[]{:S(2)}, u32[]{:S(2)}) %collective-permute-start.20) | collective-permute-done | bytes 262176 | tf_op jit(solution)/shard_map/ppermute | solution.py:321
  80.1 0.9 %convert_add_fusion = f32[512,256]{1,0:T(8,128)} fusion(bf16[512,256]{1,0:T(8,128)(2,1)S(1)} %collective-permute-done.21, bf16[512,256]{1,0:T(8,128)(2,1)S(1)} %collective-permute-done.20, f32[512,256]{1,0:T(8,128)S(1)} %get-tuple-element.49, bf16[512,256]{1,0:T(8,128)(2,1)S(1)} %collective-permute-done.17), kind=kLoop, calls=%fused_computation | loop fusion | flops 786432 | bytes 1835008 | tf_op jit(solution)/shard_map/add | solution.py:470
  (3 shorter events, 0.0 us)
Async XLA Ops:
  0.6 9.8 %collective-permute-start.4 = (bf16[512,256]{1,0:T(8,128)(2,1)}, bf16[512,256]{1,0:T(8,128)(2,1)S(1)}, u32[]{:S(2)}, u32[]{:S(2)}) collective-permute-start(bf16[512,256]{1,0:T(8,128)(2,1)} %refs_0_.5), channel_id=1, source_target_pairs={{0,2},{1,3},{2,0},{3,1},{4,6},{5,7},{6,4},{7,5},{8,10},{9,11},{10,... | collective-permute-start | bytes 786440 | tf_op jit(solution)/shard_map/ppermute | solution.py:321
  2.8 9.1 %collective-permute-start.3 = (bf16[512,256]{1,0:T(8,128)(2,1)}, bf16[512,256]{1,0:T(8,128)(2,1)S(1)}, u32[]{:S(2)}, u32[]{:S(2)}) collective-permute-start(bf16[512,256]{1,0:T(8,128)(2,1)} %refs_0_.5), channel_id=1, source_target_pairs={{0,4},{1,5},{2,6},{3,7},{4,8},{5,9},{6,10},{7,11},{8,12},{9,13},{1... | collective-permute-start | bytes 786440 | tf_op jit(solution)/shard_map/ppermute | solution.py:321
  4.1 13.4 %collective-permute-start.7 = (bf16[512,256]{1,0:T(8,128)(2,1)}, bf16[512,256]{1,0:T(8,128)(2,1)S(1)}, u32[]{:S(2)}, u32[]{:S(2)}) collective-permute-start(bf16[512,256]{1,0:T(8,128)(2,1)} %refs_0_.5), channel_id=1, source_target_pairs={{0,12},{1,13},{2,14},{3,15},{4,0},{5,1},{6,2},{7,3},{8,4},{9,5},{1... | collective-permute-start | bytes 786440 | tf_op jit(solution)/shard_map/ppermute | solution.py:321
  7.1 11.3 %collective-permute-start.2 = (f32[256,128]{1,0:T(8,128)S(1)}, f32[256,128]{1,0:T(8,128)S(1)}, u32[]{:S(2)}, u32[]{:S(2)}) collective-permute-start(f32[256,128]{1,0:T(8,128)S(1)} %get-tuple-element.56), channel_id=1, source_target_pairs={{1,2},{3,4},{5,6},{7,8},{9,10},{11,12},{13,14},{2,1},{4,3},{6,5},{... | collective-permute-start | bytes 393224 | tf_op jit(solution)/shard_map/ppermute | solution.py:321
  10.3 10.0 %collective-permute-start.1 = (f32[256,128]{1,0:T(8,128)S(1)}, f32[256,128]{1,0:T(8,128)S(1)}, u32[]{:S(2)}, u32[]{:S(2)}) collective-permute-start(f32[256,128]{1,0:T(8,128)S(1)} %get-tuple-element.57), channel_id=1, source_target_pairs={{0,1},{1,0},{2,3},{3,2},{4,5},{5,4},{6,7},{7,6},{8,9},{9,8},{10,11... | collective-permute-start | bytes 393224 | tf_op jit(solution)/shard_map/ppermute | solution.py:321
  11.9 16.9 %collective-permute-start.8 = (bf16[512,256]{1,0:T(8,128)(2,1)S(1)}, bf16[512,256]{1,0:T(8,128)(2,1)S(1)}, u32[]{:S(2)}, u32[]{:S(2)}) collective-permute-start(bf16[512,256]{1,0:T(8,128)(2,1)S(1)} %collective-permute-done.3.refs_1_), channel_id=1, source_target_pairs={{0,2},{1,3},{2,0},{3,1},{4,6},{5,7},{6,4},{7,5},{8,10},{9,11},{10,... | collective-permute-start | bytes 786440 | tf_op jit(solution)/shard_map/ppermute | solution.py:321
  12.3 13.9 %collective-permute-start.5 = (bf16[512,256]{1,0:T(8,128)(2,1)S(1)}, bf16[512,256]{1,0:T(8,128)(2,1)S(1)}, u32[]{:S(2)}, u32[]{:S(2)}) collective-permute-start(bf16[512,256]{1,0:T(8,128)(2,1)S(1)} %collective-permute-done.3.refs_1_), channel_id=1, source_target_pairs={{0,4},{1,5},{2,6},{3,7},{4,8},{5,9},{6,10},{7,11},{8,12},{9,13},{1... | collective-permute-start | bytes 786440 | tf_op jit(solution)/shard_map/ppermute | solution.py:321
  17.4 11.4 %collective-permute-start.9 = (bf16[512,256]{1,0:T(8,128)(2,1)S(1)}, bf16[512,256]{1,0:T(8,128)(2,1)S(1)}, u32[]{:S(2)}, u32[]{:S(2)}) collective-permute-start(bf16[512,256]{1,0:T(8,128)(2,1)S(1)} %collective-permute-done.7.refs_3_), channel_id=1, source_target_pairs={{0,2},{1,3},{2,0},{3,1},{4,6},{5,7},{6,4},{7,5},{8,10},{9,11},{10,... | collective-permute-start | bytes 786440 | tf_op jit(solution)/shard_map/ppermute | solution.py:321
  18.4 10.4 %copy-start = (bf16[512,256]{1,0:T(8,128)(2,1)S(1)}, bf16[512,256]{1,0:T(8,128)(2,1)}, u32[]{:S(2)}) copy-start(bf16[512,256]{1,0:T(8,128)(2,1)} %refs_0_.5) | copy-start | bytes 786436
  18.4 7.8 %collective-permute-start = (s32[2,8]{1,0:T(2,128)S(1)}, s32[2,8]{1,0:T(2,128)S(1)}, u32[]{:S(2)}, u32[]{:S(2)}) collective-permute-start(s32[2,8]{1,0:T(2,128)S(1)} %add_bitcast_fusion.ids), channel_id=1, source_target_pairs={{0,1},{1,0},{2,3},{3,2},{4,5},{5,4},{6,7},{7,6},{8,9},{9,8},{10,11... | collective-permute-start | bytes 200 | tf_op jit(solution)/shard_map/ppermute | solution.py:321
  20.4 1.0 %copy-start.2 = (f32[256,256]{1,0:T(8,128)S(1)}, f32[256,256]{1,0:T(8,128)}, u32[]{:S(2)}) copy-start(f32[256,256]{1,0:T(8,128)} %taps.1) | copy-start | bytes 786436
  26.2 8.8 %collective-permute-start.6 = (bf16[512,256]{1,0:T(8,128)(2,1)S(1)}, bf16[512,256]{1,0:T(8,128)(2,1)S(1)}, u32[]{:S(2)}, u32[]{:S(2)}) collective-permute-start(bf16[512,256]{1,0:T(8,128)(2,1)S(1)} %collective-permute-done.5.refs_2_), channel_id=1, source_target_pairs={{0,2},{1,3},{2,0},{3,1},{4,6},{5,7},{6,4},{7,5},{8,10},{9,11},{10,... | collective-permute-start | bytes 786440 | tf_op jit(solution)/shard_map/ppermute | solution.py:321
  29.7 7.6 %copy-start.1 = (bf16[2,8,128,512]{3,2,1,0:T(8,128)(2,1)S(1)}, bf16[2,8,128,512]{3,2,1,0:T(8,128)(2,1)}, u32[]{:S(2)}) copy-start(bf16[2,8,128,512]{3,2,1,0:T(8,128)(2,1)} %param.11) | copy-start | bytes 6291460
  29.7 7.6 %copy-start.3 = (s32[2,8,4]{1,2,0:T(4,128)S(1)}, s32[2,8,4]{1,2,0:T(4,128)}, u32[]{:S(2)}) copy-start(s32[2,8,4]{1,2,0:T(4,128)} %param.14) | copy-start | bytes 772
  29.7 7.6 %collective-permute-start.10 = (bf16[1024,256]{1,0:T(8,128)(2,1)S(1)}, bf16[1024,256]{1,0:T(8,128)(2,1)S(1)}, u32[]{:S(2)}, u32[]{:S(2)}) collective-permute-start(bf16[1024,256]{1,0:T(8,128)(2,1)S(1)} %pack.2), channel_id=1, source_target_pairs={{0,1},{1,0},{2,3},{3,2},{4,5},{5,4},{6,7},{7,6},{8,9},{9,8},{10,11... | collective-permute-start | bytes 1572872 | tf_op jit(solution)/shard_map/ppermute | solution.py:321
  31.3 6.0 %collective-permute-start.11 = (bf16[1024,256]{1,0:T(8,128)(2,1)S(1)}, bf16[1024,256]{1,0:T(8,128)(2,1)S(1)}, u32[]{:S(2)}, u32[]{:S(2)}) collective-permute-start(bf16[1024,256]{1,0:T(8,128)(2,1)S(1)} %pack.3), channel_id=1, source_target_pairs={{0,1},{1,0},{2,3},{3,2},{4,5},{5,4},{6,7},{7,6},{8,9},{9,8},{10,11... | collective-permute-start | bytes 1572872 | tf_op jit(solution)/shard_map/ppermute | solution.py:321
  35.0 2.2 %collective-permute-start.12 = (bf16[512,256]{1,0:T(8,128)(2,1)S(1)}, bf16[512,256]{1,0:T(8,128)(2,1)S(1)}, u32[]{:S(2)}, u32[]{:S(2)}) collective-permute-start(bf16[512,256]{1,0:T(8,128)(2,1)S(1)} %collective-permute-done.6.refs_6_), channel_id=1, source_target_pairs={{0,1},{1,0},{2,3},{3,2},{4,5},{5,4},{6,7},{7,6},{8,9},{9,8},{10,11... | collective-permute-start | bytes 786440 | tf_op jit(solution)/shard_map/ppermute | solution.py:321
  41.3 2.9 %collective-permute-start.13 = (bf16[2304,256]{1,0:T(8,128)(2,1)S(1)}, bf16[2304,256]{1,0:T(8,128)(2,1)S(1)}, u32[]{:S(2)}, u32[]{:S(2)}) collective-permute-start(bf16[2304,256]{1,0:T(8,128)(2,1)S(1)} %get-tuple-element.38.own), channel_id=1, source_target_pairs={{0,1},{1,0},{2,3},{3,2},{4,5},{5,4},{6,7},{7,6},{8,9},{9,8},{10,11... | collective-permute-start | bytes 3538952 | tf_op jit(solution)/shard_map/ppermute | solution.py:321
  45.4 7.6 %collective-permute-start.15 = (bf16[512,256]{1,0:T(8,128)(2,1)S(1)}, bf16[512,256]{1,0:T(8,128)(2,1)S(1)}, u32[]{:S(2)}, u32[]{:S(2)}) collective-permute-start(bf16[512,256]{1,0:T(8,128)(2,1)S(1)} %merge_late.1), channel_id=1, source_target_pairs={{0,2},{1,3},{2,0},{3,1},{4,6},{5,7},{6,4},{7,5},{8,10},{9,11},{10,... | collective-permute-start | bytes 786440 | tf_op jit(solution)/shard_map/ppermute | solution.py:321
  48.9 11.1 %collective-permute-start.14 = (bf16[512,256]{1,0:T(8,128)(2,1)S(1)}, bf16[512,256]{1,0:T(8,128)(2,1)S(1)}, u32[]{:S(2)}, u32[]{:S(2)}) collective-permute-start(bf16[512,256]{1,0:T(8,128)(2,1)S(1)} %get-tuple-element.40), channel_id=1, source_target_pairs={{0,2},{1,3},{2,0},{3,1},{4,6},{5,7},{6,4},{7,5},{8,10},{9,11},{10,... | collective-permute-start | bytes 786440 | tf_op jit(solution)/shard_map/ppermute | solution.py:321
  49.0 22.9 %collective-permute-start.18 = (bf16[512,256]{1,0:T(8,128)(2,1)S(1)}, bf16[512,256]{1,0:T(8,128)(2,1)S(1)}, u32[]{:S(2)}, u32[]{:S(2)}) collective-permute-start(bf16[512,256]{1,0:T(8,128)(2,1)S(1)} %get-tuple-element.52), channel_id=1, source_target_pairs={{0,2},{1,3},{2,0},{3,1},{4,6},{5,7},{6,4},{7,5},{8,10},{9,11},{10,... | collective-permute-start | bytes 786440 | tf_op jit(solution)/shard_map/ppermute | solution.py:321
  53.1 18.8 %collective-permute-start.19 = (bf16[512,256]{1,0:T(8,128)(2,1)S(1)}, bf16[512,256]{1,0:T(8,128)(2,1)S(1)}, u32[]{:S(2)}, u32[]{:S(2)}) collective-permute-start(bf16[512,256]{1,0:T(8,128)(2,1)S(1)} %hop.3), channel_id=1, source_target_pairs={{0,4},{1,5},{2,6},{3,7},{4,8},{5,9},{6,10},{7,11},{8,12},{9,13},{1... | collective-permute-start | bytes 786440 | tf_op jit(solution)/shard_map/ppermute | solution.py:321
  54.3 14.3 %collective-permute-start.16 = (bf16[256,256]{1,0:T(8,128)(2,1)S(1)}, bf16[256,256]{1,0:T(8,128)(2,1)S(1)}, u32[]{:S(2)}, u32[]{:S(2)}) collective-permute-start(bf16[256,256]{1,0:T(8,128)(2,1)S(1)} %get-tuple-element.44), channel_id=1, source_target_pairs={{1,2},{3,4},{5,6},{7,8},{9,10},{11,12},{13,14},{2,1},{4,3},{6,5},{... | collective-permute-start | bytes 393224 | tf_op jit(solution)/shard_map/ppermute | solution.py:321
  59.8 16.2 %collective-permute-start.17 = (bf16[512,256]{1,0:T(8,128)(2,1)S(1)}, bf16[512,256]{1,0:T(8,128)(2,1)S(1)}, u32[]{:S(2)}, u32[]{:S(2)}) collective-permute-start(bf16[512,256]{1,0:T(8,128)(2,1)S(1)} %get-tuple-element.50), channel_id=1, source_target_pairs={{0,2},{1,3},{2,0},{3,1},{4,6},{5,7},{6,4},{7,5},{8,10},{9,11},{10,... | collective-permute-start | bytes 786440 | tf_op jit(solution)/shard_map/ppermute | solution.py:321
  68.7 8.6 %collective-permute-start.21 = (bf16[512,256]{1,0:T(8,128)(2,1)S(1)}, bf16[512,256]{1,0:T(8,128)(2,1)S(1)}, u32[]{:S(2)}, u32[]{:S(2)}) collective-permute-start(bf16[512,256]{1,0:T(8,128)(2,1)S(1)} %hop.5), channel_id=1, source_target_pairs={{0,12},{1,13},{2,14},{3,15},{4,0},{5,1},{6,2},{7,3},{8,4},{9,5},{1... | collective-permute-start | bytes 786440 | tf_op jit(solution)/shard_map/ppermute | solution.py:321
  71.9 1.4 %copy-start.4 = (bf16[3072,256]{1,0:T(8,128)(2,1)S(1)}, bf16[3072,256]{1,0:T(8,128)(2,1)}, u32[]{:S(2)}) copy-start(bf16[3072,256]{1,0:T(8,128)(2,1)} %constant.22.clone.table) | copy-start | bytes 4718596
  72.0 8.2 %collective-permute-start.20 = (bf16[512,256]{1,0:T(8,128)(2,1)S(1)}, bf16[512,256]{1,0:T(8,128)(2,1)S(1)}, u32[]{:S(2)}, u32[]{:S(2)}) collective-permute-start(bf16[512,256]{1,0:T(8,128)(2,1)S(1)} %hop.4), channel_id=1, source_target_pairs={{0,4},{1,5},{2,6},{3,7},{4,8},{5,9},{6,10},{7,11},{8,12},{9,13},{1... | collective-permute-start | bytes 786440 | tf_op jit(solution)/shard_map/ppermute | solution.py:321

commit v9 on v8

--- a/solution.py
+++ b/solution.py
@@ -46,11 +46,32 @@
     return high, (a - high.astype(F32)).astype(BF16)
 
 
+class Tables:
+    def __init__(self, source, held, sem):
+        count = sem.shape[0]
+        rows = held.shape[0] // count
+        self.held = held
+        self.copies = [
+            pltpu.make_async_copy(source.at[cut], held.at[cut], sem.at[i])
+            for i, cut in enumerate(pl.ds(i * rows, rows) for i in range(count))
+        ]
+        for copy in self.copies:
+            copy.start()
+        self.here = set()
+
+    def __getitem__(self, index):
+        if index not in self.here:
+            self.here.add(index)
+            self.copies[index].wait()
+        size = self.held.shape[1]
+        first = 2 * index * size
+        return self.held[first : first + size], self.held[first + size : first + 2 * size]
+
+
 def times(a, tables, index):
     rows, size = a.shape
     high, low = parts(a)
-    t_high = tables[2 * index * size : (2 * index + 1) * size]
-    t_low = tables[(2 * index + 1) * size : (2 * index + 2) * size]
+    t_high, t_low = tables[index]
     out = jnp.dot(jnp.concatenate([high, low]), t_high, preferred_element_type=F32)
     return out[:rows] + out[rows:] + jnp.dot(high, t_low, preferred_element_type=F32)
 
@@ -100,30 +121,26 @@
 
 def smooth_kernel(mid, core_side, far_side, taps, table, out, *refs):
     spectrum, held, sem = refs[:3], refs[3], refs[4]
-    copy = pltpu.make_async_copy(table, held, sem)
-    copy.start()
+    tables = Tables(table, held, sem)
     thirds = thirds_of(mid[...], core_side[...], far_side[...])
-    copy.wait()
-    base = times(taps[...], held, 0)
-    kr, ki = times(taps[...], held, 1), -times(taps[...], held, 2)
+    base = times(taps[...], tables, 0)
+    kr, ki = times(taps[...], tables, 1), -times(taps[...], tables, 2)
     for ref, value in zip(spectrum, (base, kr, ki)):
         ref[...] = value
-    signal = spectrum_of(thirds, held)
-    out[...] = filtered(signal, (base, kr, ki), 1.0, held, (0, 1)).astype(out.dtype)
+    signal = spectrum_of(thirds, tables)
+    out[...] = filtered(signal, (base, kr, ki), 1.0, tables, (0, 1)).astype(out.dtype)
 
 
 def unsmooth_kernel(mid, got, far_side, base, kr, ki, table, out, held, sem):
-    copy = pltpu.make_async_copy(table, held, sem)
-    copy.start()
+    tables = Tables(table, held, sem)
     width = far_side.shape[1] // 2
     core = got[got.shape[0] - far_side.shape[0] :].astype(F32)
     far = far_side[...].astype(F32)
     thirds = thirds_of(
         mid[...], core[:, :width] + core[:, width:], far[:, :width] + far[:, width:]
     )
-    copy.wait()
-    signal = spectrum_of(thirds, held)
-    out[...] = filtered(signal, (base[...], kr[...], ki[...]), -1.0, held, (1, 2))
+    signal = spectrum_of(thirds, tables)
+    out[...] = filtered(signal, (base[...], kr[...], ki[...]), -1.0, tables, (1, 2))
 
 
 def divide(a, n):
@@ -353,7 +370,7 @@
             across[r] = flip(straight[r], 2)
 
     table = dft_tables(2 * halfwidth)
-    table_scratch = [pltpu.VMEM(table.shape, BF16), pltpu.SemaphoreType.DMA(())]
+    table_scratch = [pltpu.VMEM(table.shape, BF16), pltpu.SemaphoreType.DMA((6,))]
     mxu = 40 * 2 * latent_dim * (2 * halfwidth) ** 2
     square = jax.ShapeDtypeStruct((latent_dim, 2 * halfwidth), F32)
     smoothed, *spectrum = pl.pallas_call(
@@ -362,7 +379,7 @@
         in_specs=[VMEM] * 4 + [HBM],
         out_specs=(VMEM,) * 4,
         scratch_shapes=table_scratch,
-        compiler_params=pltpu.CompilerParams(vmem_limit_bytes=52 * MIB),
+        compiler_params=pltpu.CompilerParams(vmem_limit_bytes=53 * MIB),
         cost_estimate=pl.CostEstimate(flops=mxu, bytes_accessed=4 * 2**20, transcendentals=0),
         name="smooth",
     )(latents, core_side, far_side, kernel, table)
@@ -444,7 +461,7 @@
         name="merge",
     )(ids, asked, terms, got)
     crossed = {r: merged[chain + r - (r > half)] for r in range(chain) if r != half}
-    other = {r: flip(part, 2) for r, part in crossed.items()}
+    other = {r: flip(part, 2) for r, part in crossed.items() if r}
 
     def hop(total, *came):
         return pl.pallas_call(
@@ -453,14 +470,15 @@
             in_specs=[VMEM] * (1 + len(came)),
             out_specs=VMEM,
             compiler_params=pltpu.CompilerParams(vmem_limit_bytes=8 * MIB),
-            cost_estimate=pl.CostEstimate(flops=10**9, bytes_accessed=MIB, transcendentals=0),
+            cost_estimate=pl.CostEstimate(flops=0, bytes_accessed=MIB, transcendentals=0),
             name="hop",
         )(total, *came)
 
     rise = hop(merged[half], back)
     rise, far_side = lax.optimization_barrier((rise, far_side))
     far_side = permute(far_side, odd_even)
-    other[half + 1], far_side = lax.optimization_barrier((other[half + 1], far_side))
+    far_side, own = lax.optimization_barrier((far_side, crossed[0]))
+    other[0] = flip(own, 2)
     rise = rotate(rise, 1)
     for r in range(half - 1, 0, -1):
         rise = rotate(hop(merged[r], other[r], rise), 1)

time: 81.4 us -> 79.4 us (0.975)
  the two profiles are of different devices: /device:TPU:1 before, /device:TPU:0 now
where the time goes in v9:
time: 79.4 us; the launch traced here: 79.2 us
  starting transfers between devices  31 us (39%)
  waiting for transfers between devices  26 us (33%)
  Pallas kernels  18.8 us (24%)
  other arithmetic  2.62 us (3%)
  between operations  0.81 us (1%)
    ppermute x22, starting transfers between devices, permute(): return lax.ppermute(x, 'tm', pairs)  31 us
    ppermute x22, waiting for transfers between devices, permute(): return lax.ppermute(x, 'tm', pairs)  26 us
    pallas_call x1, Pallas kernels, local(): pl.pallas_call(smooth_kernel, out_shape=(jax.ShapeDtypeStruct((latent_dim...  5.75 us
    pallas_call x1, Pallas kernels, local(): pl.pallas_call(unsmooth_kernel, out_shape=jax.ShapeDtypeStruct((latent_di...  4.16 us
    pallas_call x1, Pallas kernels, local(): pl.pallas_call(functools.partial(session_kernel, entries, group, late), o...  3.99 us
    pallas_call x1, Pallas kernels, local(): pl.pallas_call(functools.partial(merge_kernel, entries, late), out_shape=...  1.9 us
  transfers between devices with their start and end apart: 22, of which 9 were waited for; matrix products, arithmetic and copies ran while one was open for 2% of the time, Pallas kernels for 17%

profile of v9, /device:TPU:0, one launch (start us, length us, event | category | flops | bytes accessed | tf_op | source)
XLA Modules:
  0.0 79.2 jit_solution(17760200595274104526)
XLA Ops:
  0.6 3.0 %collective-permute-start.4 = (bf16[512,256]{1,0:T(8,128)(2,1)}, bf16[512,256]{1,0:T(8,128)(2,1)S(1)}, u32[]{:S(2)}, u32[]{:S(2)}) collective-permute-start(bf16[512,256]{1,0:T(8,128)(2,1)} %refs_0_.5), channel_id=1, source_target_pairs={{0,2},{1,3},{2,0},{3,1},{4,6},{5,7},{6,4},{7,5},{8,10},{9,11},{10,... | collective-permute-start | bytes 786440 | tf_op jit(solution)/shard_map/ppermute | solution.py:338
  3.7 1.6 %collective-permute-start.3 = (bf16[512,256]{1,0:T(8,128)(2,1)}, bf16[512,256]{1,0:T(8,128)(2,1)S(1)}, u32[]{:S(2)}, u32[]{:S(2)}) collective-permute-start(bf16[512,256]{1,0:T(8,128)(2,1)} %refs_0_.5), channel_id=1, source_target_pairs={{0,4},{1,5},{2,6},{3,7},{4,8},{5,9},{6,10},{7,11},{8,12},{9,13},{1... | collective-permute-start | bytes 786440 | tf_op jit(solution)/shard_map/ppermute | solution.py:338
  5.2 2.2 %collective-permute-start.7 = (bf16[512,256]{1,0:T(8,128)(2,1)}, bf16[512,256]{1,0:T(8,128)(2,1)S(1)}, u32[]{:S(2)}, u32[]{:S(2)}) collective-permute-start(bf16[512,256]{1,0:T(8,128)(2,1)} %refs_0_.5), channel_id=1, source_target_pairs={{0,12},{1,13},{2,14},{3,15},{4,0},{5,1},{6,2},{7,3},{8,4},{9,5},{1... | collective-permute-start | bytes 786440 | tf_op jit(solution)/shard_map/ppermute | solution.py:338
  7.5 1.0 %slice_select_fusion = (f32[256,128]{1,0:T(8,128)S(1)}, f32[256,128]{1,0:T(8,128)S(1)}) fusion(f32[256,512]{1,0:T(8,128)} %mid.1, pred[]{:T(512)S(6)} %eq.5), kind=kLoop, calls=%fused_computation.1 | loop fusion | flops 65536 | bytes 524289 | tf_op jit(solution)/shard_map/jit(_where)/select_n | solution.py:356
  8.5 0.7 collective-permute-start.2
  9.2 1.7 %collective-permute-start.1 = (f32[256,128]{1,0:T(8,128)S(1)}, f32[256,128]{1,0:T(8,128)S(1)}, u32[]{:S(2)}, u32[]{:S(2)}) collective-permute-start(f32[256,128]{1,0:T(8,128)S(1)} %get-tuple-element.57), channel_id=1, source_target_pairs={{0,1},{1,0},{2,3},{3,2},{4,5},{5,4},{6,7},{7,6},{8,9},{9,8},{10,11... | collective-permute-start | bytes 393224 | tf_op jit(solution)/shard_map/ppermute | solution.py:338
  10.9 0.0 collective-permute-done.4.refs_4_
  10.9 4.1 %collective-permute-done.3.refs_1_ = bf16[512,256]{1,0:T(8,128)(2,1)S(1)} collective-permute-done((bf16[512,256]{1,0:T(8,128)(2,1)}, bf16[512,256]{1,0:T(8,128)(2,1)S(1)}, u32[]{:S(2)}, u32[]{:S(2)}) %collective-permute-start.3) | collective-permute-done | bytes 262176 | tf_op jit(solution)/shard_map/ppermute | solution.py:338
  14.9 0.3 collective-permute-start.8
  15.2 0.0 collective-permute-start.5
  15.2 4.0 %collective-permute-done.7.refs_3_ = bf16[512,256]{1,0:T(8,128)(2,1)S(1)} collective-permute-done((bf16[512,256]{1,0:T(8,128)(2,1)}, bf16[512,256]{1,0:T(8,128)(2,1)S(1)}, u32[]{:S(2)}, u32[]{:S(2)}) %collective-permute-start.7) | collective-permute-done | bytes 262176 | tf_op jit(solution)/shard_map/ppermute | solution.py:338
  19.3 0.3 collective-permute-start.9
  19.6 0.7 add_bitcast_fusion.ids
  20.3 0.0 copy-start
  20.3 0.0 collective-permute-done.2.far_side
  20.3 0.1 collective-permute-start
  20.3 0.0 collective-permute-done.1.core_side
  20.3 5.7 %smooth.1 = (bf16[256,512]{1,0:T(8,128)(2,1)S(1)}, f32[256,256]{1,0:T(8,128)S(1)}, f32[256,256]{1,0:T(8,128)}, f32[256,256]{1,0:T(8,128)}) custom-call(f32[256,512]{1,0:T(8,128)} %mid.1, f32[256,128]{1,0:T(8,128)S(1)} %collective-permute-done.1.core_side, f32[256,128]{1,0:T(8,128)S(1)} %collective-permute-done.2.far_side, f32[256,256]{1,0:T(8,128)} %taps.1, ...), custom_call_target="tpu_custom_call" | custom-call | flops 1342177280 | bytes 4194304 | tf_op jit(solution)/shard_map/smooth/pallas_call | solution.py:376
  26.1 0.0 collective-permute-done.asked
  26.1 0.1 collective-permute-done.5.refs_2_
  26.2 3.3 %collective-permute-start.6 = (bf16[512,256]{1,0:T(8,128)(2,1)S(1)}, bf16[512,256]{1,0:T(8,128)(2,1)S(1)}, u32[]{:S(2)}, u32[]{:S(2)}) collective-permute-start(bf16[512,256]{1,0:T(8,128)(2,1)S(1)} %collective-permute-done.5.refs_2_), channel_id=1, source_target_pairs={{0,2},{1,3},{2,0},{3,1},{4,6},{5,7},{6,4},{7,5},{8,10},{9,11},{10,... | collective-permute-start | bytes 786440 | tf_op jit(solution)/shard_map/ppermute | solution.py:338
  29.5 0.0 collective-permute-done.9.refs_6_.refs_7_
  29.5 0.0 collective-permute-done.8.refs_5_
  29.5 0.0 copy-done
  29.5 0.8 pack.2
  30.3 0.0 copy-start.1
  30.3 0.0 copy-start.2
  30.3 0.1 collective-permute-start.10
  30.4 0.8 pack.3
  31.2 0.6 collective-permute-start.11
  31.8 4.2 %collective-permute-done.6.refs_6_ = bf16[512,256]{1,0:T(8,128)(2,1)S(1)} collective-permute-done((bf16[512,256]{1,0:T(8,128)(2,1)S(1)}, bf16[512,256]{1,0:T(8,128)(2,1)S(1)}, u32[]{:S(2)}, u32[]{:S(2)}) %collective-permute-start.6) | collective-permute-done | bytes 262176 | tf_op jit(solution)/shard_map/ppermute | solution.py:338
  36.0 0.0 collective-permute-start.12
  36.0 1.5 %collective-permute-done.12.late_theirs = bf16[512,256]{1,0:T(8,128)(2,1)S(1)} collective-permute-done((bf16[512,256]{1,0:T(8,128)(2,1)S(1)}, bf16[512,256]{1,0:T(8,128)(2,1)S(1)}, u32[]{:S(2)}, u32[]{:S(2)}) %collective-permute-start.12) | collective-permute-done | bytes 262176 | tf_op jit(solution)/shard_map/ppermute | solution.py:338
  37.5 0.0 collective-permute-done.10.packed
  37.5 0.0 collective-permute-done.11.packed_rest
  37.5 0.0 copy-done.1
  37.5 0.0 copy-done.2
  37.5 4.0 %session.1 = (f32[256,512]{1,0:T(8,128)S(1)}, bf16[256,256]{1,0:T(8,128)(2,1)S(1)}, bf16[2304,256]{1,0:T(8,128)(2,1)S(1)}) custom-call(s32[2,8]{1,0:T(2,128)S(1)} %add_bitcast_fusion.ids, s32[2,4,8]{2,1,0:T(4,128)S(1)} %bitcast.5, bf16[256,512]{1,0:T(8,128)(2,1)S(1)} %get-tuple-element.33.smoothed, bf16[16,128,512]{2,1,0:T(8,128)(2,1)S(1)} %bitcast.4, ...), custom_call_target="tpu_custom_call" | custom-call | flops 1610612736 | bytes 8388608 | tf_op jit(solution)/shard_map/session/pallas_call | solution.py:410
  41.5 0.2 collective-permute-start.13
  41.7 2.7 %collective-permute-done.13.got = bf16[2304,256]{1,0:T(8,128)(2,1)S(1)} collective-permute-done((bf16[2304,256]{1,0:T(8,128)(2,1)S(1)}, bf16[2304,256]{1,0:T(8,128)(2,1)S(1)}, u32[]{:S(2)}, u32[]{:S(2)}) %collective-permute-start.13) | collective-permute-done | bytes 1179680 | tf_op jit(solution)/shard_map/ppermute | solution.py:338
  44.4 1.2 %merge_late.1 = bf16[512,256]{1,0:T(8,128)(2,1)S(1)} custom-call(s32[2,8]{1,0:T(2,128)S(1)} %add_bitcast_fusion.ids, s32[2,8]{1,0:T(2,128)S(1)} %collective-permute-done.asked, bf16[2304,256]{1,0:T(8,128)(2,1)S(1)} %get-tuple-element.38.own, bf16[2304,256]{1,0:T(8,128)(2,1)S(1)} %collective-permute-done.13.got), custom_call_target="tpu_custom_call" | custom-call | bytes 1048576 | tf_op jit(solution)/shard_map/merge_late/pallas_call | solution.py:440
  45.7 1.8 %collective-permute-start.14 = (bf16[512,256]{1,0:T(8,128)(2,1)S(1)}, bf16[512,256]{1,0:T(8,128)(2,1)S(1)}, u32[]{:S(2)}, u32[]{:S(2)}) collective-permute-start(bf16[512,256]{1,0:T(8,128)(2,1)S(1)} %merge_late.1), channel_id=1, source_target_pairs={{0,2},{1,3},{2,0},{3,1},{4,6},{5,7},{6,4},{7,5},{8,10},{9,11},{10,... | collective-permute-start | bytes 786440 | tf_op jit(solution)/shard_map/ppermute | solution.py:338
  47.5 1.9 %merge.1 = (f32[512,256]{1,0:T(8,128)S(1)}, f32[512,256]{1,0:T(8,128)S(1)}, f32[512,256]{1,0:T(8,128)S(1)}, f32[512,256]{1,0:T(8,128)S(1)}, bf16[512,256]{1,0:T(...) custom-call(s32[2,8]{1,0:T(2,128)S(1)} %add_bitcast_fusion.ids, ...), custom_call_target="tpu_custom_call" | custom-call | bytes 5242880 | tf_op jit(solution)/shard_map/merge/pallas_call | solution.py:453
  49.4 0.4 collective-permute-start.20
  49.7 1.7 %collective-permute-start.17 = (bf16[512,256]{1,0:T(8,128)(2,1)S(1)}, bf16[512,256]{1,0:T(8,128)(2,1)S(1)}, u32[]{:S(2)}, u32[]{:S(2)}) collective-permute-start(bf16[512,256]{1,0:T(8,128)(2,1)S(1)} %get-tuple-element.52), channel_id=1, source_target_pairs={{0,2},{1,3},{2,0},{3,1},{4,6},{5,7},{6,4},{7,5},{8,10},{9,11},{10,... | collective-permute-start | bytes 786440 | tf_op jit(solution)/shard_map/ppermute | solution.py:338
  51.5 3.4 %collective-permute-done.14.refs_0_ = bf16[512,256]{1,0:T(8,128)(2,1)S(1)} collective-permute-done((bf16[512,256]{1,0:T(8,128)(2,1)S(1)}, bf16[512,256]{1,0:T(8,128)(2,1)S(1)}, u32[]{:S(2)}, u32[]{:S(2)}) %collective-permute-start.14) | collective-permute-done | bytes 262176 | tf_op jit(solution)/shard_map/ppermute | solution.py:338
  54.9 1.5 %collective-permute-start.18 = (bf16[512,256]{1,0:T(8,128)(2,1)S(1)}, bf16[512,256]{1,0:T(8,128)(2,1)S(1)}, u32[]{:S(2)}, u32[]{:S(2)}) collective-permute-start(bf16[512,256]{1,0:T(8,128)(2,1)S(1)} %hop.3), channel_id=1, source_target_pairs={{0,4},{1,5},{2,6},{3,7},{4,8},{5,9},{6,10},{7,11},{8,12},{9,13},{1... | collective-permute-start | bytes 786440 | tf_op jit(solution)/shard_map/ppermute | solution.py:338
  56.5 0.7 collective-permute-start.15
  57.1 3.4 %collective-permute-done.20.refs_0_ = bf16[512,256]{1,0:T(8,128)(2,1)S(1)} collective-permute-done((bf16[512,256]{1,0:T(8,128)(2,1)S(1)}, bf16[512,256]{1,0:T(8,128)(2,1)S(1)}, u32[]{:S(2)}, u32[]{:S(2)}) %collective-permute-start.20) | collective-permute-done | bytes 262176 | tf_op jit(solution)/shard_map/ppermute | solution.py:338
  60.5 2.1 %collective-permute-start.21 = (bf16[512,256]{1,0:T(8,128)(2,1)S(1)}, bf16[512,256]{1,0:T(8,128)(2,1)S(1)}, u32[]{:S(2)}, u32[]{:S(2)}) collective-permute-start(bf16[512,256]{1,0:T(8,128)(2,1)S(1)} %hop.5), channel_id=1, source_target_pairs={{0,12},{1,13},{2,14},{3,15},{4,0},{5,1},{6,2},{7,3},{8,4},{9,5},{1... | collective-permute-start | bytes 786440 | tf_op jit(solution)/shard_map/ppermute | solution.py:338
  62.6 0.0 collective-permute-done.15.far_side
  62.6 7.3 %collective-permute-start.16 = (bf16[512,256]{1,0:T(8,128)(2,1)S(1)}, bf16[512,256]{1,0:T(8,128)(2,1)S(1)}, u32[]{:S(2)}, u32[]{:S(2)}) collective-permute-start(bf16[512,256]{1,0:T(8,128)(2,1)S(1)} %get-tuple-element.50), channel_id=1, source_target_pairs={{0,2},{1,3},{2,0},{3,1},{4,6},{5,7},{6,4},{7,5},{8,10},{9,11},{10,... | collective-permute-start | bytes 786440 | tf_op jit(solution)/shard_map/ppermute | solution.py:338
  69.9 0.0 collective-permute-done.17.refs_0_
  69.9 0.0 collective-permute-done.18.refs_1_
  69.9 0.1 hop.4
  70.0 1.5 %collective-permute-start.19 = (bf16[512,256]{1,0:T(8,128)(2,1)S(1)}, bf16[512,256]{1,0:T(8,128)(2,1)S(1)}, u32[]{:S(2)}, u32[]{:S(2)}) collective-permute-start(bf16[512,256]{1,0:T(8,128)(2,1)S(1)} %hop.4), channel_id=1, source_target_pairs={{0,4},{1,5},{2,6},{3,7},{4,8},{5,9},{6,10},{7,11},{8,12},{9,13},{1... | collective-permute-start | bytes 786440 | tf_op jit(solution)/shard_map/ppermute | solution.py:338
  71.5 0.0 copy-done.3
  71.5 0.0 copy-done.4
  71.5 0.0 copy-done.5
  71.5 4.2 %unsmooth.1 = f32[256,512]{1,0:T(8,128)} custom-call(f32[256,512]{1,0:T(8,128)S(1)} %get-tuple-element.37.mid, bf16[2304,256]{1,0:T(8,128)(2,1)S(1)} %collective-permute-done.13.got, bf16[256,256]{1,0:T(8,128)(2,1)S(1)} %collective-permute-done.15.far_side, f32[256,256]{1,0:T(8,128)S(1)} %get-tuple-element.46.base, f32[256,256]{1,0:T(8,128)S(1)} %copy-done.4, ...), custom_call_target="tpu_custom_call" | custom-call | flops 1342177280 | bytes 4194304 | tf_op jit(solution)/shard_map/unsmooth/pallas_call | solution.py:490
  75.7 0.0 collective-permute-done.21
  75.7 0.0 collective-permute-done.16
  75.7 2.5 %collective-permute-done.19 = bf16[512,256]{1,0:T(8,128)(2,1)S(1)} collective-permute-done((bf16[512,256]{1,0:T(8,128)(2,1)S(1)}, bf16[512,256]{1,0:T(8,128)(2,1)S(1)}, u32[]{:S(2)}, u32[]{:S(2)}) %collective-permute-start.19) | collective-permute-done | bytes 262176 | tf_op jit(solution)/shard_map/ppermute | solution.py:338
  78.2 0.9 %convert_add_fusion = f32[512,256]{1,0:T(8,128)} fusion(bf16[512,256]{1,0:T(8,128)(2,1)S(1)} %collective-permute-done.21, bf16[512,256]{1,0:T(8,128)(2,1)S(1)} %collective-permute-done.19, f32[512,256]{1,0:T(8,128)S(1)} %get-tuple-element.49, bf16[512,256]{1,0:T(8,128)(2,1)S(1)} %collective-permute-done.16), kind=kLoop, calls=%fused_computation | loop fusion | flops 786432 | bytes 1835008 | tf_op jit(solution)/shard_map/add | solution.py:488
  (5 shorter events, 0.1 us)
Async XLA Ops:
  0.6 10.2 %collective-permute-start.4 = (bf16[512,256]{1,0:T(8,128)(2,1)}, bf16[512,256]{1,0:T(8,128)(2,1)S(1)}, u32[]{:S(2)}, u32[]{:S(2)}) collective-permute-start(bf16[512,256]{1,0:T(8,128)(2,1)} %refs_0_.5), channel_id=1, source_target_pairs={{0,2},{1,3},{2,0},{3,1},{4,6},{5,7},{6,4},{7,5},{8,10},{9,11},{10,... | collective-permute-start | bytes 786440 | tf_op jit(solution)/shard_map/ppermute | solution.py:338
  3.7 11.3 %collective-permute-start.3 = (bf16[512,256]{1,0:T(8,128)(2,1)}, bf16[512,256]{1,0:T(8,128)(2,1)S(1)}, u32[]{:S(2)}, u32[]{:S(2)}) collective-permute-start(bf16[512,256]{1,0:T(8,128)(2,1)} %refs_0_.5), channel_id=1, source_target_pairs={{0,4},{1,5},{2,6},{3,7},{4,8},{5,9},{6,10},{7,11},{8,12},{9,13},{1... | collective-permute-start | bytes 786440 | tf_op jit(solution)/shard_map/ppermute | solution.py:338
  5.2 14.0 %collective-permute-start.7 = (bf16[512,256]{1,0:T(8,128)(2,1)}, bf16[512,256]{1,0:T(8,128)(2,1)S(1)}, u32[]{:S(2)}, u32[]{:S(2)}) collective-permute-start(bf16[512,256]{1,0:T(8,128)(2,1)} %refs_0_.5), channel_id=1, source_target_pairs={{0,12},{1,13},{2,14},{3,15},{4,0},{5,1},{6,2},{7,3},{8,4},{9,5},{1... | collective-permute-start | bytes 786440 | tf_op jit(solution)/shard_map/ppermute | solution.py:338
  8.5 11.8 %collective-permute-start.2 = (f32[256,128]{1,0:T(8,128)S(1)}, f32[256,128]{1,0:T(8,128)S(1)}, u32[]{:S(2)}, u32[]{:S(2)}) collective-permute-start(f32[256,128]{1,0:T(8,128)S(1)} %get-tuple-element.56), channel_id=1, source_target_pairs={{1,2},{3,4},{5,6},{7,8},{9,10},{11,12},{13,14},{2,1},{4,3},{6,5},{... | collective-permute-start | bytes 393224 | tf_op jit(solution)/shard_map/ppermute | solution.py:338
  9.2 11.2 %collective-permute-start.1 = (f32[256,128]{1,0:T(8,128)S(1)}, f32[256,128]{1,0:T(8,128)S(1)}, u32[]{:S(2)}, u32[]{:S(2)}) collective-permute-start(f32[256,128]{1,0:T(8,128)S(1)} %get-tuple-element.57), channel_id=1, source_target_pairs={{0,1},{1,0},{2,3},{3,2},{4,5},{5,4},{6,7},{7,6},{8,9},{9,8},{10,11... | collective-permute-start | bytes 393224 | tf_op jit(solution)/shard_map/ppermute | solution.py:338
  14.9 14.6 %collective-permute-start.8 = (bf16[512,256]{1,0:T(8,128)(2,1)S(1)}, bf16[512,256]{1,0:T(8,128)(2,1)S(1)}, u32[]{:S(2)}, u32[]{:S(2)}) collective-permute-start(bf16[512,256]{1,0:T(8,128)(2,1)S(1)} %collective-permute-done.3.refs_1_), channel_id=1, source_target_pairs={{0,2},{1,3},{2,0},{3,1},{4,6},{5,7},{6,4},{7,5},{8,10},{9,11},{10,... | collective-permute-start | bytes 786440 | tf_op jit(solution)/shard_map/ppermute | solution.py:338
  15.2 11.0 %collective-permute-start.5 = (bf16[512,256]{1,0:T(8,128)(2,1)S(1)}, bf16[512,256]{1,0:T(8,128)(2,1)S(1)}, u32[]{:S(2)}, u32[]{:S(2)}) collective-permute-start(bf16[512,256]{1,0:T(8,128)(2,1)S(1)} %collective-permute-done.3.refs_1_), channel_id=1, source_target_pairs={{0,4},{1,5},{2,6},{3,7},{4,8},{5,9},{6,10},{7,11},{8,12},{9,13},{1... | collective-permute-start | bytes 786440 | tf_op jit(solution)/shard_map/ppermute | solution.py:338
  19.3 10.2 %collective-permute-start.9 = (bf16[512,256]{1,0:T(8,128)(2,1)S(1)}, bf16[512,256]{1,0:T(8,128)(2,1)S(1)}, u32[]{:S(2)}, u32[]{:S(2)}) collective-permute-start(bf16[512,256]{1,0:T(8,128)(2,1)S(1)} %collective-permute-done.7.refs_3_), channel_id=1, source_target_pairs={{0,2},{1,3},{2,0},{3,1},{4,6},{5,7},{6,4},{7,5},{8,10},{9,11},{10,... | collective-permute-start | bytes 786440 | tf_op jit(solution)/shard_map/ppermute | solution.py:338
  20.3 9.2 %copy-start = (bf16[512,256]{1,0:T(8,128)(2,1)S(1)}, bf16[512,256]{1,0:T(8,128)(2,1)}, u32[]{:S(2)}) copy-start(bf16[512,256]{1,0:T(8,128)(2,1)} %refs_0_.5) | copy-start | bytes 786436
  20.3 5.8 %collective-permute-start = (s32[2,8]{1,0:T(2,128)S(1)}, s32[2,8]{1,0:T(2,128)S(1)}, u32[]{:S(2)}, u32[]{:S(2)}) collective-permute-start(s32[2,8]{1,0:T(2,128)S(1)} %add_bitcast_fusion.ids), channel_id=1, source_target_pairs={{0,1},{1,0},{2,3},{3,2},{4,5},{5,4},{6,7},{7,6},{8,9},{9,8},{10,11... | collective-permute-start | bytes 200 | tf_op jit(solution)/shard_map/ppermute | solution.py:338
  26.2 9.8 %collective-permute-start.6 = (bf16[512,256]{1,0:T(8,128)(2,1)S(1)}, bf16[512,256]{1,0:T(8,128)(2,1)S(1)}, u32[]{:S(2)}, u32[]{:S(2)}) collective-permute-start(bf16[512,256]{1,0:T(8,128)(2,1)S(1)} %collective-permute-done.5.refs_2_), channel_id=1, source_target_pairs={{0,2},{1,3},{2,0},{3,1},{4,6},{5,7},{6,4},{7,5},{8,10},{9,11},{10,... | collective-permute-start | bytes 786440 | tf_op jit(solution)/shard_map/ppermute | solution.py:338
  30.3 7.2 %copy-start.1 = (bf16[2,8,128,512]{3,2,1,0:T(8,128)(2,1)S(1)}, bf16[2,8,128,512]{3,2,1,0:T(8,128)(2,1)}, u32[]{:S(2)}) copy-start(bf16[2,8,128,512]{3,2,1,0:T(8,128)(2,1)} %param.11) | copy-start | bytes 6291460
  30.3 7.2 %copy-start.2 = (s32[2,8,4]{1,2,0:T(4,128)S(1)}, s32[2,8,4]{1,2,0:T(4,128)}, u32[]{:S(2)}) copy-start(s32[2,8,4]{1,2,0:T(4,128)} %param.14) | copy-start | bytes 772
  30.3 7.2 %collective-permute-start.10 = (bf16[1024,256]{1,0:T(8,128)(2,1)S(1)}, bf16[1024,256]{1,0:T(8,128)(2,1)S(1)}, u32[]{:S(2)}, u32[]{:S(2)}) collective-permute-start(bf16[1024,256]{1,0:T(8,128)(2,1)S(1)} %pack.2), channel_id=1, source_target_pairs={{0,1},{1,0},{2,3},{3,2},{4,5},{5,4},{6,7},{7,6},{8,9},{9,8},{10,11... | collective-permute-start | bytes 1572872 | tf_op jit(solution)/shard_map/ppermute | solution.py:338
  31.2 6.3 %collective-permute-start.11 = (bf16[1024,256]{1,0:T(8,128)(2,1)S(1)}, bf16[1024,256]{1,0:T(8,128)(2,1)S(1)}, u32[]{:S(2)}, u32[]{:S(2)}) collective-permute-start(bf16[1024,256]{1,0:T(8,128)(2,1)S(1)} %pack.3), channel_id=1, source_target_pairs={{0,1},{1,0},{2,3},{3,2},{4,5},{5,4},{6,7},{7,6},{8,9},{9,8},{10,11... | collective-permute-start | bytes 1572872 | tf_op jit(solution)/shard_map/ppermute | solution.py:338
  36.0 1.5 %collective-permute-start.12 = (bf16[512,256]{1,0:T(8,128)(2,1)S(1)}, bf16[512,256]{1,0:T(8,128)(2,1)S(1)}, u32[]{:S(2)}, u32[]{:S(2)}) collective-permute-start(bf16[512,256]{1,0:T(8,128)(2,1)S(1)} %collective-permute-done.6.refs_6_), channel_id=1, source_target_pairs={{0,1},{1,0},{2,3},{3,2},{4,5},{5,4},{6,7},{7,6},{8,9},{9,8},{10,11... | collective-permute-start | bytes 786440 | tf_op jit(solution)/shard_map/ppermute | solution.py:338
  41.5 2.9 %collective-permute-start.13 = (bf16[2304,256]{1,0:T(8,128)(2,1)S(1)}, bf16[2304,256]{1,0:T(8,128)(2,1)S(1)}, u32[]{:S(2)}, u32[]{:S(2)}) collective-permute-start(bf16[2304,256]{1,0:T(8,128)(2,1)S(1)} %get-tuple-element.38.own), channel_id=1, source_target_pairs={{0,1},{1,0},{2,3},{3,2},{4,5},{5,4},{6,7},{7,6},{8,9},{9,8},{10,11... | collective-permute-start | bytes 3538952 | tf_op jit(solution)/shard_map/ppermute | solution.py:338
  45.7 9.2 %collective-permute-start.14 = (bf16[512,256]{1,0:T(8,128)(2,1)S(1)}, bf16[512,256]{1,0:T(8,128)(2,1)S(1)}, u32[]{:S(2)}, u32[]{:S(2)}) collective-permute-start(bf16[512,256]{1,0:T(8,128)(2,1)S(1)} %merge_late.1), channel_id=1, source_target_pairs={{0,2},{1,3},{2,0},{3,1},{4,6},{5,7},{6,4},{7,5},{8,10},{9,11},{10,... | collective-permute-start | bytes 786440 | tf_op jit(solution)/shard_map/ppermute | solution.py:338
  49.4 11.1 %collective-permute-start.20 = (bf16[512,256]{1,0:T(8,128)(2,1)S(1)}, bf16[512,256]{1,0:T(8,128)(2,1)S(1)}, u32[]{:S(2)}, u32[]{:S(2)}) collective-permute-start(bf16[512,256]{1,0:T(8,128)(2,1)S(1)} %get-tuple-element.55), channel_id=1, source_target_pairs={{0,2},{1,3},{2,0},{3,1},{4,6},{5,7},{6,4},{7,5},{8,10},{9,11},{10,... | collective-permute-start | bytes 786440 | tf_op jit(solution)/shard_map/ppermute | solution.py:338
  49.7 20.2 %collective-permute-start.17 = (bf16[512,256]{1,0:T(8,128)(2,1)S(1)}, bf16[512,256]{1,0:T(8,128)(2,1)S(1)}, u32[]{:S(2)}, u32[]{:S(2)}) collective-permute-start(bf16[512,256]{1,0:T(8,128)(2,1)S(1)} %get-tuple-element.52), channel_id=1, source_target_pairs={{0,2},{1,3},{2,0},{3,1},{4,6},{5,7},{6,4},{7,5},{8,10},{9,11},{10,... | collective-permute-start | bytes 786440 | tf_op jit(solution)/shard_map/ppermute | solution.py:338
  54.9 16.6 %copy-start.3 = (bf16[3072,256]{1,0:T(8,128)(2,1)S(1)}, bf16[3072,256]{1,0:T(8,128)(2,1)}, u32[]{:S(2)}) copy-start(bf16[3072,256]{1,0:T(8,128)(2,1)} %constant.22.clone.table) | copy-start | bytes 4718596
  54.9 16.6 %copy-start.4 = (f32[256,256]{1,0:T(8,128)S(1)}, f32[256,256]{1,0:T(8,128)}, u32[]{:S(2)}) copy-start(f32[256,256]{1,0:T(8,128)} %get-tuple-element.47.kr) | copy-start | bytes 786436
  54.9 16.7 %copy-start.5 = (f32[256,256]{1,0:T(8,128)S(1)}, f32[256,256]{1,0:T(8,128)}, u32[]{:S(2)}) copy-start(f32[256,256]{1,0:T(8,128)} %get-tuple-element.48.ki) | copy-start | bytes 786436
  54.9 15.0 %collective-permute-start.18 = (bf16[512,256]{1,0:T(8,128)(2,1)S(1)}, bf16[512,256]{1,0:T(8,128)(2,1)S(1)}, u32[]{:S(2)}, u32[]{:S(2)}) collective-permute-start(bf16[512,256]{1,0:T(8,128)(2,1)S(1)} %hop.3), channel_id=1, source_target_pairs={{0,4},{1,5},{2,6},{3,7},{4,8},{5,9},{6,10},{7,11},{8,12},{9,13},{1... | collective-permute-start | bytes 786440 | tf_op jit(solution)/shard_map/ppermute | solution.py:338
  56.5 6.2 %collective-permute-start.15 = (bf16[256,256]{1,0:T(8,128)(2,1)S(1)}, bf16[256,256]{1,0:T(8,128)(2,1)S(1)}, u32[]{:S(2)}, u32[]{:S(2)}) collective-permute-start(bf16[256,256]{1,0:T(8,128)(2,1)S(1)} %get-tuple-element.43), channel_id=1, source_target_pairs={{1,2},{3,4},{5,6},{7,8},{9,10},{11,12},{13,14},{2,1},{4,3},{6,5},{... | collective-permute-start | bytes 393224 | tf_op jit(solution)/shard_map/ppermute | solution.py:338
  60.5 15.2 %collective-permute-start.21 = (bf16[512,256]{1,0:T(8,128)(2,1)S(1)}, bf16[512,256]{1,0:T(8,128)(2,1)S(1)}, u32[]{:S(2)}, u32[]{:S(2)}) collective-permute-start(bf16[512,256]{1,0:T(8,128)(2,1)S(1)} %hop.5), channel_id=1, source_target_pairs={{0,12},{1,13},{2,14},{3,15},{4,0},{5,1},{6,2},{7,3},{8,4},{9,5},{1... | collective-permute-start | bytes 786440 | tf_op jit(solution)/shard_map/ppermute | solution.py:338
  62.6 13.1 %collective-permute-start.16 = (bf16[512,256]{1,0:T(8,128)(2,1)S(1)}, bf16[512,256]{1,0:T(8,128)(2,1)S(1)}, u32[]{:S(2)}, u32[]{:S(2)}) collective-permute-start(bf16[512,256]{1,0:T(8,128)(2,1)S(1)} %get-tuple-element.50), channel_id=1, source_target_pairs={{0,2},{1,3},{2,0},{3,1},{4,6},{5,7},{6,4},{7,5},{8,10},{9,11},{10,... | collective-permute-start | bytes 786440 | tf_op jit(solution)/shard_map/ppermute | solution.py:338
  70.0 8.2 %collective-permute-start.19 = (bf16[512,256]{1,0:T(8,128)(2,1)S(1)}, bf16[512,256]{1,0:T(8,128)(2,1)S(1)}, u32[]{:S(2)}, u32[]{:S(2)}) collective-permute-start(bf16[512,256]{1,0:T(8,128)(2,1)S(1)} %hop.4), channel_id=1, source_target_pairs={{0,4},{1,5},{2,6},{3,7},{4,8},{5,9},{6,10},{7,11},{8,12},{9,13},{1... | collective-permute-start | bytes 786440 | tf_op jit(solution)/shard_map/ppermute | solution.py:338

commit v10 on v8

--- a/solution.py
+++ b/solution.py
@@ -49,8 +49,8 @@
 def times(a, tables, index):
     rows, size = a.shape
     high, low = parts(a)
-    t_high = tables[2 * index * size : (2 * index + 1) * size]
-    t_low = tables[(2 * index + 1) * size : (2 * index + 2) * size]
+    first = 2 * index * size
+    t_high, t_low = tables[first : first + size], tables[first + size : first + 2 * size]
     out = jnp.dot(jnp.concatenate([high, low]), t_high, preferred_element_type=F32)
     return out[:rows] + out[rows:] + jnp.dot(high, t_low, preferred_element_type=F32)
 
@@ -98,32 +98,42 @@
     )
 
 
-def smooth_kernel(mid, core_side, far_side, taps, table, out, *refs):
-    spectrum, held, sem = refs[:3], refs[3], refs[4]
-    copy = pltpu.make_async_copy(table, held, sem)
-    copy.start()
+def prepare_kernel(table, taps, mid, tables, bins, base, kr, ki, held, sem):
+    rows = table.shape[0] // 6
+    cuts = [pl.ds(i * rows, rows) for i in range(6)]
+    copies = [pltpu.make_async_copy(taps, held, sem.at[0])]
+    copies += [
+        pltpu.make_async_copy(table.at[cut], tables.at[cut], sem.at[1 + i])
+        for i, cut in enumerate(cuts)
+    ]
+    copies += [pltpu.make_async_copy(mid, bins, sem.at[7])]
+    for copy in copies:
+        copy.start()
+    copies[0].wait()
+    for i, (ref, sign) in enumerate(((base, 1.0), (kr, 1.0), (ki, -1.0))):
+        copies[1 + i].wait()
+        ref[...] = times(held[...], tables, i) * sign
+    for copy in copies[4:]:
+        copy.wait()
+
+
+def smooth_kernel(mid, core_side, far_side, tables, base, kr, ki, out):
     thirds = thirds_of(mid[...], core_side[...], far_side[...])
-    copy.wait()
-    base = times(taps[...], held, 0)
-    kr, ki = times(taps[...], held, 1), -times(taps[...], held, 2)
-    for ref, value in zip(spectrum, (base, kr, ki)):
-        ref[...] = value
-    signal = spectrum_of(thirds, held)
-    out[...] = filtered(signal, (base, kr, ki), 1.0, held, (0, 1)).astype(out.dtype)
-
-
-def unsmooth_kernel(mid, got, far_side, base, kr, ki, table, out, held, sem):
-    copy = pltpu.make_async_copy(table, held, sem)
-    copy.start()
+    signal = spectrum_of(thirds, tables)
+    taps = (base[...], kr[...], ki[...])
+    out[...] = filtered(signal, taps, 1.0, tables, (0, 1)).astype(out.dtype)
+
+
+def unsmooth_kernel(mid, got, far_side, tables, base, kr, ki, out):
     width = far_side.shape[1] // 2
     core = got[got.shape[0] - far_side.shape[0] :].astype(F32)
     far = far_side[...].astype(F32)
     thirds = thirds_of(
         mid[...], core[:, :width] + core[:, width:], far[:, :width] + far[:, width:]
     )
-    copy.wait()
-    signal = spectrum_of(thirds, held)
-    out[...] = filtered(signal, (base[...], kr[...], ki[...]), -1.0, held, (1, 2))
+    signal = spectrum_of(thirds, tables)
+    taps = (base[...], kr[...], ki[...])
+    out[...] = filtered(signal, taps, -1.0, tables, (1, 2))
 
 
 def divide(a, n):
@@ -348,24 +358,38 @@
     if half > 1:
         straight[1], across[0] = lax.optimization_barrier((straight[1], across[0]))
     straight[half] = rotate(straight[half - 1], 1)
+    table = dft_tables(2 * halfwidth)
+    mxu = 30 * 2 * latent_dim * (2 * halfwidth) ** 2
+    square = jax.ShapeDtypeStruct((latent_dim, 2 * halfwidth), F32)
+    prepared = pl.pallas_call(
+        prepare_kernel,
+        out_shape=(
+            jax.ShapeDtypeStruct(table.shape, BF16),
+            jax.ShapeDtypeStruct(latents.shape, F32),
+        )
+        + (square,) * 3,
+        in_specs=[HBM] * 3,
+        out_specs=(VMEM,) * 5,
+        scratch_shapes=[pltpu.VMEM(kernel.shape, F32), pltpu.SemaphoreType.DMA((8,))],
+        compiler_params=pltpu.CompilerParams(vmem_limit_bytes=50 * MIB),
+        cost_estimate=pl.CostEstimate(flops=mxu // 3, bytes_accessed=4 * MIB, transcendentals=0),
+        name="prepare",
+    )(table, kernel, latents)
+    straight[-1], *prepared = lax.optimization_barrier((straight[-1], *prepared))
+    spectrum, held_bins = [prepared[0], *prepared[2:]], prepared[1]
     for r in range(1, chain):
         if r != half:
             across[r] = flip(straight[r], 2)
 
-    table = dft_tables(2 * halfwidth)
-    table_scratch = [pltpu.VMEM(table.shape, BF16), pltpu.SemaphoreType.DMA(())]
-    mxu = 40 * 2 * latent_dim * (2 * halfwidth) ** 2
-    square = jax.ShapeDtypeStruct((latent_dim, 2 * halfwidth), F32)
-    smoothed, *spectrum = pl.pallas_call(
+    smoothed = pl.pallas_call(
         smooth_kernel,
-        out_shape=(jax.ShapeDtypeStruct((latent_dim, bins), BF16),) + (square,) * 3,
-        in_specs=[VMEM] * 4 + [HBM],
-        out_specs=(VMEM,) * 4,
-        scratch_shapes=table_scratch,
-        compiler_params=pltpu.CompilerParams(vmem_limit_bytes=52 * MIB),
-        cost_estimate=pl.CostEstimate(flops=mxu, bytes_accessed=4 * 2**20, transcendentals=0),
+        out_shape=jax.ShapeDtypeStruct((latent_dim, bins), BF16),
+        in_specs=[VMEM] * 7,
+        out_specs=VMEM,
+        compiler_params=pltpu.CompilerParams(vmem_limit_bytes=16 * MIB),
+        cost_estimate=pl.CostEstimate(flops=mxu, bytes_accessed=4 * MIB, transcendentals=0),
         name="smooth",
-    )(latents, core_side, far_side, kernel, table)
+    )(held_bins, core_side, far_side, *spectrum)
 
     slots = jax.ShapeDtypeStruct((entries * BLK, latent_dim), BF16)
     across[half] = flip(straight[half], 2)
@@ -444,7 +468,7 @@
         name="merge",
     )(ids, asked, terms, got)
     crossed = {r: merged[chain + r - (r > half)] for r in range(chain) if r != half}
-    other = {r: flip(part, 2) for r, part in crossed.items()}
+    other = {r: flip(part, 2) for r, part in crossed.items() if r}
 
     def hop(total, *came):
         return pl.pallas_call(
@@ -453,17 +477,20 @@
             in_specs=[VMEM] * (1 + len(came)),
             out_specs=VMEM,
             compiler_params=pltpu.CompilerParams(vmem_limit_bytes=8 * MIB),
-            cost_estimate=pl.CostEstimate(flops=10**9, bytes_accessed=MIB, transcendentals=0),
+            cost_estimate=pl.CostEstimate(flops=0, bytes_accessed=MIB, transcendentals=0),
             name="hop",
         )(total, *came)
 
     rise = hop(merged[half], back)
     rise, far_side = lax.optimization_barrier((rise, far_side))
     far_side = permute(far_side, odd_even)
-    other[half + 1], far_side = lax.optimization_barrier((other[half + 1], far_side))
     rise = rotate(rise, 1)
     for r in range(half - 1, 0, -1):
-        rise = rotate(hop(merged[r], other[r], rise), 1)
+        rise = hop(merged[r], other[r], rise)
+        if r == 1:
+            _, far_side, own = lax.optimization_barrier((rise, far_side, crossed[0]))
+            other[0] = flip(own, 2)
+        rise = rotate(rise, 1)
     fall = rotate(hop(merged[half + 1], other[half + 1]), -1)
     for r in range(half + 2, chain):
         fall = rotate(hop(merged[r], other[r], fall), -1)
@@ -472,13 +499,12 @@
     latent_grad = pl.pallas_call(
         unsmooth_kernel,
         out_shape=jax.ShapeDtypeStruct((latent_dim, bins), F32),
-        in_specs=[VMEM] * 6 + [HBM],
+        in_specs=[VMEM] * 7,
         out_specs=VMEM,
-        scratch_shapes=table_scratch,
         compiler_params=pltpu.CompilerParams(vmem_limit_bytes=16 * MIB),
-        cost_estimate=pl.CostEstimate(flops=mxu, bytes_accessed=4 * 2**20, transcendentals=0),
+        cost_estimate=pl.CostEstimate(flops=mxu, bytes_accessed=4 * MIB, transcendentals=0),
         name="unsmooth",
-    )(grad, got, far_side, *spectrum, table)
+    )(grad, got, far_side, *spectrum)
     return latent_grad, loading_grad
 
 

time: 81.4 us -> 82.6 us (1.015)
  the two profiles are of different devices: /device:TPU:1 before, /device:TPU:0 now
where the time goes in v10:
time: 82.6 us; the launch traced here: 82.4 us
  waiting for transfers between devices  36.9 us (45%)
  starting transfers between devices  25.6 us (31%)
  Pallas kernels  15.1 us (18%)
  local copies, waits for them, and re-layouts  2.02 us (2%)
  other arithmetic  1.92 us (2%)
  between operations  0.85 us (1%)
    ppermute x22, waiting for transfers between devices, permute(): return lax.ppermute(x, 'tm', pairs)  36.9 us
    ppermute x22, starting transfers between devices, permute(): return lax.ppermute(x, 'tm', pairs)  25.6 us
    pallas_call x1, Pallas kernels, local(): pl.pallas_call(functools.partial(session_kernel, entries, group, late), o...  4 us
    pallas_call x1, Pallas kernels, local(): pl.pallas_call(unsmooth_kernel, out_shape=jax.ShapeDtypeStruct((latent_di...  2.51 us
    unnamed x14, local copies, waits for them, and re-layouts  2.02 us
    pallas_call x1, Pallas kernels, local(): pl.pallas_call(prepare_kernel, out_shape=(jax.ShapeDtypeStruct(table.shap...  2.02 us
    pallas_call x1, Pallas kernels, local(): pl.pallas_call(functools.partial(merge_kernel, entries, late), out_shape=...  1.9 us
    pallas_call x1, Pallas kernels, local(): pl.pallas_call(smooth_kernel, out_shape=jax.ShapeDtypeStruct((latent_dim,...  1.69 us
  transfers between devices with their start and end apart: 22, of which 11 were waited for; matrix products, arithmetic and copies ran while one was open for 1% of the time, Pallas kernels for 12%

profile of v10, /device:TPU:0, one launch (start us, length us, event | category | flops | bytes accessed | tf_op | source)
XLA Modules:
  0.0 82.4 jit_solution(6246568010831776311)
XLA Ops:
  0.6 0.0 copy-start.5
  0.6 0.0 copy-start.6
  0.6 3.0 %collective-permute-start.5 = (bf16[512,256]{1,0:T(8,128)(2,1)}, bf16[512,256]{1,0:T(8,128)(2,1)S(1)}, u32[]{:S(2)}, u32[]{:S(2)}) collective-permute-start(bf16[512,256]{1,0:T(8,128)(2,1)} %refs_0_.5), channel_id=1, source_target_pairs={{0,2},{1,3},{2,0},{3,1},{4,6},{5,7},{6,4},{7,5},{8,10},{9,11},{10,... | collective-permute-start | bytes 786440 | tf_op jit(solution)/shard_map/ppermute | solution.py:331
  3.7 1.6 %collective-permute-start.4 = (bf16[512,256]{1,0:T(8,128)(2,1)}, bf16[512,256]{1,0:T(8,128)(2,1)S(1)}, u32[]{:S(2)}, u32[]{:S(2)}) collective-permute-start(bf16[512,256]{1,0:T(8,128)(2,1)} %refs_0_.5), channel_id=1, source_target_pairs={{0,4},{1,5},{2,6},{3,7},{4,8},{5,9},{6,10},{7,11},{8,12},{9,13},{1... | collective-permute-start | bytes 786440 | tf_op jit(solution)/shard_map/ppermute | solution.py:331
  5.3 2.2 %collective-permute-start.1 = (bf16[512,256]{1,0:T(8,128)(2,1)}, bf16[512,256]{1,0:T(8,128)(2,1)S(1)}, u32[]{:S(2)}, u32[]{:S(2)}) collective-permute-start(bf16[512,256]{1,0:T(8,128)(2,1)} %refs_0_.5), channel_id=1, source_target_pairs={{0,12},{1,13},{2,14},{3,15},{4,0},{5,1},{6,2},{7,3},{8,4},{9,5},{1... | collective-permute-start | bytes 786440 | tf_op jit(solution)/shard_map/ppermute | solution.py:331
  7.5 1.0 %slice_select_fusion = (f32[256,128]{1,0:T(8,128)S(1)}, f32[256,128]{1,0:T(8,128)S(1)}) fusion(f32[256,512]{1,0:T(8,128)} %mid.1, pred[]{:T(512)S(6)} %eq.5), kind=kLoop, calls=%fused_computation.1 | loop fusion | flops 65536 | bytes 524289 | tf_op jit(solution)/shard_map/jit(_where)/select_n | solution.py:349
  8.5 0.7 collective-permute-start.3
  9.2 1.7 %collective-permute-start.2 = (f32[256,128]{1,0:T(8,128)S(1)}, f32[256,128]{1,0:T(8,128)S(1)}, u32[]{:S(2)}, u32[]{:S(2)}) collective-permute-start(f32[256,128]{1,0:T(8,128)S(1)} %get-tuple-element.71), channel_id=1, source_target_pairs={{0,1},{1,0},{2,3},{3,2},{4,5},{5,4},{6,7},{7,6},{8,9},{9,8},{10,11... | collective-permute-start | bytes 393224 | tf_op jit(solution)/shard_map/ppermute | solution.py:331
  10.9 1.0 %copy-done = f32[256,512]{1,0:T(8,128)S(1)} copy-done((f32[256,512]{1,0:T(8,128)S(1)}, f32[256,512]{1,0:T(8,128)}, u32[]{:S(2)}) %copy-start) | copy-done | bytes 524312
  11.9 0.9 %copy-done.2 = f32[256,256]{1,0:T(8,128)S(1)} copy-done((f32[256,256]{1,0:T(8,128)S(1)}, f32[256,256]{1,0:T(8,128)}, u32[]{:S(2)}) %copy-start.2) | copy-done | bytes 262168
  12.9 2.0 %prepare.1 = (bf16[3072,256]{1,0:T(8,128)(2,1)S(1)}, f32[256,512]{1,0:T(8,128)S(1)}, f32[256,256]{1,0:T(8,128)S(1)}, f32[256,256]{1,0:T(8,128)S(1)}, f32[256,256]{1,0:T(8,128)S(1)}) custom-call(bf16[3072,256]{1,0:T(8,128)(2,1)} %constant.22.clone.table, f32[256,256]{1,0:T(8,128)S(1)} %copy-done.2, f32[256,512]{1,0:T(8,128)S(1)} %copy-done), custom_call_target="tpu_custom_call" | custom-call | flops 335544320 | bytes 4194304 | tf_op jit(solution)/shard_map/prepare/pallas_call | solution.py:364
  14.9 0.0 collective-permute-done.5.refs_4_
  14.9 0.0 collective-permute-done.4.refs_1_
  15.0 1.0 %collective-permute-start.8 = (bf16[512,256]{1,0:T(8,128)(2,1)S(1)}, bf16[512,256]{1,0:T(8,128)(2,1)S(1)}, u32[]{:S(2)}, u32[]{:S(2)}) collective-permute-start(bf16[512,256]{1,0:T(8,128)(2,1)S(1)} %collective-permute-done.4.refs_1_), channel_id=1, source_target_pairs={{0,2},{1,3},{2,0},{3,1},{4,6},{5,7},{6,4},{7,5},{8,10},{9,11},{10,... | collective-permute-start | bytes 786440 | tf_op jit(solution)/shard_map/ppermute | solution.py:331
  15.9 1.6 %collective-permute-start.6 = (bf16[512,256]{1,0:T(8,128)(2,1)S(1)}, bf16[512,256]{1,0:T(8,128)(2,1)S(1)}, u32[]{:S(2)}, u32[]{:S(2)}) collective-permute-start(bf16[512,256]{1,0:T(8,128)(2,1)S(1)} %collective-permute-done.4.refs_1_), channel_id=1, source_target_pairs={{0,4},{1,5},{2,6},{3,7},{4,8},{5,9},{6,10},{7,11},{8,12},{9,13},{1... | collective-permute-start | bytes 786440 | tf_op jit(solution)/shard_map/ppermute | solution.py:331
  17.5 1.1 %collective-permute-done.1.refs_3_ = bf16[512,256]{1,0:T(8,128)(2,1)S(1)} collective-permute-done((bf16[512,256]{1,0:T(8,128)(2,1)}, bf16[512,256]{1,0:T(8,128)(2,1)S(1)}, u32[]{:S(2)}, u32[]{:S(2)}) %collective-permute-start.1) | collective-permute-done | bytes 262176 | tf_op jit(solution)/shard_map/ppermute | solution.py:331
  18.6 0.5 collective-permute-start.9
  19.1 0.0 copy-done.5
  19.1 0.0 copy-start.1
  19.1 0.0 collective-permute-done.3.far_side
  19.1 0.1 collective-permute-start
  19.2 0.0 collective-permute-done.2.core_side
  19.2 1.7 %smooth.1.smoothed = bf16[256,512]{1,0:T(8,128)(2,1)S(1)} custom-call(f32[256,512]{1,0:T(8,128)S(1)} %get-tuple-element.41.mid, f32[256,128]{1,0:T(8,128)S(1)} %collective-permute-done.2.core_side, f32[256,128]{1,0:T(8,128)S(1)} %collective-permute-done.3.far_side, bf16[3072,256]{1,0:T(8,128)(2,1)S(1)} %get-tuple-element.42.tables, ...), custom_call_target="tpu_custom_call" | custom-call | flops 1006632960 | bytes 4194304 | tf_op jit(solution)/shard_map/smooth/pallas_call | solution.py:384
  20.9 0.0 collective-permute-done.asked
  20.9 5.3 %collective-permute-done.6.refs_2_ = bf16[512,256]{1,0:T(8,128)(2,1)S(1)} collective-permute-done((bf16[512,256]{1,0:T(8,128)(2,1)S(1)}, bf16[512,256]{1,0:T(8,128)(2,1)S(1)}, u32[]{:S(2)}, u32[]{:S(2)}) %collective-permute-start.6) | collective-permute-done | bytes 262176 | tf_op jit(solution)/shard_map/ppermute | solution.py:331
  26.2 1.0 %collective-permute-start.7 = (bf16[512,256]{1,0:T(8,128)(2,1)S(1)}, bf16[512,256]{1,0:T(8,128)(2,1)S(1)}, u32[]{:S(2)}, u32[]{:S(2)}) collective-permute-start(bf16[512,256]{1,0:T(8,128)(2,1)S(1)} %collective-permute-done.6.refs_2_), channel_id=1, source_target_pairs={{0,2},{1,3},{2,0},{3,1},{4,6},{5,7},{6,4},{7,5},{8,10},{9,11},{10,... | collective-permute-start | bytes 786440 | tf_op jit(solution)/shard_map/ppermute | solution.py:331
  27.3 0.0 collective-permute-done.8.refs_5_
  27.3 2.5 %collective-permute-done.9.refs_6_.refs_7_ = bf16[512,256]{1,0:T(8,128)(2,1)S(1)} collective-permute-done((bf16[512,256]{1,0:T(8,128)(2,1)S(1)}, bf16[512,256]{1,0:T(8,128)(2,1)S(1)}, u32[]{:S(2)}, u32[]{:S(2)}) %collective-permute-start.9) | collective-permute-done | bytes 262176 | tf_op jit(solution)/shard_map/ppermute | solution.py:331
  29.8 0.0 copy-done.1
  29.8 0.8 pack.2
  30.6 0.0 copy-start.3
  30.6 0.0 copy-start.4
  30.6 0.1 collective-permute-start.10
  30.7 0.8 pack.3
  31.5 0.6 collective-permute-start.11
  32.1 2.4 %collective-permute-done.7.refs_6_ = bf16[512,256]{1,0:T(8,128)(2,1)S(1)} collective-permute-done((bf16[512,256]{1,0:T(8,128)(2,1)S(1)}, bf16[512,256]{1,0:T(8,128)(2,1)S(1)}, u32[]{:S(2)}, u32[]{:S(2)}) %collective-permute-start.7) | collective-permute-done | bytes 262176 | tf_op jit(solution)/shard_map/ppermute | solution.py:331
  34.5 0.0 collective-permute-start.12
  34.5 1.5 %collective-permute-done.12.late_theirs = bf16[512,256]{1,0:T(8,128)(2,1)S(1)} collective-permute-done((bf16[512,256]{1,0:T(8,128)(2,1)S(1)}, bf16[512,256]{1,0:T(8,128)(2,1)S(1)}, u32[]{:S(2)}, u32[]{:S(2)}) %collective-permute-start.12) | collective-permute-done | bytes 262176 | tf_op jit(solution)/shard_map/ppermute | solution.py:331
  36.0 0.0 collective-permute-done.10.packed
  36.0 0.0 collective-permute-done.11.packed_rest
  36.0 4.0 %session.1 = (f32[256,512]{1,0:T(8,128)S(1)}, bf16[256,256]{1,0:T(8,128)(2,1)S(1)}, bf16[2304,256]{1,0:T(8,128)(2,1)S(1)}) custom-call(s32[2,8]{1,0:T(2,128)S(1)} %add_bitcast_fusion.ids, s32[2,4,8]{2,1,0:T(4,128)S(1)} %bitcast.5, bf16[256,512]{1,0:T(8,128)(2,1)S(1)} %smooth.1.smoothed, bf16[16,128,512]{2,1,0:T(8,128)(2,1)S(1)} %bitcast.4, ...), custom_call_target="tpu_custom_call" | custom-call | flops 1610612736 | bytes 8388608 | tf_op jit(solution)/shard_map/session/pallas_call | solution.py:417
  40.0 0.2 collective-permute-start.13
  40.2 2.7 %collective-permute-done.13.got = bf16[2304,256]{1,0:T(8,128)(2,1)S(1)} collective-permute-done((bf16[2304,256]{1,0:T(8,128)(2,1)S(1)}, bf16[2304,256]{1,0:T(8,128)(2,1)S(1)}, u32[]{:S(2)}, u32[]{:S(2)}) %collective-permute-start.13) | collective-permute-done | bytes 1179680 | tf_op jit(solution)/shard_map/ppermute | solution.py:331
  42.9 1.2 %merge_late.1 = bf16[512,256]{1,0:T(8,128)(2,1)S(1)} custom-call(s32[2,8]{1,0:T(2,128)S(1)} %add_bitcast_fusion.ids, s32[2,8]{1,0:T(2,128)S(1)} %collective-permute-done.asked, bf16[2304,256]{1,0:T(8,128)(2,1)S(1)} %get-tuple-element.55.own, bf16[2304,256]{1,0:T(8,128)(2,1)S(1)} %collective-permute-done.13.got), custom_call_target="tpu_custom_call" | custom-call | bytes 1048576 | tf_op jit(solution)/shard_map/merge_late/pallas_call | solution.py:447
  44.1 2.4 %collective-permute-start.15 = (bf16[512,256]{1,0:T(8,128)(2,1)S(1)}, bf16[512,256]{1,0:T(8,128)(2,1)S(1)}, u32[]{:S(2)}, u32[]{:S(2)}) collective-permute-start(bf16[512,256]{1,0:T(8,128)(2,1)S(1)} %merge_late.1), channel_id=1, source_target_pairs={{0,2},{1,3},{2,0},{3,1},{4,6},{5,7},{6,4},{7,5},{8,10},{9,11},{10,... | collective-permute-start | bytes 786440 | tf_op jit(solution)/shard_map/ppermute | solution.py:331
  46.6 1.9 %merge.1 = (f32[512,256]{1,0:T(8,128)S(1)}, f32[512,256]{1,0:T(8,128)S(1)}, f32[512,256]{1,0:T(8,128)S(1)}, f32[512,256]{1,0:T(8,128)S(1)}, bf16[512,256]{1,0:T(...) custom-call(s32[2,8]{1,0:T(2,128)S(1)} %add_bitcast_fusion.ids, ...), custom_call_target="tpu_custom_call" | custom-call | bytes 5242880 | tf_op jit(solution)/shard_map/merge/pallas_call | solution.py:460
  48.5 0.1 collective-permute-start.14
  48.6 2.0 %collective-permute-start.20 = (bf16[512,256]{1,0:T(8,128)(2,1)S(1)}, bf16[512,256]{1,0:T(8,128)(2,1)S(1)}, u32[]{:S(2)}, u32[]{:S(2)}) collective-permute-start(bf16[512,256]{1,0:T(8,128)(2,1)S(1)} %get-tuple-element.69), channel_id=1, source_target_pairs={{0,2},{1,3},{2,0},{3,1},{4,6},{5,7},{6,4},{7,5},{8,10},{9,11},{10,... | collective-permute-start | bytes 786440 | tf_op jit(solution)/shard_map/ppermute | solution.py:331
  50.6 3.1 %collective-permute-done.15.refs_0_ = bf16[512,256]{1,0:T(8,128)(2,1)S(1)} collective-permute-done((bf16[512,256]{1,0:T(8,128)(2,1)S(1)}, bf16[512,256]{1,0:T(8,128)(2,1)S(1)}, u32[]{:S(2)}, u32[]{:S(2)}) %collective-permute-start.15) | collective-permute-done | bytes 262176 | tf_op jit(solution)/shard_map/ppermute | solution.py:331
  53.7 1.6 %collective-permute-start.16 = (bf16[512,256]{1,0:T(8,128)(2,1)S(1)}, bf16[512,256]{1,0:T(8,128)(2,1)S(1)}, u32[]{:S(2)}, u32[]{:S(2)}) collective-permute-start(bf16[512,256]{1,0:T(8,128)(2,1)S(1)} %hop.3), channel_id=1, source_target_pairs={{0,4},{1,5},{2,6},{3,7},{4,8},{5,9},{6,10},{7,11},{8,12},{9,13},{1... | collective-permute-start | bytes 786440 | tf_op jit(solution)/shard_map/ppermute | solution.py:331
  55.3 0.7 collective-permute-start.17
  56.0 9.9 %collective-permute-done.20.refs_0_ = bf16[512,256]{1,0:T(8,128)(2,1)S(1)} collective-permute-done((bf16[512,256]{1,0:T(8,128)(2,1)S(1)}, bf16[512,256]{1,0:T(8,128)(2,1)S(1)}, u32[]{:S(2)}, u32[]{:S(2)}) %collective-permute-start.20) | collective-permute-done | bytes 262176 | tf_op jit(solution)/shard_map/ppermute | solution.py:331
  65.9 2.7 %collective-permute-start.21 = (bf16[512,256]{1,0:T(8,128)(2,1)S(1)}, bf16[512,256]{1,0:T(8,128)(2,1)S(1)}, u32[]{:S(2)}, u32[]{:S(2)}) collective-permute-start(bf16[512,256]{1,0:T(8,128)(2,1)S(1)} %hop.5), channel_id=1, source_target_pairs={{0,12},{1,13},{2,14},{3,15},{4,0},{5,1},{6,2},{7,3},{8,4},{9,5},{1... | collective-permute-start | bytes 786440 | tf_op jit(solution)/shard_map/ppermute | solution.py:331
  68.6 0.0 collective-permute-done.14.refs_0_
  68.7 0.0 collective-permute-done.16.refs_1_
  68.7 0.1 hop.4
  68.7 0.0 collective-permute-done.17.far_side
  68.8 0.2 collective-permute-start.18
  69.0 1.7 %collective-permute-start.19 = (bf16[512,256]{1,0:T(8,128)(2,1)S(1)}, bf16[512,256]{1,0:T(8,128)(2,1)S(1)}, u32[]{:S(2)}, u32[]{:S(2)}) collective-permute-start(bf16[512,256]{1,0:T(8,128)(2,1)S(1)} %hop.4), channel_id=1, source_target_pairs={{0,4},{1,5},{2,6},{3,7},{4,8},{5,9},{6,10},{7,11},{8,12},{9,13},{1... | collective-permute-start | bytes 786440 | tf_op jit(solution)/shard_map/ppermute | solution.py:331
  70.7 2.5 %unsmooth.1 = f32[256,512]{1,0:T(8,128)} custom-call(f32[256,512]{1,0:T(8,128)S(1)} %get-tuple-element.54.mid, bf16[2304,256]{1,0:T(8,128)(2,1)S(1)} %collective-permute-done.13.got, bf16[256,256]{1,0:T(8,128)(2,1)S(1)} %collective-permute-done.17.far_side, bf16[3072,256]{1,0:T(8,128)(2,1)S(1)} %get-tuple-element.42.tables, ...), custom_call_target="tpu_custom_call" | custom-call | flops 1006632960 | bytes 4194304 | tf_op jit(solution)/shard_map/unsmooth/pallas_call | solution.py:499
  73.2 2.3 %collective-permute-done.21 = bf16[512,256]{1,0:T(8,128)(2,1)S(1)} collective-permute-done((bf16[512,256]{1,0:T(8,128)(2,1)S(1)}, bf16[512,256]{1,0:T(8,128)(2,1)S(1)}, u32[]{:S(2)}, u32[]{:S(2)}) %collective-permute-start.21) | collective-permute-done | bytes 262176 | tf_op jit(solution)/shard_map/ppermute | solution.py:331
  75.5 0.7 collective-permute-done.18
  76.2 5.3 %collective-permute-done.19 = bf16[512,256]{1,0:T(8,128)(2,1)S(1)} collective-permute-done((bf16[512,256]{1,0:T(8,128)(2,1)S(1)}, bf16[512,256]{1,0:T(8,128)(2,1)S(1)}, u32[]{:S(2)}, u32[]{:S(2)}) %collective-permute-start.19) | collective-permute-done | bytes 262176 | tf_op jit(solution)/shard_map/ppermute | solution.py:331
  81.5 0.9 %convert_add_fusion = f32[512,256]{1,0:T(8,128)} fusion(bf16[512,256]{1,0:T(8,128)(2,1)S(1)} %collective-permute-done.21, bf16[512,256]{1,0:T(8,128)(2,1)S(1)} %collective-permute-done.19, f32[512,256]{1,0:T(8,128)S(1)} %get-tuple-element.66, bf16[512,256]{1,0:T(8,128)(2,1)S(1)} %collective-permute-done.18), kind=kLoop, calls=%fused_computation | loop fusion | flops 786432 | bytes 1835008 | tf_op jit(solution)/shard_map/add | solution.py:497
  (8 shorter events, 0.1 us)
Async XLA Ops:
  0.6 18.5 %copy-start.5 = (s32[1,2,8]{2,1,0:T(2,128)S(1)}, s32[1,2,8]{2,1,0:T(2,128)}, u32[]{:S(2)}) copy-start(s32[1,2,8]{2,1,0:T(2,128)} %param.13) | copy-start | bytes 196
  0.6 18.4 %copy-start.6 = (s32[1,2,8]{2,1,0:T(2,128)S(1)}, s32[1,2,8]{2,1,0:T(2,128)}, u32[]{:S(2)}) copy-start(s32[1,2,8]{2,1,0:T(2,128)} %param.12) | copy-start | bytes 196
  0.6 14.3 %collective-permute-start.5 = (bf16[512,256]{1,0:T(8,128)(2,1)}, bf16[512,256]{1,0:T(8,128)(2,1)S(1)}, u32[]{:S(2)}, u32[]{:S(2)}) collective-permute-start(bf16[512,256]{1,0:T(8,128)(2,1)} %refs_0_.5), channel_id=1, source_target_pairs={{0,2},{1,3},{2,0},{3,1},{4,6},{5,7},{6,4},{7,5},{8,10},{9,11},{10,... | collective-permute-start | bytes 786440 | tf_op jit(solution)/shard_map/ppermute | solution.py:331
  3.7 11.3 %collective-permute-start.4 = (bf16[512,256]{1,0:T(8,128)(2,1)}, bf16[512,256]{1,0:T(8,128)(2,1)S(1)}, u32[]{:S(2)}, u32[]{:S(2)}) collective-permute-start(bf16[512,256]{1,0:T(8,128)(2,1)} %refs_0_.5), channel_id=1, source_target_pairs={{0,4},{1,5},{2,6},{3,7},{4,8},{5,9},{6,10},{7,11},{8,12},{9,13},{1... | collective-permute-start | bytes 786440 | tf_op jit(solution)/shard_map/ppermute | solution.py:331
  5.3 13.3 %collective-permute-start.1 = (bf16[512,256]{1,0:T(8,128)(2,1)}, bf16[512,256]{1,0:T(8,128)(2,1)S(1)}, u32[]{:S(2)}, u32[]{:S(2)}) collective-permute-start(bf16[512,256]{1,0:T(8,128)(2,1)} %refs_0_.5), channel_id=1, source_target_pairs={{0,12},{1,13},{2,14},{3,15},{4,0},{5,1},{6,2},{7,3},{8,4},{9,5},{1... | collective-permute-start | bytes 786440 | tf_op jit(solution)/shard_map/ppermute | solution.py:331
  8.5 10.6 %collective-permute-start.3 = (f32[256,128]{1,0:T(8,128)S(1)}, f32[256,128]{1,0:T(8,128)S(1)}, u32[]{:S(2)}, u32[]{:S(2)}) collective-permute-start(f32[256,128]{1,0:T(8,128)S(1)} %get-tuple-element.70), channel_id=1, source_target_pairs={{1,2},{3,4},{5,6},{7,8},{9,10},{11,12},{13,14},{2,1},{4,3},{6,5},{... | collective-permute-start | bytes 393224 | tf_op jit(solution)/shard_map/ppermute | solution.py:331
  9.2 10.0 %collective-permute-start.2 = (f32[256,128]{1,0:T(8,128)S(1)}, f32[256,128]{1,0:T(8,128)S(1)}, u32[]{:S(2)}, u32[]{:S(2)}) collective-permute-start(f32[256,128]{1,0:T(8,128)S(1)} %get-tuple-element.71), channel_id=1, source_target_pairs={{0,1},{1,0},{2,3},{3,2},{4,5},{5,4},{6,7},{7,6},{8,9},{9,8},{10,11... | collective-permute-start | bytes 393224 | tf_op jit(solution)/shard_map/ppermute | solution.py:331
  10.9 1.0 %copy-start = (f32[256,512]{1,0:T(8,128)S(1)}, f32[256,512]{1,0:T(8,128)}, u32[]{:S(2)}) copy-start(f32[256,512]{1,0:T(8,128)} %mid.1) | copy-start | bytes 1572868
  11.9 0.9 %copy-start.2 = (f32[256,256]{1,0:T(8,128)S(1)}, f32[256,256]{1,0:T(8,128)}, u32[]{:S(2)}) copy-start(f32[256,256]{1,0:T(8,128)} %taps.1) | copy-start | bytes 786436
  15.0 12.3 %collective-permute-start.8 = (bf16[512,256]{1,0:T(8,128)(2,1)S(1)}, bf16[512,256]{1,0:T(8,128)(2,1)S(1)}, u32[]{:S(2)}, u32[]{:S(2)}) collective-permute-start(bf16[512,256]{1,0:T(8,128)(2,1)S(1)} %collective-permute-done.4.refs_1_), channel_id=1, source_target_pairs={{0,2},{1,3},{2,0},{3,1},{4,6},{5,7},{6,4},{7,5},{8,10},{9,11},{10,... | collective-permute-start | bytes 786440 | tf_op jit(solution)/shard_map/ppermute | solution.py:331
  15.9 10.3 %collective-permute-start.6 = (bf16[512,256]{1,0:T(8,128)(2,1)S(1)}, bf16[512,256]{1,0:T(8,128)(2,1)S(1)}, u32[]{:S(2)}, u32[]{:S(2)}) collective-permute-start(bf16[512,256]{1,0:T(8,128)(2,1)S(1)} %collective-permute-done.4.refs_1_), channel_id=1, source_target_pairs={{0,4},{1,5},{2,6},{3,7},{4,8},{5,9},{6,10},{7,11},{8,12},{9,13},{1... | collective-permute-start | bytes 786440 | tf_op jit(solution)/shard_map/ppermute | solution.py:331
  18.6 11.2 %collective-permute-start.9 = (bf16[512,256]{1,0:T(8,128)(2,1)S(1)}, bf16[512,256]{1,0:T(8,128)(2,1)S(1)}, u32[]{:S(2)}, u32[]{:S(2)}) collective-permute-start(bf16[512,256]{1,0:T(8,128)(2,1)S(1)} %collective-permute-done.1.refs_3_), channel_id=1, source_target_pairs={{0,2},{1,3},{2,0},{3,1},{4,6},{5,7},{6,4},{7,5},{8,10},{9,11},{10,... | collective-permute-start | bytes 786440 | tf_op jit(solution)/shard_map/ppermute | solution.py:331
  19.1 10.7 %copy-start.1 = (bf16[512,256]{1,0:T(8,128)(2,1)S(1)}, bf16[512,256]{1,0:T(8,128)(2,1)}, u32[]{:S(2)}) copy-start(bf16[512,256]{1,0:T(8,128)(2,1)} %refs_0_.5) | copy-start | bytes 786436
  19.1 1.8 %collective-permute-start = (s32[2,8]{1,0:T(2,128)S(1)}, s32[2,8]{1,0:T(2,128)S(1)}, u32[]{:S(2)}, u32[]{:S(2)}) collective-permute-start(s32[2,8]{1,0:T(2,128)S(1)} %add_bitcast_fusion.ids), channel_id=1, source_target_pairs={{0,1},{1,0},{2,3},{3,2},{4,5},{5,4},{6,7},{7,6},{8,9},{9,8},{10,11... | collective-permute-start | bytes 200 | tf_op jit(solution)/shard_map/ppermute | solution.py:331
  26.2 8.2 %collective-permute-start.7 = (bf16[512,256]{1,0:T(8,128)(2,1)S(1)}, bf16[512,256]{1,0:T(8,128)(2,1)S(1)}, u32[]{:S(2)}, u32[]{:S(2)}) collective-permute-start(bf16[512,256]{1,0:T(8,128)(2,1)S(1)} %collective-permute-done.6.refs_2_), channel_id=1, source_target_pairs={{0,2},{1,3},{2,0},{3,1},{4,6},{5,7},{6,4},{7,5},{8,10},{9,11},{10,... | collective-permute-start | bytes 786440 | tf_op jit(solution)/shard_map/ppermute | solution.py:331
  30.6 5.4 %copy-start.3 = (bf16[2,8,128,512]{3,2,1,0:T(8,128)(2,1)S(1)}, bf16[2,8,128,512]{3,2,1,0:T(8,128)(2,1)}, u32[]{:S(2)}) copy-start(bf16[2,8,128,512]{3,2,1,0:T(8,128)(2,1)} %param.11) | copy-start | bytes 6291460
  30.6 5.4 %copy-start.4 = (s32[2,8,4]{1,2,0:T(4,128)S(1)}, s32[2,8,4]{1,2,0:T(4,128)}, u32[]{:S(2)}) copy-start(s32[2,8,4]{1,2,0:T(4,128)} %param.14) | copy-start | bytes 772
  30.6 5.4 %collective-permute-start.10 = (bf16[1024,256]{1,0:T(8,128)(2,1)S(1)}, bf16[1024,256]{1,0:T(8,128)(2,1)S(1)}, u32[]{:S(2)}, u32[]{:S(2)}) collective-permute-start(bf16[1024,256]{1,0:T(8,128)(2,1)S(1)} %pack.2), channel_id=1, source_target_pairs={{0,1},{1,0},{2,3},{3,2},{4,5},{5,4},{6,7},{7,6},{8,9},{9,8},{10,11... | collective-permute-start | bytes 1572872 | tf_op jit(solution)/shard_map/ppermute | solution.py:331
  31.5 4.5 %collective-permute-start.11 = (bf16[1024,256]{1,0:T(8,128)(2,1)S(1)}, bf16[1024,256]{1,0:T(8,128)(2,1)S(1)}, u32[]{:S(2)}, u32[]{:S(2)}) collective-permute-start(bf16[1024,256]{1,0:T(8,128)(2,1)S(1)} %pack.3), channel_id=1, source_target_pairs={{0,1},{1,0},{2,3},{3,2},{4,5},{5,4},{6,7},{7,6},{8,9},{9,8},{10,11... | collective-permute-start | bytes 1572872 | tf_op jit(solution)/shard_map/ppermute | solution.py:331
  34.5 1.5 %collective-permute-start.12 = (bf16[512,256]{1,0:T(8,128)(2,1)S(1)}, bf16[512,256]{1,0:T(8,128)(2,1)S(1)}, u32[]{:S(2)}, u32[]{:S(2)}) collective-permute-start(bf16[512,256]{1,0:T(8,128)(2,1)S(1)} %collective-permute-done.7.refs_6_), channel_id=1, source_target_pairs={{0,1},{1,0},{2,3},{3,2},{4,5},{5,4},{6,7},{7,6},{8,9},{9,8},{10,11... | collective-permute-start | bytes 786440 | tf_op jit(solution)/shard_map/ppermute | solution.py:331
  40.0 2.9 %collective-permute-start.13 = (bf16[2304,256]{1,0:T(8,128)(2,1)S(1)}, bf16[2304,256]{1,0:T(8,128)(2,1)S(1)}, u32[]{:S(2)}, u32[]{:S(2)}) collective-permute-start(bf16[2304,256]{1,0:T(8,128)(2,1)S(1)} %get-tuple-element.55.own), channel_id=1, source_target_pairs={{0,1},{1,0},{2,3},{3,2},{4,5},{5,4},{6,7},{7,6},{8,9},{9,8},{10,11... | collective-permute-start | bytes 3538952 | tf_op jit(solution)/shard_map/ppermute | solution.py:331
  44.1 9.5 %collective-permute-start.15 = (bf16[512,256]{1,0:T(8,128)(2,1)S(1)}, bf16[512,256]{1,0:T(8,128)(2,1)S(1)}, u32[]{:S(2)}, u32[]{:S(2)}) collective-permute-start(bf16[512,256]{1,0:T(8,128)(2,1)S(1)} %merge_late.1), channel_id=1, source_target_pairs={{0,2},{1,3},{2,0},{3,1},{4,6},{5,7},{6,4},{7,5},{8,10},{9,11},{10,... | collective-permute-start | bytes 786440 | tf_op jit(solution)/shard_map/ppermute | solution.py:331
  48.5 20.2 %collective-permute-start.14 = (bf16[512,256]{1,0:T(8,128)(2,1)S(1)}, bf16[512,256]{1,0:T(8,128)(2,1)S(1)}, u32[]{:S(2)}, u32[]{:S(2)}) collective-permute-start(bf16[512,256]{1,0:T(8,128)(2,1)S(1)} %get-tuple-element.58), channel_id=1, source_target_pairs={{0,2},{1,3},{2,0},{3,1},{4,6},{5,7},{6,4},{7,5},{8,10},{9,11},{10,... | collective-permute-start | bytes 786440 | tf_op jit(solution)/shard_map/ppermute | solution.py:331
  48.6 17.3 %collective-permute-start.20 = (bf16[512,256]{1,0:T(8,128)(2,1)S(1)}, bf16[512,256]{1,0:T(8,128)(2,1)S(1)}, u32[]{:S(2)}, u32[]{:S(2)}) collective-permute-start(bf16[512,256]{1,0:T(8,128)(2,1)S(1)} %get-tuple-element.69), channel_id=1, source_target_pairs={{0,2},{1,3},{2,0},{3,1},{4,6},{5,7},{6,4},{7,5},{8,10},{9,11},{10,... | collective-permute-start | bytes 786440 | tf_op jit(solution)/shard_map/ppermute | solution.py:331
  53.7 14.9 %collective-permute-start.16 = (bf16[512,256]{1,0:T(8,128)(2,1)S(1)}, bf16[512,256]{1,0:T(8,128)(2,1)S(1)}, u32[]{:S(2)}, u32[]{:S(2)}) collective-permute-start(bf16[512,256]{1,0:T(8,128)(2,1)S(1)} %hop.3), channel_id=1, source_target_pairs={{0,4},{1,5},{2,6},{3,7},{4,8},{5,9},{6,10},{7,11},{8,12},{9,13},{1... | collective-permute-start | bytes 786440 | tf_op jit(solution)/shard_map/ppermute | solution.py:331
  55.3 13.4 %collective-permute-start.17 = (bf16[256,256]{1,0:T(8,128)(2,1)S(1)}, bf16[256,256]{1,0:T(8,128)(2,1)S(1)}, u32[]{:S(2)}, u32[]{:S(2)}) collective-permute-start(bf16[256,256]{1,0:T(8,128)(2,1)S(1)} %get-tuple-element.63), channel_id=1, source_target_pairs={{1,2},{3,4},{5,6},{7,8},{9,10},{11,12},{13,14},{2,1},{4,3},{6,5},{... | collective-permute-start | bytes 393224 | tf_op jit(solution)/shard_map/ppermute | solution.py:331
  65.9 9.5 %collective-permute-start.21 = (bf16[512,256]{1,0:T(8,128)(2,1)S(1)}, bf16[512,256]{1,0:T(8,128)(2,1)S(1)}, u32[]{:S(2)}, u32[]{:S(2)}) collective-permute-start(bf16[512,256]{1,0:T(8,128)(2,1)S(1)} %hop.5), channel_id=1, source_target_pairs={{0,12},{1,13},{2,14},{3,15},{4,0},{5,1},{6,2},{7,3},{8,4},{9,5},{1... | collective-permute-start | bytes 786440 | tf_op jit(solution)/shard_map/ppermute | solution.py:331
  68.8 7.4 %collective-permute-start.18 = (bf16[512,256]{1,0:T(8,128)(2,1)S(1)}, bf16[512,256]{1,0:T(8,128)(2,1)S(1)}, u32[]{:S(2)}, u32[]{:S(2)}) collective-permute-start(bf16[512,256]{1,0:T(8,128)(2,1)S(1)} %get-tuple-element.67), channel_id=1, source_target_pairs={{0,2},{1,3},{2,0},{3,1},{4,6},{5,7},{6,4},{7,5},{8,10},{9,11},{10,... | collective-permute-start | bytes 786440 | tf_op jit(solution)/shard_map/ppermute | solution.py:331
  69.0 12.5 %collective-permute-start.19 = (bf16[512,256]{1,0:T(8,128)(2,1)S(1)}, bf16[512,256]{1,0:T(8,128)(2,1)S(1)}, u32[]{:S(2)}, u32[]{:S(2)}) collective-permute-start(bf16[512,256]{1,0:T(8,128)(2,1)S(1)} %hop.4), channel_id=1, source_target_pairs={{0,4},{1,5},{2,6},{3,7},{4,8},{5,9},{6,10},{7,11},{8,12},{9,13},{1... | collective-permute-start | bytes 786440 | tf_op jit(solution)/shard_map/ppermute | solution.py:331

commit v11 on v10

--- a/solution.py
+++ b/solution.py
@@ -358,6 +358,7 @@
     if half > 1:
         straight[1], across[0] = lax.optimization_barrier((straight[1], across[0]))
     straight[half] = rotate(straight[half - 1], 1)
+    straight[1], kernel = lax.optimization_barrier((straight[1], kernel))
     table = dft_tables(2 * halfwidth)
     mxu = 30 * 2 * latent_dim * (2 * halfwidth) ** 2
     square = jax.ShapeDtypeStruct((latent_dim, 2 * halfwidth), F32)
@@ -484,13 +485,11 @@
     rise = hop(merged[half], back)
     rise, far_side = lax.optimization_barrier((rise, far_side))
     far_side = permute(far_side, odd_even)
+    far_side, own = lax.optimization_barrier((far_side, crossed[0]))
+    other[0] = flip(own, 2)
     rise = rotate(rise, 1)
     for r in range(half - 1, 0, -1):
-        rise = hop(merged[r], other[r], rise)
-        if r == 1:
-            _, far_side, own = lax.optimization_barrier((rise, far_side, crossed[0]))
-            other[0] = flip(own, 2)
-        rise = rotate(rise, 1)
+        rise = rotate(hop(merged[r], other[r], rise), 1)
     fall = rotate(hop(merged[half + 1], other[half + 1]), -1)
     for r in range(half + 2, chain):
         fall = rotate(hop(merged[r], other[r], fall), -1)

time: 82.6 us -> 77.1 us (0.933)
  waiting for transfers between devices: 36.9 us -> 22.6 us
  starting transfers between devices: 25.6 us -> 34.5 us
    ppermute x22, waiting for transfers between devices: 36.9 us -> 22.6 us  [permute(): return lax.ppermute(x, 'tm', pairs)]
    ppermute x22, starting transfers between devices: 25.6 us -> 34.5 us  [permute(): return lax.ppermute(x, 'tm', pairs)]
  transfers between devices with their start and end apart: 22 -> 22, of which waited for: 11 -> 9; matrix products, arithmetic and copies ran while one was open for 1% -> 1% of each run, Pallas kernels for 12% -> 13%
where the time goes in v11:
time: 77.1 us; the launch traced here: 76.9 us
  starting transfers between devices  34.5 us (45%)
  waiting for transfers between devices  22.6 us (29%)
  Pallas kernels  15 us (19%)
  local copies, waits for them, and re-layouts  2.02 us (3%)
  other arithmetic  1.92 us (2%)
  between operations  0.83 us (1%)
    ppermute x22, starting transfers between devices, permute(): return lax.ppermute(x, 'tm', pairs)  34.5 us
    ppermute x22, waiting for transfers between devices, permute(): return lax.ppermute(x, 'tm', pairs)  22.6 us
    pallas_call x1, Pallas kernels, local(): pl.pallas_call(functools.partial(session_kernel, entries, group, late), o...  3.99 us
    pallas_call x1, Pallas kernels, local(): pl.pallas_call(unsmooth_kernel, out_shape=jax.ShapeDtypeStruct((latent_di...  2.51 us
    unnamed x14, local copies, waits for them, and re-layouts  2.02 us
    pallas_call x1, Pallas kernels, local(): pl.pallas_call(prepare_kernel, out_shape=(jax.ShapeDtypeStruct(table.shap...  2.02 us
    pallas_call x1, Pallas kernels, local(): pl.pallas_call(functools.partial(merge_kernel, entries, late), out_shape=...  1.85 us
    pallas_call x1, Pallas kernels, local(): pl.pallas_call(smooth_kernel, out_shape=jax.ShapeDtypeStruct((latent_dim,...  1.68 us
  transfers between devices with their start and end apart: 22, of which 9 were waited for; matrix products, arithmetic and copies ran while one was open for 1% of the time, Pallas kernels for 13%

profile of v11, /device:TPU:0, one launch (start us, length us, event | category | flops | bytes accessed | tf_op | source)
XLA Modules:
  0.0 76.9 jit_solution(334096428810339661)
XLA Ops:
  0.6 0.0 copy-start.5
  0.6 0.0 copy-start.6
  0.6 3.0 %collective-permute-start.3 = (bf16[512,256]{1,0:T(8,128)(2,1)}, bf16[512,256]{1,0:T(8,128)(2,1)S(1)}, u32[]{:S(2)}, u32[]{:S(2)}) collective-permute-start(bf16[512,256]{1,0:T(8,128)(2,1)} %refs_0_.5), channel_id=1, source_target_pairs={{0,2},{1,3},{2,0},{3,1},{4,6},{5,7},{6,4},{7,5},{8,10},{9,11},{10,... | collective-permute-start | bytes 786440 | tf_op jit(solution)/shard_map/ppermute | solution.py:331
  3.7 1.6 %collective-permute-start.2 = (bf16[512,256]{1,0:T(8,128)(2,1)}, bf16[512,256]{1,0:T(8,128)(2,1)S(1)}, u32[]{:S(2)}, u32[]{:S(2)}) collective-permute-start(bf16[512,256]{1,0:T(8,128)(2,1)} %refs_0_.5), channel_id=1, source_target_pairs={{0,4},{1,5},{2,6},{3,7},{4,8},{5,9},{6,10},{7,11},{8,12},{9,13},{1... | collective-permute-start | bytes 786440 | tf_op jit(solution)/shard_map/ppermute | solution.py:331
  5.3 2.2 %collective-permute-start.1 = (bf16[512,256]{1,0:T(8,128)(2,1)}, bf16[512,256]{1,0:T(8,128)(2,1)S(1)}, u32[]{:S(2)}, u32[]{:S(2)}) collective-permute-start(bf16[512,256]{1,0:T(8,128)(2,1)} %refs_0_.5), channel_id=1, source_target_pairs={{0,12},{1,13},{2,14},{3,15},{4,0},{5,1},{6,2},{7,3},{8,4},{9,5},{1... | collective-permute-start | bytes 786440 | tf_op jit(solution)/shard_map/ppermute | solution.py:331
  7.5 1.0 %slice_select_fusion = (f32[256,128]{1,0:T(8,128)S(1)}, f32[256,128]{1,0:T(8,128)S(1)}) fusion(f32[256,512]{1,0:T(8,128)} %mid.1, pred[]{:T(512)S(6)} %eq.5), kind=kLoop, calls=%fused_computation.1 | loop fusion | flops 65536 | bytes 524289 | tf_op jit(solution)/shard_map/jit(_where)/select_n | solution.py:349
  8.5 0.7 collective-permute-start.5
  9.2 1.7 %collective-permute-start.4 = (f32[256,128]{1,0:T(8,128)S(1)}, f32[256,128]{1,0:T(8,128)S(1)}, u32[]{:S(2)}, u32[]{:S(2)}) collective-permute-start(f32[256,128]{1,0:T(8,128)S(1)} %get-tuple-element.75), channel_id=1, source_target_pairs={{0,1},{1,0},{2,3},{3,2},{4,5},{5,4},{6,7},{7,6},{8,9},{9,8},{10,11... | collective-permute-start | bytes 393224 | tf_op jit(solution)/shard_map/ppermute | solution.py:331
  10.9 0.0 collective-permute-done.3.refs_4_
  10.9 4.1 %collective-permute-done.2.refs_1_ = bf16[512,256]{1,0:T(8,128)(2,1)S(1)} collective-permute-done((bf16[512,256]{1,0:T(8,128)(2,1)}, bf16[512,256]{1,0:T(8,128)(2,1)S(1)}, u32[]{:S(2)}, u32[]{:S(2)}) %collective-permute-start.2) | collective-permute-done | bytes 262176 | tf_op jit(solution)/shard_map/ppermute | solution.py:331
  15.0 0.0 collective-permute-start.6
  15.0 0.3 collective-permute-start.8
  15.3 1.0 %copy-done = f32[256,512]{1,0:T(8,128)S(1)} copy-done((f32[256,512]{1,0:T(8,128)S(1)}, f32[256,512]{1,0:T(8,128)}, u32[]{:S(2)}) %copy-start) | copy-done | bytes 524312
  16.3 0.9 %copy-done.2 = f32[256,256]{1,0:T(8,128)S(1)} copy-done((f32[256,256]{1,0:T(8,128)S(1)}, f32[256,256]{1,0:T(8,128)}, u32[]{:S(2)}) %copy-start.2) | copy-done | bytes 262168
  17.2 2.0 %prepare.1 = (bf16[3072,256]{1,0:T(8,128)(2,1)S(1)}, f32[256,512]{1,0:T(8,128)S(1)}, f32[256,256]{1,0:T(8,128)S(1)}, f32[256,256]{1,0:T(8,128)S(1)}, f32[256,256]{1,0:T(8,128)S(1)}) custom-call(bf16[3072,256]{1,0:T(8,128)(2,1)} %constant.22.clone.table, f32[256,256]{1,0:T(8,128)S(1)} %copy-done.2, f32[256,512]{1,0:T(8,128)S(1)} %copy-done), custom_call_target="tpu_custom_call" | custom-call | flops 335544320 | bytes 4194304 | tf_op jit(solution)/shard_map/prepare/pallas_call | solution.py:365
  19.3 0.0 collective-permute-done.1.refs_3_
  19.3 1.8 %collective-permute-start.9 = (bf16[512,256]{1,0:T(8,128)(2,1)S(1)}, bf16[512,256]{1,0:T(8,128)(2,1)S(1)}, u32[]{:S(2)}, u32[]{:S(2)}) collective-permute-start(bf16[512,256]{1,0:T(8,128)(2,1)S(1)} %collective-permute-done.1.refs_3_), channel_id=1, source_target_pairs={{0,2},{1,3},{2,0},{3,1},{4,6},{5,7},{6,4},{7,5},{8,10},{9,11},{10,... | collective-permute-start | bytes 786440 | tf_op jit(solution)/shard_map/ppermute | solution.py:331
  21.1 0.0 copy-done.5
  21.1 0.0 copy-start.1
  21.1 0.0 collective-permute-done.5.far_side
  21.1 0.1 collective-permute-start
  21.2 0.0 collective-permute-done.4.core_side
  21.2 1.7 %smooth.1.smoothed = bf16[256,512]{1,0:T(8,128)(2,1)S(1)} custom-call(f32[256,512]{1,0:T(8,128)S(1)} %get-tuple-element.45.mid, f32[256,128]{1,0:T(8,128)S(1)} %collective-permute-done.4.core_side, f32[256,128]{1,0:T(8,128)S(1)} %collective-permute-done.5.far_side, bf16[3072,256]{1,0:T(8,128)(2,1)S(1)} %get-tuple-element.46.tables, ...), custom_call_target="tpu_custom_call" | custom-call | flops 1006632960 | bytes 4194304 | tf_op jit(solution)/shard_map/smooth/pallas_call | solution.py:385
  22.9 0.0 collective-permute-done.asked
  22.9 3.3 %collective-permute-done.6.refs_2_ = bf16[512,256]{1,0:T(8,128)(2,1)S(1)} collective-permute-done((bf16[512,256]{1,0:T(8,128)(2,1)S(1)}, bf16[512,256]{1,0:T(8,128)(2,1)S(1)}, u32[]{:S(2)}, u32[]{:S(2)}) %collective-permute-start.6) | collective-permute-done | bytes 262176 | tf_op jit(solution)/shard_map/ppermute | solution.py:331
  26.2 0.0 collective-permute-start.7
  26.2 0.0 collective-permute-done.8.refs_5_
  26.2 1.3 %collective-permute-done.9.refs_6_.refs_7_ = bf16[512,256]{1,0:T(8,128)(2,1)S(1)} collective-permute-done((bf16[512,256]{1,0:T(8,128)(2,1)S(1)}, bf16[512,256]{1,0:T(8,128)(2,1)S(1)}, u32[]{:S(2)}, u32[]{:S(2)}) %collective-permute-start.9) | collective-permute-done | bytes 262176 | tf_op jit(solution)/shard_map/ppermute | solution.py:331
  27.5 0.8 %pack.2 = bf16[1024,256]{1,0:T(8,128)(2,1)S(1)} custom-call(s32[2,8]{1,0:T(2,128)S(1)} %collective-permute-done.asked, bf16[512,256]{1,0:T(8,128)(2,1)S(1)} %copy-done.1, bf16[512,256]{1,0:T(8,128)(2,1)S(1)} %collective-permute-done.2.refs_1_, bf16[512,256]{1,0:T(8,128)(2,1)S(1)} %collective-permute-done.6.refs_2_, ...), custom_call_target="tpu_custom_call" | custom-call | bytes 1048576 | tf_op jit(solution)/shard_map/pack/pallas_call | solution.py:400
  28.3 0.0 copy-start.3
  28.3 0.0 copy-start.4
  28.3 0.1 collective-permute-start.10
  28.4 0.8 %pack.3 = bf16[1024,256]{1,0:T(8,128)(2,1)S(1)} custom-call(s32[2,8]{1,0:T(2,128)S(1)} %collective-permute-done.asked, bf16[512,256]{1,0:T(8,128)(2,1)S(1)} %copy-done.1, bf16[512,256]{1,0:T(8,128)(2,1)S(1)} %collective-permute-done.2.refs_1_, bf16[512,256]{1,0:T(8,128)(2,1)S(1)} %collective-permute-done.6.refs_2_, ...), custom_call_target="tpu_custom_call" | custom-call | bytes 1048576 | tf_op jit(solution)/shard_map/pack/pallas_call | solution.py:400
  29.2 0.6 collective-permute-start.11
  29.8 2.8 %collective-permute-done.7.refs_6_ = bf16[512,256]{1,0:T(8,128)(2,1)S(1)} collective-permute-done((bf16[512,256]{1,0:T(8,128)(2,1)S(1)}, bf16[512,256]{1,0:T(8,128)(2,1)S(1)}, u32[]{:S(2)}, u32[]{:S(2)}) %collective-permute-start.7) | collective-permute-done | bytes 262176 | tf_op jit(solution)/shard_map/ppermute | solution.py:331
  32.6 0.0 collective-permute-start.12
  32.6 1.5 %collective-permute-done.12.late_theirs = bf16[512,256]{1,0:T(8,128)(2,1)S(1)} collective-permute-done((bf16[512,256]{1,0:T(8,128)(2,1)S(1)}, bf16[512,256]{1,0:T(8,128)(2,1)S(1)}, u32[]{:S(2)}, u32[]{:S(2)}) %collective-permute-start.12) | collective-permute-done | bytes 262176 | tf_op jit(solution)/shard_map/ppermute | solution.py:331
  34.1 0.0 collective-permute-done.10.packed
  34.1 0.0 collective-permute-done.11.packed_rest
  34.2 0.0 copy-done.4
  34.2 4.0 %session.1 = (f32[256,512]{1,0:T(8,128)S(1)}, bf16[256,256]{1,0:T(8,128)(2,1)S(1)}, bf16[2304,256]{1,0:T(8,128)(2,1)S(1)}) custom-call(s32[2,8]{1,0:T(2,128)S(1)} %add_bitcast_fusion.ids, s32[2,4,8]{2,1,0:T(4,128)S(1)} %bitcast.5, bf16[256,512]{1,0:T(8,128)(2,1)S(1)} %smooth.1.smoothed, bf16[16,128,512]{2,1,0:T(8,128)(2,1)S(1)} %bitcast.4, ...), custom_call_target="tpu_custom_call" | custom-call | flops 1610612736 | bytes 8388608 | tf_op jit(solution)/shard_map/session/pallas_call | solution.py:418
  38.2 0.2 collective-permute-start.13
  38.4 2.7 %collective-permute-done.13.got = bf16[2304,256]{1,0:T(8,128)(2,1)S(1)} collective-permute-done((bf16[2304,256]{1,0:T(8,128)(2,1)S(1)}, bf16[2304,256]{1,0:T(8,128)(2,1)S(1)}, u32[]{:S(2)}, u32[]{:S(2)}) %collective-permute-start.13) | collective-permute-done | bytes 1179680 | tf_op jit(solution)/shard_map/ppermute | solution.py:331
  41.1 1.2 %merge_late.1 = bf16[512,256]{1,0:T(8,128)(2,1)S(1)} custom-call(s32[2,8]{1,0:T(2,128)S(1)} %add_bitcast_fusion.ids, s32[2,8]{1,0:T(2,128)S(1)} %collective-permute-done.asked, bf16[2304,256]{1,0:T(8,128)(2,1)S(1)} %get-tuple-element.59.own, bf16[2304,256]{1,0:T(8,128)(2,1)S(1)} %collective-permute-done.13.got), custom_call_target="tpu_custom_call" | custom-call | bytes 1048576 | tf_op jit(solution)/shard_map/merge_late/pallas_call | solution.py:448
  42.3 1.7 %collective-permute-start.14 = (bf16[512,256]{1,0:T(8,128)(2,1)S(1)}, bf16[512,256]{1,0:T(8,128)(2,1)S(1)}, u32[]{:S(2)}, u32[]{:S(2)}) collective-permute-start(bf16[512,256]{1,0:T(8,128)(2,1)S(1)} %merge_late.1), channel_id=1, source_target_pairs={{0,2},{1,3},{2,0},{3,1},{4,6},{5,7},{6,4},{7,5},{8,10},{9,11},{10,... | collective-permute-start | bytes 786440 | tf_op jit(solution)/shard_map/ppermute | solution.py:331
  44.0 1.9 %merge.1 = (f32[512,256]{1,0:T(8,128)S(1)}, f32[512,256]{1,0:T(8,128)S(1)}, f32[512,256]{1,0:T(8,128)S(1)}, f32[512,256]{1,0:T(8,128)S(1)}, bf16[512,256]{1,0:T(...) custom-call(s32[2,8]{1,0:T(2,128)S(1)} %add_bitcast_fusion.ids, ...), custom_call_target="tpu_custom_call" | custom-call | bytes 5242880 | tf_op jit(solution)/shard_map/merge/pallas_call | solution.py:461
  45.9 0.5 collective-permute-start.20
  46.4 1.6 %collective-permute-start.17 = (bf16[512,256]{1,0:T(8,128)(2,1)S(1)}, bf16[512,256]{1,0:T(8,128)(2,1)S(1)}, u32[]{:S(2)}, u32[]{:S(2)}) collective-permute-start(bf16[512,256]{1,0:T(8,128)(2,1)S(1)} %get-tuple-element.70), channel_id=1, source_target_pairs={{0,2},{1,3},{2,0},{3,1},{4,6},{5,7},{6,4},{7,5},{8,10},{9,11},{10,... | collective-permute-start | bytes 786440 | tf_op jit(solution)/shard_map/ppermute | solution.py:331
  48.0 3.5 %collective-permute-done.14.refs_0_ = bf16[512,256]{1,0:T(8,128)(2,1)S(1)} collective-permute-done((bf16[512,256]{1,0:T(8,128)(2,1)S(1)}, bf16[512,256]{1,0:T(8,128)(2,1)S(1)}, u32[]{:S(2)}, u32[]{:S(2)}) %collective-permute-start.14) | collective-permute-done | bytes 262176 | tf_op jit(solution)/shard_map/ppermute | solution.py:331
  51.6 4.2 %collective-permute-start.18 = (bf16[512,256]{1,0:T(8,128)(2,1)S(1)}, bf16[512,256]{1,0:T(8,128)(2,1)S(1)}, u32[]{:S(2)}, u32[]{:S(2)}) collective-permute-start(bf16[512,256]{1,0:T(8,128)(2,1)S(1)} %hop.3), channel_id=1, source_target_pairs={{0,4},{1,5},{2,6},{3,7},{4,8},{5,9},{6,10},{7,11},{8,12},{9,13},{1... | collective-permute-start | bytes 786440 | tf_op jit(solution)/shard_map/ppermute | solution.py:331
  55.7 0.7 collective-permute-start.15
  56.4 0.7 collective-permute-done.20.refs_0_
  57.2 4.5 %collective-permute-start.21 = (bf16[512,256]{1,0:T(8,128)(2,1)S(1)}, bf16[512,256]{1,0:T(8,128)(2,1)S(1)}, u32[]{:S(2)}, u32[]{:S(2)}) collective-permute-start(bf16[512,256]{1,0:T(8,128)(2,1)S(1)} %hop.5), channel_id=1, source_target_pairs={{0,12},{1,13},{2,14},{3,15},{4,0},{5,1},{6,2},{7,3},{8,4},{9,5},{1... | collective-permute-start | bytes 786440 | tf_op jit(solution)/shard_map/ppermute | solution.py:331
  61.7 0.0 collective-permute-done.15.far_side
  61.7 4.7 %collective-permute-start.16 = (bf16[512,256]{1,0:T(8,128)(2,1)S(1)}, bf16[512,256]{1,0:T(8,128)(2,1)S(1)}, u32[]{:S(2)}, u32[]{:S(2)}) collective-permute-start(bf16[512,256]{1,0:T(8,128)(2,1)S(1)} %get-tuple-element.68), channel_id=1, source_target_pairs={{0,2},{1,3},{2,0},{3,1},{4,6},{5,7},{6,4},{7,5},{8,10},{9,11},{10,... | collective-permute-start | bytes 786440 | tf_op jit(solution)/shard_map/ppermute | solution.py:331
  66.4 0.0 collective-permute-done.17.refs_0_
  66.4 0.0 collective-permute-done.18.refs_1_
  66.4 0.1 hop.4
  66.5 4.3 %collective-permute-start.19 = (bf16[512,256]{1,0:T(8,128)(2,1)S(1)}, bf16[512,256]{1,0:T(8,128)(2,1)S(1)}, u32[]{:S(2)}, u32[]{:S(2)}) collective-permute-start(bf16[512,256]{1,0:T(8,128)(2,1)S(1)} %hop.4), channel_id=1, source_target_pairs={{0,4},{1,5},{2,6},{3,7},{4,8},{5,9},{6,10},{7,11},{8,12},{9,13},{1... | collective-permute-start | bytes 786440 | tf_op jit(solution)/shard_map/ppermute | solution.py:331
  70.8 2.5 %unsmooth.1 = f32[256,512]{1,0:T(8,128)} custom-call(f32[256,512]{1,0:T(8,128)S(1)} %get-tuple-element.58.mid, bf16[2304,256]{1,0:T(8,128)(2,1)S(1)} %collective-permute-done.13.got, bf16[256,256]{1,0:T(8,128)(2,1)S(1)} %collective-permute-done.15.far_side, bf16[3072,256]{1,0:T(8,128)(2,1)S(1)} %get-tuple-element.46.tables, ...), custom_call_target="tpu_custom_call" | custom-call | flops 1006632960 | bytes 4194304 | tf_op jit(solution)/shard_map/unsmooth/pallas_call | solution.py:498
  73.3 0.0 collective-permute-done.21
  73.3 0.0 collective-permute-done.16
  73.3 2.6 %collective-permute-done.19 = bf16[512,256]{1,0:T(8,128)(2,1)S(1)} collective-permute-done((bf16[512,256]{1,0:T(8,128)(2,1)S(1)}, bf16[512,256]{1,0:T(8,128)(2,1)S(1)}, u32[]{:S(2)}, u32[]{:S(2)}) %collective-permute-start.19) | collective-permute-done | bytes 262176 | tf_op jit(solution)/shard_map/ppermute | solution.py:331
  76.0 0.9 %convert_add_fusion = f32[512,256]{1,0:T(8,128)} fusion(bf16[512,256]{1,0:T(8,128)(2,1)S(1)} %collective-permute-done.21, bf16[512,256]{1,0:T(8,128)(2,1)S(1)} %collective-permute-done.19, f32[512,256]{1,0:T(8,128)S(1)} %get-tuple-element.67, bf16[512,256]{1,0:T(8,128)(2,1)S(1)} %collective-permute-done.16), kind=kLoop, calls=%fused_computation | loop fusion | flops 786432 | bytes 1835008 | tf_op jit(solution)/shard_map/add | solution.py:496
  (8 shorter events, 0.1 us)
Async XLA Ops:
  0.6 20.5 %copy-start.5 = (s32[1,2,8]{2,1,0:T(2,128)S(1)}, s32[1,2,8]{2,1,0:T(2,128)}, u32[]{:S(2)}) copy-start(s32[1,2,8]{2,1,0:T(2,128)} %param.13) | copy-start | bytes 196
  0.6 20.4 %copy-start.6 = (s32[1,2,8]{2,1,0:T(2,128)S(1)}, s32[1,2,8]{2,1,0:T(2,128)}, u32[]{:S(2)}) copy-start(s32[1,2,8]{2,1,0:T(2,128)} %param.12) | copy-start | bytes 196
  0.6 10.2 %collective-permute-start.3 = (bf16[512,256]{1,0:T(8,128)(2,1)}, bf16[512,256]{1,0:T(8,128)(2,1)S(1)}, u32[]{:S(2)}, u32[]{:S(2)}) collective-permute-start(bf16[512,256]{1,0:T(8,128)(2,1)} %refs_0_.5), channel_id=1, source_target_pairs={{0,2},{1,3},{2,0},{3,1},{4,6},{5,7},{6,4},{7,5},{8,10},{9,11},{10,... | collective-permute-start | bytes 786440 | tf_op jit(solution)/shard_map/ppermute | solution.py:331
  3.7 11.3 %collective-permute-start.2 = (bf16[512,256]{1,0:T(8,128)(2,1)}, bf16[512,256]{1,0:T(8,128)(2,1)S(1)}, u32[]{:S(2)}, u32[]{:S(2)}) collective-permute-start(bf16[512,256]{1,0:T(8,128)(2,1)} %refs_0_.5), channel_id=1, source_target_pairs={{0,4},{1,5},{2,6},{3,7},{4,8},{5,9},{6,10},{7,11},{8,12},{9,13},{1... | collective-permute-start | bytes 786440 | tf_op jit(solution)/shard_map/ppermute | solution.py:331
  5.3 14.0 %collective-permute-start.1 = (bf16[512,256]{1,0:T(8,128)(2,1)}, bf16[512,256]{1,0:T(8,128)(2,1)S(1)}, u32[]{:S(2)}, u32[]{:S(2)}) collective-permute-start(bf16[512,256]{1,0:T(8,128)(2,1)} %refs_0_.5), channel_id=1, source_target_pairs={{0,12},{1,13},{2,14},{3,15},{4,0},{5,1},{6,2},{7,3},{8,4},{9,5},{1... | collective-permute-start | bytes 786440 | tf_op jit(solution)/shard_map/ppermute | solution.py:331
  8.5 12.6 %collective-permute-start.5 = (f32[256,128]{1,0:T(8,128)S(1)}, f32[256,128]{1,0:T(8,128)S(1)}, u32[]{:S(2)}, u32[]{:S(2)}) collective-permute-start(f32[256,128]{1,0:T(8,128)S(1)} %get-tuple-element.74), channel_id=1, source_target_pairs={{1,2},{3,4},{5,6},{7,8},{9,10},{11,12},{13,14},{2,1},{4,3},{6,5},{... | collective-permute-start | bytes 393224 | tf_op jit(solution)/shard_map/ppermute | solution.py:331
  9.2 12.0 %collective-permute-start.4 = (f32[256,128]{1,0:T(8,128)S(1)}, f32[256,128]{1,0:T(8,128)S(1)}, u32[]{:S(2)}, u32[]{:S(2)}) collective-permute-start(f32[256,128]{1,0:T(8,128)S(1)} %get-tuple-element.75), channel_id=1, source_target_pairs={{0,1},{1,0},{2,3},{3,2},{4,5},{5,4},{6,7},{7,6},{8,9},{9,8},{10,11... | collective-permute-start | bytes 393224 | tf_op jit(solution)/shard_map/ppermute | solution.py:331
  15.0 11.3 %collective-permute-start.6 = (bf16[512,256]{1,0:T(8,128)(2,1)S(1)}, bf16[512,256]{1,0:T(8,128)(2,1)S(1)}, u32[]{:S(2)}, u32[]{:S(2)}) collective-permute-start(bf16[512,256]{1,0:T(8,128)(2,1)S(1)} %collective-permute-done.2.refs_1_), channel_id=1, source_target_pairs={{0,4},{1,5},{2,6},{3,7},{4,8},{5,9},{6,10},{7,11},{8,12},{9,13},{1... | collective-permute-start | bytes 786440 | tf_op jit(solution)/shard_map/ppermute | solution.py:331
  15.0 11.3 %collective-permute-start.8 = (bf16[512,256]{1,0:T(8,128)(2,1)S(1)}, bf16[512,256]{1,0:T(8,128)(2,1)S(1)}, u32[]{:S(2)}, u32[]{:S(2)}) collective-permute-start(bf16[512,256]{1,0:T(8,128)(2,1)S(1)} %collective-permute-done.2.refs_1_), channel_id=1, source_target_pairs={{0,2},{1,3},{2,0},{3,1},{4,6},{5,7},{6,4},{7,5},{8,10},{9,11},{10,... | collective-permute-start | bytes 786440 | tf_op jit(solution)/shard_map/ppermute | solution.py:331
  15.3 1.0 %copy-start = (f32[256,512]{1,0:T(8,128)S(1)}, f32[256,512]{1,0:T(8,128)}, u32[]{:S(2)}) copy-start(f32[256,512]{1,0:T(8,128)} %mid.1) | copy-start | bytes 1572868
  16.3 0.9 %copy-start.2 = (f32[256,256]{1,0:T(8,128)S(1)}, f32[256,256]{1,0:T(8,128)}, u32[]{:S(2)}) copy-start(f32[256,256]{1,0:T(8,128)} %taps) | copy-start | bytes 786436
  19.3 8.2 %collective-permute-start.9 = (bf16[512,256]{1,0:T(8,128)(2,1)S(1)}, bf16[512,256]{1,0:T(8,128)(2,1)S(1)}, u32[]{:S(2)}, u32[]{:S(2)}) collective-permute-start(bf16[512,256]{1,0:T(8,128)(2,1)S(1)} %collective-permute-done.1.refs_3_), channel_id=1, source_target_pairs={{0,2},{1,3},{2,0},{3,1},{4,6},{5,7},{6,4},{7,5},{8,10},{9,11},{10,... | collective-permute-start | bytes 786440 | tf_op jit(solution)/shard_map/ppermute | solution.py:331
  21.1 6.4 %copy-start.1 = (bf16[512,256]{1,0:T(8,128)(2,1)S(1)}, bf16[512,256]{1,0:T(8,128)(2,1)}, u32[]{:S(2)}) copy-start(bf16[512,256]{1,0:T(8,128)(2,1)} %refs_0_.5) | copy-start | bytes 786436
  21.1 1.8 %collective-permute-start = (s32[2,8]{1,0:T(2,128)S(1)}, s32[2,8]{1,0:T(2,128)S(1)}, u32[]{:S(2)}, u32[]{:S(2)}) collective-permute-start(s32[2,8]{1,0:T(2,128)S(1)} %add_bitcast_fusion.ids), channel_id=1, source_target_pairs={{0,1},{1,0},{2,3},{3,2},{4,5},{5,4},{6,7},{7,6},{8,9},{9,8},{10,11... | collective-permute-start | bytes 200 | tf_op jit(solution)/shard_map/ppermute | solution.py:331
  26.2 6.4 %collective-permute-start.7 = (bf16[512,256]{1,0:T(8,128)(2,1)S(1)}, bf16[512,256]{1,0:T(8,128)(2,1)S(1)}, u32[]{:S(2)}, u32[]{:S(2)}) collective-permute-start(bf16[512,256]{1,0:T(8,128)(2,1)S(1)} %collective-permute-done.6.refs_2_), channel_id=1, source_target_pairs={{0,2},{1,3},{2,0},{3,1},{4,6},{5,7},{6,4},{7,5},{8,10},{9,11},{10,... | collective-permute-start | bytes 786440 | tf_op jit(solution)/shard_map/ppermute | solution.py:331
  28.3 5.8 %copy-start.3 = (bf16[2,8,128,512]{3,2,1,0:T(8,128)(2,1)S(1)}, bf16[2,8,128,512]{3,2,1,0:T(8,128)(2,1)}, u32[]{:S(2)}) copy-start(bf16[2,8,128,512]{3,2,1,0:T(8,128)(2,1)} %param.11) | copy-start | bytes 6291460
  28.3 5.8 %copy-start.4 = (s32[2,8,4]{1,2,0:T(4,128)S(1)}, s32[2,8,4]{1,2,0:T(4,128)}, u32[]{:S(2)}) copy-start(s32[2,8,4]{1,2,0:T(4,128)} %param.14) | copy-start | bytes 772
  28.3 5.8 %collective-permute-start.10 = (bf16[1024,256]{1,0:T(8,128)(2,1)S(1)}, bf16[1024,256]{1,0:T(8,128)(2,1)S(1)}, u32[]{:S(2)}, u32[]{:S(2)}) collective-permute-start(bf16[1024,256]{1,0:T(8,128)(2,1)S(1)} %pack.2), channel_id=1, source_target_pairs={{0,1},{1,0},{2,3},{3,2},{4,5},{5,4},{6,7},{7,6},{8,9},{9,8},{10,11... | collective-permute-start | bytes 1572872 | tf_op jit(solution)/shard_map/ppermute | solution.py:331
  29.2 4.9 %collective-permute-start.11 = (bf16[1024,256]{1,0:T(8,128)(2,1)S(1)}, bf16[1024,256]{1,0:T(8,128)(2,1)S(1)}, u32[]{:S(2)}, u32[]{:S(2)}) collective-permute-start(bf16[1024,256]{1,0:T(8,128)(2,1)S(1)} %pack.3), channel_id=1, source_target_pairs={{0,1},{1,0},{2,3},{3,2},{4,5},{5,4},{6,7},{7,6},{8,9},{9,8},{10,11... | collective-permute-start | bytes 1572872 | tf_op jit(solution)/shard_map/ppermute | solution.py:331
  32.6 1.5 %collective-permute-start.12 = (bf16[512,256]{1,0:T(8,128)(2,1)S(1)}, bf16[512,256]{1,0:T(8,128)(2,1)S(1)}, u32[]{:S(2)}, u32[]{:S(2)}) collective-permute-start(bf16[512,256]{1,0:T(8,128)(2,1)S(1)} %collective-permute-done.7.refs_6_), channel_id=1, source_target_pairs={{0,1},{1,0},{2,3},{3,2},{4,5},{5,4},{6,7},{7,6},{8,9},{9,8},{10,11... | collective-permute-start | bytes 786440 | tf_op jit(solution)/shard_map/ppermute | solution.py:331
  38.2 2.9 %collective-permute-start.13 = (bf16[2304,256]{1,0:T(8,128)(2,1)S(1)}, bf16[2304,256]{1,0:T(8,128)(2,1)S(1)}, u32[]{:S(2)}, u32[]{:S(2)}) collective-permute-start(bf16[2304,256]{1,0:T(8,128)(2,1)S(1)} %get-tuple-element.59.own), channel_id=1, source_target_pairs={{0,1},{1,0},{2,3},{3,2},{4,5},{5,4},{6,7},{7,6},{8,9},{9,8},{10,11... | collective-permute-start | bytes 3538952 | tf_op jit(solution)/shard_map/ppermute | solution.py:331
  42.3 9.2 %collective-permute-start.14 = (bf16[512,256]{1,0:T(8,128)(2,1)S(1)}, bf16[512,256]{1,0:T(8,128)(2,1)S(1)}, u32[]{:S(2)}, u32[]{:S(2)}) collective-permute-start(bf16[512,256]{1,0:T(8,128)(2,1)S(1)} %merge_late.1), channel_id=1, source_target_pairs={{0,2},{1,3},{2,0},{3,1},{4,6},{5,7},{6,4},{7,5},{8,10},{9,11},{10,... | collective-permute-start | bytes 786440 | tf_op jit(solution)/shard_map/ppermute | solution.py:331
  45.9 11.2 %collective-permute-start.20 = (bf16[512,256]{1,0:T(8,128)(2,1)S(1)}, bf16[512,256]{1,0:T(8,128)(2,1)S(1)}, u32[]{:S(2)}, u32[]{:S(2)}) collective-permute-start(bf16[512,256]{1,0:T(8,128)(2,1)S(1)} %get-tuple-element.73), channel_id=1, source_target_pairs={{0,2},{1,3},{2,0},{3,1},{4,6},{5,7},{6,4},{7,5},{8,10},{9,11},{10,... | collective-permute-start | bytes 786440 | tf_op jit(solution)/shard_map/ppermute | solution.py:331
  46.4 20.1 %collective-permute-start.17 = (bf16[512,256]{1,0:T(8,128)(2,1)S(1)}, bf16[512,256]{1,0:T(8,128)(2,1)S(1)}, u32[]{:S(2)}, u32[]{:S(2)}) collective-permute-start(bf16[512,256]{1,0:T(8,128)(2,1)S(1)} %get-tuple-element.70), channel_id=1, source_target_pairs={{0,2},{1,3},{2,0},{3,1},{4,6},{5,7},{6,4},{7,5},{8,10},{9,11},{10,... | collective-permute-start | bytes 786440 | tf_op jit(solution)/shard_map/ppermute | solution.py:331
  51.6 14.9 %collective-permute-start.18 = (bf16[512,256]{1,0:T(8,128)(2,1)S(1)}, bf16[512,256]{1,0:T(8,128)(2,1)S(1)}, u32[]{:S(2)}, u32[]{:S(2)}) collective-permute-start(bf16[512,256]{1,0:T(8,128)(2,1)S(1)} %hop.3), channel_id=1, source_target_pairs={{0,4},{1,5},{2,6},{3,7},{4,8},{5,9},{6,10},{7,11},{8,12},{9,13},{1... | collective-permute-start | bytes 786440 | tf_op jit(solution)/shard_map/ppermute | solution.py:331
  55.7 6.0 %collective-permute-start.15 = (bf16[256,256]{1,0:T(8,128)(2,1)S(1)}, bf16[256,256]{1,0:T(8,128)(2,1)S(1)}, u32[]{:S(2)}, u32[]{:S(2)}) collective-permute-start(bf16[256,256]{1,0:T(8,128)(2,1)S(1)} %get-tuple-element.64), channel_id=1, source_target_pairs={{1,2},{3,4},{5,6},{7,8},{9,10},{11,12},{13,14},{2,1},{4,3},{6,5},{... | collective-permute-start | bytes 393224 | tf_op jit(solution)/shard_map/ppermute | solution.py:331
  57.2 16.2 %collective-permute-start.21 = (bf16[512,256]{1,0:T(8,128)(2,1)S(1)}, bf16[512,256]{1,0:T(8,128)(2,1)S(1)}, u32[]{:S(2)}, u32[]{:S(2)}) collective-permute-start(bf16[512,256]{1,0:T(8,128)(2,1)S(1)} %hop.5), channel_id=1, source_target_pairs={{0,12},{1,13},{2,14},{3,15},{4,0},{5,1},{6,2},{7,3},{8,4},{9,5},{1... | collective-permute-start | bytes 786440 | tf_op jit(solution)/shard_map/ppermute | solution.py:331
  61.7 11.7 %collective-permute-start.16 = (bf16[512,256]{1,0:T(8,128)(2,1)S(1)}, bf16[512,256]{1,0:T(8,128)(2,1)S(1)}, u32[]{:S(2)}, u32[]{:S(2)}) collective-permute-start(bf16[512,256]{1,0:T(8,128)(2,1)S(1)} %get-tuple-element.68), channel_id=1, source_target_pairs={{0,2},{1,3},{2,0},{3,1},{4,6},{5,7},{6,4},{7,5},{8,10},{9,11},{10,... | collective-permute-start | bytes 786440 | tf_op jit(solution)/shard_map/ppermute | solution.py:331
  66.5 9.4 %collective-permute-start.19 = (bf16[512,256]{1,0:T(8,128)(2,1)S(1)}, bf16[512,256]{1,0:T(8,128)(2,1)S(1)}, u32[]{:S(2)}, u32[]{:S(2)}) collective-permute-start(bf16[512,256]{1,0:T(8,128)(2,1)S(1)} %hop.4), channel_id=1, source_target_pairs={{0,4},{1,5},{2,6},{3,7},{4,8},{5,9},{6,10},{7,11},{8,12},{9,13},{1... | collective-permute-start | bytes 786440 | tf_op jit(solution)/shard_map/ppermute | solution.py:331

commit v12 on v11

--- a/solution.py
+++ b/solution.py
@@ -349,15 +349,15 @@
     far_side = permute(jnp.where(even, earlier, later), odd_even)
 
     half = chain // 2
-    late = chain + half
+    late, late_sum = 2 * chain - 1, chain + half
     straight = [loadings] * chain
-    for r in range(1, half):
+    straight[1] = rotate(loadings, 1)
+    across = [flip(loadings, 2)] + [None] * (chain - 1)
+    straight[1], across[0], core_side, far_side = lax.optimization_barrier(
+        (straight[1], across[0], core_side, far_side)
+    )
+    for r in range(2, half + 1):
         straight[r] = rotate(straight[r - 1], 1)
-        straight[-r] = rotate(straight[1 - r], -1)
-    across = [flip(loadings, 2)] + [None] * (chain - 1)
-    if half > 1:
-        straight[1], across[0] = lax.optimization_barrier((straight[1], across[0]))
-    straight[half] = rotate(straight[half - 1], 1)
     straight[1], kernel = lax.optimization_barrier((straight[1], kernel))
     table = dft_tables(2 * halfwidth)
     mxu = 30 * 2 * latent_dim * (2 * halfwidth) ** 2
@@ -376,11 +376,14 @@
         cost_estimate=pl.CostEstimate(flops=mxu // 3, bytes_accessed=4 * MIB, transcendentals=0),
         name="prepare",
     )(table, kernel, latents)
-    straight[-1], *prepared = lax.optimization_barrier((straight[-1], *prepared))
+    other_way, *prepared = lax.optimization_barrier((loadings, *prepared))
     spectrum, held_bins = [prepared[0], *prepared[2:]], prepared[1]
+    for r in range(1, half):
+        other_way = straight[-r] = rotate(other_way, -1)
     for r in range(1, chain):
-        if r != half:
-            across[r] = flip(straight[r], 2)
+        across[r] = flip(straight[r], 2)
+    pieces = straight + across
+    early = pieces[:late] + pieces[late + 1 :]
 
     smoothed = pl.pallas_call(
         smooth_kernel,
@@ -393,8 +396,6 @@
     )(held_bins, core_side, far_side, *spectrum)
 
     slots = jax.ShapeDtypeStruct((entries * BLK, latent_dim), BF16)
-    across[half] = flip(straight[half], 2)
-    early = straight + across[:half] + across[half + 1 :]
 
     def pack(first, total):
         return pl.pallas_call(
@@ -409,9 +410,8 @@
 
     asked, smoothed, mask = lax.optimization_barrier((asked, smoothed, mask))
     packed = [flip(pack(first, entries // 2), 1) for first in (0, entries // 2)]
-    last, smoothed = lax.optimization_barrier((across[half], smoothed))
-    late_theirs = flip(last, 1)
-    pieces = straight + across
+    pieces[late], smoothed = lax.optimization_barrier((pieces[late], smoothed))
+    late_theirs = flip(pieces[late], 1)
 
     group = 4
     extended = jax.ShapeDtypeStruct((entries * BLK + latent_dim, latent_dim), BF16)
@@ -446,7 +446,7 @@
     got = flip(terms, 1)
     narrow = jax.ShapeDtypeStruct((chunk, latent_dim), BF16)
     sent = pl.pallas_call(
-        functools.partial(merge_late_kernel, entries, late),
+        functools.partial(merge_late_kernel, entries, late_sum),
         out_shape=narrow,
         in_specs=[smem] * 2 + [VMEM] * 2,
         out_specs=VMEM,
@@ -459,7 +459,7 @@
     sent, ids = lax.optimization_barrier((sent, ids))
     back = flip(sent, 2)
     merged = pl.pallas_call(
-        functools.partial(merge_kernel, entries, late),
+        functools.partial(merge_kernel, entries, late_sum),
         out_shape=(wide,) * chain + (narrow,) * (chain - 1),
         in_specs=[smem] * 2 + [VMEM] * 2,
         out_specs=(VMEM,) * (2 * chain - 1),

time: 77.1 us -> 81.1 us (1.052)
  waiting for transfers between devices: 22.6 us -> 31.5 us
  starting transfers between devices: 34.5 us -> 29.5 us
    ppermute x22, waiting for transfers between devices: 22.6 us -> 31.5 us  [permute(): return lax.ppermute(x, 'tm', pairs)]
    ppermute x22, starting transfers between devices: 34.5 us -> 29.5 us  [permute(): return lax.ppermute(x, 'tm', pairs)]
  transfers between devices with their start and end apart: 22 -> 22, of which waited for: 9 -> 13; matrix products, arithmetic and copies ran while one was open for 1% -> 1% of each run, Pallas kernels for 13% -> 12%
where the time goes in v12:
time: 81.1 us; the launch traced here: 80.8 us
  waiting for transfers between devices  31.5 us (39%)
  starting transfers between devices  29.5 us (36%)
  Pallas kernels  15.1 us (19%)
  local copies, waits for them, and re-layouts  2.02 us (2%)
  other arithmetic  1.92 us (2%)
  between operations  0.83 us (1%)
    ppermute x22, waiting for transfers between devices, permute(): return lax.ppermute(x, 'tm', pairs)  31.5 us
    ppermute x22, starting transfers between devices, permute(): return lax.ppermute(x, 'tm', pairs)  29.5 us
    pallas_call x1, Pallas kernels, local(): pl.pallas_call(functools.partial(session_kernel, entries, group, late), o...  4 us
    pallas_call x1, Pallas kernels, local(): pl.pallas_call(unsmooth_kernel, out_shape=jax.ShapeDtypeStruct((latent_di...  2.52 us
    pallas_call x1, Pallas kernels, local(): pl.pallas_call(prepare_kernel, out_shape=(jax.ShapeDtypeStruct(table.shap...  2.02 us
    unnamed x14, local copies, waits for them, and re-layouts  2.02 us
    pallas_call x1, Pallas kernels, local(): pl.pallas_call(functools.partial(merge_kernel, entries, late_sum), out_sh...  1.89 us
    pallas_call x1, Pallas kernels, local(): pl.pallas_call(smooth_kernel, out_shape=jax.ShapeDtypeStruct((latent_dim,...  1.68 us
  transfers between devices with their start and end apart: 22, of which 13 were waited for; matrix products, arithmetic and copies ran while one was open for 1% of the time, Pallas kernels for 12%

profile of v12, /device:TPU:0, one launch (start us, length us, event | category | flops | bytes accessed | tf_op | source)
XLA Modules:
  0.0 80.8 jit_solution(15025029365826301918)
XLA Ops:
  0.6 0.0 copy-start.1
  0.6 0.0 copy-start.5
  0.7 0.0 copy-start.6
  0.7 3.0 %collective-permute-start.2 = (bf16[512,256]{1,0:T(8,128)(2,1)}, bf16[512,256]{1,0:T(8,128)(2,1)S(1)}, u32[]{:S(2)}, u32[]{:S(2)}) collective-permute-start(bf16[512,256]{1,0:T(8,128)(2,1)} %refs_0_.5), channel_id=1, source_target_pairs={{0,2},{1,3},{2,0},{3,1},{4,6},{5,7},{6,4},{7,5},{8,10},{9,11},{10,... | collective-permute-start | bytes 786440 | tf_op jit(solution)/shard_map/ppermute | solution.py:331
  3.7 1.6 %collective-permute-start.1 = (bf16[512,256]{1,0:T(8,128)(2,1)}, bf16[512,256]{1,0:T(8,128)(2,1)S(1)}, u32[]{:S(2)}, u32[]{:S(2)}) collective-permute-start(bf16[512,256]{1,0:T(8,128)(2,1)} %refs_0_.5), channel_id=1, source_target_pairs={{0,4},{1,5},{2,6},{3,7},{4,8},{5,9},{6,10},{7,11},{8,12},{9,13},{1... | collective-permute-start | bytes 786440 | tf_op jit(solution)/shard_map/ppermute | solution.py:331
  5.3 1.0 %slice_select_fusion = (f32[256,128]{1,0:T(8,128)S(1)}, f32[256,128]{1,0:T(8,128)S(1)}) fusion(f32[256,512]{1,0:T(8,128)} %mid.1, pred[]{:T(512)S(6)} %eq.5), kind=kLoop, calls=%fused_computation.1 | loop fusion | flops 65536 | bytes 524289 | tf_op jit(solution)/shard_map/jit(_where)/select_n | solution.py:349
  6.3 0.7 collective-permute-start.4
  6.9 1.9 %collective-permute-start.3 = (f32[256,128]{1,0:T(8,128)S(1)}, f32[256,128]{1,0:T(8,128)S(1)}, u32[]{:S(2)}, u32[]{:S(2)}) collective-permute-start(f32[256,128]{1,0:T(8,128)S(1)} %get-tuple-element.79), channel_id=1, source_target_pairs={{0,1},{1,0},{2,3},{3,2},{4,5},{5,4},{6,7},{7,6},{8,9},{9,8},{10,11... | collective-permute-start | bytes 393224 | tf_op jit(solution)/shard_map/ppermute | solution.py:331
  8.9 0.0 collective-permute-done.4.far_side
  8.9 1.0 %collective-permute-done.3.core_side = f32[256,128]{1,0:T(8,128)S(1)} collective-permute-done((f32[256,128]{1,0:T(8,128)S(1)}, f32[256,128]{1,0:T(8,128)S(1)}, u32[]{:S(2)}, u32[]{:S(2)}) %collective-permute-start.3) | collective-permute-done | bytes 131104 | tf_op jit(solution)/shard_map/ppermute | solution.py:331
  9.9 0.4 collective-permute-done.2.refs_4_
  10.2 3.5 %collective-permute-done.1.refs_1_ = bf16[512,256]{1,0:T(8,128)(2,1)S(1)} collective-permute-done((bf16[512,256]{1,0:T(8,128)(2,1)}, bf16[512,256]{1,0:T(8,128)(2,1)S(1)}, u32[]{:S(2)}, u32[]{:S(2)}) %collective-permute-start.1) | collective-permute-done | bytes 262176 | tf_op jit(solution)/shard_map/ppermute | solution.py:331
  13.7 1.4 %collective-permute-start.7 = (bf16[512,256]{1,0:T(8,128)(2,1)S(1)}, bf16[512,256]{1,0:T(8,128)(2,1)S(1)}, u32[]{:S(2)}, u32[]{:S(2)}) collective-permute-start(bf16[512,256]{1,0:T(8,128)(2,1)S(1)} %collective-permute-done.1.refs_1_), channel_id=1, source_target_pairs={{0,4},{1,5},{2,6},{3,7},{4,8},{5,9},{6,10},{7,11},{8,12},{9,13},{1... | collective-permute-start | bytes 786440 | tf_op jit(solution)/shard_map/ppermute | solution.py:331
  15.1 0.0 collective-permute-start.8
  15.1 1.0 %copy-done = f32[256,512]{1,0:T(8,128)S(1)} copy-done((f32[256,512]{1,0:T(8,128)S(1)}, f32[256,512]{1,0:T(8,128)}, u32[]{:S(2)}) %copy-start) | copy-done | bytes 524312
  16.1 0.9 %copy-done.2 = f32[256,256]{1,0:T(8,128)S(1)} copy-done((f32[256,256]{1,0:T(8,128)S(1)}, f32[256,256]{1,0:T(8,128)}, u32[]{:S(2)}) %copy-start.2) | copy-done | bytes 262168
  17.1 2.0 %prepare.1 = (bf16[3072,256]{1,0:T(8,128)(2,1)S(1)}, f32[256,512]{1,0:T(8,128)S(1)}, f32[256,256]{1,0:T(8,128)S(1)}, f32[256,256]{1,0:T(8,128)S(1)}, f32[256,256]{1,0:T(8,128)S(1)}) custom-call(bf16[3072,256]{1,0:T(8,128)(2,1)} %constant.22.clone.table, f32[256,256]{1,0:T(8,128)S(1)} %copy-done.2, f32[256,512]{1,0:T(8,128)S(1)} %copy-done), custom_call_target="tpu_custom_call" | custom-call | flops 335544320 | bytes 4194304 | tf_op jit(solution)/shard_map/prepare/pallas_call | solution.py:365
  19.1 0.0 copy-done.1
  19.1 2.9 %collective-permute-start.5 = (bf16[512,256]{1,0:T(8,128)(2,1)S(1)}, bf16[512,256]{1,0:T(8,128)(2,1)S(1)}, u32[]{:S(2)}, u32[]{:S(2)}) collective-permute-start(bf16[512,256]{1,0:T(8,128)(2,1)S(1)} %copy-done.1), channel_id=1, source_target_pairs={{0,12},{1,13},{2,14},{3,15},{4,0},{5,1},{6,2},{7,3},{8,4},{9,5},{1... | collective-permute-start | bytes 786440 | tf_op jit(solution)/shard_map/ppermute | solution.py:331
  22.0 1.3 %collective-permute-done.7.refs_2_ = bf16[512,256]{1,0:T(8,128)(2,1)S(1)} collective-permute-done((bf16[512,256]{1,0:T(8,128)(2,1)S(1)}, bf16[512,256]{1,0:T(8,128)(2,1)S(1)}, u32[]{:S(2)}, u32[]{:S(2)}) %collective-permute-start.7) | collective-permute-done | bytes 262176 | tf_op jit(solution)/shard_map/ppermute | solution.py:331
  23.3 0.5 collective-permute-start.9
  23.8 0.0 copy-done.6
  23.8 1.0 %collective-permute-start = (s32[2,8]{1,0:T(2,128)S(1)}, s32[2,8]{1,0:T(2,128)S(1)}, u32[]{:S(2)}, u32[]{:S(2)}) collective-permute-start(s32[2,8]{1,0:T(2,128)S(1)} %add_bitcast_fusion.ids), channel_id=1, source_target_pairs={{0,1},{1,0},{2,3},{3,2},{4,5},{5,4},{6,7},{7,6},{8,9},{9,8},{10,11... | collective-permute-start | bytes 200 | tf_op jit(solution)/shard_map/ppermute | solution.py:331
  24.8 1.7 %smooth.1.smoothed = bf16[256,512]{1,0:T(8,128)(2,1)S(1)} custom-call(f32[256,512]{1,0:T(8,128)S(1)} %get-tuple-element.47.mid, f32[256,128]{1,0:T(8,128)S(1)} %collective-permute-done.3.core_side, f32[256,128]{1,0:T(8,128)S(1)} %collective-permute-done.4.far_side, bf16[3072,256]{1,0:T(8,128)(2,1)S(1)} %get-tuple-element.50.tables, ...), custom_call_target="tpu_custom_call" | custom-call | flops 1006632960 | bytes 4194304 | tf_op jit(solution)/shard_map/smooth/pallas_call | solution.py:388
  26.5 0.0 collective-permute-done.asked
  26.5 2.4 %collective-permute-done.5.refs_3_ = bf16[512,256]{1,0:T(8,128)(2,1)S(1)} collective-permute-done((bf16[512,256]{1,0:T(8,128)(2,1)S(1)}, bf16[512,256]{1,0:T(8,128)(2,1)S(1)}, u32[]{:S(2)}, u32[]{:S(2)}) %collective-permute-start.5) | collective-permute-done | bytes 262176 | tf_op jit(solution)/shard_map/ppermute | solution.py:331
  28.9 1.8 %collective-permute-start.6 = (bf16[512,256]{1,0:T(8,128)(2,1)S(1)}, bf16[512,256]{1,0:T(8,128)(2,1)S(1)}, u32[]{:S(2)}, u32[]{:S(2)}) collective-permute-start(bf16[512,256]{1,0:T(8,128)(2,1)S(1)} %collective-permute-done.5.refs_3_), channel_id=1, source_target_pairs={{0,2},{1,3},{2,0},{3,1},{4,6},{5,7},{6,4},{7,5},{8,10},{9,11},{10,... | collective-permute-start | bytes 786440 | tf_op jit(solution)/shard_map/ppermute | solution.py:331
  30.7 0.0 collective-permute-done.8.refs_5_
  30.7 1.0 %collective-permute-done.9.refs_6_ = bf16[512,256]{1,0:T(8,128)(2,1)S(1)} collective-permute-done((bf16[512,256]{1,0:T(8,128)(2,1)S(1)}, bf16[512,256]{1,0:T(8,128)(2,1)S(1)}, u32[]{:S(2)}, u32[]{:S(2)}) %collective-permute-start.9) | collective-permute-done | bytes 262176 | tf_op jit(solution)/shard_map/ppermute | solution.py:331
  31.6 0.8 %pack.2 = bf16[1024,256]{1,0:T(8,128)(2,1)S(1)} custom-call(s32[2,8]{1,0:T(2,128)S(1)} %collective-permute-done.asked, bf16[512,256]{1,0:T(8,128)(2,1)S(1)} %copy-done.1, bf16[512,256]{1,0:T(8,128)(2,1)S(1)} %collective-permute-done.1.refs_1_, bf16[512,256]{1,0:T(8,128)(2,1)S(1)} %collective-permute-done.7.refs_2_, ...), custom_call_target="tpu_custom_call" | custom-call | bytes 1048576 | tf_op jit(solution)/shard_map/pack/pallas_call | solution.py:401
  32.5 0.0 copy-start.3
  32.5 0.0 copy-start.4
  32.5 0.1 collective-permute-start.10
  32.6 0.8 pack.3
  33.3 0.6 collective-permute-start.11
  33.9 3.3 %collective-permute-done.6.refs_7_ = bf16[512,256]{1,0:T(8,128)(2,1)S(1)} collective-permute-done((bf16[512,256]{1,0:T(8,128)(2,1)S(1)}, bf16[512,256]{1,0:T(8,128)(2,1)S(1)}, u32[]{:S(2)}, u32[]{:S(2)}) %collective-permute-start.6) | collective-permute-done | bytes 262176 | tf_op jit(solution)/shard_map/ppermute | solution.py:331
  37.2 0.0 collective-permute-start.12
  37.2 1.5 %collective-permute-done.12.late_theirs = bf16[512,256]{1,0:T(8,128)(2,1)S(1)} collective-permute-done((bf16[512,256]{1,0:T(8,128)(2,1)S(1)}, bf16[512,256]{1,0:T(8,128)(2,1)S(1)}, u32[]{:S(2)}, u32[]{:S(2)}) %collective-permute-start.12) | collective-permute-done | bytes 262176 | tf_op jit(solution)/shard_map/ppermute | solution.py:331
  38.7 0.0 collective-permute-done.10.packed
  38.8 0.0 collective-permute-done.11.packed_rest
  38.8 4.0 %session.1 = (f32[256,512]{1,0:T(8,128)S(1)}, bf16[256,256]{1,0:T(8,128)(2,1)S(1)}, bf16[2304,256]{1,0:T(8,128)(2,1)S(1)}) custom-call(s32[2,8]{1,0:T(2,128)S(1)} %add_bitcast_fusion.ids, s32[2,4,8]{2,1,0:T(4,128)S(1)} %bitcast.5, bf16[256,512]{1,0:T(8,128)(2,1)S(1)} %smooth.1.smoothed, bf16[16,128,512]{2,1,0:T(8,128)(2,1)S(1)} %bitcast.4, ...), custom_call_target="tpu_custom_call" | custom-call | flops 1610612736 | bytes 8388608 | tf_op jit(solution)/shard_map/session/pallas_call | solution.py:418
  42.8 0.2 collective-permute-start.13
  43.0 2.7 %collective-permute-done.13.got = bf16[2304,256]{1,0:T(8,128)(2,1)S(1)} collective-permute-done((bf16[2304,256]{1,0:T(8,128)(2,1)S(1)}, bf16[2304,256]{1,0:T(8,128)(2,1)S(1)}, u32[]{:S(2)}, u32[]{:S(2)}) %collective-permute-start.13) | collective-permute-done | bytes 1179680 | tf_op jit(solution)/shard_map/ppermute | solution.py:331
  45.7 1.2 %merge_late.1 = bf16[512,256]{1,0:T(8,128)(2,1)S(1)} custom-call(s32[2,8]{1,0:T(2,128)S(1)} %add_bitcast_fusion.ids, s32[2,8]{1,0:T(2,128)S(1)} %collective-permute-done.asked, bf16[2304,256]{1,0:T(8,128)(2,1)S(1)} %get-tuple-element.63.own, bf16[2304,256]{1,0:T(8,128)(2,1)S(1)} %collective-permute-done.13.got), custom_call_target="tpu_custom_call" | custom-call | bytes 1048576 | tf_op jit(solution)/shard_map/merge_late/pallas_call | solution.py:448
  46.9 1.7 %collective-permute-start.14 = (bf16[512,256]{1,0:T(8,128)(2,1)S(1)}, bf16[512,256]{1,0:T(8,128)(2,1)S(1)}, u32[]{:S(2)}, u32[]{:S(2)}) collective-permute-start(bf16[512,256]{1,0:T(8,128)(2,1)S(1)} %merge_late.1), channel_id=1, source_target_pairs={{0,2},{1,3},{2,0},{3,1},{4,6},{5,7},{6,4},{7,5},{8,10},{9,11},{10,... | collective-permute-start | bytes 786440 | tf_op jit(solution)/shard_map/ppermute | solution.py:331
  48.6 1.9 %merge.1 = (f32[512,256]{1,0:T(8,128)S(1)}, f32[512,256]{1,0:T(8,128)S(1)}, f32[512,256]{1,0:T(8,128)S(1)}, f32[512,256]{1,0:T(8,128)S(1)}, bf16[512,256]{1,0:T(...) custom-call(s32[2,8]{1,0:T(2,128)S(1)} %add_bitcast_fusion.ids, ...), custom_call_target="tpu_custom_call" | custom-call | bytes 5242880 | tf_op jit(solution)/shard_map/merge/pallas_call | solution.py:461
  50.5 0.5 collective-permute-start.20
  51.0 1.6 %collective-permute-start.17 = (bf16[512,256]{1,0:T(8,128)(2,1)S(1)}, bf16[512,256]{1,0:T(8,128)(2,1)S(1)}, u32[]{:S(2)}, u32[]{:S(2)}) collective-permute-start(bf16[512,256]{1,0:T(8,128)(2,1)S(1)} %get-tuple-element.74), channel_id=1, source_target_pairs={{0,2},{1,3},{2,0},{3,1},{4,6},{5,7},{6,4},{7,5},{8,10},{9,11},{10,... | collective-permute-start | bytes 786440 | tf_op jit(solution)/shard_map/ppermute | solution.py:331
  52.6 3.5 %collective-permute-done.14.refs_0_ = bf16[512,256]{1,0:T(8,128)(2,1)S(1)} collective-permute-done((bf16[512,256]{1,0:T(8,128)(2,1)S(1)}, bf16[512,256]{1,0:T(8,128)(2,1)S(1)}, u32[]{:S(2)}, u32[]{:S(2)}) %collective-permute-start.14) | collective-permute-done | bytes 262176 | tf_op jit(solution)/shard_map/ppermute | solution.py:331
  56.2 0.1 collective-permute-start.18
  56.2 0.7 collective-permute-start.15
  56.9 4.8 %collective-permute-done.20.refs_0_ = bf16[512,256]{1,0:T(8,128)(2,1)S(1)} collective-permute-done((bf16[512,256]{1,0:T(8,128)(2,1)S(1)}, bf16[512,256]{1,0:T(8,128)(2,1)S(1)}, u32[]{:S(2)}, u32[]{:S(2)}) %collective-permute-start.20) | collective-permute-done | bytes 262176 | tf_op jit(solution)/shard_map/ppermute | solution.py:331
  61.8 3.8 %collective-permute-start.21 = (bf16[512,256]{1,0:T(8,128)(2,1)S(1)}, bf16[512,256]{1,0:T(8,128)(2,1)S(1)}, u32[]{:S(2)}, u32[]{:S(2)}) collective-permute-start(bf16[512,256]{1,0:T(8,128)(2,1)S(1)} %hop.5), channel_id=1, source_target_pairs={{0,12},{1,13},{2,14},{3,15},{4,0},{5,1},{6,2},{7,3},{8,4},{9,5},{1... | collective-permute-start | bytes 786440 | tf_op jit(solution)/shard_map/ppermute | solution.py:331
  65.6 0.0 collective-permute-done.15.far_side
  65.6 5.4 %collective-permute-start.16 = (bf16[512,256]{1,0:T(8,128)(2,1)S(1)}, bf16[512,256]{1,0:T(8,128)(2,1)S(1)}, u32[]{:S(2)}, u32[]{:S(2)}) collective-permute-start(bf16[512,256]{1,0:T(8,128)(2,1)S(1)} %get-tuple-element.72), channel_id=1, source_target_pairs={{0,2},{1,3},{2,0},{3,1},{4,6},{5,7},{6,4},{7,5},{8,10},{9,11},{10,... | collective-permute-start | bytes 786440 | tf_op jit(solution)/shard_map/ppermute | solution.py:331
  71.0 0.0 collective-permute-done.17.refs_0_
  71.0 0.0 collective-permute-done.18.refs_1_
  71.0 0.1 hop.4
  71.1 0.1 collective-permute-start.19
  71.2 2.5 %unsmooth.1 = f32[256,512]{1,0:T(8,128)} custom-call(f32[256,512]{1,0:T(8,128)S(1)} %get-tuple-element.62.mid, bf16[2304,256]{1,0:T(8,128)(2,1)S(1)} %collective-permute-done.13.got, bf16[256,256]{1,0:T(8,128)(2,1)S(1)} %collective-permute-done.15.far_side, bf16[3072,256]{1,0:T(8,128)(2,1)S(1)} %get-tuple-element.50.tables, ...), custom_call_target="tpu_custom_call" | custom-call | flops 1006632960 | bytes 4194304 | tf_op jit(solution)/shard_map/unsmooth/pallas_call | solution.py:498
  73.7 0.0 collective-permute-done.21
  73.7 3.2 %collective-permute-done.16 = bf16[512,256]{1,0:T(8,128)(2,1)S(1)} collective-permute-done((bf16[512,256]{1,0:T(8,128)(2,1)S(1)}, bf16[512,256]{1,0:T(8,128)(2,1)S(1)}, u32[]{:S(2)}, u32[]{:S(2)}) %collective-permute-start.16) | collective-permute-done | bytes 262176 | tf_op jit(solution)/shard_map/ppermute | solution.py:331
  76.9 3.0 %collective-permute-done.19 = bf16[512,256]{1,0:T(8,128)(2,1)S(1)} collective-permute-done((bf16[512,256]{1,0:T(8,128)(2,1)S(1)}, bf16[512,256]{1,0:T(8,128)(2,1)S(1)}, u32[]{:S(2)}, u32[]{:S(2)}) %collective-permute-start.19) | collective-permute-done | bytes 262176 | tf_op jit(solution)/shard_map/ppermute | solution.py:331
  79.9 0.9 %convert_add_fusion = f32[512,256]{1,0:T(8,128)} fusion(bf16[512,256]{1,0:T(8,128)(2,1)S(1)} %collective-permute-done.21, bf16[512,256]{1,0:T(8,128)(2,1)S(1)} %collective-permute-done.19, f32[512,256]{1,0:T(8,128)S(1)} %get-tuple-element.71, bf16[512,256]{1,0:T(8,128)(2,1)S(1)} %collective-permute-done.16), kind=kLoop, calls=%fused_computation | loop fusion | flops 786432 | bytes 1835008 | tf_op jit(solution)/shard_map/add | solution.py:496
  (8 shorter events, 0.1 us)
Async XLA Ops:
  0.6 18.5 %copy-start.1 = (bf16[512,256]{1,0:T(8,128)(2,1)S(1)}, bf16[512,256]{1,0:T(8,128)(2,1)}, u32[]{:S(2)}) copy-start(bf16[512,256]{1,0:T(8,128)(2,1)} %refs_0_.5) | copy-start | bytes 786436
  0.6 23.1 %copy-start.5 = (s32[1,2,8]{2,1,0:T(2,128)S(1)}, s32[1,2,8]{2,1,0:T(2,128)}, u32[]{:S(2)}) copy-start(s32[1,2,8]{2,1,0:T(2,128)} %param.13) | copy-start | bytes 196
  0.7 23.1 %copy-start.6 = (s32[1,2,8]{2,1,0:T(2,128)S(1)}, s32[1,2,8]{2,1,0:T(2,128)}, u32[]{:S(2)}) copy-start(s32[1,2,8]{2,1,0:T(2,128)} %param.12) | copy-start | bytes 196
  0.7 9.5 %collective-permute-start.2 = (bf16[512,256]{1,0:T(8,128)(2,1)}, bf16[512,256]{1,0:T(8,128)(2,1)S(1)}, u32[]{:S(2)}, u32[]{:S(2)}) collective-permute-start(bf16[512,256]{1,0:T(8,128)(2,1)} %refs_0_.5), channel_id=1, source_target_pairs={{0,2},{1,3},{2,0},{3,1},{4,6},{5,7},{6,4},{7,5},{8,10},{9,11},{10,... | collective-permute-start | bytes 786440 | tf_op jit(solution)/shard_map/ppermute | solution.py:331
  3.7 10.0 %collective-permute-start.1 = (bf16[512,256]{1,0:T(8,128)(2,1)}, bf16[512,256]{1,0:T(8,128)(2,1)S(1)}, u32[]{:S(2)}, u32[]{:S(2)}) collective-permute-start(bf16[512,256]{1,0:T(8,128)(2,1)} %refs_0_.5), channel_id=1, source_target_pairs={{0,4},{1,5},{2,6},{3,7},{4,8},{5,9},{6,10},{7,11},{8,12},{9,13},{1... | collective-permute-start | bytes 786440 | tf_op jit(solution)/shard_map/ppermute | solution.py:331
  6.3 2.6 %collective-permute-start.4 = (f32[256,128]{1,0:T(8,128)S(1)}, f32[256,128]{1,0:T(8,128)S(1)}, u32[]{:S(2)}, u32[]{:S(2)}) collective-permute-start(f32[256,128]{1,0:T(8,128)S(1)} %get-tuple-element.78), channel_id=1, source_target_pairs={{1,2},{3,4},{5,6},{7,8},{9,10},{11,12},{13,14},{2,1},{4,3},{6,5},{... | collective-permute-start | bytes 393224 | tf_op jit(solution)/shard_map/ppermute | solution.py:331
  6.9 2.9 %collective-permute-start.3 = (f32[256,128]{1,0:T(8,128)S(1)}, f32[256,128]{1,0:T(8,128)S(1)}, u32[]{:S(2)}, u32[]{:S(2)}) collective-permute-start(f32[256,128]{1,0:T(8,128)S(1)} %get-tuple-element.79), channel_id=1, source_target_pairs={{0,1},{1,0},{2,3},{3,2},{4,5},{5,4},{6,7},{7,6},{8,9},{9,8},{10,11... | collective-permute-start | bytes 393224 | tf_op jit(solution)/shard_map/ppermute | solution.py:331
  13.7 9.6 %collective-permute-start.7 = (bf16[512,256]{1,0:T(8,128)(2,1)S(1)}, bf16[512,256]{1,0:T(8,128)(2,1)S(1)}, u32[]{:S(2)}, u32[]{:S(2)}) collective-permute-start(bf16[512,256]{1,0:T(8,128)(2,1)S(1)} %collective-permute-done.1.refs_1_), channel_id=1, source_target_pairs={{0,4},{1,5},{2,6},{3,7},{4,8},{5,9},{6,10},{7,11},{8,12},{9,13},{1... | collective-permute-start | bytes 786440 | tf_op jit(solution)/shard_map/ppermute | solution.py:331
  15.1 15.6 %collective-permute-start.8 = (bf16[512,256]{1,0:T(8,128)(2,1)S(1)}, bf16[512,256]{1,0:T(8,128)(2,1)S(1)}, u32[]{:S(2)}, u32[]{:S(2)}) collective-permute-start(bf16[512,256]{1,0:T(8,128)(2,1)S(1)} %collective-permute-done.1.refs_1_), channel_id=1, source_target_pairs={{0,2},{1,3},{2,0},{3,1},{4,6},{5,7},{6,4},{7,5},{8,10},{9,11},{10,... | collective-permute-start | bytes 786440 | tf_op jit(solution)/shard_map/ppermute | solution.py:331
  15.1 1.0 %copy-start = (f32[256,512]{1,0:T(8,128)S(1)}, f32[256,512]{1,0:T(8,128)}, u32[]{:S(2)}) copy-start(f32[256,512]{1,0:T(8,128)} %mid.1) | copy-start | bytes 1572868
  16.1 0.9 %copy-start.2 = (f32[256,256]{1,0:T(8,128)S(1)}, f32[256,256]{1,0:T(8,128)}, u32[]{:S(2)}) copy-start(f32[256,256]{1,0:T(8,128)} %taps) | copy-start | bytes 786436
  19.1 9.8 %collective-permute-start.5 = (bf16[512,256]{1,0:T(8,128)(2,1)S(1)}, bf16[512,256]{1,0:T(8,128)(2,1)S(1)}, u32[]{:S(2)}, u32[]{:S(2)}) collective-permute-start(bf16[512,256]{1,0:T(8,128)(2,1)S(1)} %copy-done.1), channel_id=1, source_target_pairs={{0,12},{1,13},{2,14},{3,15},{4,0},{5,1},{6,2},{7,3},{8,4},{9,5},{1... | collective-permute-start | bytes 786440 | tf_op jit(solution)/shard_map/ppermute | solution.py:331
  23.3 8.3 %collective-permute-start.9 = (bf16[512,256]{1,0:T(8,128)(2,1)S(1)}, bf16[512,256]{1,0:T(8,128)(2,1)S(1)}, u32[]{:S(2)}, u32[]{:S(2)}) collective-permute-start(bf16[512,256]{1,0:T(8,128)(2,1)S(1)} %collective-permute-done.7.refs_2_), channel_id=1, source_target_pairs={{0,2},{1,3},{2,0},{3,1},{4,6},{5,7},{6,4},{7,5},{8,10},{9,11},{10,... | collective-permute-start | bytes 786440 | tf_op jit(solution)/shard_map/ppermute | solution.py:331
  23.8 2.7 %collective-permute-start = (s32[2,8]{1,0:T(2,128)S(1)}, s32[2,8]{1,0:T(2,128)S(1)}, u32[]{:S(2)}, u32[]{:S(2)}) collective-permute-start(s32[2,8]{1,0:T(2,128)S(1)} %add_bitcast_fusion.ids), channel_id=1, source_target_pairs={{0,1},{1,0},{2,3},{3,2},{4,5},{5,4},{6,7},{7,6},{8,9},{9,8},{10,11... | collective-permute-start | bytes 200 | tf_op jit(solution)/shard_map/ppermute | solution.py:331
  28.9 8.3 %collective-permute-start.6 = (bf16[512,256]{1,0:T(8,128)(2,1)S(1)}, bf16[512,256]{1,0:T(8,128)(2,1)S(1)}, u32[]{:S(2)}, u32[]{:S(2)}) collective-permute-start(bf16[512,256]{1,0:T(8,128)(2,1)S(1)} %collective-permute-done.5.refs_3_), channel_id=1, source_target_pairs={{0,2},{1,3},{2,0},{3,1},{4,6},{5,7},{6,4},{7,5},{8,10},{9,11},{10,... | collective-permute-start | bytes 786440 | tf_op jit(solution)/shard_map/ppermute | solution.py:331
  32.5 6.3 %copy-start.3 = (bf16[2,8,128,512]{3,2,1,0:T(8,128)(2,1)S(1)}, bf16[2,8,128,512]{3,2,1,0:T(8,128)(2,1)}, u32[]{:S(2)}) copy-start(bf16[2,8,128,512]{3,2,1,0:T(8,128)(2,1)} %param.11) | copy-start | bytes 6291460
  32.5 6.3 %copy-start.4 = (s32[2,8,4]{1,2,0:T(4,128)S(1)}, s32[2,8,4]{1,2,0:T(4,128)}, u32[]{:S(2)}) copy-start(s32[2,8,4]{1,2,0:T(4,128)} %param.14) | copy-start | bytes 772
  32.5 6.3 %collective-permute-start.10 = (bf16[1024,256]{1,0:T(8,128)(2,1)S(1)}, bf16[1024,256]{1,0:T(8,128)(2,1)S(1)}, u32[]{:S(2)}, u32[]{:S(2)}) collective-permute-start(bf16[1024,256]{1,0:T(8,128)(2,1)S(1)} %pack.2), channel_id=1, source_target_pairs={{0,1},{1,0},{2,3},{3,2},{4,5},{5,4},{6,7},{7,6},{8,9},{9,8},{10,11... | collective-permute-start | bytes 1572872 | tf_op jit(solution)/shard_map/ppermute | solution.py:331
  33.3 5.4 %collective-permute-start.11 = (bf16[1024,256]{1,0:T(8,128)(2,1)S(1)}, bf16[1024,256]{1,0:T(8,128)(2,1)S(1)}, u32[]{:S(2)}, u32[]{:S(2)}) collective-permute-start(bf16[1024,256]{1,0:T(8,128)(2,1)S(1)} %pack.3), channel_id=1, source_target_pairs={{0,1},{1,0},{2,3},{3,2},{4,5},{5,4},{6,7},{7,6},{8,9},{9,8},{10,11... | collective-permute-start | bytes 1572872 | tf_op jit(solution)/shard_map/ppermute | solution.py:331
  37.2 1.5 %collective-permute-start.12 = (bf16[512,256]{1,0:T(8,128)(2,1)S(1)}, bf16[512,256]{1,0:T(8,128)(2,1)S(1)}, u32[]{:S(2)}, u32[]{:S(2)}) collective-permute-start(bf16[512,256]{1,0:T(8,128)(2,1)S(1)} %collective-permute-done.6.refs_7_), channel_id=1, source_target_pairs={{0,1},{1,0},{2,3},{3,2},{4,5},{5,4},{6,7},{7,6},{8,9},{9,8},{10,11... | collective-permute-start | bytes 786440 | tf_op jit(solution)/shard_map/ppermute | solution.py:331
  42.8 2.9 %collective-permute-start.13 = (bf16[2304,256]{1,0:T(8,128)(2,1)S(1)}, bf16[2304,256]{1,0:T(8,128)(2,1)S(1)}, u32[]{:S(2)}, u32[]{:S(2)}) collective-permute-start(bf16[2304,256]{1,0:T(8,128)(2,1)S(1)} %get-tuple-element.63.own), channel_id=1, source_target_pairs={{0,1},{1,0},{2,3},{3,2},{4,5},{5,4},{6,7},{7,6},{8,9},{9,8},{10,11... | collective-permute-start | bytes 3538952 | tf_op jit(solution)/shard_map/ppermute | solution.py:331
  46.9 9.2 %collective-permute-start.14 = (bf16[512,256]{1,0:T(8,128)(2,1)S(1)}, bf16[512,256]{1,0:T(8,128)(2,1)S(1)}, u32[]{:S(2)}, u32[]{:S(2)}) collective-permute-start(bf16[512,256]{1,0:T(8,128)(2,1)S(1)} %merge_late.1), channel_id=1, source_target_pairs={{0,2},{1,3},{2,0},{3,1},{4,6},{5,7},{6,4},{7,5},{8,10},{9,11},{10,... | collective-permute-start | bytes 786440 | tf_op jit(solution)/shard_map/ppermute | solution.py:331
  50.5 11.2 %collective-permute-start.20 = (bf16[512,256]{1,0:T(8,128)(2,1)S(1)}, bf16[512,256]{1,0:T(8,128)(2,1)S(1)}, u32[]{:S(2)}, u32[]{:S(2)}) collective-permute-start(bf16[512,256]{1,0:T(8,128)(2,1)S(1)} %get-tuple-element.77), channel_id=1, source_target_pairs={{0,2},{1,3},{2,0},{3,1},{4,6},{5,7},{6,4},{7,5},{8,10},{9,11},{10,... | collective-permute-start | bytes 786440 | tf_op jit(solution)/shard_map/ppermute | solution.py:331
  51.0 20.0 %collective-permute-start.17 = (bf16[512,256]{1,0:T(8,128)(2,1)S(1)}, bf16[512,256]{1,0:T(8,128)(2,1)S(1)}, u32[]{:S(2)}, u32[]{:S(2)}) collective-permute-start(bf16[512,256]{1,0:T(8,128)(2,1)S(1)} %get-tuple-element.74), channel_id=1, source_target_pairs={{0,2},{1,3},{2,0},{3,1},{4,6},{5,7},{6,4},{7,5},{8,10},{9,11},{10,... | collective-permute-start | bytes 786440 | tf_op jit(solution)/shard_map/ppermute | solution.py:331
  56.2 14.9 %collective-permute-start.18 = (bf16[512,256]{1,0:T(8,128)(2,1)S(1)}, bf16[512,256]{1,0:T(8,128)(2,1)S(1)}, u32[]{:S(2)}, u32[]{:S(2)}) collective-permute-start(bf16[512,256]{1,0:T(8,128)(2,1)S(1)} %hop.3), channel_id=1, source_target_pairs={{0,4},{1,5},{2,6},{3,7},{4,8},{5,9},{6,10},{7,11},{8,12},{9,13},{1... | collective-permute-start | bytes 786440 | tf_op jit(solution)/shard_map/ppermute | solution.py:331
  56.2 9.4 %collective-permute-start.15 = (bf16[256,256]{1,0:T(8,128)(2,1)S(1)}, bf16[256,256]{1,0:T(8,128)(2,1)S(1)}, u32[]{:S(2)}, u32[]{:S(2)}) collective-permute-start(bf16[256,256]{1,0:T(8,128)(2,1)S(1)} %get-tuple-element.68), channel_id=1, source_target_pairs={{1,2},{3,4},{5,6},{7,8},{9,10},{11,12},{13,14},{2,1},{4,3},{6,5},{... | collective-permute-start | bytes 393224 | tf_op jit(solution)/shard_map/ppermute | solution.py:331
  61.8 11.9 %collective-permute-start.21 = (bf16[512,256]{1,0:T(8,128)(2,1)S(1)}, bf16[512,256]{1,0:T(8,128)(2,1)S(1)}, u32[]{:S(2)}, u32[]{:S(2)}) collective-permute-start(bf16[512,256]{1,0:T(8,128)(2,1)S(1)} %hop.5), channel_id=1, source_target_pairs={{0,12},{1,13},{2,14},{3,15},{4,0},{5,1},{6,2},{7,3},{8,4},{9,5},{1... | collective-permute-start | bytes 786440 | tf_op jit(solution)/shard_map/ppermute | solution.py:331
  65.6 11.3 %collective-permute-start.16 = (bf16[512,256]{1,0:T(8,128)(2,1)S(1)}, bf16[512,256]{1,0:T(8,128)(2,1)S(1)}, u32[]{:S(2)}, u32[]{:S(2)}) collective-permute-start(bf16[512,256]{1,0:T(8,128)(2,1)S(1)} %get-tuple-element.72), channel_id=1, source_target_pairs={{0,2},{1,3},{2,0},{3,1},{4,6},{5,7},{6,4},{7,5},{8,10},{9,11},{10,... | collective-permute-start | bytes 786440 | tf_op jit(solution)/shard_map/ppermute | solution.py:331
  71.1 8.8 %collective-permute-start.19 = (bf16[512,256]{1,0:T(8,128)(2,1)S(1)}, bf16[512,256]{1,0:T(8,128)(2,1)S(1)}, u32[]{:S(2)}, u32[]{:S(2)}) collective-permute-start(bf16[512,256]{1,0:T(8,128)(2,1)S(1)} %hop.4), channel_id=1, source_target_pairs={{0,4},{1,5},{2,6},{3,7},{4,8},{5,9},{6,10},{7,11},{8,12},{9,13},{1... | collective-permute-start | bytes 786440 | tf_op jit(solution)/shard_map/ppermute | solution.py:331

commit v13 on v11

--- a/solution.py
+++ b/solution.py
@@ -469,7 +469,10 @@
         name="merge",
     )(ids, asked, terms, got)
     crossed = {r: merged[chain + r - (r > half)] for r in range(chain) if r != half}
-    other = {r: flip(part, 2) for r, part in crossed.items() if r}
+    back, *held = lax.optimization_barrier((back, *(crossed[r] for r in range(1, half))))
+    other = {r: flip(part, 2) for r, part in enumerate(held, 1)}
+    for r in range(half + 1, chain):
+        other[r] = flip(crossed[r], 2)
 
     def hop(total, *came):
         return pl.pallas_call(

time: 77.1 us -> 77.1 us (level)
  starting transfers between devices: 34.5 us -> 33.6 us
  waiting for transfers between devices: 22.6 us -> 23.5 us
    ppermute x22, starting transfers between devices: 34.5 us -> 33.6 us  [permute(): return lax.ppermute(x, 'tm', pairs)]
    ppermute x22, waiting for transfers between devices: 22.6 us -> 23.5 us  [permute(): return lax.ppermute(x, 'tm', pairs)]
  transfers between devices with their start and end apart: 22 -> 22, of which waited for: 9 -> 8; matrix products, arithmetic and copies ran while one was open for 1% -> 1% of each run, Pallas kernels for 13% -> 13%
where the time goes in v13:
time: 77.1 us; the launch traced here: 76.9 us
  starting transfers between devices  33.6 us (44%)
  waiting for transfers between devices  23.5 us (30%)
  Pallas kernels  15.1 us (20%)
  local copies, waits for them, and re-layouts  2.02 us (3%)
  other arithmetic  1.92 us (2%)
  between operations  0.84 us (1%)
    ppermute x22, starting transfers between devices, permute(): return lax.ppermute(x, 'tm', pairs)  33.6 us
    ppermute x22, waiting for transfers between devices, permute(): return lax.ppermute(x, 'tm', pairs)  23.5 us
    pallas_call x1, Pallas kernels, local(): pl.pallas_call(functools.partial(session_kernel, entries, group, late), o...  4.01 us
    pallas_call x1, Pallas kernels, local(): pl.pallas_call(unsmooth_kernel, out_shape=jax.ShapeDtypeStruct((latent_di...  2.51 us
    unnamed x14, local copies, waits for them, and re-layouts  2.02 us
    pallas_call x1, Pallas kernels, local(): pl.pallas_call(prepare_kernel, out_shape=(jax.ShapeDtypeStruct(table.shap...  2.02 us
    pallas_call x1, Pallas kernels, local(): pl.pallas_call(functools.partial(merge_kernel, entries, late), out_shape=...  1.88 us
    pallas_call x1, Pallas kernels, local(): pl.pallas_call(smooth_kernel, out_shape=jax.ShapeDtypeStruct((latent_dim,...  1.68 us
  transfers between devices with their start and end apart: 22, of which 8 were waited for; matrix products, arithmetic and copies ran while one was open for 1% of the time, Pallas kernels for 13%

profile of v13, /device:TPU:0, one launch (start us, length us, event | category | flops | bytes accessed | tf_op | source)
XLA Modules:
  0.0 76.9 jit_solution(14678280495375334494)
XLA Ops:
  0.6 0.0 copy-start.5
  0.6 0.0 copy-start.6
  0.6 3.0 %collective-permute-start.3 = (bf16[512,256]{1,0:T(8,128)(2,1)}, bf16[512,256]{1,0:T(8,128)(2,1)S(1)}, u32[]{:S(2)}, u32[]{:S(2)}) collective-permute-start(bf16[512,256]{1,0:T(8,128)(2,1)} %refs_0_.5), channel_id=1, source_target_pairs={{0,2},{1,3},{2,0},{3,1},{4,6},{5,7},{6,4},{7,5},{8,10},{9,11},{10,... | collective-permute-start | bytes 786440 | tf_op jit(solution)/shard_map/ppermute | solution.py:331
  3.7 1.6 %collective-permute-start.2 = (bf16[512,256]{1,0:T(8,128)(2,1)}, bf16[512,256]{1,0:T(8,128)(2,1)S(1)}, u32[]{:S(2)}, u32[]{:S(2)}) collective-permute-start(bf16[512,256]{1,0:T(8,128)(2,1)} %refs_0_.5), channel_id=1, source_target_pairs={{0,4},{1,5},{2,6},{3,7},{4,8},{5,9},{6,10},{7,11},{8,12},{9,13},{1... | collective-permute-start | bytes 786440 | tf_op jit(solution)/shard_map/ppermute | solution.py:331
  5.3 2.2 %collective-permute-start.1 = (bf16[512,256]{1,0:T(8,128)(2,1)}, bf16[512,256]{1,0:T(8,128)(2,1)S(1)}, u32[]{:S(2)}, u32[]{:S(2)}) collective-permute-start(bf16[512,256]{1,0:T(8,128)(2,1)} %refs_0_.5), channel_id=1, source_target_pairs={{0,12},{1,13},{2,14},{3,15},{4,0},{5,1},{6,2},{7,3},{8,4},{9,5},{1... | collective-permute-start | bytes 786440 | tf_op jit(solution)/shard_map/ppermute | solution.py:331
  7.5 1.0 %slice_select_fusion = (f32[256,128]{1,0:T(8,128)S(1)}, f32[256,128]{1,0:T(8,128)S(1)}) fusion(f32[256,512]{1,0:T(8,128)} %mid.1, pred[]{:T(512)S(6)} %eq.5), kind=kLoop, calls=%fused_computation.1 | loop fusion | flops 65536 | bytes 524289 | tf_op jit(solution)/shard_map/jit(_where)/select_n | solution.py:349
  8.5 0.7 collective-permute-start.5
  9.2 1.7 %collective-permute-start.4 = (f32[256,128]{1,0:T(8,128)S(1)}, f32[256,128]{1,0:T(8,128)S(1)}, u32[]{:S(2)}, u32[]{:S(2)}) collective-permute-start(f32[256,128]{1,0:T(8,128)S(1)} %get-tuple-element.79), channel_id=1, source_target_pairs={{0,1},{1,0},{2,3},{3,2},{4,5},{5,4},{6,7},{7,6},{8,9},{9,8},{10,11... | collective-permute-start | bytes 393224 | tf_op jit(solution)/shard_map/ppermute | solution.py:331
  10.9 0.0 collective-permute-done.3.refs_4_
  10.9 4.1 %collective-permute-done.2.refs_1_ = bf16[512,256]{1,0:T(8,128)(2,1)S(1)} collective-permute-done((bf16[512,256]{1,0:T(8,128)(2,1)}, bf16[512,256]{1,0:T(8,128)(2,1)S(1)}, u32[]{:S(2)}, u32[]{:S(2)}) %collective-permute-start.2) | collective-permute-done | bytes 262176 | tf_op jit(solution)/shard_map/ppermute | solution.py:331
  15.0 0.0 collective-permute-start.6
  15.0 0.3 collective-permute-start.8
  15.3 1.0 %copy-done = f32[256,512]{1,0:T(8,128)S(1)} copy-done((f32[256,512]{1,0:T(8,128)S(1)}, f32[256,512]{1,0:T(8,128)}, u32[]{:S(2)}) %copy-start) | copy-done | bytes 524312
  16.3 0.9 %copy-done.2 = f32[256,256]{1,0:T(8,128)S(1)} copy-done((f32[256,256]{1,0:T(8,128)S(1)}, f32[256,256]{1,0:T(8,128)}, u32[]{:S(2)}) %copy-start.2) | copy-done | bytes 262168
  17.2 2.0 %prepare.1 = (bf16[3072,256]{1,0:T(8,128)(2,1)S(1)}, f32[256,512]{1,0:T(8,128)S(1)}, f32[256,256]{1,0:T(8,128)S(1)}, f32[256,256]{1,0:T(8,128)S(1)}, f32[256,256]{1,0:T(8,128)S(1)}) custom-call(bf16[3072,256]{1,0:T(8,128)(2,1)} %constant.22.clone.table, f32[256,256]{1,0:T(8,128)S(1)} %copy-done.2, f32[256,512]{1,0:T(8,128)S(1)} %copy-done), custom_call_target="tpu_custom_call" | custom-call | flops 335544320 | bytes 4194304 | tf_op jit(solution)/shard_map/prepare/pallas_call | solution.py:365
  19.3 0.0 collective-permute-done.1.refs_3_
  19.3 1.8 %collective-permute-start.9 = (bf16[512,256]{1,0:T(8,128)(2,1)S(1)}, bf16[512,256]{1,0:T(8,128)(2,1)S(1)}, u32[]{:S(2)}, u32[]{:S(2)}) collective-permute-start(bf16[512,256]{1,0:T(8,128)(2,1)S(1)} %collective-permute-done.1.refs_3_), channel_id=1, source_target_pairs={{0,2},{1,3},{2,0},{3,1},{4,6},{5,7},{6,4},{7,5},{8,10},{9,11},{10,... | collective-permute-start | bytes 786440 | tf_op jit(solution)/shard_map/ppermute | solution.py:331
  21.1 0.0 copy-done.5
  21.1 0.0 copy-start.1
  21.1 0.0 collective-permute-done.5.far_side
  21.1 0.1 collective-permute-start
  21.2 0.0 collective-permute-done.4.core_side
  21.2 1.7 %smooth.1.smoothed = bf16[256,512]{1,0:T(8,128)(2,1)S(1)} custom-call(f32[256,512]{1,0:T(8,128)S(1)} %get-tuple-element.47.mid, f32[256,128]{1,0:T(8,128)S(1)} %collective-permute-done.4.core_side, f32[256,128]{1,0:T(8,128)S(1)} %collective-permute-done.5.far_side, bf16[3072,256]{1,0:T(8,128)(2,1)S(1)} %get-tuple-element.48.tables, ...), custom_call_target="tpu_custom_call" | custom-call | flops 1006632960 | bytes 4194304 | tf_op jit(solution)/shard_map/smooth/pallas_call | solution.py:385
  22.9 0.0 collective-permute-done.asked
  22.9 3.3 %collective-permute-done.6.refs_2_ = bf16[512,256]{1,0:T(8,128)(2,1)S(1)} collective-permute-done((bf16[512,256]{1,0:T(8,128)(2,1)S(1)}, bf16[512,256]{1,0:T(8,128)(2,1)S(1)}, u32[]{:S(2)}, u32[]{:S(2)}) %collective-permute-start.6) | collective-permute-done | bytes 262176 | tf_op jit(solution)/shard_map/ppermute | solution.py:331
  26.2 0.0 collective-permute-start.7
  26.2 0.0 collective-permute-done.8.refs_5_
  26.2 1.3 %collective-permute-done.9.refs_6_.refs_7_ = bf16[512,256]{1,0:T(8,128)(2,1)S(1)} collective-permute-done((bf16[512,256]{1,0:T(8,128)(2,1)S(1)}, bf16[512,256]{1,0:T(8,128)(2,1)S(1)}, u32[]{:S(2)}, u32[]{:S(2)}) %collective-permute-start.9) | collective-permute-done | bytes 262176 | tf_op jit(solution)/shard_map/ppermute | solution.py:331
  27.5 0.0 copy-done.1
  27.5 0.8 %pack.2 = bf16[1024,256]{1,0:T(8,128)(2,1)S(1)} custom-call(s32[2,8]{1,0:T(2,128)S(1)} %collective-permute-done.asked, bf16[512,256]{1,0:T(8,128)(2,1)S(1)} %copy-done.1, bf16[512,256]{1,0:T(8,128)(2,1)S(1)} %collective-permute-done.2.refs_1_, bf16[512,256]{1,0:T(8,128)(2,1)S(1)} %collective-permute-done.6.refs_2_, ...), custom_call_target="tpu_custom_call" | custom-call | bytes 1048576 | tf_op jit(solution)/shard_map/pack/pallas_call | solution.py:400
  28.3 0.0 copy-start.3
  28.3 0.0 copy-start.4
  28.4 0.1 collective-permute-start.10
  28.4 0.8 pack.3
  29.2 0.6 collective-permute-start.11
  29.8 2.8 %collective-permute-done.7.refs_6_ = bf16[512,256]{1,0:T(8,128)(2,1)S(1)} collective-permute-done((bf16[512,256]{1,0:T(8,128)(2,1)S(1)}, bf16[512,256]{1,0:T(8,128)(2,1)S(1)}, u32[]{:S(2)}, u32[]{:S(2)}) %collective-permute-start.7) | collective-permute-done | bytes 262176 | tf_op jit(solution)/shard_map/ppermute | solution.py:331
  32.6 0.0 collective-permute-start.12
  32.6 1.5 %collective-permute-done.12.late_theirs = bf16[512,256]{1,0:T(8,128)(2,1)S(1)} collective-permute-done((bf16[512,256]{1,0:T(8,128)(2,1)S(1)}, bf16[512,256]{1,0:T(8,128)(2,1)S(1)}, u32[]{:S(2)}, u32[]{:S(2)}) %collective-permute-start.12) | collective-permute-done | bytes 262176 | tf_op jit(solution)/shard_map/ppermute | solution.py:331
  34.1 0.0 collective-permute-done.10.packed
  34.1 0.0 collective-permute-done.11.packed_rest
  34.2 4.0 %session.1 = (f32[256,512]{1,0:T(8,128)S(1)}, bf16[256,256]{1,0:T(8,128)(2,1)S(1)}, bf16[2304,256]{1,0:T(8,128)(2,1)S(1)}) custom-call(s32[2,8]{1,0:T(2,128)S(1)} %add_bitcast_fusion.ids, s32[2,4,8]{2,1,0:T(4,128)S(1)} %bitcast.5, bf16[256,512]{1,0:T(8,128)(2,1)S(1)} %smooth.1.smoothed, bf16[16,128,512]{2,1,0:T(8,128)(2,1)S(1)} %bitcast.4, ...), custom_call_target="tpu_custom_call" | custom-call | flops 1610612736 | bytes 8388608 | tf_op jit(solution)/shard_map/session/pallas_call | solution.py:418
  38.2 0.2 collective-permute-start.13
  38.4 2.7 %collective-permute-done.13.got = bf16[2304,256]{1,0:T(8,128)(2,1)S(1)} collective-permute-done((bf16[2304,256]{1,0:T(8,128)(2,1)S(1)}, bf16[2304,256]{1,0:T(8,128)(2,1)S(1)}, u32[]{:S(2)}, u32[]{:S(2)}) %collective-permute-start.13) | collective-permute-done | bytes 1179680 | tf_op jit(solution)/shard_map/ppermute | solution.py:331
  41.1 1.2 %merge_late.1 = bf16[512,256]{1,0:T(8,128)(2,1)S(1)} custom-call(s32[2,8]{1,0:T(2,128)S(1)} %add_bitcast_fusion.ids, s32[2,8]{1,0:T(2,128)S(1)} %collective-permute-done.asked, bf16[2304,256]{1,0:T(8,128)(2,1)S(1)} %get-tuple-element.61.own, bf16[2304,256]{1,0:T(8,128)(2,1)S(1)} %collective-permute-done.13.got), custom_call_target="tpu_custom_call" | custom-call | bytes 1048576 | tf_op jit(solution)/shard_map/merge_late/pallas_call | solution.py:448
  42.3 1.7 %collective-permute-start.14 = (bf16[512,256]{1,0:T(8,128)(2,1)S(1)}, bf16[512,256]{1,0:T(8,128)(2,1)S(1)}, u32[]{:S(2)}, u32[]{:S(2)}) collective-permute-start(bf16[512,256]{1,0:T(8,128)(2,1)S(1)} %merge_late.1), channel_id=1, source_target_pairs={{0,2},{1,3},{2,0},{3,1},{4,6},{5,7},{6,4},{7,5},{8,10},{9,11},{10,... | collective-permute-start | bytes 786440 | tf_op jit(solution)/shard_map/ppermute | solution.py:331
  44.0 1.9 %merge.1 = (f32[512,256]{1,0:T(8,128)S(1)}, f32[512,256]{1,0:T(8,128)S(1)}, f32[512,256]{1,0:T(8,128)S(1)}, f32[512,256]{1,0:T(8,128)S(1)}, bf16[512,256]{1,0:T(...) custom-call(s32[2,8]{1,0:T(2,128)S(1)} %add_bitcast_fusion.ids, ...), custom_call_target="tpu_custom_call" | custom-call | bytes 5242880 | tf_op jit(solution)/shard_map/merge/pallas_call | solution.py:461
  45.9 0.5 collective-permute-start.20
  46.4 5.1 %collective-permute-done.14.refs_0_ = bf16[512,256]{1,0:T(8,128)(2,1)S(1)} collective-permute-done((bf16[512,256]{1,0:T(8,128)(2,1)S(1)}, bf16[512,256]{1,0:T(8,128)(2,1)S(1)}, u32[]{:S(2)}, u32[]{:S(2)}) %collective-permute-start.14) | collective-permute-done | bytes 262176 | tf_op jit(solution)/shard_map/ppermute | solution.py:331
  51.6 4.2 %collective-permute-start.18 = (bf16[512,256]{1,0:T(8,128)(2,1)S(1)}, bf16[512,256]{1,0:T(8,128)(2,1)S(1)}, u32[]{:S(2)}, u32[]{:S(2)}) collective-permute-start(bf16[512,256]{1,0:T(8,128)(2,1)S(1)} %hop.3), channel_id=1, source_target_pairs={{0,4},{1,5},{2,6},{3,7},{4,8},{5,9},{6,10},{7,11},{8,12},{9,13},{1... | collective-permute-start | bytes 786440 | tf_op jit(solution)/shard_map/ppermute | solution.py:331
  55.8 1.8 %collective-permute-start.17 = (bf16[512,256]{1,0:T(8,128)(2,1)S(1)}, bf16[512,256]{1,0:T(8,128)(2,1)S(1)}, u32[]{:S(2)}, u32[]{:S(2)}) collective-permute-start(bf16[512,256]{1,0:T(8,128)(2,1)S(1)} %get-tuple-element.74), channel_id=1, source_target_pairs={{0,2},{1,3},{2,0},{3,1},{4,6},{5,7},{6,4},{7,5},{8,10},{9,11},{10,... | collective-permute-start | bytes 786440 | tf_op jit(solution)/shard_map/ppermute | solution.py:331
  57.5 0.7 collective-permute-start.15
  58.2 0.0 collective-permute-done.20.refs_0_
  58.2 3.4 %collective-permute-start.21 = (bf16[512,256]{1,0:T(8,128)(2,1)S(1)}, bf16[512,256]{1,0:T(8,128)(2,1)S(1)}, u32[]{:S(2)}, u32[]{:S(2)}) collective-permute-start(bf16[512,256]{1,0:T(8,128)(2,1)S(1)} %hop.5), channel_id=1, source_target_pairs={{0,12},{1,13},{2,14},{3,15},{4,0},{5,1},{6,2},{7,3},{8,4},{9,5},{1... | collective-permute-start | bytes 786440 | tf_op jit(solution)/shard_map/ppermute | solution.py:331
  61.7 0.0 collective-permute-done.15.far_side
  61.7 5.2 %collective-permute-start.16 = (bf16[512,256]{1,0:T(8,128)(2,1)S(1)}, bf16[512,256]{1,0:T(8,128)(2,1)S(1)}, u32[]{:S(2)}, u32[]{:S(2)}) collective-permute-start(bf16[512,256]{1,0:T(8,128)(2,1)S(1)} %get-tuple-element.72), channel_id=1, source_target_pairs={{0,2},{1,3},{2,0},{3,1},{4,6},{5,7},{6,4},{7,5},{8,10},{9,11},{10,... | collective-permute-start | bytes 786440 | tf_op jit(solution)/shard_map/ppermute | solution.py:331
  66.9 0.0 collective-permute-done.18.refs_1_
  66.9 0.0 collective-permute-done.17.refs_0_
  66.9 0.1 hop.4
  67.0 3.9 %collective-permute-start.19 = (bf16[512,256]{1,0:T(8,128)(2,1)S(1)}, bf16[512,256]{1,0:T(8,128)(2,1)S(1)}, u32[]{:S(2)}, u32[]{:S(2)}) collective-permute-start(bf16[512,256]{1,0:T(8,128)(2,1)S(1)} %hop.4), channel_id=1, source_target_pairs={{0,4},{1,5},{2,6},{3,7},{4,8},{5,9},{6,10},{7,11},{8,12},{9,13},{1... | collective-permute-start | bytes 786440 | tf_op jit(solution)/shard_map/ppermute | solution.py:331
  70.9 2.5 %unsmooth.1 = f32[256,512]{1,0:T(8,128)} custom-call(f32[256,512]{1,0:T(8,128)S(1)} %get-tuple-element.60.mid, bf16[2304,256]{1,0:T(8,128)(2,1)S(1)} %collective-permute-done.13.got, bf16[256,256]{1,0:T(8,128)(2,1)S(1)} %collective-permute-done.15.far_side, bf16[3072,256]{1,0:T(8,128)(2,1)S(1)} %get-tuple-element.48.tables, ...), custom_call_target="tpu_custom_call" | custom-call | flops 1006632960 | bytes 4194304 | tf_op jit(solution)/shard_map/unsmooth/pallas_call | solution.py:501
  73.4 0.0 collective-permute-done.21
  73.4 0.0 collective-permute-done.16
  73.4 2.6 %collective-permute-done.19 = bf16[512,256]{1,0:T(8,128)(2,1)S(1)} collective-permute-done((bf16[512,256]{1,0:T(8,128)(2,1)S(1)}, bf16[512,256]{1,0:T(8,128)(2,1)S(1)}, u32[]{:S(2)}, u32[]{:S(2)}) %collective-permute-start.19) | collective-permute-done | bytes 262176 | tf_op jit(solution)/shard_map/ppermute | solution.py:331
  76.0 0.9 %convert_add_fusion = f32[512,256]{1,0:T(8,128)} fusion(bf16[512,256]{1,0:T(8,128)(2,1)S(1)} %collective-permute-done.21, bf16[512,256]{1,0:T(8,128)(2,1)S(1)} %collective-permute-done.19, f32[512,256]{1,0:T(8,128)S(1)} %get-tuple-element.71, bf16[512,256]{1,0:T(8,128)(2,1)S(1)} %collective-permute-done.16), kind=kLoop, calls=%fused_computation | loop fusion | flops 786432 | bytes 1835008 | tf_op jit(solution)/shard_map/add | solution.py:499
  (8 shorter events, 0.1 us)
Async XLA Ops:
  0.6 20.5 %copy-start.5 = (s32[1,2,8]{2,1,0:T(2,128)S(1)}, s32[1,2,8]{2,1,0:T(2,128)}, u32[]{:S(2)}) copy-start(s32[1,2,8]{2,1,0:T(2,128)} %param.13) | copy-start | bytes 196
  0.6 20.4 %copy-start.6 = (s32[1,2,8]{2,1,0:T(2,128)S(1)}, s32[1,2,8]{2,1,0:T(2,128)}, u32[]{:S(2)}) copy-start(s32[1,2,8]{2,1,0:T(2,128)} %param.12) | copy-start | bytes 196
  0.6 10.2 %collective-permute-start.3 = (bf16[512,256]{1,0:T(8,128)(2,1)}, bf16[512,256]{1,0:T(8,128)(2,1)S(1)}, u32[]{:S(2)}, u32[]{:S(2)}) collective-permute-start(bf16[512,256]{1,0:T(8,128)(2,1)} %refs_0_.5), channel_id=1, source_target_pairs={{0,2},{1,3},{2,0},{3,1},{4,6},{5,7},{6,4},{7,5},{8,10},{9,11},{10,... | collective-permute-start | bytes 786440 | tf_op jit(solution)/shard_map/ppermute | solution.py:331
  3.7 11.3 %collective-permute-start.2 = (bf16[512,256]{1,0:T(8,128)(2,1)}, bf16[512,256]{1,0:T(8,128)(2,1)S(1)}, u32[]{:S(2)}, u32[]{:S(2)}) collective-permute-start(bf16[512,256]{1,0:T(8,128)(2,1)} %refs_0_.5), channel_id=1, source_target_pairs={{0,4},{1,5},{2,6},{3,7},{4,8},{5,9},{6,10},{7,11},{8,12},{9,13},{1... | collective-permute-start | bytes 786440 | tf_op jit(solution)/shard_map/ppermute | solution.py:331
  5.3 14.0 %collective-permute-start.1 = (bf16[512,256]{1,0:T(8,128)(2,1)}, bf16[512,256]{1,0:T(8,128)(2,1)S(1)}, u32[]{:S(2)}, u32[]{:S(2)}) collective-permute-start(bf16[512,256]{1,0:T(8,128)(2,1)} %refs_0_.5), channel_id=1, source_target_pairs={{0,12},{1,13},{2,14},{3,15},{4,0},{5,1},{6,2},{7,3},{8,4},{9,5},{1... | collective-permute-start | bytes 786440 | tf_op jit(solution)/shard_map/ppermute | solution.py:331
  8.5 12.6 %collective-permute-start.5 = (f32[256,128]{1,0:T(8,128)S(1)}, f32[256,128]{1,0:T(8,128)S(1)}, u32[]{:S(2)}, u32[]{:S(2)}) collective-permute-start(f32[256,128]{1,0:T(8,128)S(1)} %get-tuple-element.78), channel_id=1, source_target_pairs={{1,2},{3,4},{5,6},{7,8},{9,10},{11,12},{13,14},{2,1},{4,3},{6,5},{... | collective-permute-start | bytes 393224 | tf_op jit(solution)/shard_map/ppermute | solution.py:331
  9.2 12.0 %collective-permute-start.4 = (f32[256,128]{1,0:T(8,128)S(1)}, f32[256,128]{1,0:T(8,128)S(1)}, u32[]{:S(2)}, u32[]{:S(2)}) collective-permute-start(f32[256,128]{1,0:T(8,128)S(1)} %get-tuple-element.79), channel_id=1, source_target_pairs={{0,1},{1,0},{2,3},{3,2},{4,5},{5,4},{6,7},{7,6},{8,9},{9,8},{10,11... | collective-permute-start | bytes 393224 | tf_op jit(solution)/shard_map/ppermute | solution.py:331
  15.0 11.3 %collective-permute-start.6 = (bf16[512,256]{1,0:T(8,128)(2,1)S(1)}, bf16[512,256]{1,0:T(8,128)(2,1)S(1)}, u32[]{:S(2)}, u32[]{:S(2)}) collective-permute-start(bf16[512,256]{1,0:T(8,128)(2,1)S(1)} %collective-permute-done.2.refs_1_), channel_id=1, source_target_pairs={{0,4},{1,5},{2,6},{3,7},{4,8},{5,9},{6,10},{7,11},{8,12},{9,13},{1... | collective-permute-start | bytes 786440 | tf_op jit(solution)/shard_map/ppermute | solution.py:331
  15.0 11.3 %collective-permute-start.8 = (bf16[512,256]{1,0:T(8,128)(2,1)S(1)}, bf16[512,256]{1,0:T(8,128)(2,1)S(1)}, u32[]{:S(2)}, u32[]{:S(2)}) collective-permute-start(bf16[512,256]{1,0:T(8,128)(2,1)S(1)} %collective-permute-done.2.refs_1_), channel_id=1, source_target_pairs={{0,2},{1,3},{2,0},{3,1},{4,6},{5,7},{6,4},{7,5},{8,10},{9,11},{10,... | collective-permute-start | bytes 786440 | tf_op jit(solution)/shard_map/ppermute | solution.py:331
  15.3 1.0 %copy-start = (f32[256,512]{1,0:T(8,128)S(1)}, f32[256,512]{1,0:T(8,128)}, u32[]{:S(2)}) copy-start(f32[256,512]{1,0:T(8,128)} %mid.1) | copy-start | bytes 1572868
  16.3 0.9 %copy-start.2 = (f32[256,256]{1,0:T(8,128)S(1)}, f32[256,256]{1,0:T(8,128)}, u32[]{:S(2)}) copy-start(f32[256,256]{1,0:T(8,128)} %taps) | copy-start | bytes 786436
  19.3 8.2 %collective-permute-start.9 = (bf16[512,256]{1,0:T(8,128)(2,1)S(1)}, bf16[512,256]{1,0:T(8,128)(2,1)S(1)}, u32[]{:S(2)}, u32[]{:S(2)}) collective-permute-start(bf16[512,256]{1,0:T(8,128)(2,1)S(1)} %collective-permute-done.1.refs_3_), channel_id=1, source_target_pairs={{0,2},{1,3},{2,0},{3,1},{4,6},{5,7},{6,4},{7,5},{8,10},{9,11},{10,... | collective-permute-start | bytes 786440 | tf_op jit(solution)/shard_map/ppermute | solution.py:331
  21.1 6.4 %copy-start.1 = (bf16[512,256]{1,0:T(8,128)(2,1)S(1)}, bf16[512,256]{1,0:T(8,128)(2,1)}, u32[]{:S(2)}) copy-start(bf16[512,256]{1,0:T(8,128)(2,1)} %refs_0_.5) | copy-start | bytes 786436
  21.1 1.8 %collective-permute-start = (s32[2,8]{1,0:T(2,128)S(1)}, s32[2,8]{1,0:T(2,128)S(1)}, u32[]{:S(2)}, u32[]{:S(2)}) collective-permute-start(s32[2,8]{1,0:T(2,128)S(1)} %add_bitcast_fusion.ids), channel_id=1, source_target_pairs={{0,1},{1,0},{2,3},{3,2},{4,5},{5,4},{6,7},{7,6},{8,9},{9,8},{10,11... | collective-permute-start | bytes 200 | tf_op jit(solution)/shard_map/ppermute | solution.py:331
  26.2 6.4 %collective-permute-start.7 = (bf16[512,256]{1,0:T(8,128)(2,1)S(1)}, bf16[512,256]{1,0:T(8,128)(2,1)S(1)}, u32[]{:S(2)}, u32[]{:S(2)}) collective-permute-start(bf16[512,256]{1,0:T(8,128)(2,1)S(1)} %collective-permute-done.6.refs_2_), channel_id=1, source_target_pairs={{0,2},{1,3},{2,0},{3,1},{4,6},{5,7},{6,4},{7,5},{8,10},{9,11},{10,... | collective-permute-start | bytes 786440 | tf_op jit(solution)/shard_map/ppermute | solution.py:331
  28.3 5.8 %copy-start.3 = (bf16[2,8,128,512]{3,2,1,0:T(8,128)(2,1)S(1)}, bf16[2,8,128,512]{3,2,1,0:T(8,128)(2,1)}, u32[]{:S(2)}) copy-start(bf16[2,8,128,512]{3,2,1,0:T(8,128)(2,1)} %param.11) | copy-start | bytes 6291460
  28.3 5.8 %copy-start.4 = (s32[2,8,4]{1,2,0:T(4,128)S(1)}, s32[2,8,4]{1,2,0:T(4,128)}, u32[]{:S(2)}) copy-start(s32[2,8,4]{1,2,0:T(4,128)} %param.14) | copy-start | bytes 772
  28.4 5.8 %collective-permute-start.10 = (bf16[1024,256]{1,0:T(8,128)(2,1)S(1)}, bf16[1024,256]{1,0:T(8,128)(2,1)S(1)}, u32[]{:S(2)}, u32[]{:S(2)}) collective-permute-start(bf16[1024,256]{1,0:T(8,128)(2,1)S(1)} %pack.2), channel_id=1, source_target_pairs={{0,1},{1,0},{2,3},{3,2},{4,5},{5,4},{6,7},{7,6},{8,9},{9,8},{10,11... | collective-permute-start | bytes 1572872 | tf_op jit(solution)/shard_map/ppermute | solution.py:331
  29.2 4.9 %collective-permute-start.11 = (bf16[1024,256]{1,0:T(8,128)(2,1)S(1)}, bf16[1024,256]{1,0:T(8,128)(2,1)S(1)}, u32[]{:S(2)}, u32[]{:S(2)}) collective-permute-start(bf16[1024,256]{1,0:T(8,128)(2,1)S(1)} %pack.3), channel_id=1, source_target_pairs={{0,1},{1,0},{2,3},{3,2},{4,5},{5,4},{6,7},{7,6},{8,9},{9,8},{10,11... | collective-permute-start | bytes 1572872 | tf_op jit(solution)/shard_map/ppermute | solution.py:331
  32.6 1.5 %collective-permute-start.12 = (bf16[512,256]{1,0:T(8,128)(2,1)S(1)}, bf16[512,256]{1,0:T(8,128)(2,1)S(1)}, u32[]{:S(2)}, u32[]{:S(2)}) collective-permute-start(bf16[512,256]{1,0:T(8,128)(2,1)S(1)} %collective-permute-done.7.refs_6_), channel_id=1, source_target_pairs={{0,1},{1,0},{2,3},{3,2},{4,5},{5,4},{6,7},{7,6},{8,9},{9,8},{10,11... | collective-permute-start | bytes 786440 | tf_op jit(solution)/shard_map/ppermute | solution.py:331
  38.2 2.9 %collective-permute-start.13 = (bf16[2304,256]{1,0:T(8,128)(2,1)S(1)}, bf16[2304,256]{1,0:T(8,128)(2,1)S(1)}, u32[]{:S(2)}, u32[]{:S(2)}) collective-permute-start(bf16[2304,256]{1,0:T(8,128)(2,1)S(1)} %get-tuple-element.61.own), channel_id=1, source_target_pairs={{0,1},{1,0},{2,3},{3,2},{4,5},{5,4},{6,7},{7,6},{8,9},{9,8},{10,11... | collective-permute-start | bytes 3538952 | tf_op jit(solution)/shard_map/ppermute | solution.py:331
  42.3 9.2 %collective-permute-start.14 = (bf16[512,256]{1,0:T(8,128)(2,1)S(1)}, bf16[512,256]{1,0:T(8,128)(2,1)S(1)}, u32[]{:S(2)}, u32[]{:S(2)}) collective-permute-start(bf16[512,256]{1,0:T(8,128)(2,1)S(1)} %merge_late.1), channel_id=1, source_target_pairs={{0,2},{1,3},{2,0},{3,1},{4,6},{5,7},{6,4},{7,5},{8,10},{9,11},{10,... | collective-permute-start | bytes 786440 | tf_op jit(solution)/shard_map/ppermute | solution.py:331
  45.9 12.3 %collective-permute-start.20 = (bf16[512,256]{1,0:T(8,128)(2,1)S(1)}, bf16[512,256]{1,0:T(8,128)(2,1)S(1)}, u32[]{:S(2)}, u32[]{:S(2)}) collective-permute-start(bf16[512,256]{1,0:T(8,128)(2,1)S(1)} %get-tuple-element.77), channel_id=1, source_target_pairs={{0,2},{1,3},{2,0},{3,1},{4,6},{5,7},{6,4},{7,5},{8,10},{9,11},{10,... | collective-permute-start | bytes 786440 | tf_op jit(solution)/shard_map/ppermute | solution.py:331
  51.6 15.3 %collective-permute-start.18 = (bf16[512,256]{1,0:T(8,128)(2,1)S(1)}, bf16[512,256]{1,0:T(8,128)(2,1)S(1)}, u32[]{:S(2)}, u32[]{:S(2)}) collective-permute-start(bf16[512,256]{1,0:T(8,128)(2,1)S(1)} %hop.3), channel_id=1, source_target_pairs={{0,4},{1,5},{2,6},{3,7},{4,8},{5,9},{6,10},{7,11},{8,12},{9,13},{1... | collective-permute-start | bytes 786440 | tf_op jit(solution)/shard_map/ppermute | solution.py:331
  55.8 11.1 %collective-permute-start.17 = (bf16[512,256]{1,0:T(8,128)(2,1)S(1)}, bf16[512,256]{1,0:T(8,128)(2,1)S(1)}, u32[]{:S(2)}, u32[]{:S(2)}) collective-permute-start(bf16[512,256]{1,0:T(8,128)(2,1)S(1)} %get-tuple-element.74), channel_id=1, source_target_pairs={{0,2},{1,3},{2,0},{3,1},{4,6},{5,7},{6,4},{7,5},{8,10},{9,11},{10,... | collective-permute-start | bytes 786440 | tf_op jit(solution)/shard_map/ppermute | solution.py:331
  57.5 4.2 %collective-permute-start.15 = (bf16[256,256]{1,0:T(8,128)(2,1)S(1)}, bf16[256,256]{1,0:T(8,128)(2,1)S(1)}, u32[]{:S(2)}, u32[]{:S(2)}) collective-permute-start(bf16[256,256]{1,0:T(8,128)(2,1)S(1)} %get-tuple-element.68), channel_id=1, source_target_pairs={{1,2},{3,4},{5,6},{7,8},{9,10},{11,12},{13,14},{2,1},{4,3},{6,5},{... | collective-permute-start | bytes 393224 | tf_op jit(solution)/shard_map/ppermute | solution.py:331
  58.2 15.1 %collective-permute-start.21 = (bf16[512,256]{1,0:T(8,128)(2,1)S(1)}, bf16[512,256]{1,0:T(8,128)(2,1)S(1)}, u32[]{:S(2)}, u32[]{:S(2)}) collective-permute-start(bf16[512,256]{1,0:T(8,128)(2,1)S(1)} %hop.5), channel_id=1, source_target_pairs={{0,12},{1,13},{2,14},{3,15},{4,0},{5,1},{6,2},{7,3},{8,4},{9,5},{1... | collective-permute-start | bytes 786440 | tf_op jit(solution)/shard_map/ppermute | solution.py:331
  61.7 11.7 %collective-permute-start.16 = (bf16[512,256]{1,0:T(8,128)(2,1)S(1)}, bf16[512,256]{1,0:T(8,128)(2,1)S(1)}, u32[]{:S(2)}, u32[]{:S(2)}) collective-permute-start(bf16[512,256]{1,0:T(8,128)(2,1)S(1)} %get-tuple-element.72), channel_id=1, source_target_pairs={{0,2},{1,3},{2,0},{3,1},{4,6},{5,7},{6,4},{7,5},{8,10},{9,11},{10,... | collective-permute-start | bytes 786440 | tf_op jit(solution)/shard_map/ppermute | solution.py:331
  67.0 9.0 %collective-permute-start.19 = (bf16[512,256]{1,0:T(8,128)(2,1)S(1)}, bf16[512,256]{1,0:T(8,128)(2,1)S(1)}, u32[]{:S(2)}, u32[]{:S(2)}) collective-permute-start(bf16[512,256]{1,0:T(8,128)(2,1)S(1)} %hop.4), channel_id=1, source_target_pairs={{0,4},{1,5},{2,6},{3,7},{4,8},{5,9},{6,10},{7,11},{8,12},{9,13},{1... | collective-permute-start | bytes 786440 | tf_op jit(solution)/shard_map/ppermute | solution.py:331

commit v14 on v13

--- a/solution.py
+++ b/solution.py
@@ -444,6 +444,8 @@
     )
 
     got = flip(terms, 1)
+    far_side = permute(far_side, odd_even)
+    got, far_side = lax.optimization_barrier((got, far_side))
     narrow = jax.ShapeDtypeStruct((chunk, latent_dim), BF16)
     sent = pl.pallas_call(
         functools.partial(merge_late_kernel, entries, late),
@@ -469,8 +471,8 @@
         name="merge",
     )(ids, asked, terms, got)
     crossed = {r: merged[chain + r - (r > half)] for r in range(chain) if r != half}
-    back, *held = lax.optimization_barrier((back, *(crossed[r] for r in range(1, half))))
-    other = {r: flip(part, 2) for r, part in enumerate(held, 1)}
+    back, *held = lax.optimization_barrier((back, *(crossed[r] for r in range(half))))
+    other = {r: flip(part, 2) for r, part in enumerate(held)}
     for r in range(half + 1, chain):
         other[r] = flip(crossed[r], 2)
 
@@ -486,10 +488,6 @@
         )(total, *came)
 
     rise = hop(merged[half], back)
-    rise, far_side = lax.optimization_barrier((rise, far_side))
-    far_side = permute(far_side, odd_even)
-    far_side, own = lax.optimization_barrier((far_side, crossed[0]))
-    other[0] = flip(own, 2)
     rise = rotate(rise, 1)
     for r in range(half - 1, 0, -1):
         rise = rotate(hop(merged[r], other[r], rise), 1)

time: 77.1 us -> 80.8 us (1.048)
  waiting for transfers between devices: 23.5 us -> 26 us
  starting transfers between devices: 33.6 us -> 34.7 us
    ppermute x22, waiting for transfers between devices: 23.5 us -> 26 us  [permute(): return lax.ppermute(x, 'tm', pairs)]
    ppermute x22, starting transfers between devices: 33.6 us -> 34.7 us  [permute(): return lax.ppermute(x, 'tm', pairs)]
  transfers between devices with their start and end apart: 22 -> 22, of which waited for: 8 -> 10; matrix products, arithmetic and copies ran while one was open for 1% -> 1% of each run, Pallas kernels for 13% -> 12%
where the time goes in v14:
time: 80.8 us; the launch traced here: 80.5 us
  starting transfers between devices  34.7 us (43%)
  waiting for transfers between devices  26 us (32%)
  Pallas kernels  15.1 us (19%)
  local copies, waits for them, and re-layouts  2.02 us (2%)
  other arithmetic  1.92 us (2%)
  between operations  0.84 us (1%)
    ppermute x22, starting transfers between devices, permute(): return lax.ppermute(x, 'tm', pairs)  34.7 us
    ppermute x22, waiting for transfers between devices, permute(): return lax.ppermute(x, 'tm', pairs)  26 us
    pallas_call x1, Pallas kernels, local(): pl.pallas_call(functools.partial(session_kernel, entries, group, late), o...  4.01 us
    pallas_call x1, Pallas kernels, local(): pl.pallas_call(unsmooth_kernel, out_shape=jax.ShapeDtypeStruct((latent_di...  2.51 us
    unnamed x14, local copies, waits for them, and re-layouts  2.02 us
    pallas_call x1, Pallas kernels, local(): pl.pallas_call(prepare_kernel, out_shape=(jax.ShapeDtypeStruct(table.shap...  2.02 us
    pallas_call x1, Pallas kernels, local(): pl.pallas_call(functools.partial(merge_kernel, entries, late), out_shape=...  1.89 us
    pallas_call x1, Pallas kernels, local(): pl.pallas_call(smooth_kernel, out_shape=jax.ShapeDtypeStruct((latent_dim,...  1.68 us
  transfers between devices with their start and end apart: 22, of which 10 were waited for; matrix products, arithmetic and copies ran while one was open for 1% of the time, Pallas kernels for 12%

profile of v14, /device:TPU:0, one launch (start us, length us, event | category | flops | bytes accessed | tf_op | source)
XLA Modules:
  0.0 80.5 jit_solution(1271641850084801668)
XLA Ops:
  0.6 0.0 copy-start.5
  0.6 0.0 copy-start.6
  0.6 3.0 %collective-permute-start.3 = (bf16[512,256]{1,0:T(8,128)(2,1)}, bf16[512,256]{1,0:T(8,128)(2,1)S(1)}, u32[]{:S(2)}, u32[]{:S(2)}) collective-permute-start(bf16[512,256]{1,0:T(8,128)(2,1)} %refs_0_.5), channel_id=1, source_target_pairs={{0,2},{1,3},{2,0},{3,1},{4,6},{5,7},{6,4},{7,5},{8,10},{9,11},{10,... | collective-permute-start | bytes 786440 | tf_op jit(solution)/shard_map/ppermute | solution.py:331
  3.7 1.6 %collective-permute-start.2 = (bf16[512,256]{1,0:T(8,128)(2,1)}, bf16[512,256]{1,0:T(8,128)(2,1)S(1)}, u32[]{:S(2)}, u32[]{:S(2)}) collective-permute-start(bf16[512,256]{1,0:T(8,128)(2,1)} %refs_0_.5), channel_id=1, source_target_pairs={{0,4},{1,5},{2,6},{3,7},{4,8},{5,9},{6,10},{7,11},{8,12},{9,13},{1... | collective-permute-start | bytes 786440 | tf_op jit(solution)/shard_map/ppermute | solution.py:331
  5.3 2.2 %collective-permute-start.1 = (bf16[512,256]{1,0:T(8,128)(2,1)}, bf16[512,256]{1,0:T(8,128)(2,1)S(1)}, u32[]{:S(2)}, u32[]{:S(2)}) collective-permute-start(bf16[512,256]{1,0:T(8,128)(2,1)} %refs_0_.5), channel_id=1, source_target_pairs={{0,12},{1,13},{2,14},{3,15},{4,0},{5,1},{6,2},{7,3},{8,4},{9,5},{1... | collective-permute-start | bytes 786440 | tf_op jit(solution)/shard_map/ppermute | solution.py:331
  7.5 1.0 %slice_select_fusion = (f32[256,128]{1,0:T(8,128)S(1)}, f32[256,128]{1,0:T(8,128)S(1)}) fusion(f32[256,512]{1,0:T(8,128)} %mid.1, pred[]{:T(512)S(6)} %eq.5), kind=kLoop, calls=%fused_computation.1 | loop fusion | flops 65536 | bytes 524289 | tf_op jit(solution)/shard_map/jit(_where)/select_n | solution.py:349
  8.5 0.7 collective-permute-start.5
  9.2 1.7 %collective-permute-start.4 = (f32[256,128]{1,0:T(8,128)S(1)}, f32[256,128]{1,0:T(8,128)S(1)}, u32[]{:S(2)}, u32[]{:S(2)}) collective-permute-start(f32[256,128]{1,0:T(8,128)S(1)} %get-tuple-element.77), channel_id=1, source_target_pairs={{0,1},{1,0},{2,3},{3,2},{4,5},{5,4},{6,7},{7,6},{8,9},{9,8},{10,11... | collective-permute-start | bytes 393224 | tf_op jit(solution)/shard_map/ppermute | solution.py:331
  10.9 0.0 collective-permute-done.3.refs_4_
  10.9 4.1 %collective-permute-done.2.refs_1_ = bf16[512,256]{1,0:T(8,128)(2,1)S(1)} collective-permute-done((bf16[512,256]{1,0:T(8,128)(2,1)}, bf16[512,256]{1,0:T(8,128)(2,1)S(1)}, u32[]{:S(2)}, u32[]{:S(2)}) %collective-permute-start.2) | collective-permute-done | bytes 262176 | tf_op jit(solution)/shard_map/ppermute | solution.py:331
  15.0 0.0 collective-permute-start.6
  15.0 0.3 collective-permute-start.8
  15.3 1.0 %copy-done = f32[256,512]{1,0:T(8,128)S(1)} copy-done((f32[256,512]{1,0:T(8,128)S(1)}, f32[256,512]{1,0:T(8,128)}, u32[]{:S(2)}) %copy-start) | copy-done | bytes 524312
  16.3 0.9 %copy-done.2 = f32[256,256]{1,0:T(8,128)S(1)} copy-done((f32[256,256]{1,0:T(8,128)S(1)}, f32[256,256]{1,0:T(8,128)}, u32[]{:S(2)}) %copy-start.2) | copy-done | bytes 262168
  17.2 2.0 %prepare.1 = (bf16[3072,256]{1,0:T(8,128)(2,1)S(1)}, f32[256,512]{1,0:T(8,128)S(1)}, f32[256,256]{1,0:T(8,128)S(1)}, f32[256,256]{1,0:T(8,128)S(1)}, f32[256,256]{1,0:T(8,128)S(1)}) custom-call(bf16[3072,256]{1,0:T(8,128)(2,1)} %constant.22.clone.table, f32[256,256]{1,0:T(8,128)S(1)} %copy-done.2, f32[256,512]{1,0:T(8,128)S(1)} %copy-done), custom_call_target="tpu_custom_call" | custom-call | flops 335544320 | bytes 4194304 | tf_op jit(solution)/shard_map/prepare/pallas_call | solution.py:365
  19.3 0.0 collective-permute-done.1.refs_3_
  19.3 1.8 %collective-permute-start.9 = (bf16[512,256]{1,0:T(8,128)(2,1)S(1)}, bf16[512,256]{1,0:T(8,128)(2,1)S(1)}, u32[]{:S(2)}, u32[]{:S(2)}) collective-permute-start(bf16[512,256]{1,0:T(8,128)(2,1)S(1)} %collective-permute-done.1.refs_3_), channel_id=1, source_target_pairs={{0,2},{1,3},{2,0},{3,1},{4,6},{5,7},{6,4},{7,5},{8,10},{9,11},{10,... | collective-permute-start | bytes 786440 | tf_op jit(solution)/shard_map/ppermute | solution.py:331
  21.1 0.0 copy-done.5
  21.1 0.0 copy-done.6
  21.1 0.0 copy-start.1
  21.1 0.0 collective-permute-done.5.far_side
  21.1 0.1 collective-permute-start
  21.2 0.0 collective-permute-done.4.core_side
  21.2 1.7 %smooth.1.smoothed = bf16[256,512]{1,0:T(8,128)(2,1)S(1)} custom-call(f32[256,512]{1,0:T(8,128)S(1)} %get-tuple-element.46.mid, f32[256,128]{1,0:T(8,128)S(1)} %collective-permute-done.4.core_side, f32[256,128]{1,0:T(8,128)S(1)} %collective-permute-done.5.far_side, bf16[3072,256]{1,0:T(8,128)(2,1)S(1)} %get-tuple-element.47.tables, ...), custom_call_target="tpu_custom_call" | custom-call | flops 1006632960 | bytes 4194304 | tf_op jit(solution)/shard_map/smooth/pallas_call | solution.py:385
  22.9 0.0 collective-permute-done.asked
  22.9 3.3 %collective-permute-done.6.refs_2_ = bf16[512,256]{1,0:T(8,128)(2,1)S(1)} collective-permute-done((bf16[512,256]{1,0:T(8,128)(2,1)S(1)}, bf16[512,256]{1,0:T(8,128)(2,1)S(1)}, u32[]{:S(2)}, u32[]{:S(2)}) %collective-permute-start.6) | collective-permute-done | bytes 262176 | tf_op jit(solution)/shard_map/ppermute | solution.py:331
  26.2 0.0 collective-permute-start.7
  26.2 0.0 collective-permute-done.8.refs_5_
  26.2 1.3 %collective-permute-done.9.refs_6_.refs_7_ = bf16[512,256]{1,0:T(8,128)(2,1)S(1)} collective-permute-done((bf16[512,256]{1,0:T(8,128)(2,1)S(1)}, bf16[512,256]{1,0:T(8,128)(2,1)S(1)}, u32[]{:S(2)}, u32[]{:S(2)}) %collective-permute-start.9) | collective-permute-done | bytes 262176 | tf_op jit(solution)/shard_map/ppermute | solution.py:331
  27.5 0.8 %pack.2 = bf16[1024,256]{1,0:T(8,128)(2,1)S(1)} custom-call(s32[2,8]{1,0:T(2,128)S(1)} %collective-permute-done.asked, bf16[512,256]{1,0:T(8,128)(2,1)S(1)} %copy-done.1, bf16[512,256]{1,0:T(8,128)(2,1)S(1)} %collective-permute-done.2.refs_1_, bf16[512,256]{1,0:T(8,128)(2,1)S(1)} %collective-permute-done.6.refs_2_, ...), custom_call_target="tpu_custom_call" | custom-call | bytes 1048576 | tf_op jit(solution)/shard_map/pack/pallas_call | solution.py:400
  28.4 0.0 copy-start.3
  28.4 0.0 copy-start.4
  28.4 0.1 collective-permute-start.10
  28.5 0.8 pack.3
  29.2 0.6 collective-permute-start.11
  29.8 2.8 %collective-permute-done.7.refs_6_ = bf16[512,256]{1,0:T(8,128)(2,1)S(1)} collective-permute-done((bf16[512,256]{1,0:T(8,128)(2,1)S(1)}, bf16[512,256]{1,0:T(8,128)(2,1)S(1)}, u32[]{:S(2)}, u32[]{:S(2)}) %collective-permute-start.7) | collective-permute-done | bytes 262176 | tf_op jit(solution)/shard_map/ppermute | solution.py:331
  32.6 0.0 collective-permute-start.12
  32.6 1.5 %collective-permute-done.12.late_theirs = bf16[512,256]{1,0:T(8,128)(2,1)S(1)} collective-permute-done((bf16[512,256]{1,0:T(8,128)(2,1)S(1)}, bf16[512,256]{1,0:T(8,128)(2,1)S(1)}, u32[]{:S(2)}, u32[]{:S(2)}) %collective-permute-start.12) | collective-permute-done | bytes 262176 | tf_op jit(solution)/shard_map/ppermute | solution.py:331
  34.1 0.0 collective-permute-done.10.packed
  34.1 0.0 collective-permute-done.11.packed_rest
  34.2 4.0 %session.1 = (f32[256,512]{1,0:T(8,128)S(1)}, bf16[256,256]{1,0:T(8,128)(2,1)S(1)}, bf16[2304,256]{1,0:T(8,128)(2,1)S(1)}) custom-call(s32[2,8]{1,0:T(2,128)S(1)} %add_bitcast_fusion.ids, s32[2,4,8]{2,1,0:T(4,128)S(1)} %bitcast.5, bf16[256,512]{1,0:T(8,128)(2,1)S(1)} %smooth.1.smoothed, bf16[16,128,512]{2,1,0:T(8,128)(2,1)S(1)} %bitcast.4, ...), custom_call_target="tpu_custom_call" | custom-call | flops 1610612736 | bytes 8388608 | tf_op jit(solution)/shard_map/session/pallas_call | solution.py:418
  38.2 0.2 collective-permute-start.13
  38.4 0.7 collective-permute-start.14
  39.0 0.0 collective-permute-done.14.far_side
  39.0 2.1 %collective-permute-done.13.got = bf16[2304,256]{1,0:T(8,128)(2,1)S(1)} collective-permute-done((bf16[2304,256]{1,0:T(8,128)(2,1)S(1)}, bf16[2304,256]{1,0:T(8,128)(2,1)S(1)}, u32[]{:S(2)}, u32[]{:S(2)}) %collective-permute-start.13) | collective-permute-done | bytes 1179680 | tf_op jit(solution)/shard_map/ppermute | solution.py:331
  41.1 1.2 %merge_late.1 = bf16[512,256]{1,0:T(8,128)(2,1)S(1)} custom-call(s32[2,8]{1,0:T(2,128)S(1)} %add_bitcast_fusion.ids, s32[2,8]{1,0:T(2,128)S(1)} %collective-permute-done.asked, bf16[2304,256]{1,0:T(8,128)(2,1)S(1)} %get-tuple-element.60.own, bf16[2304,256]{1,0:T(8,128)(2,1)S(1)} %collective-permute-done.13.got), custom_call_target="tpu_custom_call" | custom-call | bytes 1048576 | tf_op jit(solution)/shard_map/merge_late/pallas_call | solution.py:450
  42.3 5.3 %collective-permute-start.15 = (bf16[512,256]{1,0:T(8,128)(2,1)S(1)}, bf16[512,256]{1,0:T(8,128)(2,1)S(1)}, u32[]{:S(2)}, u32[]{:S(2)}) collective-permute-start(bf16[512,256]{1,0:T(8,128)(2,1)S(1)} %merge_late.1), channel_id=1, source_target_pairs={{0,2},{1,3},{2,0},{3,1},{4,6},{5,7},{6,4},{7,5},{8,10},{9,11},{10,... | collective-permute-start | bytes 786440 | tf_op jit(solution)/shard_map/ppermute | solution.py:331
  47.6 1.9 %merge.1 = (f32[512,256]{1,0:T(8,128)S(1)}, f32[512,256]{1,0:T(8,128)S(1)}, f32[512,256]{1,0:T(8,128)S(1)}, f32[512,256]{1,0:T(8,128)S(1)}, bf16[512,256]{1,0:T(...) custom-call(s32[2,8]{1,0:T(2,128)S(1)} %add_bitcast_fusion.ids, ...), custom_call_target="tpu_custom_call" | custom-call | bytes 5242880 | tf_op jit(solution)/shard_map/merge/pallas_call | solution.py:463
  49.5 0.1 collective-permute-start.20
  49.6 3.5 %collective-permute-done.15.refs_0_ = bf16[512,256]{1,0:T(8,128)(2,1)S(1)} collective-permute-done((bf16[512,256]{1,0:T(8,128)(2,1)S(1)}, bf16[512,256]{1,0:T(8,128)(2,1)S(1)}, u32[]{:S(2)}, u32[]{:S(2)}) %collective-permute-start.15) | collective-permute-done | bytes 262176 | tf_op jit(solution)/shard_map/ppermute | solution.py:331
  53.1 2.3 %collective-permute-start.17 = (bf16[512,256]{1,0:T(8,128)(2,1)S(1)}, bf16[512,256]{1,0:T(8,128)(2,1)S(1)}, u32[]{:S(2)}, u32[]{:S(2)}) collective-permute-start(bf16[512,256]{1,0:T(8,128)(2,1)S(1)} %get-tuple-element.71), channel_id=1, source_target_pairs={{0,2},{1,3},{2,0},{3,1},{4,6},{5,7},{6,4},{7,5},{8,10},{9,11},{10,... | collective-permute-start | bytes 786440 | tf_op jit(solution)/shard_map/ppermute | solution.py:331
  55.5 5.3 %collective-permute-start.18 = (bf16[512,256]{1,0:T(8,128)(2,1)S(1)}, bf16[512,256]{1,0:T(8,128)(2,1)S(1)}, u32[]{:S(2)}, u32[]{:S(2)}) collective-permute-start(bf16[512,256]{1,0:T(8,128)(2,1)S(1)} %hop.3), channel_id=1, source_target_pairs={{0,4},{1,5},{2,6},{3,7},{4,8},{5,9},{6,10},{7,11},{8,12},{9,13},{1... | collective-permute-start | bytes 786440 | tf_op jit(solution)/shard_map/ppermute | solution.py:331
  60.8 1.6 %collective-permute-start.16 = (bf16[512,256]{1,0:T(8,128)(2,1)S(1)}, bf16[512,256]{1,0:T(8,128)(2,1)S(1)}, u32[]{:S(2)}, u32[]{:S(2)}) collective-permute-start(bf16[512,256]{1,0:T(8,128)(2,1)S(1)} %get-tuple-element.69), channel_id=1, source_target_pairs={{0,2},{1,3},{2,0},{3,1},{4,6},{5,7},{6,4},{7,5},{8,10},{9,11},{10,... | collective-permute-start | bytes 786440 | tf_op jit(solution)/shard_map/ppermute | solution.py:331
  62.4 0.0 collective-permute-done.20.refs_0_
  62.4 3.9 %collective-permute-start.21 = (bf16[512,256]{1,0:T(8,128)(2,1)S(1)}, bf16[512,256]{1,0:T(8,128)(2,1)S(1)}, u32[]{:S(2)}, u32[]{:S(2)}) collective-permute-start(bf16[512,256]{1,0:T(8,128)(2,1)S(1)} %hop.5), channel_id=1, source_target_pairs={{0,12},{1,13},{2,14},{3,15},{4,0},{5,1},{6,2},{7,3},{8,4},{9,5},{1... | collective-permute-start | bytes 786440 | tf_op jit(solution)/shard_map/ppermute | solution.py:331
  66.3 0.0 collective-permute-done.17.refs_0_
  66.3 1.9 %collective-permute-done.18.refs_1_ = bf16[512,256]{1,0:T(8,128)(2,1)S(1)} collective-permute-done((bf16[512,256]{1,0:T(8,128)(2,1)S(1)}, bf16[512,256]{1,0:T(8,128)(2,1)S(1)}, u32[]{:S(2)}, u32[]{:S(2)}) %collective-permute-start.18) | collective-permute-done | bytes 262176 | tf_op jit(solution)/shard_map/ppermute | solution.py:331
  68.2 0.1 hop.4
  68.3 3.3 %collective-permute-start.19 = (bf16[512,256]{1,0:T(8,128)(2,1)S(1)}, bf16[512,256]{1,0:T(8,128)(2,1)S(1)}, u32[]{:S(2)}, u32[]{:S(2)}) collective-permute-start(bf16[512,256]{1,0:T(8,128)(2,1)S(1)} %hop.4), channel_id=1, source_target_pairs={{0,4},{1,5},{2,6},{3,7},{4,8},{5,9},{6,10},{7,11},{8,12},{9,13},{1... | collective-permute-start | bytes 786440 | tf_op jit(solution)/shard_map/ppermute | solution.py:331
  71.6 2.5 %unsmooth.1 = f32[256,512]{1,0:T(8,128)} custom-call(f32[256,512]{1,0:T(8,128)S(1)} %get-tuple-element.59.mid, bf16[2304,256]{1,0:T(8,128)(2,1)S(1)} %collective-permute-done.13.got, bf16[256,256]{1,0:T(8,128)(2,1)S(1)} %collective-permute-done.14.far_side, bf16[3072,256]{1,0:T(8,128)(2,1)S(1)} %get-tuple-element.47.tables, ...), custom_call_target="tpu_custom_call" | custom-call | flops 1006632960 | bytes 4194304 | tf_op jit(solution)/shard_map/unsmooth/pallas_call | solution.py:499
  74.1 0.0 collective-permute-done.16
  74.1 0.6 collective-permute-done.21
  74.8 4.9 %collective-permute-done.19 = bf16[512,256]{1,0:T(8,128)(2,1)S(1)} collective-permute-done((bf16[512,256]{1,0:T(8,128)(2,1)S(1)}, bf16[512,256]{1,0:T(8,128)(2,1)S(1)}, u32[]{:S(2)}, u32[]{:S(2)}) %collective-permute-start.19) | collective-permute-done | bytes 262176 | tf_op jit(solution)/shard_map/ppermute | solution.py:331
  79.6 0.9 %convert_add_fusion = f32[512,256]{1,0:T(8,128)} fusion(bf16[512,256]{1,0:T(8,128)(2,1)S(1)} %collective-permute-done.21, bf16[512,256]{1,0:T(8,128)(2,1)S(1)} %collective-permute-done.19, f32[512,256]{1,0:T(8,128)S(1)} %get-tuple-element.65, bf16[512,256]{1,0:T(8,128)(2,1)S(1)} %collective-permute-done.16), kind=kLoop, calls=%fused_computation | loop fusion | flops 786432 | bytes 1835008 | tf_op jit(solution)/shard_map/add | solution.py:497
  (8 shorter events, 0.1 us)
Async XLA Ops:
  0.6 20.5 %copy-start.5 = (s32[1,2,8]{2,1,0:T(2,128)S(1)}, s32[1,2,8]{2,1,0:T(2,128)}, u32[]{:S(2)}) copy-start(s32[1,2,8]{2,1,0:T(2,128)} %param.13) | copy-start | bytes 196
  0.6 20.4 %copy-start.6 = (s32[1,2,8]{2,1,0:T(2,128)S(1)}, s32[1,2,8]{2,1,0:T(2,128)}, u32[]{:S(2)}) copy-start(s32[1,2,8]{2,1,0:T(2,128)} %param.12) | copy-start | bytes 196
  0.6 10.2 %collective-permute-start.3 = (bf16[512,256]{1,0:T(8,128)(2,1)}, bf16[512,256]{1,0:T(8,128)(2,1)S(1)}, u32[]{:S(2)}, u32[]{:S(2)}) collective-permute-start(bf16[512,256]{1,0:T(8,128)(2,1)} %refs_0_.5), channel_id=1, source_target_pairs={{0,2},{1,3},{2,0},{3,1},{4,6},{5,7},{6,4},{7,5},{8,10},{9,11},{10,... | collective-permute-start | bytes 786440 | tf_op jit(solution)/shard_map/ppermute | solution.py:331
  3.7 11.3 %collective-permute-start.2 = (bf16[512,256]{1,0:T(8,128)(2,1)}, bf16[512,256]{1,0:T(8,128)(2,1)S(1)}, u32[]{:S(2)}, u32[]{:S(2)}) collective-permute-start(bf16[512,256]{1,0:T(8,128)(2,1)} %refs_0_.5), channel_id=1, source_target_pairs={{0,4},{1,5},{2,6},{3,7},{4,8},{5,9},{6,10},{7,11},{8,12},{9,13},{1... | collective-permute-start | bytes 786440 | tf_op jit(solution)/shard_map/ppermute | solution.py:331
  5.3 14.0 %collective-permute-start.1 = (bf16[512,256]{1,0:T(8,128)(2,1)}, bf16[512,256]{1,0:T(8,128)(2,1)S(1)}, u32[]{:S(2)}, u32[]{:S(2)}) collective-permute-start(bf16[512,256]{1,0:T(8,128)(2,1)} %refs_0_.5), channel_id=1, source_target_pairs={{0,12},{1,13},{2,14},{3,15},{4,0},{5,1},{6,2},{7,3},{8,4},{9,5},{1... | collective-permute-start | bytes 786440 | tf_op jit(solution)/shard_map/ppermute | solution.py:331
  8.5 12.6 %collective-permute-start.5 = (f32[256,128]{1,0:T(8,128)S(1)}, f32[256,128]{1,0:T(8,128)S(1)}, u32[]{:S(2)}, u32[]{:S(2)}) collective-permute-start(f32[256,128]{1,0:T(8,128)S(1)} %get-tuple-element.76), channel_id=1, source_target_pairs={{1,2},{3,4},{5,6},{7,8},{9,10},{11,12},{13,14},{2,1},{4,3},{6,5},{... | collective-permute-start | bytes 393224 | tf_op jit(solution)/shard_map/ppermute | solution.py:331
  9.2 12.0 %collective-permute-start.4 = (f32[256,128]{1,0:T(8,128)S(1)}, f32[256,128]{1,0:T(8,128)S(1)}, u32[]{:S(2)}, u32[]{:S(2)}) collective-permute-start(f32[256,128]{1,0:T(8,128)S(1)} %get-tuple-element.77), channel_id=1, source_target_pairs={{0,1},{1,0},{2,3},{3,2},{4,5},{5,4},{6,7},{7,6},{8,9},{9,8},{10,11... | collective-permute-start | bytes 393224 | tf_op jit(solution)/shard_map/ppermute | solution.py:331
  15.0 11.3 %collective-permute-start.6 = (bf16[512,256]{1,0:T(8,128)(2,1)S(1)}, bf16[512,256]{1,0:T(8,128)(2,1)S(1)}, u32[]{:S(2)}, u32[]{:S(2)}) collective-permute-start(bf16[512,256]{1,0:T(8,128)(2,1)S(1)} %collective-permute-done.2.refs_1_), channel_id=1, source_target_pairs={{0,4},{1,5},{2,6},{3,7},{4,8},{5,9},{6,10},{7,11},{8,12},{9,13},{1... | collective-permute-start | bytes 786440 | tf_op jit(solution)/shard_map/ppermute | solution.py:331
  15.0 11.3 %collective-permute-start.8 = (bf16[512,256]{1,0:T(8,128)(2,1)S(1)}, bf16[512,256]{1,0:T(8,128)(2,1)S(1)}, u32[]{:S(2)}, u32[]{:S(2)}) collective-permute-start(bf16[512,256]{1,0:T(8,128)(2,1)S(1)} %collective-permute-done.2.refs_1_), channel_id=1, source_target_pairs={{0,2},{1,3},{2,0},{3,1},{4,6},{5,7},{6,4},{7,5},{8,10},{9,11},{10,... | collective-permute-start | bytes 786440 | tf_op jit(solution)/shard_map/ppermute | solution.py:331
  15.3 1.0 %copy-start = (f32[256,512]{1,0:T(8,128)S(1)}, f32[256,512]{1,0:T(8,128)}, u32[]{:S(2)}) copy-start(f32[256,512]{1,0:T(8,128)} %mid.1) | copy-start | bytes 1572868
  16.3 0.9 %copy-start.2 = (f32[256,256]{1,0:T(8,128)S(1)}, f32[256,256]{1,0:T(8,128)}, u32[]{:S(2)}) copy-start(f32[256,256]{1,0:T(8,128)} %taps) | copy-start | bytes 786436
  19.3 8.2 %collective-permute-start.9 = (bf16[512,256]{1,0:T(8,128)(2,1)S(1)}, bf16[512,256]{1,0:T(8,128)(2,1)S(1)}, u32[]{:S(2)}, u32[]{:S(2)}) collective-permute-start(bf16[512,256]{1,0:T(8,128)(2,1)S(1)} %collective-permute-done.1.refs_3_), channel_id=1, source_target_pairs={{0,2},{1,3},{2,0},{3,1},{4,6},{5,7},{6,4},{7,5},{8,10},{9,11},{10,... | collective-permute-start | bytes 786440 | tf_op jit(solution)/shard_map/ppermute | solution.py:331
  21.1 6.4 %copy-start.1 = (bf16[512,256]{1,0:T(8,128)(2,1)S(1)}, bf16[512,256]{1,0:T(8,128)(2,1)}, u32[]{:S(2)}) copy-start(bf16[512,256]{1,0:T(8,128)(2,1)} %refs_0_.5) | copy-start | bytes 786436
  21.1 1.8 %collective-permute-start = (s32[2,8]{1,0:T(2,128)S(1)}, s32[2,8]{1,0:T(2,128)S(1)}, u32[]{:S(2)}, u32[]{:S(2)}) collective-permute-start(s32[2,8]{1,0:T(2,128)S(1)} %add_bitcast_fusion.ids), channel_id=1, source_target_pairs={{0,1},{1,0},{2,3},{3,2},{4,5},{5,4},{6,7},{7,6},{8,9},{9,8},{10,11... | collective-permute-start | bytes 200 | tf_op jit(solution)/shard_map/ppermute | solution.py:331
  26.2 6.4 %collective-permute-start.7 = (bf16[512,256]{1,0:T(8,128)(2,1)S(1)}, bf16[512,256]{1,0:T(8,128)(2,1)S(1)}, u32[]{:S(2)}, u32[]{:S(2)}) collective-permute-start(bf16[512,256]{1,0:T(8,128)(2,1)S(1)} %collective-permute-done.6.refs_2_), channel_id=1, source_target_pairs={{0,2},{1,3},{2,0},{3,1},{4,6},{5,7},{6,4},{7,5},{8,10},{9,11},{10,... | collective-permute-start | bytes 786440 | tf_op jit(solution)/shard_map/ppermute | solution.py:331
  28.4 5.8 %copy-start.3 = (bf16[2,8,128,512]{3,2,1,0:T(8,128)(2,1)S(1)}, bf16[2,8,128,512]{3,2,1,0:T(8,128)(2,1)}, u32[]{:S(2)}) copy-start(bf16[2,8,128,512]{3,2,1,0:T(8,128)(2,1)} %param.11) | copy-start | bytes 6291460
  28.4 5.8 %copy-start.4 = (s32[2,8,4]{1,2,0:T(4,128)S(1)}, s32[2,8,4]{1,2,0:T(4,128)}, u32[]{:S(2)}) copy-start(s32[2,8,4]{1,2,0:T(4,128)} %param.14) | copy-start | bytes 772
  28.4 5.7 %collective-permute-start.10 = (bf16[1024,256]{1,0:T(8,128)(2,1)S(1)}, bf16[1024,256]{1,0:T(8,128)(2,1)S(1)}, u32[]{:S(2)}, u32[]{:S(2)}) collective-permute-start(bf16[1024,256]{1,0:T(8,128)(2,1)S(1)} %pack.2), channel_id=1, source_target_pairs={{0,1},{1,0},{2,3},{3,2},{4,5},{5,4},{6,7},{7,6},{8,9},{9,8},{10,11... | collective-permute-start | bytes 1572872 | tf_op jit(solution)/shard_map/ppermute | solution.py:331
  29.2 4.9 %collective-permute-start.11 = (bf16[1024,256]{1,0:T(8,128)(2,1)S(1)}, bf16[1024,256]{1,0:T(8,128)(2,1)S(1)}, u32[]{:S(2)}, u32[]{:S(2)}) collective-permute-start(bf16[1024,256]{1,0:T(8,128)(2,1)S(1)} %pack.3), channel_id=1, source_target_pairs={{0,1},{1,0},{2,3},{3,2},{4,5},{5,4},{6,7},{7,6},{8,9},{9,8},{10,11... | collective-permute-start | bytes 1572872 | tf_op jit(solution)/shard_map/ppermute | solution.py:331
  32.6 1.5 %collective-permute-start.12 = (bf16[512,256]{1,0:T(8,128)(2,1)S(1)}, bf16[512,256]{1,0:T(8,128)(2,1)S(1)}, u32[]{:S(2)}, u32[]{:S(2)}) collective-permute-start(bf16[512,256]{1,0:T(8,128)(2,1)S(1)} %collective-permute-done.7.refs_6_), channel_id=1, source_target_pairs={{0,1},{1,0},{2,3},{3,2},{4,5},{5,4},{6,7},{7,6},{8,9},{9,8},{10,11... | collective-permute-start | bytes 786440 | tf_op jit(solution)/shard_map/ppermute | solution.py:331
  38.2 2.9 %collective-permute-start.13 = (bf16[2304,256]{1,0:T(8,128)(2,1)S(1)}, bf16[2304,256]{1,0:T(8,128)(2,1)S(1)}, u32[]{:S(2)}, u32[]{:S(2)}) collective-permute-start(bf16[2304,256]{1,0:T(8,128)(2,1)S(1)} %get-tuple-element.60.own), channel_id=1, source_target_pairs={{0,1},{1,0},{2,3},{3,2},{4,5},{5,4},{6,7},{7,6},{8,9},{9,8},{10,11... | collective-permute-start | bytes 3538952 | tf_op jit(solution)/shard_map/ppermute | solution.py:331
  38.4 0.7 collective-permute-start.14
  42.3 10.8 %collective-permute-start.15 = (bf16[512,256]{1,0:T(8,128)(2,1)S(1)}, bf16[512,256]{1,0:T(8,128)(2,1)S(1)}, u32[]{:S(2)}, u32[]{:S(2)}) collective-permute-start(bf16[512,256]{1,0:T(8,128)(2,1)S(1)} %merge_late.1), channel_id=1, source_target_pairs={{0,2},{1,3},{2,0},{3,1},{4,6},{5,7},{6,4},{7,5},{8,10},{9,11},{10,... | collective-permute-start | bytes 786440 | tf_op jit(solution)/shard_map/ppermute | solution.py:331
  49.5 12.9 %collective-permute-start.20 = (bf16[512,256]{1,0:T(8,128)(2,1)S(1)}, bf16[512,256]{1,0:T(8,128)(2,1)S(1)}, u32[]{:S(2)}, u32[]{:S(2)}) collective-permute-start(bf16[512,256]{1,0:T(8,128)(2,1)S(1)} %get-tuple-element.75), channel_id=1, source_target_pairs={{0,2},{1,3},{2,0},{3,1},{4,6},{5,7},{6,4},{7,5},{8,10},{9,11},{10,... | collective-permute-start | bytes 786440 | tf_op jit(solution)/shard_map/ppermute | solution.py:331
  53.1 13.2 %collective-permute-start.17 = (bf16[512,256]{1,0:T(8,128)(2,1)S(1)}, bf16[512,256]{1,0:T(8,128)(2,1)S(1)}, u32[]{:S(2)}, u32[]{:S(2)}) collective-permute-start(bf16[512,256]{1,0:T(8,128)(2,1)S(1)} %get-tuple-element.71), channel_id=1, source_target_pairs={{0,2},{1,3},{2,0},{3,1},{4,6},{5,7},{6,4},{7,5},{8,10},{9,11},{10,... | collective-permute-start | bytes 786440 | tf_op jit(solution)/shard_map/ppermute | solution.py:331
  55.5 12.7 %collective-permute-start.18 = (bf16[512,256]{1,0:T(8,128)(2,1)S(1)}, bf16[512,256]{1,0:T(8,128)(2,1)S(1)}, u32[]{:S(2)}, u32[]{:S(2)}) collective-permute-start(bf16[512,256]{1,0:T(8,128)(2,1)S(1)} %hop.3), channel_id=1, source_target_pairs={{0,4},{1,5},{2,6},{3,7},{4,8},{5,9},{6,10},{7,11},{8,12},{9,13},{1... | collective-permute-start | bytes 786440 | tf_op jit(solution)/shard_map/ppermute | solution.py:331
  60.8 13.3 %collective-permute-start.16 = (bf16[512,256]{1,0:T(8,128)(2,1)S(1)}, bf16[512,256]{1,0:T(8,128)(2,1)S(1)}, u32[]{:S(2)}, u32[]{:S(2)}) collective-permute-start(bf16[512,256]{1,0:T(8,128)(2,1)S(1)} %get-tuple-element.69), channel_id=1, source_target_pairs={{0,2},{1,3},{2,0},{3,1},{4,6},{5,7},{6,4},{7,5},{8,10},{9,11},{10,... | collective-permute-start | bytes 786440 | tf_op jit(solution)/shard_map/ppermute | solution.py:331
  62.4 12.3 %collective-permute-start.21 = (bf16[512,256]{1,0:T(8,128)(2,1)S(1)}, bf16[512,256]{1,0:T(8,128)(2,1)S(1)}, u32[]{:S(2)}, u32[]{:S(2)}) collective-permute-start(bf16[512,256]{1,0:T(8,128)(2,1)S(1)} %hop.5), channel_id=1, source_target_pairs={{0,12},{1,13},{2,14},{3,15},{4,0},{5,1},{6,2},{7,3},{8,4},{9,5},{1... | collective-permute-start | bytes 786440 | tf_op jit(solution)/shard_map/ppermute | solution.py:331
  68.3 11.3 %collective-permute-start.19 = (bf16[512,256]{1,0:T(8,128)(2,1)S(1)}, bf16[512,256]{1,0:T(8,128)(2,1)S(1)}, u32[]{:S(2)}, u32[]{:S(2)}) collective-permute-start(bf16[512,256]{1,0:T(8,128)(2,1)S(1)} %hop.4), channel_id=1, source_target_pairs={{0,4},{1,5},{2,6},{3,7},{4,8},{5,9},{6,10},{7,11},{8,12},{9,13},{1... | collective-permute-start | bytes 786440 | tf_op jit(solution)/shard_map/ppermute | solution.py:331

commit v15 on v14

--- a/solution.py
+++ b/solution.py
@@ -445,7 +445,6 @@
 
     got = flip(terms, 1)
     far_side = permute(far_side, odd_even)
-    got, far_side = lax.optimization_barrier((got, far_side))
     narrow = jax.ShapeDtypeStruct((chunk, latent_dim), BF16)
     sent = pl.pallas_call(
         functools.partial(merge_late_kernel, entries, late),
@@ -470,6 +469,7 @@
         cost_estimate=pl.CostEstimate(flops=0, bytes_accessed=5 * 2**20, transcendentals=0),
         name="merge",
     )(ids, asked, terms, got)
+    far_side, *merged = lax.optimization_barrier((far_side, *merged))
     crossed = {r: merged[chain + r - (r > half)] for r in range(chain) if r != half}
     back, *held = lax.optimization_barrier((back, *(crossed[r] for r in range(half))))
     other = {r: flip(part, 2) for r, part in enumerate(held)}

time: 80.8 us -> 81 us (level)
  waiting for transfers between devices: 26 us -> 24.9 us
  starting transfers between devices: 34.7 us -> 35.8 us
    ppermute x22, starting transfers between devices: 34.7 us -> 35.8 us  [permute(): return lax.ppermute(x, 'tm', pairs)]
    ppermute x22, waiting for transfers between devices: 26 us -> 24.9 us  [permute(): return lax.ppermute(x, 'tm', pairs)]
  transfers between devices with their start and end apart: 22 -> 22, of which waited for: 10 -> 9; matrix products, arithmetic and copies ran while one was open for 1% -> 1% of each run, Pallas kernels for 12% -> 12%
where the time goes in v15:
time: 81 us; the launch traced here: 80.7 us
  starting transfers between devices  35.8 us (44%)
  waiting for transfers between devices  24.9 us (31%)
  Pallas kernels  15.2 us (19%)
  local copies, waits for them, and re-layouts  2.02 us (2%)
  other arithmetic  1.92 us (2%)
  between operations  0.84 us (1%)
    ppermute x22, starting transfers between devices, permute(): return lax.ppermute(x, 'tm', pairs)  35.8 us
    ppermute x22, waiting for transfers between devices, permute(): return lax.ppermute(x, 'tm', pairs)  24.9 us
    pallas_call x1, Pallas kernels, local(): pl.pallas_call(functools.partial(session_kernel, entries, group, late), o...  4 us
    pallas_call x1, Pallas kernels, local(): pl.pallas_call(unsmooth_kernel, out_shape=jax.ShapeDtypeStruct((latent_di...  2.51 us
    unnamed x14, local copies, waits for them, and re-layouts  2.02 us
    pallas_call x1, Pallas kernels, local(): pl.pallas_call(prepare_kernel, out_shape=(jax.ShapeDtypeStruct(table.shap...  2.02 us
    pallas_call x1, Pallas kernels, local(): pl.pallas_call(functools.partial(merge_kernel, entries, late), out_shape=...  1.94 us
    pallas_call x1, Pallas kernels, local(): pl.pallas_call(smooth_kernel, out_shape=jax.ShapeDtypeStruct((latent_dim,...  1.68 us
  transfers between devices with their start and end apart: 22, of which 9 were waited for; matrix products, arithmetic and copies ran while one was open for 1% of the time, Pallas kernels for 12%

profile of v15, /device:TPU:0, one launch (start us, length us, event | category | flops | bytes accessed | tf_op | source)
XLA Modules:
  0.0 80.7 jit_solution(12721798813832287581)
XLA Ops:
  0.6 0.0 copy-start.5
  0.6 0.0 copy-start.6
  0.6 3.0 %collective-permute-start.3 = (bf16[512,256]{1,0:T(8,128)(2,1)}, bf16[512,256]{1,0:T(8,128)(2,1)S(1)}, u32[]{:S(2)}, u32[]{:S(2)}) collective-permute-start(bf16[512,256]{1,0:T(8,128)(2,1)} %refs_0_.5), channel_id=1, source_target_pairs={{0,2},{1,3},{2,0},{3,1},{4,6},{5,7},{6,4},{7,5},{8,10},{9,11},{10,... | collective-permute-start | bytes 786440 | tf_op jit(solution)/shard_map/ppermute | solution.py:331
  3.7 1.6 %collective-permute-start.2 = (bf16[512,256]{1,0:T(8,128)(2,1)}, bf16[512,256]{1,0:T(8,128)(2,1)S(1)}, u32[]{:S(2)}, u32[]{:S(2)}) collective-permute-start(bf16[512,256]{1,0:T(8,128)(2,1)} %refs_0_.5), channel_id=1, source_target_pairs={{0,4},{1,5},{2,6},{3,7},{4,8},{5,9},{6,10},{7,11},{8,12},{9,13},{1... | collective-permute-start | bytes 786440 | tf_op jit(solution)/shard_map/ppermute | solution.py:331
  5.3 2.2 %collective-permute-start.1 = (bf16[512,256]{1,0:T(8,128)(2,1)}, bf16[512,256]{1,0:T(8,128)(2,1)S(1)}, u32[]{:S(2)}, u32[]{:S(2)}) collective-permute-start(bf16[512,256]{1,0:T(8,128)(2,1)} %refs_0_.5), channel_id=1, source_target_pairs={{0,12},{1,13},{2,14},{3,15},{4,0},{5,1},{6,2},{7,3},{8,4},{9,5},{1... | collective-permute-start | bytes 786440 | tf_op jit(solution)/shard_map/ppermute | solution.py:331
  7.5 1.0 %slice_select_fusion = (f32[256,128]{1,0:T(8,128)S(1)}, f32[256,128]{1,0:T(8,128)S(1)}) fusion(f32[256,512]{1,0:T(8,128)} %mid.1, pred[]{:T(512)S(6)} %eq.5), kind=kLoop, calls=%fused_computation.1 | loop fusion | flops 65536 | bytes 524289 | tf_op jit(solution)/shard_map/jit(_where)/select_n | solution.py:349
  8.5 0.7 collective-permute-start.5
  9.2 1.7 %collective-permute-start.4 = (f32[256,128]{1,0:T(8,128)S(1)}, f32[256,128]{1,0:T(8,128)S(1)}, u32[]{:S(2)}, u32[]{:S(2)}) collective-permute-start(f32[256,128]{1,0:T(8,128)S(1)} %get-tuple-element.89), channel_id=1, source_target_pairs={{0,1},{1,0},{2,3},{3,2},{4,5},{5,4},{6,7},{7,6},{8,9},{9,8},{10,11... | collective-permute-start | bytes 393224 | tf_op jit(solution)/shard_map/ppermute | solution.py:331
  10.9 0.0 collective-permute-done.3.refs_4_
  10.9 4.1 %collective-permute-done.2.refs_1_ = bf16[512,256]{1,0:T(8,128)(2,1)S(1)} collective-permute-done((bf16[512,256]{1,0:T(8,128)(2,1)}, bf16[512,256]{1,0:T(8,128)(2,1)S(1)}, u32[]{:S(2)}, u32[]{:S(2)}) %collective-permute-start.2) | collective-permute-done | bytes 262176 | tf_op jit(solution)/shard_map/ppermute | solution.py:331
  15.0 0.0 collective-permute-start.6
  15.0 0.3 collective-permute-start.8
  15.3 1.0 %copy-done = f32[256,512]{1,0:T(8,128)S(1)} copy-done((f32[256,512]{1,0:T(8,128)S(1)}, f32[256,512]{1,0:T(8,128)}, u32[]{:S(2)}) %copy-start) | copy-done | bytes 524312
  16.3 0.9 %copy-done.2 = f32[256,256]{1,0:T(8,128)S(1)} copy-done((f32[256,256]{1,0:T(8,128)S(1)}, f32[256,256]{1,0:T(8,128)}, u32[]{:S(2)}) %copy-start.2) | copy-done | bytes 262168
  17.2 2.0 %prepare.1 = (bf16[3072,256]{1,0:T(8,128)(2,1)S(1)}, f32[256,512]{1,0:T(8,128)S(1)}, f32[256,256]{1,0:T(8,128)S(1)}, f32[256,256]{1,0:T(8,128)S(1)}, f32[256,256]{1,0:T(8,128)S(1)}) custom-call(bf16[3072,256]{1,0:T(8,128)(2,1)} %constant.22.clone.table, f32[256,256]{1,0:T(8,128)S(1)} %copy-done.2, f32[256,512]{1,0:T(8,128)S(1)} %copy-done), custom_call_target="tpu_custom_call" | custom-call | flops 335544320 | bytes 4194304 | tf_op jit(solution)/shard_map/prepare/pallas_call | solution.py:365
  19.3 0.0 collective-permute-done.1.refs_3_
  19.3 1.8 %collective-permute-start.9 = (bf16[512,256]{1,0:T(8,128)(2,1)S(1)}, bf16[512,256]{1,0:T(8,128)(2,1)S(1)}, u32[]{:S(2)}, u32[]{:S(2)}) collective-permute-start(bf16[512,256]{1,0:T(8,128)(2,1)S(1)} %collective-permute-done.1.refs_3_), channel_id=1, source_target_pairs={{0,2},{1,3},{2,0},{3,1},{4,6},{5,7},{6,4},{7,5},{8,10},{9,11},{10,... | collective-permute-start | bytes 786440 | tf_op jit(solution)/shard_map/ppermute | solution.py:331
  21.1 0.0 copy-done.5
  21.1 0.0 copy-start.1
  21.1 0.0 collective-permute-done.5.far_side
  21.1 0.1 collective-permute-start
  21.2 0.0 collective-permute-done.4.core_side
  21.2 1.7 %smooth.1.smoothed = bf16[256,512]{1,0:T(8,128)(2,1)S(1)} custom-call(f32[256,512]{1,0:T(8,128)S(1)} %get-tuple-element.52.mid, f32[256,128]{1,0:T(8,128)S(1)} %collective-permute-done.4.core_side, f32[256,128]{1,0:T(8,128)S(1)} %collective-permute-done.5.far_side, bf16[3072,256]{1,0:T(8,128)(2,1)S(1)} %get-tuple-element.53.tables, ...), custom_call_target="tpu_custom_call" | custom-call | flops 1006632960 | bytes 4194304 | tf_op jit(solution)/shard_map/smooth/pallas_call | solution.py:385
  22.9 0.0 collective-permute-done.asked
  22.9 3.3 %collective-permute-done.6.refs_2_ = bf16[512,256]{1,0:T(8,128)(2,1)S(1)} collective-permute-done((bf16[512,256]{1,0:T(8,128)(2,1)S(1)}, bf16[512,256]{1,0:T(8,128)(2,1)S(1)}, u32[]{:S(2)}, u32[]{:S(2)}) %collective-permute-start.6) | collective-permute-done | bytes 262176 | tf_op jit(solution)/shard_map/ppermute | solution.py:331
  26.2 0.0 collective-permute-start.7
  26.2 0.0 collective-permute-done.8.refs_5_
  26.2 1.3 %collective-permute-done.9.refs_6_.refs_7_ = bf16[512,256]{1,0:T(8,128)(2,1)S(1)} collective-permute-done((bf16[512,256]{1,0:T(8,128)(2,1)S(1)}, bf16[512,256]{1,0:T(8,128)(2,1)S(1)}, u32[]{:S(2)}, u32[]{:S(2)}) %collective-permute-start.9) | collective-permute-done | bytes 262176 | tf_op jit(solution)/shard_map/ppermute | solution.py:331
  27.5 0.0 copy-done.1
  27.5 0.8 pack.2
  28.3 0.0 copy-start.3
  28.3 0.0 copy-start.4
  28.3 0.1 collective-permute-start.10
  28.4 0.8 %pack.3 = bf16[1024,256]{1,0:T(8,128)(2,1)S(1)} custom-call(s32[2,8]{1,0:T(2,128)S(1)} %collective-permute-done.asked, bf16[512,256]{1,0:T(8,128)(2,1)S(1)} %copy-done.1, bf16[512,256]{1,0:T(8,128)(2,1)S(1)} %collective-permute-done.2.refs_1_, bf16[512,256]{1,0:T(8,128)(2,1)S(1)} %collective-permute-done.6.refs_2_, ...), custom_call_target="tpu_custom_call" | custom-call | bytes 1048576 | tf_op jit(solution)/shard_map/pack/pallas_call | solution.py:400
  29.3 0.5 collective-permute-start.11
  29.7 2.9 %collective-permute-done.7.refs_6_ = bf16[512,256]{1,0:T(8,128)(2,1)S(1)} collective-permute-done((bf16[512,256]{1,0:T(8,128)(2,1)S(1)}, bf16[512,256]{1,0:T(8,128)(2,1)S(1)}, u32[]{:S(2)}, u32[]{:S(2)}) %collective-permute-start.7) | collective-permute-done | bytes 262176 | tf_op jit(solution)/shard_map/ppermute | solution.py:331
  32.6 0.0 collective-permute-start.12
  32.6 1.5 %collective-permute-done.12.late_theirs = bf16[512,256]{1,0:T(8,128)(2,1)S(1)} collective-permute-done((bf16[512,256]{1,0:T(8,128)(2,1)S(1)}, bf16[512,256]{1,0:T(8,128)(2,1)S(1)}, u32[]{:S(2)}, u32[]{:S(2)}) %collective-permute-start.12) | collective-permute-done | bytes 262176 | tf_op jit(solution)/shard_map/ppermute | solution.py:331
  34.1 0.0 collective-permute-done.10.packed
  34.1 0.0 collective-permute-done.11.packed_rest
  34.2 4.0 %session.1 = (f32[256,512]{1,0:T(8,128)S(1)}, bf16[256,256]{1,0:T(8,128)(2,1)S(1)}, bf16[2304,256]{1,0:T(8,128)(2,1)S(1)}) custom-call(s32[2,8]{1,0:T(2,128)S(1)} %add_bitcast_fusion.ids, s32[2,4,8]{2,1,0:T(4,128)S(1)} %bitcast.5, bf16[256,512]{1,0:T(8,128)(2,1)S(1)} %smooth.1.smoothed, bf16[16,128,512]{2,1,0:T(8,128)(2,1)S(1)} %bitcast.4, ...), custom_call_target="tpu_custom_call" | custom-call | flops 1610612736 | bytes 8388608 | tf_op jit(solution)/shard_map/session/pallas_call | solution.py:418
  38.2 0.2 collective-permute-start.13
  38.4 2.7 %collective-permute-done.13.got = bf16[2304,256]{1,0:T(8,128)(2,1)S(1)} collective-permute-done((bf16[2304,256]{1,0:T(8,128)(2,1)S(1)}, bf16[2304,256]{1,0:T(8,128)(2,1)S(1)}, u32[]{:S(2)}, u32[]{:S(2)}) %collective-permute-start.13) | collective-permute-done | bytes 1179680 | tf_op jit(solution)/shard_map/ppermute | solution.py:331
  41.1 1.2 %merge_late.1 = bf16[512,256]{1,0:T(8,128)(2,1)S(1)} custom-call(s32[2,8]{1,0:T(2,128)S(1)} %add_bitcast_fusion.ids, s32[2,8]{1,0:T(2,128)S(1)} %collective-permute-done.asked, bf16[2304,256]{1,0:T(8,128)(2,1)S(1)} %get-tuple-element.66.own, bf16[2304,256]{1,0:T(8,128)(2,1)S(1)} %collective-permute-done.13.got), custom_call_target="tpu_custom_call" | custom-call | bytes 1048576 | tf_op jit(solution)/shard_map/merge_late/pallas_call | solution.py:449
  42.3 1.7 %collective-permute-start.15 = (bf16[512,256]{1,0:T(8,128)(2,1)S(1)}, bf16[512,256]{1,0:T(8,128)(2,1)S(1)}, u32[]{:S(2)}, u32[]{:S(2)}) collective-permute-start(bf16[512,256]{1,0:T(8,128)(2,1)S(1)} %merge_late.1), channel_id=1, source_target_pairs={{0,2},{1,3},{2,0},{3,1},{4,6},{5,7},{6,4},{7,5},{8,10},{9,11},{10,... | collective-permute-start | bytes 786440 | tf_op jit(solution)/shard_map/ppermute | solution.py:331
  44.0 0.7 collective-permute-start.14
  44.7 1.9 %merge.1 = (f32[512,256]{1,0:T(8,128)S(1)}, f32[512,256]{1,0:T(8,128)S(1)}, f32[512,256]{1,0:T(8,128)S(1)}, f32[512,256]{1,0:T(8,128)S(1)}, bf16[512,256]{1,0:T(...) custom-call(s32[2,8]{1,0:T(2,128)S(1)} %add_bitcast_fusion.ids, ...), custom_call_target="tpu_custom_call" | custom-call | bytes 5242880 | tf_op jit(solution)/shard_map/merge/pallas_call | solution.py:462
  46.6 0.0 collective-permute-done.14.far_side
  46.7 8.5 %collective-permute-start.20 = (bf16[512,256]{1,0:T(8,128)(2,1)S(1)}, bf16[512,256]{1,0:T(8,128)(2,1)S(1)}, u32[]{:S(2)}, u32[]{:S(2)}) collective-permute-start(bf16[512,256]{1,0:T(8,128)(2,1)S(1)} %get-tuple-element.87), channel_id=1, source_target_pairs={{0,2},{1,3},{2,0},{3,1},{4,6},{5,7},{6,4},{7,5},{8,10},{9,11},{10,... | collective-permute-start | bytes 786440 | tf_op jit(solution)/shard_map/ppermute | solution.py:331
  55.2 0.0 collective-permute-done.15.refs_0_
  55.2 0.0 collective-permute-start.17
  55.3 4.3 %collective-permute-start.18 = (bf16[512,256]{1,0:T(8,128)(2,1)S(1)}, bf16[512,256]{1,0:T(8,128)(2,1)S(1)}, u32[]{:S(2)}, u32[]{:S(2)}) collective-permute-start(bf16[512,256]{1,0:T(8,128)(2,1)S(1)} %hop.3), channel_id=1, source_target_pairs={{0,4},{1,5},{2,6},{3,7},{4,8},{5,9},{6,10},{7,11},{8,12},{9,13},{1... | collective-permute-start | bytes 786440 | tf_op jit(solution)/shard_map/ppermute | solution.py:331
  59.6 2.0 %collective-permute-start.16 = (bf16[512,256]{1,0:T(8,128)(2,1)S(1)}, bf16[512,256]{1,0:T(8,128)(2,1)S(1)}, u32[]{:S(2)}, u32[]{:S(2)}) collective-permute-start(bf16[512,256]{1,0:T(8,128)(2,1)S(1)} %get-tuple-element.81), channel_id=1, source_target_pairs={{0,2},{1,3},{2,0},{3,1},{4,6},{5,7},{6,4},{7,5},{8,10},{9,11},{10,... | collective-permute-start | bytes 786440 | tf_op jit(solution)/shard_map/ppermute | solution.py:331
  61.6 0.8 collective-permute-done.20.refs_0_
  62.4 2.2 %collective-permute-start.21 = (bf16[512,256]{1,0:T(8,128)(2,1)S(1)}, bf16[512,256]{1,0:T(8,128)(2,1)S(1)}, u32[]{:S(2)}, u32[]{:S(2)}) collective-permute-start(bf16[512,256]{1,0:T(8,128)(2,1)S(1)} %hop.5), channel_id=1, source_target_pairs={{0,12},{1,13},{2,14},{3,15},{4,0},{5,1},{6,2},{7,3},{8,4},{9,5},{1... | collective-permute-start | bytes 786440 | tf_op jit(solution)/shard_map/ppermute | solution.py:331
  64.7 3.4 %collective-permute-done.17.refs_0_ = bf16[512,256]{1,0:T(8,128)(2,1)S(1)} collective-permute-done((bf16[512,256]{1,0:T(8,128)(2,1)S(1)}, bf16[512,256]{1,0:T(8,128)(2,1)S(1)}, u32[]{:S(2)}, u32[]{:S(2)}) %collective-permute-start.17) | collective-permute-done | bytes 262176 | tf_op jit(solution)/shard_map/ppermute | solution.py:331
  68.0 0.0 collective-permute-done.18.refs_1_
  68.0 0.1 hop.4
  68.1 4.2 %collective-permute-start.19 = (bf16[512,256]{1,0:T(8,128)(2,1)S(1)}, bf16[512,256]{1,0:T(8,128)(2,1)S(1)}, u32[]{:S(2)}, u32[]{:S(2)}) collective-permute-start(bf16[512,256]{1,0:T(8,128)(2,1)S(1)} %hop.4), channel_id=1, source_target_pairs={{0,4},{1,5},{2,6},{3,7},{4,8},{5,9},{6,10},{7,11},{8,12},{9,13},{1... | collective-permute-start | bytes 786440 | tf_op jit(solution)/shard_map/ppermute | solution.py:331
  72.4 2.5 %unsmooth.1 = f32[256,512]{1,0:T(8,128)} custom-call(f32[256,512]{1,0:T(8,128)S(1)} %get-tuple-element.65.mid, bf16[2304,256]{1,0:T(8,128)(2,1)S(1)} %collective-permute-done.13.got, bf16[256,256]{1,0:T(8,128)(2,1)S(1)} %collective-permute-done.14.far_side, bf16[3072,256]{1,0:T(8,128)(2,1)S(1)} %get-tuple-element.53.tables, ...), custom_call_target="tpu_custom_call" | custom-call | flops 1006632960 | bytes 4194304 | tf_op jit(solution)/shard_map/unsmooth/pallas_call | solution.py:499
  74.9 0.0 collective-permute-done.16
  74.9 0.0 collective-permute-done.21
  74.9 4.9 %collective-permute-done.19 = bf16[512,256]{1,0:T(8,128)(2,1)S(1)} collective-permute-done((bf16[512,256]{1,0:T(8,128)(2,1)S(1)}, bf16[512,256]{1,0:T(8,128)(2,1)S(1)}, u32[]{:S(2)}, u32[]{:S(2)}) %collective-permute-start.19) | collective-permute-done | bytes 262176 | tf_op jit(solution)/shard_map/ppermute | solution.py:331
  79.8 0.9 %convert_add_fusion = f32[512,256]{1,0:T(8,128)} fusion(bf16[512,256]{1,0:T(8,128)(2,1)S(1)} %collective-permute-done.21, bf16[512,256]{1,0:T(8,128)(2,1)S(1)} %collective-permute-done.19, f32[512,256]{1,0:T(8,128)S(1)} %get-tuple-element.77, bf16[512,256]{1,0:T(8,128)(2,1)S(1)} %collective-permute-done.16), kind=kLoop, calls=%fused_computation | loop fusion | flops 786432 | bytes 1835008 | tf_op jit(solution)/shard_map/add | solution.py:497
  (8 shorter events, 0.1 us)
Async XLA Ops:
  0.6 20.5 %copy-start.5 = (s32[1,2,8]{2,1,0:T(2,128)S(1)}, s32[1,2,8]{2,1,0:T(2,128)}, u32[]{:S(2)}) copy-start(s32[1,2,8]{2,1,0:T(2,128)} %param.13) | copy-start | bytes 196
  0.6 20.4 %copy-start.6 = (s32[1,2,8]{2,1,0:T(2,128)S(1)}, s32[1,2,8]{2,1,0:T(2,128)}, u32[]{:S(2)}) copy-start(s32[1,2,8]{2,1,0:T(2,128)} %param.12) | copy-start | bytes 196
  0.6 10.2 %collective-permute-start.3 = (bf16[512,256]{1,0:T(8,128)(2,1)}, bf16[512,256]{1,0:T(8,128)(2,1)S(1)}, u32[]{:S(2)}, u32[]{:S(2)}) collective-permute-start(bf16[512,256]{1,0:T(8,128)(2,1)} %refs_0_.5), channel_id=1, source_target_pairs={{0,2},{1,3},{2,0},{3,1},{4,6},{5,7},{6,4},{7,5},{8,10},{9,11},{10,... | collective-permute-start | bytes 786440 | tf_op jit(solution)/shard_map/ppermute | solution.py:331
  3.7 11.3 %collective-permute-start.2 = (bf16[512,256]{1,0:T(8,128)(2,1)}, bf16[512,256]{1,0:T(8,128)(2,1)S(1)}, u32[]{:S(2)}, u32[]{:S(2)}) collective-permute-start(bf16[512,256]{1,0:T(8,128)(2,1)} %refs_0_.5), channel_id=1, source_target_pairs={{0,4},{1,5},{2,6},{3,7},{4,8},{5,9},{6,10},{7,11},{8,12},{9,13},{1... | collective-permute-start | bytes 786440 | tf_op jit(solution)/shard_map/ppermute | solution.py:331
  5.3 14.0 %collective-permute-start.1 = (bf16[512,256]{1,0:T(8,128)(2,1)}, bf16[512,256]{1,0:T(8,128)(2,1)S(1)}, u32[]{:S(2)}, u32[]{:S(2)}) collective-permute-start(bf16[512,256]{1,0:T(8,128)(2,1)} %refs_0_.5), channel_id=1, source_target_pairs={{0,12},{1,13},{2,14},{3,15},{4,0},{5,1},{6,2},{7,3},{8,4},{9,5},{1... | collective-permute-start | bytes 786440 | tf_op jit(solution)/shard_map/ppermute | solution.py:331
  8.5 12.6 %collective-permute-start.5 = (f32[256,128]{1,0:T(8,128)S(1)}, f32[256,128]{1,0:T(8,128)S(1)}, u32[]{:S(2)}, u32[]{:S(2)}) collective-permute-start(f32[256,128]{1,0:T(8,128)S(1)} %get-tuple-element.88), channel_id=1, source_target_pairs={{1,2},{3,4},{5,6},{7,8},{9,10},{11,12},{13,14},{2,1},{4,3},{6,5},{... | collective-permute-start | bytes 393224 | tf_op jit(solution)/shard_map/ppermute | solution.py:331
  9.2 12.0 %collective-permute-start.4 = (f32[256,128]{1,0:T(8,128)S(1)}, f32[256,128]{1,0:T(8,128)S(1)}, u32[]{:S(2)}, u32[]{:S(2)}) collective-permute-start(f32[256,128]{1,0:T(8,128)S(1)} %get-tuple-element.89), channel_id=1, source_target_pairs={{0,1},{1,0},{2,3},{3,2},{4,5},{5,4},{6,7},{7,6},{8,9},{9,8},{10,11... | collective-permute-start | bytes 393224 | tf_op jit(solution)/shard_map/ppermute | solution.py:331
  15.0 11.3 %collective-permute-start.6 = (bf16[512,256]{1,0:T(8,128)(2,1)S(1)}, bf16[512,256]{1,0:T(8,128)(2,1)S(1)}, u32[]{:S(2)}, u32[]{:S(2)}) collective-permute-start(bf16[512,256]{1,0:T(8,128)(2,1)S(1)} %collective-permute-done.2.refs_1_), channel_id=1, source_target_pairs={{0,4},{1,5},{2,6},{3,7},{4,8},{5,9},{6,10},{7,11},{8,12},{9,13},{1... | collective-permute-start | bytes 786440 | tf_op jit(solution)/shard_map/ppermute | solution.py:331
  15.0 11.3 %collective-permute-start.8 = (bf16[512,256]{1,0:T(8,128)(2,1)S(1)}, bf16[512,256]{1,0:T(8,128)(2,1)S(1)}, u32[]{:S(2)}, u32[]{:S(2)}) collective-permute-start(bf16[512,256]{1,0:T(8,128)(2,1)S(1)} %collective-permute-done.2.refs_1_), channel_id=1, source_target_pairs={{0,2},{1,3},{2,0},{3,1},{4,6},{5,7},{6,4},{7,5},{8,10},{9,11},{10,... | collective-permute-start | bytes 786440 | tf_op jit(solution)/shard_map/ppermute | solution.py:331
  15.3 1.0 %copy-start = (f32[256,512]{1,0:T(8,128)S(1)}, f32[256,512]{1,0:T(8,128)}, u32[]{:S(2)}) copy-start(f32[256,512]{1,0:T(8,128)} %mid.1) | copy-start | bytes 1572868
  16.3 0.9 %copy-start.2 = (f32[256,256]{1,0:T(8,128)S(1)}, f32[256,256]{1,0:T(8,128)}, u32[]{:S(2)}) copy-start(f32[256,256]{1,0:T(8,128)} %taps) | copy-start | bytes 786436
  19.3 8.2 %collective-permute-start.9 = (bf16[512,256]{1,0:T(8,128)(2,1)S(1)}, bf16[512,256]{1,0:T(8,128)(2,1)S(1)}, u32[]{:S(2)}, u32[]{:S(2)}) collective-permute-start(bf16[512,256]{1,0:T(8,128)(2,1)S(1)} %collective-permute-done.1.refs_3_), channel_id=1, source_target_pairs={{0,2},{1,3},{2,0},{3,1},{4,6},{5,7},{6,4},{7,5},{8,10},{9,11},{10,... | collective-permute-start | bytes 786440 | tf_op jit(solution)/shard_map/ppermute | solution.py:331
  21.1 6.4 %copy-start.1 = (bf16[512,256]{1,0:T(8,128)(2,1)S(1)}, bf16[512,256]{1,0:T(8,128)(2,1)}, u32[]{:S(2)}) copy-start(bf16[512,256]{1,0:T(8,128)(2,1)} %refs_0_.5) | copy-start | bytes 786436
  21.1 1.8 %collective-permute-start = (s32[2,8]{1,0:T(2,128)S(1)}, s32[2,8]{1,0:T(2,128)S(1)}, u32[]{:S(2)}, u32[]{:S(2)}) collective-permute-start(s32[2,8]{1,0:T(2,128)S(1)} %add_bitcast_fusion.ids), channel_id=1, source_target_pairs={{0,1},{1,0},{2,3},{3,2},{4,5},{5,4},{6,7},{7,6},{8,9},{9,8},{10,11... | collective-permute-start | bytes 200 | tf_op jit(solution)/shard_map/ppermute | solution.py:331
  26.2 6.4 %collective-permute-start.7 = (bf16[512,256]{1,0:T(8,128)(2,1)S(1)}, bf16[512,256]{1,0:T(8,128)(2,1)S(1)}, u32[]{:S(2)}, u32[]{:S(2)}) collective-permute-start(bf16[512,256]{1,0:T(8,128)(2,1)S(1)} %collective-permute-done.6.refs_2_), channel_id=1, source_target_pairs={{0,2},{1,3},{2,0},{3,1},{4,6},{5,7},{6,4},{7,5},{8,10},{9,11},{10,... | collective-permute-start | bytes 786440 | tf_op jit(solution)/shard_map/ppermute | solution.py:331
  28.3 5.9 %copy-start.3 = (bf16[2,8,128,512]{3,2,1,0:T(8,128)(2,1)S(1)}, bf16[2,8,128,512]{3,2,1,0:T(8,128)(2,1)}, u32[]{:S(2)}) copy-start(bf16[2,8,128,512]{3,2,1,0:T(8,128)(2,1)} %param.11) | copy-start | bytes 6291460
  28.3 5.8 %copy-start.4 = (s32[2,8,4]{1,2,0:T(4,128)S(1)}, s32[2,8,4]{1,2,0:T(4,128)}, u32[]{:S(2)}) copy-start(s32[2,8,4]{1,2,0:T(4,128)} %param.14) | copy-start | bytes 772
  28.3 5.8 %collective-permute-start.10 = (bf16[1024,256]{1,0:T(8,128)(2,1)S(1)}, bf16[1024,256]{1,0:T(8,128)(2,1)S(1)}, u32[]{:S(2)}, u32[]{:S(2)}) collective-permute-start(bf16[1024,256]{1,0:T(8,128)(2,1)S(1)} %pack.2), channel_id=1, source_target_pairs={{0,1},{1,0},{2,3},{3,2},{4,5},{5,4},{6,7},{7,6},{8,9},{9,8},{10,11... | collective-permute-start | bytes 1572872 | tf_op jit(solution)/shard_map/ppermute | solution.py:331
  29.3 4.9 %collective-permute-start.11 = (bf16[1024,256]{1,0:T(8,128)(2,1)S(1)}, bf16[1024,256]{1,0:T(8,128)(2,1)S(1)}, u32[]{:S(2)}, u32[]{:S(2)}) collective-permute-start(bf16[1024,256]{1,0:T(8,128)(2,1)S(1)} %pack.3), channel_id=1, source_target_pairs={{0,1},{1,0},{2,3},{3,2},{4,5},{5,4},{6,7},{7,6},{8,9},{9,8},{10,11... | collective-permute-start | bytes 1572872 | tf_op jit(solution)/shard_map/ppermute | solution.py:331
  32.6 1.5 %collective-permute-start.12 = (bf16[512,256]{1,0:T(8,128)(2,1)S(1)}, bf16[512,256]{1,0:T(8,128)(2,1)S(1)}, u32[]{:S(2)}, u32[]{:S(2)}) collective-permute-start(bf16[512,256]{1,0:T(8,128)(2,1)S(1)} %collective-permute-done.7.refs_6_), channel_id=1, source_target_pairs={{0,1},{1,0},{2,3},{3,2},{4,5},{5,4},{6,7},{7,6},{8,9},{9,8},{10,11... | collective-permute-start | bytes 786440 | tf_op jit(solution)/shard_map/ppermute | solution.py:331
  38.2 2.9 %collective-permute-start.13 = (bf16[2304,256]{1,0:T(8,128)(2,1)S(1)}, bf16[2304,256]{1,0:T(8,128)(2,1)S(1)}, u32[]{:S(2)}, u32[]{:S(2)}) collective-permute-start(bf16[2304,256]{1,0:T(8,128)(2,1)S(1)} %get-tuple-element.66.own), channel_id=1, source_target_pairs={{0,1},{1,0},{2,3},{3,2},{4,5},{5,4},{6,7},{7,6},{8,9},{9,8},{10,11... | collective-permute-start | bytes 3538952 | tf_op jit(solution)/shard_map/ppermute | solution.py:331
  42.3 12.9 %collective-permute-start.15 = (bf16[512,256]{1,0:T(8,128)(2,1)S(1)}, bf16[512,256]{1,0:T(8,128)(2,1)S(1)}, u32[]{:S(2)}, u32[]{:S(2)}) collective-permute-start(bf16[512,256]{1,0:T(8,128)(2,1)S(1)} %merge_late.1), channel_id=1, source_target_pairs={{0,2},{1,3},{2,0},{3,1},{4,6},{5,7},{6,4},{7,5},{8,10},{9,11},{10,... | collective-permute-start | bytes 786440 | tf_op jit(solution)/shard_map/ppermute | solution.py:331
  44.0 2.6 %collective-permute-start.14 = (bf16[256,256]{1,0:T(8,128)(2,1)S(1)}, bf16[256,256]{1,0:T(8,128)(2,1)S(1)}, u32[]{:S(2)}, u32[]{:S(2)}) collective-permute-start(bf16[256,256]{1,0:T(8,128)(2,1)S(1)} %get-tuple-element.67), channel_id=1, source_target_pairs={{1,2},{3,4},{5,6},{7,8},{9,10},{11,12},{13,14},{2,1},{4,3},{6,5},{... | collective-permute-start | bytes 393224 | tf_op jit(solution)/shard_map/ppermute | solution.py:331
  46.7 15.7 %collective-permute-start.20 = (bf16[512,256]{1,0:T(8,128)(2,1)S(1)}, bf16[512,256]{1,0:T(8,128)(2,1)S(1)}, u32[]{:S(2)}, u32[]{:S(2)}) collective-permute-start(bf16[512,256]{1,0:T(8,128)(2,1)S(1)} %get-tuple-element.87), channel_id=1, source_target_pairs={{0,2},{1,3},{2,0},{3,1},{4,6},{5,7},{6,4},{7,5},{8,10},{9,11},{10,... | collective-permute-start | bytes 786440 | tf_op jit(solution)/shard_map/ppermute | solution.py:331
  55.2 12.8 %collective-permute-start.17 = (bf16[512,256]{1,0:T(8,128)(2,1)S(1)}, bf16[512,256]{1,0:T(8,128)(2,1)S(1)}, u32[]{:S(2)}, u32[]{:S(2)}) collective-permute-start(bf16[512,256]{1,0:T(8,128)(2,1)S(1)} %get-tuple-element.83), channel_id=1, source_target_pairs={{0,2},{1,3},{2,0},{3,1},{4,6},{5,7},{6,4},{7,5},{8,10},{9,11},{10,... | collective-permute-start | bytes 786440 | tf_op jit(solution)/shard_map/ppermute | solution.py:331
  55.3 12.7 %collective-permute-start.18 = (bf16[512,256]{1,0:T(8,128)(2,1)S(1)}, bf16[512,256]{1,0:T(8,128)(2,1)S(1)}, u32[]{:S(2)}, u32[]{:S(2)}) collective-permute-start(bf16[512,256]{1,0:T(8,128)(2,1)S(1)} %hop.3), channel_id=1, source_target_pairs={{0,4},{1,5},{2,6},{3,7},{4,8},{5,9},{6,10},{7,11},{8,12},{9,13},{1... | collective-permute-start | bytes 786440 | tf_op jit(solution)/shard_map/ppermute | solution.py:331
  59.6 15.3 %collective-permute-start.16 = (bf16[512,256]{1,0:T(8,128)(2,1)S(1)}, bf16[512,256]{1,0:T(8,128)(2,1)S(1)}, u32[]{:S(2)}, u32[]{:S(2)}) collective-permute-start(bf16[512,256]{1,0:T(8,128)(2,1)S(1)} %get-tuple-element.81), channel_id=1, source_target_pairs={{0,2},{1,3},{2,0},{3,1},{4,6},{5,7},{6,4},{7,5},{8,10},{9,11},{10,... | collective-permute-start | bytes 786440 | tf_op jit(solution)/shard_map/ppermute | solution.py:331
  62.4 12.4 %collective-permute-start.21 = (bf16[512,256]{1,0:T(8,128)(2,1)S(1)}, bf16[512,256]{1,0:T(8,128)(2,1)S(1)}, u32[]{:S(2)}, u32[]{:S(2)}) collective-permute-start(bf16[512,256]{1,0:T(8,128)(2,1)S(1)} %hop.5), channel_id=1, source_target_pairs={{0,12},{1,13},{2,14},{3,15},{4,0},{5,1},{6,2},{7,3},{8,4},{9,5},{1... | collective-permute-start | bytes 786440 | tf_op jit(solution)/shard_map/ppermute | solution.py:331
  68.1 11.7 %collective-permute-start.19 = (bf16[512,256]{1,0:T(8,128)(2,1)S(1)}, bf16[512,256]{1,0:T(8,128)(2,1)S(1)}, u32[]{:S(2)}, u32[]{:S(2)}) collective-permute-start(bf16[512,256]{1,0:T(8,128)(2,1)S(1)} %hop.4), channel_id=1, source_target_pairs={{0,4},{1,5},{2,6},{3,7},{4,8},{5,9},{6,10},{7,11},{8,12},{9,13},{1... | collective-permute-start | bytes 786440 | tf_op jit(solution)/shard_map/ppermute | solution.py:331

commit v16 on v11

--- a/solution.py
+++ b/solution.py
@@ -485,7 +485,8 @@
     rise = hop(merged[half], back)
     rise, far_side = lax.optimization_barrier((rise, far_side))
     far_side = permute(far_side, odd_even)
-    far_side, own = lax.optimization_barrier((far_side, crossed[0]))
+    other[1], far_side = lax.optimization_barrier((other[1], far_side))
+    _, own = lax.optimization_barrier((other[half + 1], crossed[0]))
     other[0] = flip(own, 2)
     rise = rotate(rise, 1)
     for r in range(half - 1, 0, -1):

time: 77.1 us -> 76.5 us (level)
  the two profiles are of different devices: /device:TPU:0 before, /device:TPU:1 now
where the time goes in v16:
time: 76.5 us; the launch traced here: 76.2 us
  starting transfers between devices  40.3 us (53%)
  waiting for transfers between devices  16.1 us (21%)
  Pallas kernels  15 us (20%)
  local copies, waits for them, and re-layouts  2.02 us (3%)
  other arithmetic  1.92 us (3%)
  between operations  0.84 us (1%)
    ppermute x22, starting transfers between devices, permute(): return lax.ppermute(x, 'tm', pairs)  40.3 us
    ppermute x22, waiting for transfers between devices, permute(): return lax.ppermute(x, 'tm', pairs)  16.1 us
    pallas_call x1, Pallas kernels, local(): pl.pallas_call(functools.partial(session_kernel, entries, group, late), o...  3.99 us
    pallas_call x1, Pallas kernels, local(): pl.pallas_call(unsmooth_kernel, out_shape=jax.ShapeDtypeStruct((latent_di...  2.51 us
    unnamed x14, local copies, waits for them, and re-layouts  2.02 us
    pallas_call x1, Pallas kernels, local(): pl.pallas_call(prepare_kernel, out_shape=(jax.ShapeDtypeStruct(table.shap...  2.02 us
    pallas_call x1, Pallas kernels, local(): pl.pallas_call(functools.partial(merge_kernel, entries, late), out_shape=...  1.87 us
    pallas_call x1, Pallas kernels, local(): pl.pallas_call(smooth_kernel, out_shape=jax.ShapeDtypeStruct((latent_dim,...  1.69 us
  transfers between devices with their start and end apart: 22, of which 11 were waited for; matrix products, arithmetic and copies ran while one was open for 1% of the time, Pallas kernels for 13%

profile of v16, /device:TPU:1, one launch (start us, length us, event | category | flops | bytes accessed | tf_op | source)
XLA Modules:
  0.0 76.2 jit_solution(14062136439863876846)
XLA Ops:
  0.6 0.0 copy-start.5
  0.6 0.0 copy-start.6
  0.6 2.1 %collective-permute-start.3 = (bf16[512,256]{1,0:T(8,128)(2,1)}, bf16[512,256]{1,0:T(8,128)(2,1)S(1)}, u32[]{:S(2)}, u32[]{:S(2)}) collective-permute-start(bf16[512,256]{1,0:T(8,128)(2,1)} %refs_0_.5), channel_id=1, source_target_pairs={{0,2},{1,3},{2,0},{3,1},{4,6},{5,7},{6,4},{7,5},{8,10},{9,11},{10,... | collective-permute-start | bytes 786440 | tf_op jit(solution)/shard_map/ppermute | solution.py:331
  2.8 1.3 %collective-permute-start.2 = (bf16[512,256]{1,0:T(8,128)(2,1)}, bf16[512,256]{1,0:T(8,128)(2,1)S(1)}, u32[]{:S(2)}, u32[]{:S(2)}) collective-permute-start(bf16[512,256]{1,0:T(8,128)(2,1)} %refs_0_.5), channel_id=1, source_target_pairs={{0,4},{1,5},{2,6},{3,7},{4,8},{5,9},{6,10},{7,11},{8,12},{9,13},{1... | collective-permute-start | bytes 786440 | tf_op jit(solution)/shard_map/ppermute | solution.py:331
  4.1 2.0 %collective-permute-start.1 = (bf16[512,256]{1,0:T(8,128)(2,1)}, bf16[512,256]{1,0:T(8,128)(2,1)S(1)}, u32[]{:S(2)}, u32[]{:S(2)}) collective-permute-start(bf16[512,256]{1,0:T(8,128)(2,1)} %refs_0_.5), channel_id=1, source_target_pairs={{0,12},{1,13},{2,14},{3,15},{4,0},{5,1},{6,2},{7,3},{8,4},{9,5},{1... | collective-permute-start | bytes 786440 | tf_op jit(solution)/shard_map/ppermute | solution.py:331
  6.1 1.0 %slice_select_fusion = (f32[256,128]{1,0:T(8,128)S(1)}, f32[256,128]{1,0:T(8,128)S(1)}) fusion(f32[256,512]{1,0:T(8,128)} %mid.1, pred[]{:T(512)S(6)} %eq.5), kind=kLoop, calls=%fused_computation.1 | loop fusion | flops 65536 | bytes 524289 | tf_op jit(solution)/shard_map/jit(_where)/select_n | solution.py:349
  7.1 3.3 %collective-permute-start.5 = (f32[256,128]{1,0:T(8,128)S(1)}, f32[256,128]{1,0:T(8,128)S(1)}, u32[]{:S(2)}, u32[]{:S(2)}) collective-permute-start(f32[256,128]{1,0:T(8,128)S(1)} %get-tuple-element.76), channel_id=1, source_target_pairs={{1,2},{3,4},{5,6},{7,8},{9,10},{11,12},{13,14},{2,1},{4,3},{6,5},{... | collective-permute-start | bytes 393224 | tf_op jit(solution)/shard_map/ppermute | solution.py:331
  10.4 0.1 collective-permute-start.4
  10.4 0.0 collective-permute-done.3.refs_4_
  10.5 1.4 %collective-permute-done.2.refs_1_ = bf16[512,256]{1,0:T(8,128)(2,1)S(1)} collective-permute-done((bf16[512,256]{1,0:T(8,128)(2,1)}, bf16[512,256]{1,0:T(8,128)(2,1)S(1)}, u32[]{:S(2)}, u32[]{:S(2)}) %collective-permute-start.2) | collective-permute-done | bytes 262176 | tf_op jit(solution)/shard_map/ppermute | solution.py:331
  11.9 0.0 collective-permute-start.6
  11.9 0.6 collective-permute-start.8
  12.5 1.0 %copy-done = f32[256,512]{1,0:T(8,128)S(1)} copy-done((f32[256,512]{1,0:T(8,128)S(1)}, f32[256,512]{1,0:T(8,128)}, u32[]{:S(2)}) %copy-start) | copy-done | bytes 524312
  13.5 0.9 %copy-done.2 = f32[256,256]{1,0:T(8,128)S(1)} copy-done((f32[256,256]{1,0:T(8,128)S(1)}, f32[256,256]{1,0:T(8,128)}, u32[]{:S(2)}) %copy-start.2) | copy-done | bytes 262168
  14.5 2.0 %prepare.1 = (bf16[3072,256]{1,0:T(8,128)(2,1)S(1)}, f32[256,512]{1,0:T(8,128)S(1)}, f32[256,256]{1,0:T(8,128)S(1)}, f32[256,256]{1,0:T(8,128)S(1)}, f32[256,256]{1,0:T(8,128)S(1)}) custom-call(bf16[3072,256]{1,0:T(8,128)(2,1)} %constant.22.clone.table, f32[256,256]{1,0:T(8,128)S(1)} %copy-done.2, f32[256,512]{1,0:T(8,128)S(1)} %copy-done), custom_call_target="tpu_custom_call" | custom-call | flops 335544320 | bytes 4194304 | tf_op jit(solution)/shard_map/prepare/pallas_call | solution.py:365
  16.5 1.0 %collective-permute-done.1.refs_3_ = bf16[512,256]{1,0:T(8,128)(2,1)S(1)} collective-permute-done((bf16[512,256]{1,0:T(8,128)(2,1)}, bf16[512,256]{1,0:T(8,128)(2,1)S(1)}, u32[]{:S(2)}, u32[]{:S(2)}) %collective-permute-start.1) | collective-permute-done | bytes 262176 | tf_op jit(solution)/shard_map/ppermute | solution.py:331
  17.5 0.2 collective-permute-start.9
  17.7 0.0 copy-done.5
  17.7 0.0 copy-start.1
  17.7 0.0 collective-permute-done.5.far_side
  17.7 3.5 %collective-permute-start = (s32[2,8]{1,0:T(2,128)S(1)}, s32[2,8]{1,0:T(2,128)S(1)}, u32[]{:S(2)}, u32[]{:S(2)}) collective-permute-start(s32[2,8]{1,0:T(2,128)S(1)} %add_bitcast_fusion.ids), channel_id=1, source_target_pairs={{0,1},{1,0},{2,3},{3,2},{4,5},{5,4},{6,7},{7,6},{8,9},{9,8},{10,11... | collective-permute-start | bytes 200 | tf_op jit(solution)/shard_map/ppermute | solution.py:331
  21.2 0.0 collective-permute-done.4.core_side
  21.2 1.7 %smooth.1.smoothed = bf16[256,512]{1,0:T(8,128)(2,1)S(1)} custom-call(f32[256,512]{1,0:T(8,128)S(1)} %get-tuple-element.46.mid, f32[256,128]{1,0:T(8,128)S(1)} %collective-permute-done.4.core_side, f32[256,128]{1,0:T(8,128)S(1)} %collective-permute-done.5.far_side, bf16[3072,256]{1,0:T(8,128)(2,1)S(1)} %get-tuple-element.47.tables, ...), custom_call_target="tpu_custom_call" | custom-call | flops 1006632960 | bytes 4194304 | tf_op jit(solution)/shard_map/smooth/pallas_call | solution.py:385
  22.9 0.0 collective-permute-done.asked
  22.9 0.2 collective-permute-done.6.refs_2_
  23.1 1.6 %collective-permute-start.7 = (bf16[512,256]{1,0:T(8,128)(2,1)S(1)}, bf16[512,256]{1,0:T(8,128)(2,1)S(1)}, u32[]{:S(2)}, u32[]{:S(2)}) collective-permute-start(bf16[512,256]{1,0:T(8,128)(2,1)S(1)} %collective-permute-done.6.refs_2_), channel_id=1, source_target_pairs={{0,2},{1,3},{2,0},{3,1},{4,6},{5,7},{6,4},{7,5},{8,10},{9,11},{10,... | collective-permute-start | bytes 786440 | tf_op jit(solution)/shard_map/ppermute | solution.py:331
  24.7 0.0 collective-permute-done.8.refs_5_
  24.7 0.2 collective-permute-done.9.refs_6_.refs_7_
  25.0 0.0 copy-done.1
  25.0 0.7 pack.2
  25.7 0.0 copy-start.3
  25.7 0.0 copy-start.4
  25.7 2.8 %collective-permute-start.10 = (bf16[1024,256]{1,0:T(8,128)(2,1)S(1)}, bf16[1024,256]{1,0:T(8,128)(2,1)S(1)}, u32[]{:S(2)}, u32[]{:S(2)}) collective-permute-start(bf16[1024,256]{1,0:T(8,128)(2,1)S(1)} %pack.2), channel_id=1, source_target_pairs={{0,1},{1,0},{2,3},{3,2},{4,5},{5,4},{6,7},{7,6},{8,9},{9,8},{10,11... | collective-permute-start | bytes 1572872 | tf_op jit(solution)/shard_map/ppermute | solution.py:331
  28.5 0.8 %pack.3 = bf16[1024,256]{1,0:T(8,128)(2,1)S(1)} custom-call(s32[2,8]{1,0:T(2,128)S(1)} %collective-permute-done.asked, bf16[512,256]{1,0:T(8,128)(2,1)S(1)} %copy-done.1, bf16[512,256]{1,0:T(8,128)(2,1)S(1)} %collective-permute-done.2.refs_1_, bf16[512,256]{1,0:T(8,128)(2,1)S(1)} %collective-permute-done.6.refs_2_, ...), custom_call_target="tpu_custom_call" | custom-call | bytes 1048576 | tf_op jit(solution)/shard_map/pack/pallas_call | solution.py:400
  29.4 0.1 collective-permute-start.11
  29.4 0.8 %collective-permute-done.7.refs_6_ = bf16[512,256]{1,0:T(8,128)(2,1)S(1)} collective-permute-done((bf16[512,256]{1,0:T(8,128)(2,1)S(1)}, bf16[512,256]{1,0:T(8,128)(2,1)S(1)}, u32[]{:S(2)}, u32[]{:S(2)}) %collective-permute-start.7) | collective-permute-done | bytes 262176 | tf_op jit(solution)/shard_map/ppermute | solution.py:331
  30.2 2.4 %collective-permute-start.12 = (bf16[512,256]{1,0:T(8,128)(2,1)S(1)}, bf16[512,256]{1,0:T(8,128)(2,1)S(1)}, u32[]{:S(2)}, u32[]{:S(2)}) collective-permute-start(bf16[512,256]{1,0:T(8,128)(2,1)S(1)} %collective-permute-done.7.refs_6_), channel_id=1, source_target_pairs={{0,1},{1,0},{2,3},{3,2},{4,5},{5,4},{6,7},{7,6},{8,9},{9,8},{10,11... | collective-permute-start | bytes 786440 | tf_op jit(solution)/shard_map/ppermute | solution.py:331
  32.7 1.2 %collective-permute-done.12.late_theirs = bf16[512,256]{1,0:T(8,128)(2,1)S(1)} collective-permute-done((bf16[512,256]{1,0:T(8,128)(2,1)S(1)}, bf16[512,256]{1,0:T(8,128)(2,1)S(1)}, u32[]{:S(2)}, u32[]{:S(2)}) %collective-permute-start.12) | collective-permute-done | bytes 262176 | tf_op jit(solution)/shard_map/ppermute | solution.py:331
  33.8 0.0 collective-permute-done.10.packed
  33.8 0.0 collective-permute-done.11.packed_rest
  33.8 4.0 %session.1 = (f32[256,512]{1,0:T(8,128)S(1)}, bf16[256,256]{1,0:T(8,128)(2,1)S(1)}, bf16[2304,256]{1,0:T(8,128)(2,1)S(1)}) custom-call(s32[2,8]{1,0:T(2,128)S(1)} %add_bitcast_fusion.ids, s32[2,4,8]{2,1,0:T(4,128)S(1)} %bitcast.5, bf16[256,512]{1,0:T(8,128)(2,1)S(1)} %smooth.1.smoothed, bf16[16,128,512]{2,1,0:T(8,128)(2,1)S(1)} %bitcast.4, ...), custom_call_target="tpu_custom_call" | custom-call | flops 1610612736 | bytes 8388608 | tf_op jit(solution)/shard_map/session/pallas_call | solution.py:418
  37.8 0.5 collective-permute-start.13
  38.3 2.5 %collective-permute-done.13.got = bf16[2304,256]{1,0:T(8,128)(2,1)S(1)} collective-permute-done((bf16[2304,256]{1,0:T(8,128)(2,1)S(1)}, bf16[2304,256]{1,0:T(8,128)(2,1)S(1)}, u32[]{:S(2)}, u32[]{:S(2)}) %collective-permute-start.13) | collective-permute-done | bytes 1179680 | tf_op jit(solution)/shard_map/ppermute | solution.py:331
  40.8 1.2 %merge_late.1 = bf16[512,256]{1,0:T(8,128)(2,1)S(1)} custom-call(s32[2,8]{1,0:T(2,128)S(1)} %add_bitcast_fusion.ids, s32[2,8]{1,0:T(2,128)S(1)} %collective-permute-done.asked, bf16[2304,256]{1,0:T(8,128)(2,1)S(1)} %get-tuple-element.60.own, bf16[2304,256]{1,0:T(8,128)(2,1)S(1)} %collective-permute-done.13.got), custom_call_target="tpu_custom_call" | custom-call | bytes 1048576 | tf_op jit(solution)/shard_map/merge_late/pallas_call | solution.py:448
  42.0 1.4 %collective-permute-start.15 = (bf16[512,256]{1,0:T(8,128)(2,1)S(1)}, bf16[512,256]{1,0:T(8,128)(2,1)S(1)}, u32[]{:S(2)}, u32[]{:S(2)}) collective-permute-start(bf16[512,256]{1,0:T(8,128)(2,1)S(1)} %merge_late.1), channel_id=1, source_target_pairs={{0,2},{1,3},{2,0},{3,1},{4,6},{5,7},{6,4},{7,5},{8,10},{9,11},{10,... | collective-permute-start | bytes 786440 | tf_op jit(solution)/shard_map/ppermute | solution.py:331
  43.4 1.9 %merge.1 = (f32[512,256]{1,0:T(8,128)S(1)}, f32[512,256]{1,0:T(8,128)S(1)}, f32[512,256]{1,0:T(8,128)S(1)}, f32[512,256]{1,0:T(8,128)S(1)}, bf16[512,256]{1,0:T(...) custom-call(s32[2,8]{1,0:T(2,128)S(1)} %add_bitcast_fusion.ids, ...), custom_call_target="tpu_custom_call" | custom-call | bytes 5242880 | tf_op jit(solution)/shard_map/merge/pallas_call | solution.py:461
  45.3 0.2 collective-permute-start.17
  45.5 1.3 %collective-permute-start.14 = (bf16[512,256]{1,0:T(8,128)(2,1)S(1)}, bf16[512,256]{1,0:T(8,128)(2,1)S(1)}, u32[]{:S(2)}, u32[]{:S(2)}) collective-permute-start(bf16[512,256]{1,0:T(8,128)(2,1)S(1)} %get-tuple-element.62), channel_id=1, source_target_pairs={{0,2},{1,3},{2,0},{3,1},{4,6},{5,7},{6,4},{7,5},{8,10},{9,11},{10,... | collective-permute-start | bytes 786440 | tf_op jit(solution)/shard_map/ppermute | solution.py:331
  46.8 2.7 %collective-permute-done.15.refs_0_ = bf16[512,256]{1,0:T(8,128)(2,1)S(1)} collective-permute-done((bf16[512,256]{1,0:T(8,128)(2,1)S(1)}, bf16[512,256]{1,0:T(8,128)(2,1)S(1)}, u32[]{:S(2)}, u32[]{:S(2)}) %collective-permute-start.15) | collective-permute-done | bytes 262176 | tf_op jit(solution)/shard_map/ppermute | solution.py:331
  49.6 4.0 %collective-permute-start.19 = (bf16[512,256]{1,0:T(8,128)(2,1)S(1)}, bf16[512,256]{1,0:T(8,128)(2,1)S(1)}, u32[]{:S(2)}, u32[]{:S(2)}) collective-permute-start(bf16[512,256]{1,0:T(8,128)(2,1)S(1)} %hop.3), channel_id=1, source_target_pairs={{0,4},{1,5},{2,6},{3,7},{4,8},{5,9},{6,10},{7,11},{8,12},{9,13},{1... | collective-permute-start | bytes 786440 | tf_op jit(solution)/shard_map/ppermute | solution.py:331
  53.6 5.5 %collective-permute-start.16 = (bf16[256,256]{1,0:T(8,128)(2,1)S(1)}, bf16[256,256]{1,0:T(8,128)(2,1)S(1)}, u32[]{:S(2)}, u32[]{:S(2)}) collective-permute-start(bf16[256,256]{1,0:T(8,128)(2,1)S(1)} %get-tuple-element.66), channel_id=1, source_target_pairs={{1,2},{3,4},{5,6},{7,8},{9,10},{11,12},{13,14},{2,1},{4,3},{6,5},{... | collective-permute-start | bytes 393224 | tf_op jit(solution)/shard_map/ppermute | solution.py:331
  59.2 0.0 collective-permute-done.17.refs_0_
  59.2 0.7 collective-permute-start.18
  59.9 0.6 collective-permute-start.21
  60.5 0.3 collective-permute-done.14.refs_0_
  60.8 3.4 %collective-permute-done.16.far_side = bf16[256,256]{1,0:T(8,128)(2,1)S(1)} collective-permute-done((bf16[256,256]{1,0:T(8,128)(2,1)S(1)}, bf16[256,256]{1,0:T(8,128)(2,1)S(1)}, u32[]{:S(2)}, u32[]{:S(2)}) %collective-permute-start.16) | collective-permute-done | bytes 131104 | tf_op jit(solution)/shard_map/ppermute | solution.py:331
  64.2 0.0 collective-permute-done.19.refs_1_
  64.2 0.1 hop.4
  64.3 6.1 %collective-permute-start.20 = (bf16[512,256]{1,0:T(8,128)(2,1)S(1)}, bf16[512,256]{1,0:T(8,128)(2,1)S(1)}, u32[]{:S(2)}, u32[]{:S(2)}) collective-permute-start(bf16[512,256]{1,0:T(8,128)(2,1)S(1)} %hop.4), channel_id=1, source_target_pairs={{0,4},{1,5},{2,6},{3,7},{4,8},{5,9},{6,10},{7,11},{8,12},{9,13},{1... | collective-permute-start | bytes 786440 | tf_op jit(solution)/shard_map/ppermute | solution.py:331
  70.3 2.5 %unsmooth.1 = f32[256,512]{1,0:T(8,128)} custom-call(f32[256,512]{1,0:T(8,128)S(1)} %get-tuple-element.59.mid, bf16[2304,256]{1,0:T(8,128)(2,1)S(1)} %collective-permute-done.13.got, bf16[256,256]{1,0:T(8,128)(2,1)S(1)} %collective-permute-done.16.far_side, bf16[3072,256]{1,0:T(8,128)(2,1)S(1)} %get-tuple-element.47.tables, ...), custom_call_target="tpu_custom_call" | custom-call | flops 1006632960 | bytes 4194304 | tf_op jit(solution)/shard_map/unsmooth/pallas_call | solution.py:499
  72.9 0.0 collective-permute-done.18
  72.9 0.0 collective-permute-done.21
  72.9 2.4 %collective-permute-done.20 = bf16[512,256]{1,0:T(8,128)(2,1)S(1)} collective-permute-done((bf16[512,256]{1,0:T(8,128)(2,1)S(1)}, bf16[512,256]{1,0:T(8,128)(2,1)S(1)}, u32[]{:S(2)}, u32[]{:S(2)}) %collective-permute-start.20) | collective-permute-done | bytes 262176 | tf_op jit(solution)/shard_map/ppermute | solution.py:331
  75.3 0.9 %convert_add_fusion = f32[512,256]{1,0:T(8,128)} fusion(bf16[512,256]{1,0:T(8,128)(2,1)S(1)} %collective-permute-done.21, bf16[512,256]{1,0:T(8,128)(2,1)S(1)} %collective-permute-done.20, f32[512,256]{1,0:T(8,128)S(1)} %get-tuple-element.68, bf16[512,256]{1,0:T(8,128)(2,1)S(1)} %collective-permute-done.18), kind=kLoop, calls=%fused_computation | loop fusion | flops 786432 | bytes 1835008 | tf_op jit(solution)/shard_map/add | solution.py:497
  (8 shorter events, 0.1 us)
Async XLA Ops:
  0.6 17.1 %copy-start.5 = (s32[1,2,8]{2,1,0:T(2,128)S(1)}, s32[1,2,8]{2,1,0:T(2,128)}, u32[]{:S(2)}) copy-start(s32[1,2,8]{2,1,0:T(2,128)} %param.13) | copy-start | bytes 196
  0.6 17.1 %copy-start.6 = (s32[1,2,8]{2,1,0:T(2,128)S(1)}, s32[1,2,8]{2,1,0:T(2,128)}, u32[]{:S(2)}) copy-start(s32[1,2,8]{2,1,0:T(2,128)} %param.12) | copy-start | bytes 196
  0.6 9.8 %collective-permute-start.3 = (bf16[512,256]{1,0:T(8,128)(2,1)}, bf16[512,256]{1,0:T(8,128)(2,1)S(1)}, u32[]{:S(2)}, u32[]{:S(2)}) collective-permute-start(bf16[512,256]{1,0:T(8,128)(2,1)} %refs_0_.5), channel_id=1, source_target_pairs={{0,2},{1,3},{2,0},{3,1},{4,6},{5,7},{6,4},{7,5},{8,10},{9,11},{10,... | collective-permute-start | bytes 786440 | tf_op jit(solution)/shard_map/ppermute | solution.py:331
  2.8 9.1 %collective-permute-start.2 = (bf16[512,256]{1,0:T(8,128)(2,1)}, bf16[512,256]{1,0:T(8,128)(2,1)S(1)}, u32[]{:S(2)}, u32[]{:S(2)}) collective-permute-start(bf16[512,256]{1,0:T(8,128)(2,1)} %refs_0_.5), channel_id=1, source_target_pairs={{0,4},{1,5},{2,6},{3,7},{4,8},{5,9},{6,10},{7,11},{8,12},{9,13},{1... | collective-permute-start | bytes 786440 | tf_op jit(solution)/shard_map/ppermute | solution.py:331
  4.1 13.4 %collective-permute-start.1 = (bf16[512,256]{1,0:T(8,128)(2,1)}, bf16[512,256]{1,0:T(8,128)(2,1)S(1)}, u32[]{:S(2)}, u32[]{:S(2)}) collective-permute-start(bf16[512,256]{1,0:T(8,128)(2,1)} %refs_0_.5), channel_id=1, source_target_pairs={{0,12},{1,13},{2,14},{3,15},{4,0},{5,1},{6,2},{7,3},{8,4},{9,5},{1... | collective-permute-start | bytes 786440 | tf_op jit(solution)/shard_map/ppermute | solution.py:331
  7.1 10.6 %collective-permute-start.5 = (f32[256,128]{1,0:T(8,128)S(1)}, f32[256,128]{1,0:T(8,128)S(1)}, u32[]{:S(2)}, u32[]{:S(2)}) collective-permute-start(f32[256,128]{1,0:T(8,128)S(1)} %get-tuple-element.76), channel_id=1, source_target_pairs={{1,2},{3,4},{5,6},{7,8},{9,10},{11,12},{13,14},{2,1},{4,3},{6,5},{... | collective-permute-start | bytes 393224 | tf_op jit(solution)/shard_map/ppermute | solution.py:331
  10.4 10.9 %collective-permute-start.4 = (f32[256,128]{1,0:T(8,128)S(1)}, f32[256,128]{1,0:T(8,128)S(1)}, u32[]{:S(2)}, u32[]{:S(2)}) collective-permute-start(f32[256,128]{1,0:T(8,128)S(1)} %get-tuple-element.77), channel_id=1, source_target_pairs={{0,1},{1,0},{2,3},{3,2},{4,5},{5,4},{6,7},{7,6},{8,9},{9,8},{10,11... | collective-permute-start | bytes 393224 | tf_op jit(solution)/shard_map/ppermute | solution.py:331
  11.9 11.2 %collective-permute-start.6 = (bf16[512,256]{1,0:T(8,128)(2,1)S(1)}, bf16[512,256]{1,0:T(8,128)(2,1)S(1)}, u32[]{:S(2)}, u32[]{:S(2)}) collective-permute-start(bf16[512,256]{1,0:T(8,128)(2,1)S(1)} %collective-permute-done.2.refs_1_), channel_id=1, source_target_pairs={{0,4},{1,5},{2,6},{3,7},{4,8},{5,9},{6,10},{7,11},{8,12},{9,13},{1... | collective-permute-start | bytes 786440 | tf_op jit(solution)/shard_map/ppermute | solution.py:331
  11.9 12.8 %collective-permute-start.8 = (bf16[512,256]{1,0:T(8,128)(2,1)S(1)}, bf16[512,256]{1,0:T(8,128)(2,1)S(1)}, u32[]{:S(2)}, u32[]{:S(2)}) collective-permute-start(bf16[512,256]{1,0:T(8,128)(2,1)S(1)} %collective-permute-done.2.refs_1_), channel_id=1, source_target_pairs={{0,2},{1,3},{2,0},{3,1},{4,6},{5,7},{6,4},{7,5},{8,10},{9,11},{10,... | collective-permute-start | bytes 786440 | tf_op jit(solution)/shard_map/ppermute | solution.py:331
  12.5 1.0 %copy-start = (f32[256,512]{1,0:T(8,128)S(1)}, f32[256,512]{1,0:T(8,128)}, u32[]{:S(2)}) copy-start(f32[256,512]{1,0:T(8,128)} %mid.1) | copy-start | bytes 1572868
  13.5 0.9 %copy-start.2 = (f32[256,256]{1,0:T(8,128)S(1)}, f32[256,256]{1,0:T(8,128)}, u32[]{:S(2)}) copy-start(f32[256,256]{1,0:T(8,128)} %taps) | copy-start | bytes 786436
  17.5 7.5 %collective-permute-start.9 = (bf16[512,256]{1,0:T(8,128)(2,1)S(1)}, bf16[512,256]{1,0:T(8,128)(2,1)S(1)}, u32[]{:S(2)}, u32[]{:S(2)}) collective-permute-start(bf16[512,256]{1,0:T(8,128)(2,1)S(1)} %collective-permute-done.1.refs_3_), channel_id=1, source_target_pairs={{0,2},{1,3},{2,0},{3,1},{4,6},{5,7},{6,4},{7,5},{8,10},{9,11},{10,... | collective-permute-start | bytes 786440 | tf_op jit(solution)/shard_map/ppermute | solution.py:331
  17.7 7.3 %copy-start.1 = (bf16[512,256]{1,0:T(8,128)(2,1)S(1)}, bf16[512,256]{1,0:T(8,128)(2,1)}, u32[]{:S(2)}) copy-start(bf16[512,256]{1,0:T(8,128)(2,1)} %refs_0_.5) | copy-start | bytes 786436
  17.7 5.2 %collective-permute-start = (s32[2,8]{1,0:T(2,128)S(1)}, s32[2,8]{1,0:T(2,128)S(1)}, u32[]{:S(2)}, u32[]{:S(2)}) collective-permute-start(s32[2,8]{1,0:T(2,128)S(1)} %add_bitcast_fusion.ids), channel_id=1, source_target_pairs={{0,1},{1,0},{2,3},{3,2},{4,5},{5,4},{6,7},{7,6},{8,9},{9,8},{10,11... | collective-permute-start | bytes 200 | tf_op jit(solution)/shard_map/ppermute | solution.py:331
  23.1 7.1 %collective-permute-start.7 = (bf16[512,256]{1,0:T(8,128)(2,1)S(1)}, bf16[512,256]{1,0:T(8,128)(2,1)S(1)}, u32[]{:S(2)}, u32[]{:S(2)}) collective-permute-start(bf16[512,256]{1,0:T(8,128)(2,1)S(1)} %collective-permute-done.6.refs_2_), channel_id=1, source_target_pairs={{0,2},{1,3},{2,0},{3,1},{4,6},{5,7},{6,4},{7,5},{8,10},{9,11},{10,... | collective-permute-start | bytes 786440 | tf_op jit(solution)/shard_map/ppermute | solution.py:331
  25.7 8.1 %copy-start.3 = (bf16[2,8,128,512]{3,2,1,0:T(8,128)(2,1)S(1)}, bf16[2,8,128,512]{3,2,1,0:T(8,128)(2,1)}, u32[]{:S(2)}) copy-start(bf16[2,8,128,512]{3,2,1,0:T(8,128)(2,1)} %param.11) | copy-start | bytes 6291460
  25.7 8.1 %copy-start.4 = (s32[2,8,4]{1,2,0:T(4,128)S(1)}, s32[2,8,4]{1,2,0:T(4,128)}, u32[]{:S(2)}) copy-start(s32[2,8,4]{1,2,0:T(4,128)} %param.14) | copy-start | bytes 772
  25.7 8.1 %collective-permute-start.10 = (bf16[1024,256]{1,0:T(8,128)(2,1)S(1)}, bf16[1024,256]{1,0:T(8,128)(2,1)S(1)}, u32[]{:S(2)}, u32[]{:S(2)}) collective-permute-start(bf16[1024,256]{1,0:T(8,128)(2,1)S(1)} %pack.2), channel_id=1, source_target_pairs={{0,1},{1,0},{2,3},{3,2},{4,5},{5,4},{6,7},{7,6},{8,9},{9,8},{10,11... | collective-permute-start | bytes 1572872 | tf_op jit(solution)/shard_map/ppermute | solution.py:331
  29.4 4.5 %collective-permute-start.11 = (bf16[1024,256]{1,0:T(8,128)(2,1)S(1)}, bf16[1024,256]{1,0:T(8,128)(2,1)S(1)}, u32[]{:S(2)}, u32[]{:S(2)}) collective-permute-start(bf16[1024,256]{1,0:T(8,128)(2,1)S(1)} %pack.3), channel_id=1, source_target_pairs={{0,1},{1,0},{2,3},{3,2},{4,5},{5,4},{6,7},{7,6},{8,9},{9,8},{10,11... | collective-permute-start | bytes 1572872 | tf_op jit(solution)/shard_map/ppermute | solution.py:331
  30.2 3.6 %collective-permute-start.12 = (bf16[512,256]{1,0:T(8,128)(2,1)S(1)}, bf16[512,256]{1,0:T(8,128)(2,1)S(1)}, u32[]{:S(2)}, u32[]{:S(2)}) collective-permute-start(bf16[512,256]{1,0:T(8,128)(2,1)S(1)} %collective-permute-done.7.refs_6_), channel_id=1, source_target_pairs={{0,1},{1,0},{2,3},{3,2},{4,5},{5,4},{6,7},{7,6},{8,9},{9,8},{10,11... | collective-permute-start | bytes 786440 | tf_op jit(solution)/shard_map/ppermute | solution.py:331
  37.8 2.9 %collective-permute-start.13 = (bf16[2304,256]{1,0:T(8,128)(2,1)S(1)}, bf16[2304,256]{1,0:T(8,128)(2,1)S(1)}, u32[]{:S(2)}, u32[]{:S(2)}) collective-permute-start(bf16[2304,256]{1,0:T(8,128)(2,1)S(1)} %get-tuple-element.60.own), channel_id=1, source_target_pairs={{0,1},{1,0},{2,3},{3,2},{4,5},{5,4},{6,7},{7,6},{8,9},{9,8},{10,11... | collective-permute-start | bytes 3538952 | tf_op jit(solution)/shard_map/ppermute | solution.py:331
  42.0 7.6 %collective-permute-start.15 = (bf16[512,256]{1,0:T(8,128)(2,1)S(1)}, bf16[512,256]{1,0:T(8,128)(2,1)S(1)}, u32[]{:S(2)}, u32[]{:S(2)}) collective-permute-start(bf16[512,256]{1,0:T(8,128)(2,1)S(1)} %merge_late.1), channel_id=1, source_target_pairs={{0,2},{1,3},{2,0},{3,1},{4,6},{5,7},{6,4},{7,5},{8,10},{9,11},{10,... | collective-permute-start | bytes 786440 | tf_op jit(solution)/shard_map/ppermute | solution.py:331
  45.3 13.8 %collective-permute-start.17 = (bf16[512,256]{1,0:T(8,128)(2,1)S(1)}, bf16[512,256]{1,0:T(8,128)(2,1)S(1)}, u32[]{:S(2)}, u32[]{:S(2)}) collective-permute-start(bf16[512,256]{1,0:T(8,128)(2,1)S(1)} %get-tuple-element.69), channel_id=1, source_target_pairs={{0,2},{1,3},{2,0},{3,1},{4,6},{5,7},{6,4},{7,5},{8,10},{9,11},{10,... | collective-permute-start | bytes 786440 | tf_op jit(solution)/shard_map/ppermute | solution.py:331
  45.5 15.3 %collective-permute-start.14 = (bf16[512,256]{1,0:T(8,128)(2,1)S(1)}, bf16[512,256]{1,0:T(8,128)(2,1)S(1)}, u32[]{:S(2)}, u32[]{:S(2)}) collective-permute-start(bf16[512,256]{1,0:T(8,128)(2,1)S(1)} %get-tuple-element.62), channel_id=1, source_target_pairs={{0,2},{1,3},{2,0},{3,1},{4,6},{5,7},{6,4},{7,5},{8,10},{9,11},{10,... | collective-permute-start | bytes 786440 | tf_op jit(solution)/shard_map/ppermute | solution.py:331
  49.6 14.6 %collective-permute-start.19 = (bf16[512,256]{1,0:T(8,128)(2,1)S(1)}, bf16[512,256]{1,0:T(8,128)(2,1)S(1)}, u32[]{:S(2)}, u32[]{:S(2)}) collective-permute-start(bf16[512,256]{1,0:T(8,128)(2,1)S(1)} %hop.3), channel_id=1, source_target_pairs={{0,4},{1,5},{2,6},{3,7},{4,8},{5,9},{6,10},{7,11},{8,12},{9,13},{1... | collective-permute-start | bytes 786440 | tf_op jit(solution)/shard_map/ppermute | solution.py:331
  53.6 10.6 %collective-permute-start.16 = (bf16[256,256]{1,0:T(8,128)(2,1)S(1)}, bf16[256,256]{1,0:T(8,128)(2,1)S(1)}, u32[]{:S(2)}, u32[]{:S(2)}) collective-permute-start(bf16[256,256]{1,0:T(8,128)(2,1)S(1)} %get-tuple-element.66), channel_id=1, source_target_pairs={{1,2},{3,4},{5,6},{7,8},{9,10},{11,12},{13,14},{2,1},{4,3},{6,5},{... | collective-permute-start | bytes 393224 | tf_op jit(solution)/shard_map/ppermute | solution.py:331
  59.2 13.7 %collective-permute-start.18 = (bf16[512,256]{1,0:T(8,128)(2,1)S(1)}, bf16[512,256]{1,0:T(8,128)(2,1)S(1)}, u32[]{:S(2)}, u32[]{:S(2)}) collective-permute-start(bf16[512,256]{1,0:T(8,128)(2,1)S(1)} %get-tuple-element.71), channel_id=1, source_target_pairs={{0,2},{1,3},{2,0},{3,1},{4,6},{5,7},{6,4},{7,5},{8,10},{9,11},{10,... | collective-permute-start | bytes 786440 | tf_op jit(solution)/shard_map/ppermute | solution.py:331
  59.9 13.0 %collective-permute-start.21 = (bf16[512,256]{1,0:T(8,128)(2,1)S(1)}, bf16[512,256]{1,0:T(8,128)(2,1)S(1)}, u32[]{:S(2)}, u32[]{:S(2)}) collective-permute-start(bf16[512,256]{1,0:T(8,128)(2,1)S(1)} %hop.5), channel_id=1, source_target_pairs={{0,12},{1,13},{2,14},{3,15},{4,0},{5,1},{6,2},{7,3},{8,4},{9,5},{1... | collective-permute-start | bytes 786440 | tf_op jit(solution)/shard_map/ppermute | solution.py:331
  64.3 11.0 %collective-permute-start.20 = (bf16[512,256]{1,0:T(8,128)(2,1)S(1)}, bf16[512,256]{1,0:T(8,128)(2,1)S(1)}, u32[]{:S(2)}, u32[]{:S(2)}) collective-permute-start(bf16[512,256]{1,0:T(8,128)(2,1)S(1)} %hop.4), channel_id=1, source_target_pairs={{0,4},{1,5},{2,6},{3,7},{4,8},{5,9},{6,10},{7,11},{8,12},{9,13},{1... | collective-permute-start | bytes 786440 | tf_op jit(solution)/shard_map/ppermute | solution.py:331

commit v17 on v13

--- a/solution.py
+++ b/solution.py
@@ -488,7 +488,8 @@
     rise = hop(merged[half], back)
     rise, far_side = lax.optimization_barrier((rise, far_side))
     far_side = permute(far_side, odd_even)
-    far_side, own = lax.optimization_barrier((far_side, crossed[0]))
+    other[1], far_side = lax.optimization_barrier((other[1], far_side))
+    _, own = lax.optimization_barrier((other[half + 1], crossed[0]))
     other[0] = flip(own, 2)
     rise = rotate(rise, 1)
     for r in range(half - 1, 0, -1):

time: 77.1 us -> 76.5 us (level)
  the two profiles are of different devices: /device:TPU:0 before, /device:TPU:1 now
where the time goes in v17:
time: 76.5 us; the launch traced here: 76.2 us
  starting transfers between devices  39.1 us (51%)
  waiting for transfers between devices  17.2 us (22%)
  Pallas kernels  15.1 us (20%)
  local copies, waits for them, and re-layouts  2.02 us (3%)
  other arithmetic  1.92 us (3%)
  between operations  0.84 us (1%)
    ppermute x22, starting transfers between devices, permute(): return lax.ppermute(x, 'tm', pairs)  39.1 us
    ppermute x22, waiting for transfers between devices, permute(): return lax.ppermute(x, 'tm', pairs)  17.2 us
    pallas_call x1, Pallas kernels, local(): pl.pallas_call(functools.partial(session_kernel, entries, group, late), o...  4.01 us
    pallas_call x1, Pallas kernels, local(): pl.pallas_call(unsmooth_kernel, out_shape=jax.ShapeDtypeStruct((latent_di...  2.51 us
    unnamed x14, local copies, waits for them, and re-layouts  2.02 us
    pallas_call x1, Pallas kernels, local(): pl.pallas_call(prepare_kernel, out_shape=(jax.ShapeDtypeStruct(table.shap...  2.02 us
    pallas_call x1, Pallas kernels, local(): pl.pallas_call(functools.partial(merge_kernel, entries, late), out_shape=...  1.91 us
    pallas_call x1, Pallas kernels, local(): pl.pallas_call(smooth_kernel, out_shape=jax.ShapeDtypeStruct((latent_dim,...  1.69 us
  transfers between devices with their start and end apart: 22, of which 10 were waited for; matrix products, arithmetic and copies ran while one was open for 1% of the time, Pallas kernels for 13%

profile of v17, /device:TPU:1, one launch (start us, length us, event | category | flops | bytes accessed | tf_op | source)
XLA Modules:
  0.0 76.2 jit_solution(8661567365240373666)
XLA Ops:
  0.6 0.0 copy-start.5
  0.6 0.0 copy-start.6
  0.6 2.1 %collective-permute-start.3 = (bf16[512,256]{1,0:T(8,128)(2,1)}, bf16[512,256]{1,0:T(8,128)(2,1)S(1)}, u32[]{:S(2)}, u32[]{:S(2)}) collective-permute-start(bf16[512,256]{1,0:T(8,128)(2,1)} %refs_0_.5), channel_id=1, source_target_pairs={{0,2},{1,3},{2,0},{3,1},{4,6},{5,7},{6,4},{7,5},{8,10},{9,11},{10,... | collective-permute-start | bytes 786440 | tf_op jit(solution)/shard_map/ppermute | solution.py:331
  2.8 1.3 %collective-permute-start.2 = (bf16[512,256]{1,0:T(8,128)(2,1)}, bf16[512,256]{1,0:T(8,128)(2,1)S(1)}, u32[]{:S(2)}, u32[]{:S(2)}) collective-permute-start(bf16[512,256]{1,0:T(8,128)(2,1)} %refs_0_.5), channel_id=1, source_target_pairs={{0,4},{1,5},{2,6},{3,7},{4,8},{5,9},{6,10},{7,11},{8,12},{9,13},{1... | collective-permute-start | bytes 786440 | tf_op jit(solution)/shard_map/ppermute | solution.py:331
  4.1 2.0 %collective-permute-start.1 = (bf16[512,256]{1,0:T(8,128)(2,1)}, bf16[512,256]{1,0:T(8,128)(2,1)S(1)}, u32[]{:S(2)}, u32[]{:S(2)}) collective-permute-start(bf16[512,256]{1,0:T(8,128)(2,1)} %refs_0_.5), channel_id=1, source_target_pairs={{0,12},{1,13},{2,14},{3,15},{4,0},{5,1},{6,2},{7,3},{8,4},{9,5},{1... | collective-permute-start | bytes 786440 | tf_op jit(solution)/shard_map/ppermute | solution.py:331
  6.1 1.0 %slice_select_fusion = (f32[256,128]{1,0:T(8,128)S(1)}, f32[256,128]{1,0:T(8,128)S(1)}) fusion(f32[256,512]{1,0:T(8,128)} %mid.1, pred[]{:T(512)S(6)} %eq.5), kind=kLoop, calls=%fused_computation.1 | loop fusion | flops 65536 | bytes 524289 | tf_op jit(solution)/shard_map/jit(_where)/select_n | solution.py:349
  7.1 3.3 %collective-permute-start.5 = (f32[256,128]{1,0:T(8,128)S(1)}, f32[256,128]{1,0:T(8,128)S(1)}, u32[]{:S(2)}, u32[]{:S(2)}) collective-permute-start(f32[256,128]{1,0:T(8,128)S(1)} %get-tuple-element.80), channel_id=1, source_target_pairs={{1,2},{3,4},{5,6},{7,8},{9,10},{11,12},{13,14},{2,1},{4,3},{6,5},{... | collective-permute-start | bytes 393224 | tf_op jit(solution)/shard_map/ppermute | solution.py:331
  10.4 0.1 collective-permute-start.4
  10.4 0.0 collective-permute-done.3.refs_4_
  10.5 1.4 %collective-permute-done.2.refs_1_ = bf16[512,256]{1,0:T(8,128)(2,1)S(1)} collective-permute-done((bf16[512,256]{1,0:T(8,128)(2,1)}, bf16[512,256]{1,0:T(8,128)(2,1)S(1)}, u32[]{:S(2)}, u32[]{:S(2)}) %collective-permute-start.2) | collective-permute-done | bytes 262176 | tf_op jit(solution)/shard_map/ppermute | solution.py:331
  11.9 0.0 collective-permute-start.6
  11.9 0.6 collective-permute-start.8
  12.5 1.0 %copy-done = f32[256,512]{1,0:T(8,128)S(1)} copy-done((f32[256,512]{1,0:T(8,128)S(1)}, f32[256,512]{1,0:T(8,128)}, u32[]{:S(2)}) %copy-start) | copy-done | bytes 524312
  13.5 0.9 %copy-done.2 = f32[256,256]{1,0:T(8,128)S(1)} copy-done((f32[256,256]{1,0:T(8,128)S(1)}, f32[256,256]{1,0:T(8,128)}, u32[]{:S(2)}) %copy-start.2) | copy-done | bytes 262168
  14.5 2.0 %prepare.1 = (bf16[3072,256]{1,0:T(8,128)(2,1)S(1)}, f32[256,512]{1,0:T(8,128)S(1)}, f32[256,256]{1,0:T(8,128)S(1)}, f32[256,256]{1,0:T(8,128)S(1)}, f32[256,256]{1,0:T(8,128)S(1)}) custom-call(bf16[3072,256]{1,0:T(8,128)(2,1)} %constant.22.clone.table, f32[256,256]{1,0:T(8,128)S(1)} %copy-done.2, f32[256,512]{1,0:T(8,128)S(1)} %copy-done), custom_call_target="tpu_custom_call" | custom-call | flops 335544320 | bytes 4194304 | tf_op jit(solution)/shard_map/prepare/pallas_call | solution.py:365
  16.5 1.0 %collective-permute-done.1.refs_3_ = bf16[512,256]{1,0:T(8,128)(2,1)S(1)} collective-permute-done((bf16[512,256]{1,0:T(8,128)(2,1)}, bf16[512,256]{1,0:T(8,128)(2,1)S(1)}, u32[]{:S(2)}, u32[]{:S(2)}) %collective-permute-start.1) | collective-permute-done | bytes 262176 | tf_op jit(solution)/shard_map/ppermute | solution.py:331
  17.5 0.2 collective-permute-start.9
  17.7 0.0 copy-done.5
  17.7 0.0 copy-done.6
  17.7 0.0 copy-start.1
  17.7 0.0 collective-permute-done.5.far_side
  17.7 3.5 %collective-permute-start = (s32[2,8]{1,0:T(2,128)S(1)}, s32[2,8]{1,0:T(2,128)S(1)}, u32[]{:S(2)}, u32[]{:S(2)}) collective-permute-start(s32[2,8]{1,0:T(2,128)S(1)} %add_bitcast_fusion.ids), channel_id=1, source_target_pairs={{0,1},{1,0},{2,3},{3,2},{4,5},{5,4},{6,7},{7,6},{8,9},{9,8},{10,11... | collective-permute-start | bytes 200 | tf_op jit(solution)/shard_map/ppermute | solution.py:331
  21.2 0.0 collective-permute-done.4.core_side
  21.2 1.7 %smooth.1.smoothed = bf16[256,512]{1,0:T(8,128)(2,1)S(1)} custom-call(f32[256,512]{1,0:T(8,128)S(1)} %get-tuple-element.48.mid, f32[256,128]{1,0:T(8,128)S(1)} %collective-permute-done.4.core_side, f32[256,128]{1,0:T(8,128)S(1)} %collective-permute-done.5.far_side, bf16[3072,256]{1,0:T(8,128)(2,1)S(1)} %get-tuple-element.49.tables, ...), custom_call_target="tpu_custom_call" | custom-call | flops 1006632960 | bytes 4194304 | tf_op jit(solution)/shard_map/smooth/pallas_call | solution.py:385
  22.9 0.0 collective-permute-done.asked
  22.9 0.2 collective-permute-done.6.refs_2_
  23.1 1.6 %collective-permute-start.7 = (bf16[512,256]{1,0:T(8,128)(2,1)S(1)}, bf16[512,256]{1,0:T(8,128)(2,1)S(1)}, u32[]{:S(2)}, u32[]{:S(2)}) collective-permute-start(bf16[512,256]{1,0:T(8,128)(2,1)S(1)} %collective-permute-done.6.refs_2_), channel_id=1, source_target_pairs={{0,2},{1,3},{2,0},{3,1},{4,6},{5,7},{6,4},{7,5},{8,10},{9,11},{10,... | collective-permute-start | bytes 786440 | tf_op jit(solution)/shard_map/ppermute | solution.py:331
  24.7 0.0 collective-permute-done.8.refs_5_
  24.7 0.2 collective-permute-done.9.refs_6_.refs_7_
  25.0 0.8 %pack.2 = bf16[1024,256]{1,0:T(8,128)(2,1)S(1)} custom-call(s32[2,8]{1,0:T(2,128)S(1)} %collective-permute-done.asked, bf16[512,256]{1,0:T(8,128)(2,1)S(1)} %copy-done.1, bf16[512,256]{1,0:T(8,128)(2,1)S(1)} %collective-permute-done.2.refs_1_, bf16[512,256]{1,0:T(8,128)(2,1)S(1)} %collective-permute-done.6.refs_2_, ...), custom_call_target="tpu_custom_call" | custom-call | bytes 1048576 | tf_op jit(solution)/shard_map/pack/pallas_call | solution.py:400
  25.7 0.0 copy-start.3
  25.8 0.0 copy-start.4
  25.8 2.7 %collective-permute-start.10 = (bf16[1024,256]{1,0:T(8,128)(2,1)S(1)}, bf16[1024,256]{1,0:T(8,128)(2,1)S(1)}, u32[]{:S(2)}, u32[]{:S(2)}) collective-permute-start(bf16[1024,256]{1,0:T(8,128)(2,1)S(1)} %pack.2), channel_id=1, source_target_pairs={{0,1},{1,0},{2,3},{3,2},{4,5},{5,4},{6,7},{7,6},{8,9},{9,8},{10,11... | collective-permute-start | bytes 1572872 | tf_op jit(solution)/shard_map/ppermute | solution.py:331
  28.5 0.8 %pack.3 = bf16[1024,256]{1,0:T(8,128)(2,1)S(1)} custom-call(s32[2,8]{1,0:T(2,128)S(1)} %collective-permute-done.asked, bf16[512,256]{1,0:T(8,128)(2,1)S(1)} %copy-done.1, bf16[512,256]{1,0:T(8,128)(2,1)S(1)} %collective-permute-done.2.refs_1_, bf16[512,256]{1,0:T(8,128)(2,1)S(1)} %collective-permute-done.6.refs_2_, ...), custom_call_target="tpu_custom_call" | custom-call | bytes 1048576 | tf_op jit(solution)/shard_map/pack/pallas_call | solution.py:400
  29.3 0.1 collective-permute-start.11
  29.4 0.8 %collective-permute-done.7.refs_6_ = bf16[512,256]{1,0:T(8,128)(2,1)S(1)} collective-permute-done((bf16[512,256]{1,0:T(8,128)(2,1)S(1)}, bf16[512,256]{1,0:T(8,128)(2,1)S(1)}, u32[]{:S(2)}, u32[]{:S(2)}) %collective-permute-start.7) | collective-permute-done | bytes 262176 | tf_op jit(solution)/shard_map/ppermute | solution.py:331
  30.2 2.4 %collective-permute-start.12 = (bf16[512,256]{1,0:T(8,128)(2,1)S(1)}, bf16[512,256]{1,0:T(8,128)(2,1)S(1)}, u32[]{:S(2)}, u32[]{:S(2)}) collective-permute-start(bf16[512,256]{1,0:T(8,128)(2,1)S(1)} %collective-permute-done.7.refs_6_), channel_id=1, source_target_pairs={{0,1},{1,0},{2,3},{3,2},{4,5},{5,4},{6,7},{7,6},{8,9},{9,8},{10,11... | collective-permute-start | bytes 786440 | tf_op jit(solution)/shard_map/ppermute | solution.py:331
  32.7 1.2 %collective-permute-done.12.late_theirs = bf16[512,256]{1,0:T(8,128)(2,1)S(1)} collective-permute-done((bf16[512,256]{1,0:T(8,128)(2,1)S(1)}, bf16[512,256]{1,0:T(8,128)(2,1)S(1)}, u32[]{:S(2)}, u32[]{:S(2)}) %collective-permute-start.12) | collective-permute-done | bytes 262176 | tf_op jit(solution)/shard_map/ppermute | solution.py:331
  33.8 0.0 collective-permute-done.10.packed
  33.8 0.0 collective-permute-done.11.packed_rest
  33.8 4.0 %session.1 = (f32[256,512]{1,0:T(8,128)S(1)}, bf16[256,256]{1,0:T(8,128)(2,1)S(1)}, bf16[2304,256]{1,0:T(8,128)(2,1)S(1)}) custom-call(s32[2,8]{1,0:T(2,128)S(1)} %add_bitcast_fusion.ids, s32[2,4,8]{2,1,0:T(4,128)S(1)} %bitcast.5, bf16[256,512]{1,0:T(8,128)(2,1)S(1)} %smooth.1.smoothed, bf16[16,128,512]{2,1,0:T(8,128)(2,1)S(1)} %bitcast.4, ...), custom_call_target="tpu_custom_call" | custom-call | flops 1610612736 | bytes 8388608 | tf_op jit(solution)/shard_map/session/pallas_call | solution.py:418
  37.9 0.4 collective-permute-start.13
  38.3 2.5 %collective-permute-done.13.got = bf16[2304,256]{1,0:T(8,128)(2,1)S(1)} collective-permute-done((bf16[2304,256]{1,0:T(8,128)(2,1)S(1)}, bf16[2304,256]{1,0:T(8,128)(2,1)S(1)}, u32[]{:S(2)}, u32[]{:S(2)}) %collective-permute-start.13) | collective-permute-done | bytes 1179680 | tf_op jit(solution)/shard_map/ppermute | solution.py:331
  40.8 1.2 %merge_late.1 = bf16[512,256]{1,0:T(8,128)(2,1)S(1)} custom-call(s32[2,8]{1,0:T(2,128)S(1)} %add_bitcast_fusion.ids, s32[2,8]{1,0:T(2,128)S(1)} %collective-permute-done.asked, bf16[2304,256]{1,0:T(8,128)(2,1)S(1)} %get-tuple-element.62.own, bf16[2304,256]{1,0:T(8,128)(2,1)S(1)} %collective-permute-done.13.got), custom_call_target="tpu_custom_call" | custom-call | bytes 1048576 | tf_op jit(solution)/shard_map/merge_late/pallas_call | solution.py:448
  42.0 1.5 %collective-permute-start.14 = (bf16[512,256]{1,0:T(8,128)(2,1)S(1)}, bf16[512,256]{1,0:T(8,128)(2,1)S(1)}, u32[]{:S(2)}, u32[]{:S(2)}) collective-permute-start(bf16[512,256]{1,0:T(8,128)(2,1)S(1)} %merge_late.1), channel_id=1, source_target_pairs={{0,2},{1,3},{2,0},{3,1},{4,6},{5,7},{6,4},{7,5},{8,10},{9,11},{10,... | collective-permute-start | bytes 786440 | tf_op jit(solution)/shard_map/ppermute | solution.py:331
  43.4 1.9 %merge.1 = (f32[512,256]{1,0:T(8,128)S(1)}, f32[512,256]{1,0:T(8,128)S(1)}, f32[512,256]{1,0:T(8,128)S(1)}, f32[512,256]{1,0:T(8,128)S(1)}, bf16[512,256]{1,0:T(...) custom-call(s32[2,8]{1,0:T(2,128)S(1)} %add_bitcast_fusion.ids, ...), custom_call_target="tpu_custom_call" | custom-call | bytes 5242880 | tf_op jit(solution)/shard_map/merge/pallas_call | solution.py:461
  45.4 0.1 collective-permute-start.17
  45.5 4.1 %collective-permute-done.14.refs_0_ = bf16[512,256]{1,0:T(8,128)(2,1)S(1)} collective-permute-done((bf16[512,256]{1,0:T(8,128)(2,1)S(1)}, bf16[512,256]{1,0:T(8,128)(2,1)S(1)}, u32[]{:S(2)}, u32[]{:S(2)}) %collective-permute-start.14) | collective-permute-done | bytes 262176 | tf_op jit(solution)/shard_map/ppermute | solution.py:331
  49.6 1.4 %collective-permute-start.15 = (bf16[512,256]{1,0:T(8,128)(2,1)S(1)}, bf16[512,256]{1,0:T(8,128)(2,1)S(1)}, u32[]{:S(2)}, u32[]{:S(2)}) collective-permute-start(bf16[512,256]{1,0:T(8,128)(2,1)S(1)} %get-tuple-element.66), channel_id=1, source_target_pairs={{0,2},{1,3},{2,0},{3,1},{4,6},{5,7},{6,4},{7,5},{8,10},{9,11},{10,... | collective-permute-start | bytes 786440 | tf_op jit(solution)/shard_map/ppermute | solution.py:331
  51.0 4.0 %collective-permute-start.19 = (bf16[512,256]{1,0:T(8,128)(2,1)S(1)}, bf16[512,256]{1,0:T(8,128)(2,1)S(1)}, u32[]{:S(2)}, u32[]{:S(2)}) collective-permute-start(bf16[512,256]{1,0:T(8,128)(2,1)S(1)} %hop.3), channel_id=1, source_target_pairs={{0,4},{1,5},{2,6},{3,7},{4,8},{5,9},{6,10},{7,11},{8,12},{9,13},{1... | collective-permute-start | bytes 786440 | tf_op jit(solution)/shard_map/ppermute | solution.py:331
  55.1 4.3 %collective-permute-start.16 = (bf16[256,256]{1,0:T(8,128)(2,1)S(1)}, bf16[256,256]{1,0:T(8,128)(2,1)S(1)}, u32[]{:S(2)}, u32[]{:S(2)}) collective-permute-start(bf16[256,256]{1,0:T(8,128)(2,1)S(1)} %get-tuple-element.70), channel_id=1, source_target_pairs={{1,2},{3,4},{5,6},{7,8},{9,10},{11,12},{13,14},{2,1},{4,3},{6,5},{... | collective-permute-start | bytes 393224 | tf_op jit(solution)/shard_map/ppermute | solution.py:331
  59.3 0.0 collective-permute-done.17.refs_0_
  59.4 1.4 %collective-permute-start.18 = (bf16[512,256]{1,0:T(8,128)(2,1)S(1)}, bf16[512,256]{1,0:T(8,128)(2,1)S(1)}, u32[]{:S(2)}, u32[]{:S(2)}) collective-permute-start(bf16[512,256]{1,0:T(8,128)(2,1)S(1)} %get-tuple-element.75), channel_id=1, source_target_pairs={{0,2},{1,3},{2,0},{3,1},{4,6},{5,7},{6,4},{7,5},{8,10},{9,11},{10,... | collective-permute-start | bytes 786440 | tf_op jit(solution)/shard_map/ppermute | solution.py:331
  60.8 0.1 collective-permute-start.21
  60.9 3.3 %collective-permute-done.16.far_side = bf16[256,256]{1,0:T(8,128)(2,1)S(1)} collective-permute-done((bf16[256,256]{1,0:T(8,128)(2,1)S(1)}, bf16[256,256]{1,0:T(8,128)(2,1)S(1)}, u32[]{:S(2)}, u32[]{:S(2)}) %collective-permute-start.16) | collective-permute-done | bytes 131104 | tf_op jit(solution)/shard_map/ppermute | solution.py:331
  64.2 0.0 collective-permute-done.15.refs_0_
  64.2 0.0 collective-permute-done.19.refs_1_
  64.2 0.1 hop.4
  64.3 6.0 %collective-permute-start.20 = (bf16[512,256]{1,0:T(8,128)(2,1)S(1)}, bf16[512,256]{1,0:T(8,128)(2,1)S(1)}, u32[]{:S(2)}, u32[]{:S(2)}) collective-permute-start(bf16[512,256]{1,0:T(8,128)(2,1)S(1)} %hop.4), channel_id=1, source_target_pairs={{0,4},{1,5},{2,6},{3,7},{4,8},{5,9},{6,10},{7,11},{8,12},{9,13},{1... | collective-permute-start | bytes 786440 | tf_op jit(solution)/shard_map/ppermute | solution.py:331
  70.3 2.5 %unsmooth.1 = f32[256,512]{1,0:T(8,128)} custom-call(f32[256,512]{1,0:T(8,128)S(1)} %get-tuple-element.61.mid, bf16[2304,256]{1,0:T(8,128)(2,1)S(1)} %collective-permute-done.13.got, bf16[256,256]{1,0:T(8,128)(2,1)S(1)} %collective-permute-done.16.far_side, bf16[3072,256]{1,0:T(8,128)(2,1)S(1)} %get-tuple-element.49.tables, ...), custom_call_target="tpu_custom_call" | custom-call | flops 1006632960 | bytes 4194304 | tf_op jit(solution)/shard_map/unsmooth/pallas_call | solution.py:502
  72.8 0.0 collective-permute-done.18
  72.9 0.0 collective-permute-done.21
  72.9 2.5 %collective-permute-done.20 = bf16[512,256]{1,0:T(8,128)(2,1)S(1)} collective-permute-done((bf16[512,256]{1,0:T(8,128)(2,1)S(1)}, bf16[512,256]{1,0:T(8,128)(2,1)S(1)}, u32[]{:S(2)}, u32[]{:S(2)}) %collective-permute-start.20) | collective-permute-done | bytes 262176 | tf_op jit(solution)/shard_map/ppermute | solution.py:331
  75.3 0.9 %convert_add_fusion = f32[512,256]{1,0:T(8,128)} fusion(bf16[512,256]{1,0:T(8,128)(2,1)S(1)} %collective-permute-done.21, bf16[512,256]{1,0:T(8,128)(2,1)S(1)} %collective-permute-done.20, f32[512,256]{1,0:T(8,128)S(1)} %get-tuple-element.72, bf16[512,256]{1,0:T(8,128)(2,1)S(1)} %collective-permute-done.18), kind=kLoop, calls=%fused_computation | loop fusion | flops 786432 | bytes 1835008 | tf_op jit(solution)/shard_map/add | solution.py:500
  (8 shorter events, 0.1 us)
Async XLA Ops:
  0.6 17.1 %copy-start.5 = (s32[1,2,8]{2,1,0:T(2,128)S(1)}, s32[1,2,8]{2,1,0:T(2,128)}, u32[]{:S(2)}) copy-start(s32[1,2,8]{2,1,0:T(2,128)} %param.13) | copy-start | bytes 196
  0.6 17.1 %copy-start.6 = (s32[1,2,8]{2,1,0:T(2,128)S(1)}, s32[1,2,8]{2,1,0:T(2,128)}, u32[]{:S(2)}) copy-start(s32[1,2,8]{2,1,0:T(2,128)} %param.12) | copy-start | bytes 196
  0.6 9.8 %collective-permute-start.3 = (bf16[512,256]{1,0:T(8,128)(2,1)}, bf16[512,256]{1,0:T(8,128)(2,1)S(1)}, u32[]{:S(2)}, u32[]{:S(2)}) collective-permute-start(bf16[512,256]{1,0:T(8,128)(2,1)} %refs_0_.5), channel_id=1, source_target_pairs={{0,2},{1,3},{2,0},{3,1},{4,6},{5,7},{6,4},{7,5},{8,10},{9,11},{10,... | collective-permute-start | bytes 786440 | tf_op jit(solution)/shard_map/ppermute | solution.py:331
  2.8 9.1 %collective-permute-start.2 = (bf16[512,256]{1,0:T(8,128)(2,1)}, bf16[512,256]{1,0:T(8,128)(2,1)S(1)}, u32[]{:S(2)}, u32[]{:S(2)}) collective-permute-start(bf16[512,256]{1,0:T(8,128)(2,1)} %refs_0_.5), channel_id=1, source_target_pairs={{0,4},{1,5},{2,6},{3,7},{4,8},{5,9},{6,10},{7,11},{8,12},{9,13},{1... | collective-permute-start | bytes 786440 | tf_op jit(solution)/shard_map/ppermute | solution.py:331
  4.1 13.4 %collective-permute-start.1 = (bf16[512,256]{1,0:T(8,128)(2,1)}, bf16[512,256]{1,0:T(8,128)(2,1)S(1)}, u32[]{:S(2)}, u32[]{:S(2)}) collective-permute-start(bf16[512,256]{1,0:T(8,128)(2,1)} %refs_0_.5), channel_id=1, source_target_pairs={{0,12},{1,13},{2,14},{3,15},{4,0},{5,1},{6,2},{7,3},{8,4},{9,5},{1... | collective-permute-start | bytes 786440 | tf_op jit(solution)/shard_map/ppermute | solution.py:331
  7.1 10.6 %collective-permute-start.5 = (f32[256,128]{1,0:T(8,128)S(1)}, f32[256,128]{1,0:T(8,128)S(1)}, u32[]{:S(2)}, u32[]{:S(2)}) collective-permute-start(f32[256,128]{1,0:T(8,128)S(1)} %get-tuple-element.80), channel_id=1, source_target_pairs={{1,2},{3,4},{5,6},{7,8},{9,10},{11,12},{13,14},{2,1},{4,3},{6,5},{... | collective-permute-start | bytes 393224 | tf_op jit(solution)/shard_map/ppermute | solution.py:331
  10.4 10.9 %collective-permute-start.4 = (f32[256,128]{1,0:T(8,128)S(1)}, f32[256,128]{1,0:T(8,128)S(1)}, u32[]{:S(2)}, u32[]{:S(2)}) collective-permute-start(f32[256,128]{1,0:T(8,128)S(1)} %get-tuple-element.81), channel_id=1, source_target_pairs={{0,1},{1,0},{2,3},{3,2},{4,5},{5,4},{6,7},{7,6},{8,9},{9,8},{10,11... | collective-permute-start | bytes 393224 | tf_op jit(solution)/shard_map/ppermute | solution.py:331
  11.9 11.2 %collective-permute-start.6 = (bf16[512,256]{1,0:T(8,128)(2,1)S(1)}, bf16[512,256]{1,0:T(8,128)(2,1)S(1)}, u32[]{:S(2)}, u32[]{:S(2)}) collective-permute-start(bf16[512,256]{1,0:T(8,128)(2,1)S(1)} %collective-permute-done.2.refs_1_), channel_id=1, source_target_pairs={{0,4},{1,5},{2,6},{3,7},{4,8},{5,9},{6,10},{7,11},{8,12},{9,13},{1... | collective-permute-start | bytes 786440 | tf_op jit(solution)/shard_map/ppermute | solution.py:331
  11.9 12.8 %collective-permute-start.8 = (bf16[512,256]{1,0:T(8,128)(2,1)S(1)}, bf16[512,256]{1,0:T(8,128)(2,1)S(1)}, u32[]{:S(2)}, u32[]{:S(2)}) collective-permute-start(bf16[512,256]{1,0:T(8,128)(2,1)S(1)} %collective-permute-done.2.refs_1_), channel_id=1, source_target_pairs={{0,2},{1,3},{2,0},{3,1},{4,6},{5,7},{6,4},{7,5},{8,10},{9,11},{10,... | collective-permute-start | bytes 786440 | tf_op jit(solution)/shard_map/ppermute | solution.py:331
  12.5 1.0 %copy-start = (f32[256,512]{1,0:T(8,128)S(1)}, f32[256,512]{1,0:T(8,128)}, u32[]{:S(2)}) copy-start(f32[256,512]{1,0:T(8,128)} %mid.1) | copy-start | bytes 1572868
  13.5 0.9 %copy-start.2 = (f32[256,256]{1,0:T(8,128)S(1)}, f32[256,256]{1,0:T(8,128)}, u32[]{:S(2)}) copy-start(f32[256,256]{1,0:T(8,128)} %taps) | copy-start | bytes 786436
  17.5 7.5 %collective-permute-start.9 = (bf16[512,256]{1,0:T(8,128)(2,1)S(1)}, bf16[512,256]{1,0:T(8,128)(2,1)S(1)}, u32[]{:S(2)}, u32[]{:S(2)}) collective-permute-start(bf16[512,256]{1,0:T(8,128)(2,1)S(1)} %collective-permute-done.1.refs_3_), channel_id=1, source_target_pairs={{0,2},{1,3},{2,0},{3,1},{4,6},{5,7},{6,4},{7,5},{8,10},{9,11},{10,... | collective-permute-start | bytes 786440 | tf_op jit(solution)/shard_map/ppermute | solution.py:331
  17.7 7.3 %copy-start.1 = (bf16[512,256]{1,0:T(8,128)(2,1)S(1)}, bf16[512,256]{1,0:T(8,128)(2,1)}, u32[]{:S(2)}) copy-start(bf16[512,256]{1,0:T(8,128)(2,1)} %refs_0_.5) | copy-start | bytes 786436
  17.7 5.2 %collective-permute-start = (s32[2,8]{1,0:T(2,128)S(1)}, s32[2,8]{1,0:T(2,128)S(1)}, u32[]{:S(2)}, u32[]{:S(2)}) collective-permute-start(s32[2,8]{1,0:T(2,128)S(1)} %add_bitcast_fusion.ids), channel_id=1, source_target_pairs={{0,1},{1,0},{2,3},{3,2},{4,5},{5,4},{6,7},{7,6},{8,9},{9,8},{10,11... | collective-permute-start | bytes 200 | tf_op jit(solution)/shard_map/ppermute | solution.py:331
  23.1 7.1 %collective-permute-start.7 = (bf16[512,256]{1,0:T(8,128)(2,1)S(1)}, bf16[512,256]{1,0:T(8,128)(2,1)S(1)}, u32[]{:S(2)}, u32[]{:S(2)}) collective-permute-start(bf16[512,256]{1,0:T(8,128)(2,1)S(1)} %collective-permute-done.6.refs_2_), channel_id=1, source_target_pairs={{0,2},{1,3},{2,0},{3,1},{4,6},{5,7},{6,4},{7,5},{8,10},{9,11},{10,... | collective-permute-start | bytes 786440 | tf_op jit(solution)/shard_map/ppermute | solution.py:331
  25.7 8.1 %copy-start.3 = (bf16[2,8,128,512]{3,2,1,0:T(8,128)(2,1)S(1)}, bf16[2,8,128,512]{3,2,1,0:T(8,128)(2,1)}, u32[]{:S(2)}) copy-start(bf16[2,8,128,512]{3,2,1,0:T(8,128)(2,1)} %param.11) | copy-start | bytes 6291460
  25.8 8.1 %copy-start.4 = (s32[2,8,4]{1,2,0:T(4,128)S(1)}, s32[2,8,4]{1,2,0:T(4,128)}, u32[]{:S(2)}) copy-start(s32[2,8,4]{1,2,0:T(4,128)} %param.14) | copy-start | bytes 772
  25.8 8.1 %collective-permute-start.10 = (bf16[1024,256]{1,0:T(8,128)(2,1)S(1)}, bf16[1024,256]{1,0:T(8,128)(2,1)S(1)}, u32[]{:S(2)}, u32[]{:S(2)}) collective-permute-start(bf16[1024,256]{1,0:T(8,128)(2,1)S(1)} %pack.2), channel_id=1, source_target_pairs={{0,1},{1,0},{2,3},{3,2},{4,5},{5,4},{6,7},{7,6},{8,9},{9,8},{10,11... | collective-permute-start | bytes 1572872 | tf_op jit(solution)/shard_map/ppermute | solution.py:331
  29.3 4.5 %collective-permute-start.11 = (bf16[1024,256]{1,0:T(8,128)(2,1)S(1)}, bf16[1024,256]{1,0:T(8,128)(2,1)S(1)}, u32[]{:S(2)}, u32[]{:S(2)}) collective-permute-start(bf16[1024,256]{1,0:T(8,128)(2,1)S(1)} %pack.3), channel_id=1, source_target_pairs={{0,1},{1,0},{2,3},{3,2},{4,5},{5,4},{6,7},{7,6},{8,9},{9,8},{10,11... | collective-permute-start | bytes 1572872 | tf_op jit(solution)/shard_map/ppermute | solution.py:331
  30.2 3.6 %collective-permute-start.12 = (bf16[512,256]{1,0:T(8,128)(2,1)S(1)}, bf16[512,256]{1,0:T(8,128)(2,1)S(1)}, u32[]{:S(2)}, u32[]{:S(2)}) collective-permute-start(bf16[512,256]{1,0:T(8,128)(2,1)S(1)} %collective-permute-done.7.refs_6_), channel_id=1, source_target_pairs={{0,1},{1,0},{2,3},{3,2},{4,5},{5,4},{6,7},{7,6},{8,9},{9,8},{10,11... | collective-permute-start | bytes 786440 | tf_op jit(solution)/shard_map/ppermute | solution.py:331
  37.9 2.9 %collective-permute-start.13 = (bf16[2304,256]{1,0:T(8,128)(2,1)S(1)}, bf16[2304,256]{1,0:T(8,128)(2,1)S(1)}, u32[]{:S(2)}, u32[]{:S(2)}) collective-permute-start(bf16[2304,256]{1,0:T(8,128)(2,1)S(1)} %get-tuple-element.62.own), channel_id=1, source_target_pairs={{0,1},{1,0},{2,3},{3,2},{4,5},{5,4},{6,7},{7,6},{8,9},{9,8},{10,11... | collective-permute-start | bytes 3538952 | tf_op jit(solution)/shard_map/ppermute | solution.py:331
  42.0 7.6 %collective-permute-start.14 = (bf16[512,256]{1,0:T(8,128)(2,1)S(1)}, bf16[512,256]{1,0:T(8,128)(2,1)S(1)}, u32[]{:S(2)}, u32[]{:S(2)}) collective-permute-start(bf16[512,256]{1,0:T(8,128)(2,1)S(1)} %merge_late.1), channel_id=1, source_target_pairs={{0,2},{1,3},{2,0},{3,1},{4,6},{5,7},{6,4},{7,5},{8,10},{9,11},{10,... | collective-permute-start | bytes 786440 | tf_op jit(solution)/shard_map/ppermute | solution.py:331
  45.4 14.0 %collective-permute-start.17 = (bf16[512,256]{1,0:T(8,128)(2,1)S(1)}, bf16[512,256]{1,0:T(8,128)(2,1)S(1)}, u32[]{:S(2)}, u32[]{:S(2)}) collective-permute-start(bf16[512,256]{1,0:T(8,128)(2,1)S(1)} %get-tuple-element.73), channel_id=1, source_target_pairs={{0,2},{1,3},{2,0},{3,1},{4,6},{5,7},{6,4},{7,5},{8,10},{9,11},{10,... | collective-permute-start | bytes 786440 | tf_op jit(solution)/shard_map/ppermute | solution.py:331
  49.6 14.7 %collective-permute-start.15 = (bf16[512,256]{1,0:T(8,128)(2,1)S(1)}, bf16[512,256]{1,0:T(8,128)(2,1)S(1)}, u32[]{:S(2)}, u32[]{:S(2)}) collective-permute-start(bf16[512,256]{1,0:T(8,128)(2,1)S(1)} %get-tuple-element.66), channel_id=1, source_target_pairs={{0,2},{1,3},{2,0},{3,1},{4,6},{5,7},{6,4},{7,5},{8,10},{9,11},{10,... | collective-permute-start | bytes 786440 | tf_op jit(solution)/shard_map/ppermute | solution.py:331
  51.0 13.2 %collective-permute-start.19 = (bf16[512,256]{1,0:T(8,128)(2,1)S(1)}, bf16[512,256]{1,0:T(8,128)(2,1)S(1)}, u32[]{:S(2)}, u32[]{:S(2)}) collective-permute-start(bf16[512,256]{1,0:T(8,128)(2,1)S(1)} %hop.3), channel_id=1, source_target_pairs={{0,4},{1,5},{2,6},{3,7},{4,8},{5,9},{6,10},{7,11},{8,12},{9,13},{1... | collective-permute-start | bytes 786440 | tf_op jit(solution)/shard_map/ppermute | solution.py:331
  55.1 9.2 %collective-permute-start.16 = (bf16[256,256]{1,0:T(8,128)(2,1)S(1)}, bf16[256,256]{1,0:T(8,128)(2,1)S(1)}, u32[]{:S(2)}, u32[]{:S(2)}) collective-permute-start(bf16[256,256]{1,0:T(8,128)(2,1)S(1)} %get-tuple-element.70), channel_id=1, source_target_pairs={{1,2},{3,4},{5,6},{7,8},{9,10},{11,12},{13,14},{2,1},{4,3},{6,5},{... | collective-permute-start | bytes 393224 | tf_op jit(solution)/shard_map/ppermute | solution.py:331
  59.4 13.5 %collective-permute-start.18 = (bf16[512,256]{1,0:T(8,128)(2,1)S(1)}, bf16[512,256]{1,0:T(8,128)(2,1)S(1)}, u32[]{:S(2)}, u32[]{:S(2)}) collective-permute-start(bf16[512,256]{1,0:T(8,128)(2,1)S(1)} %get-tuple-element.75), channel_id=1, source_target_pairs={{0,2},{1,3},{2,0},{3,1},{4,6},{5,7},{6,4},{7,5},{8,10},{9,11},{10,... | collective-permute-start | bytes 786440 | tf_op jit(solution)/shard_map/ppermute | solution.py:331
  60.8 12.0 %collective-permute-start.21 = (bf16[512,256]{1,0:T(8,128)(2,1)S(1)}, bf16[512,256]{1,0:T(8,128)(2,1)S(1)}, u32[]{:S(2)}, u32[]{:S(2)}) collective-permute-start(bf16[512,256]{1,0:T(8,128)(2,1)S(1)} %hop.5), channel_id=1, source_target_pairs={{0,12},{1,13},{2,14},{3,15},{4,0},{5,1},{6,2},{7,3},{8,4},{9,5},{1... | collective-permute-start | bytes 786440 | tf_op jit(solution)/shard_map/ppermute | solution.py:331
  64.3 11.0 %collective-permute-start.20 = (bf16[512,256]{1,0:T(8,128)(2,1)S(1)}, bf16[512,256]{1,0:T(8,128)(2,1)S(1)}, u32[]{:S(2)}, u32[]{:S(2)}) collective-permute-start(bf16[512,256]{1,0:T(8,128)(2,1)S(1)} %hop.4), channel_id=1, source_target_pairs={{0,4},{1,5},{2,6},{3,7},{4,8},{5,9},{6,10},{7,11},{8,12},{9,13},{1... | collective-permute-start | bytes 786440 | tf_op jit(solution)/shard_map/ppermute | solution.py:331
